TPU v7x, 256 devices: a whole 4x4x8 slice. The times are simulated.
256 devices in a mesh: rep: 8 (over z_hi, x), fsdp: 32 (over y, z_lo, core).
Axes of the slice: x: 4, y: 4, z: 8 (z_hi: 2, z_lo: 4; z = z_hi * 4 + z_lo), core: 2. Of those that a mesh axis runs over, the one named last changes fastest.
Arguments:
- momentum: float32 [8, 2048, 4096], P('rep', 'fsdp'), may hold values from -6 to 6
- gradient: bfloat16 [8, 2048, 4096], P('rep', 'fsdp'), may hold values from -6 to 6
- weight: bfloat16 [2048, 4096], P('fsdp'), may hold values from -0.09375 to 0.09375
- activations: bfloat16 [131072, 4096], P(('rep', 'fsdp')), may hold values from -6 to 6
Outputs:
- new_momentum: float32 [8, 2048, 4096], P('rep', 'fsdp')
- direction: float32 [2048, 4096], P('fsdp')
- projected: bfloat16 [131072, 2048], P(('rep', 'fsdp'))
All inputs are finite; a program needn't handle non-finite values.
Results may differ from a plain program's by a relative error of at most 0.012.
Values may be sent and summed in bfloat16 or wider, within the bound.
No kernel may reach another device: no remote copies, remote signals or barrier semaphores. Data moves between devices by JAX's collectives and lax.ppermute only.
A program may use at most 192 MiB of HBM per device.

v0:
```python
import math

import jax
import jax.numpy as jnp
from jax import lax
from jax.sharding import PartitionSpec as P

TILE = 64
BAND = 16


highest = lax.Precision.HIGHEST
momentum_decay = 0.9
step_rate = 0.02
soft_width = 0.25


def cosine_rows():
    freq = jnp.arange(BAND, dtype=jnp.float32)[:, None]
    place = jnp.arange(TILE, dtype=jnp.float32)[None, :]
    factor = jnp.where(freq == 0.0, math.sqrt(1.0 / TILE), math.sqrt(2.0 / TILE))
    return factor * jnp.cos(math.pi * (2.0 * place + 1.0) * freq / (2.0 * TILE))


def low_band(field, cosines):
    blocks = field.shape[0] // TILE
    width = field.shape[1]
    row_pass = jnp.einsum(
        "ai,kic->kac", cosines, field.reshape(blocks, TILE, width), precision=highest
    )
    row_pass = row_pass.reshape(blocks, BAND, width // TILE, TILE)
    coefficients = jnp.einsum("bj,katj->katb", cosines, row_pass, precision=highest)
    return coefficients.reshape(blocks * BAND, width // TILE * BAND)


def restore(coefficients, cosines, width):
    blocks = coefficients.shape[0] // BAND
    tiles = width // TILE
    col_pass = jnp.einsum(
        "katb,bj->katj", coefficients.reshape(blocks, BAND, tiles, BAND), cosines, precision=highest
    )
    col_pass = col_pass.reshape(blocks, BAND, width)
    return jnp.einsum("ai,kac->kic", cosines, col_pass, precision=highest).reshape(
        blocks * TILE, width
    )


def soft_sign(update):
    return update * lax.rsqrt(update * update + soft_width)


def forward_rows(activations, rows):
    product = lax.dot_general(
        activations, rows, (((1,), (1,)), ((), ())), preferred_element_type=jnp.float32
    )
    return product.astype(jnp.bfloat16)


def on_device(momentum, gradient, weight, activations):
    cosines = cosine_rows()
    width = weight.shape[1]
    mixed = momentum_decay * momentum[0] + gradient[0].astype(jnp.float32)
    bands = low_band(mixed, cosines)
    new_momentum = (mixed - restore(bands, cosines, width))[None]
    everyone = lax.all_gather(bands.astype(jnp.bfloat16), "rep", axis=0, tiled=True).astype(
        bands.dtype
    )
    total = jnp.sum(everyone.reshape(lax.axis_size("rep"), bands.shape[0], bands.shape[1]), axis=0)
    direction = soft_sign(restore(total, cosines, width))
    new_weight = (weight.astype(jnp.float32) - step_rate * direction).astype(jnp.bfloat16)
    projected = forward_rows(activations, lax.all_gather(new_weight, "fsdp", axis=0, tiled=True))
    return (new_momentum, direction, projected)


def solution(mesh):
    return jax.shard_map(
        on_device,
        mesh=mesh,
        in_specs=(
            P("rep", "fsdp", None),
            P("rep", "fsdp", None),
            P("fsdp", None),
            P(("rep", "fsdp"), None),
        ),
        out_specs=(P("rep", "fsdp", None), P("fsdp", None), P(("rep", "fsdp"), None)),
        check_vma=False,
    )
```

profile of v0, /device:TPU:1, one launch (start us, length us, event | category | flops | bytes accessed | tf_op | source)
XLA Modules:
  0.0 185.8 jit_solution(2072092826363121232)
XLA Ops:
  7.2 0.0 copy-start.2
  7.2 0.0 all-gather.2.cloned.1.call-start
  7.2 2.2 %convolution_bitcast_fusion.2 = f32[1,16,4096]{2,1,0:T(8,128)S(1)} fusion(bf16[1,64,4096]{2,1,0:T(8,128)(2,1)} %param.5, f32[1,64,4096]{2,1,0:T(8,128)} %param.4, f32[64]{0:T(128)S(1)} %add_multiply_fusion, f32[16]{0:T(128)S(1)} %compare_select_fusion), kind=kOutput, calls=%fused_computation.3 | convolution fusion | flops 51121152 | bytes 1835328 | tf_op jit(solution)/shard_map/ai,kic->kac/dot_general | solution.py:28
  9.5 0.2 reshape.70
  9.7 0.0 copy-start
  9.7 0.0 copy-start.1
  9.7 1.3 fusion.35
  11.0 0.2 copy.8
  11.2 0.3 convert_element_type.26
  11.6 40.7 %all_gather.6 = bf16[128,1024]{1,0:T(8,128)(2,1)S(1)} all-gather(bf16[16,1024]{1,0:T(8,128)(2,1)S(1)} %convert_element_type.26), channel_id=1, replica_groups=mesh['rep'=8,'fsdp'=32] {'rep'}, dimensions={0}, use_global_device_ids=true | all-gather | bytes 294912 | tf_op jit(solution)/shard_map/all_gather | solution.py:65
  52.3 0.2 reshape.74
  52.5 0.6 fusion.4
  53.1 0.2 reshape.75
  53.3 0.0 copy-done.2
  53.3 2.4 %subtract_convert_fusion = (bf16[64,4096]{1,0:T(8,128)(2,1)}, f32[64,4096]{1,0:T(8,128)}) fusion(bf16[64,4096]{1,0:T(8,128)(2,1)S(1)} %copy-done.2, f32[16,4096]{1,0:T(8,128)S(1)} %reshape.75, f32[64]{0:T(128)S(1)} %add_multiply_fusion, f32[16]{0:T(128)S(1)} %compare_select_fusion), kind=kOutput, calls=%fused_computation.7 | convolution fusion | flops 52169728 | bytes 2359616 | tf_op jit(solution)/shard_map/ai,kac->kic/dot_general | solution.py:43
  55.7 0.0 all-gather.2.cloned.1.call-update
  55.8 1.0 fusion.6
  56.8 0.2 reshape.71
  57.0 0.0 copy-done
  57.0 0.0 copy-done.1
  57.0 2.1 %fusion = f32[1,64,4096]{2,1,0:T(8,128)} fusion(f32[16,4096]{1,0:T(8,128)S(1)} %reshape.71, bf16[1,64,4096]{2,1,0:T(8,128)(2,1)S(1)} %copy-done.1, f32[1,64,4096]{2,1,0:T(8,128)S(1)} %copy-done, f32[64]{0:T(128)S(1)} %add_multiply_fusion, f32[16]{0:T(128)S(1)} %compare_select_fusion), kind=kOutput, calls=%fused_computation.2 | convolution fusion | flops 51383296 | bytes 2883904 | tf_op jit(solution)/shard_map/ai,kac->kic/dot_general | solution.py:43
  59.1 103.9 %all-gather.2.cloned.1.call-done = bf16[2048,4096]{1,0:T(8,128)(2,1)} async-done(((bf16[64,4096]{1,0:T(8,128)(2,1)}), bf16[2048,4096]{1,0:T(8,128)(2,1)}) %all-gather.2.cloned.1.call-update) | async-done | bytes 16777232 | tf_op jit(solution)/shard_map/all_gather | solution.py:71
  163.0 13.6 %fusion.1 = bf16[512,2048]{0,1:T(8,128)(2,1)S(1)} fusion(bf16[2048,4096]{1,0:T(8,128)(2,1)} %all-gather.2.cloned.1.call-done, bf16[512,4096]{1,0:T(8,128)(2,1)} %param.7), kind=kOutput, calls=%fused_computation.5 | convolution fusion | flops 8590983168 | bytes 23068672 | tf_op jit(solution)/shard_map/dot_general | solution.py:53
  176.6 2.4 %copy.10 = bf16[512,2048]{1,0:T(8,128)(2,1)} copy(bf16[512,2048]{0,1:T(8,128)(2,1)S(1)} %fusion.1) | data formatting | bytes 4194304
  (3 shorter events, 0.1 us)
Async XLA Ops:
  7.2 46.1 %copy-start.2 = (bf16[64,4096]{1,0:T(8,128)(2,1)S(1)}, bf16[64,4096]{1,0:T(8,128)(2,1)}, u32[]{:S(2)}) copy-start(bf16[64,4096]{1,0:T(8,128)(2,1)} %param.6) | copy-start | bytes 1572868
  7.2 155.8 %all-gather.2.cloned.1.call-start = ((), (), s32[]{:S(2)}) async-start(), calls=%async_computation | async-start | bytes 17301504 | tf_op jit(solution)/shard_map/all_gather | solution.py:71
  9.7 47.3 %copy-start = (f32[1,64,4096]{2,1,0:T(8,128)S(1)}, f32[1,64,4096]{2,1,0:T(8,128)}, u32[]{:S(2)}) copy-start(f32[1,64,4096]{2,1,0:T(8,128)} %param.4) | copy-start | bytes 3145732
  9.7 47.3 %copy-start.1 = (bf16[1,64,4096]{2,1,0:T(8,128)(2,1)S(1)}, bf16[1,64,4096]{2,1,0:T(8,128)(2,1)}, u32[]{:S(2)}) copy-start(bf16[1,64,4096]{2,1,0:T(8,128)(2,1)} %param.5) | copy-start | bytes 1572868
Sparse Core Ops, SparseCore 0:
  55.9 107.0 all-gather.1
where the time goes:
time: 186 us
  waiting for transfers between devices  104 us (56%)
  blocking collectives  40.7 us (22%)
  matrix products  23.4 us (13%)
  between operations  14.1 us (8%)
  local copies, waits for them, and re-layouts  3.7 us (2%)
    all_gather x1, waiting for transfers between devices, on_device(): lax.all_gather(new_weight, 'fsdp', axis=0, tiled=True)  104 us
    all_gather x1, blocking collectives, on_device(): lax.all_gather(bands.astype(jnp.bfloat16), 'rep', axis=0, tiled=True)  40.7 us
    dot_general x1, matrix products, forward_rows(): lax.dot_general(activations, rows, (((1,), (1,)), ((), ())), preferred_el...  13.6 us
    dot_general x2, matrix products, restore(): jnp.einsum('ai,kac->kic', cosines, col_pass, precision=highest)  4.54 us
  transfers between devices with their start and end apart: 1, of which 1 were waited for; matrix products, arithmetic and copies ran while one was open for 2% of the time, Pallas kernels for 0%

commit v1 on v0

v1 whole, which is shorter than its diff:
```python
import math

import jax
import jax.numpy as jnp
import numpy as np
from jax import lax
from jax.experimental import pallas as pl
from jax.experimental.pallas import tpu as pltpu
from jax.sharding import PartitionSpec as P

TILE = 64
BAND = 16
WIDE = 8
AXES = ("rep", "fsdp")

momentum_decay = 0.9
step_rate = 0.02
soft_width = 0.25

F32 = jnp.float32
BF16 = jnp.bfloat16
NT = (((1,), (1,)), ((), ()))


def cosine_rows():
    freq = np.arange(BAND, dtype=np.float64)[:, None]
    place = np.arange(TILE, dtype=np.float64)[None, :]
    factor = np.where(freq == 0.0, math.sqrt(1.0 / TILE), math.sqrt(2.0 / TILE))
    return factor * np.cos(math.pi * (2.0 * place + 1.0) * freq / (2.0 * TILE))


def halves(array):
    high = np.asarray(array, np.float32).astype(jnp.bfloat16)
    low = (np.asarray(array, np.float64) - high.astype(np.float64)).astype(jnp.bfloat16)
    return high, low


def split(value):
    high = value.astype(BF16)
    return high, (value - high.astype(F32)).astype(BF16)


def dot(a, b):
    return jnp.dot(a, b, preferred_element_type=F32)


def spot(index):
    rep, rest = divmod(index, 32)
    high, x = divmod(rep, 4)
    y, rest = divmod(rest, 8)
    low, core = divmod(rest, 2)
    return x, y, high * 4 + low, core


def place(x, y, z, core):
    x, y, z = x % 4, y % 4, z % 8
    return ((z // 4) * 4 + x) * 32 + y * 8 + (z % 4) * 2 + core


def fetch(value, source):
    return lax.ppermute(value, AXES, [(place(*source(*spot(i))), i) for i in range(256)])


def along(axis, step):
    def source(x, y, z, core):
        if (core + axis) % 2 == 0:
            return x, y + step, z, core
        if step == 2 and z % 2:
            return x, y, z - 2, core
        return x, y, z + step, core

    return source


def along_x(step):
    return lambda x, y, z, core: (x + step, y, z, core)


def far_z(x, y, z, core):
    return x, y, z + 4, core


def sibling(x, y, z, core):
    return x, y, z, 1 - core


def call(kernel, out_shape, inputs, scratch=(), limit=16, flops=0, smem=0):
    specs = [pl.BlockSpec(memory_space=pltpu.SMEM)] * smem
    specs += [pl.BlockSpec(memory_space=pltpu.VMEM)] * (len(inputs) - smem)
    moved = sum(math.prod(v.shape) * v.dtype.itemsize for v in inputs)
    return pl.pallas_call(
        kernel,
        out_shape=out_shape,
        in_specs=specs,
        out_specs=jax.tree.map(lambda _: pl.BlockSpec(memory_space=pltpu.VMEM), out_shape),
        scratch_shapes=list(scratch),
        compiler_params=pltpu.CompilerParams(vmem_limit_bytes=limit << 20),
        cost_estimate=pl.CostEstimate(flops=flops, bytes_accessed=moved, transcendentals=0),
    )(*inputs)


def stacked(value, wide):
    return jnp.concatenate(
        [value[:, k * wide : (k + 1) * wide] for k in range(value.shape[1] // wide)], axis=0
    )


def mixed_of(momentum, gradient):
    return momentum_decay * momentum[0] + gradient[0].astype(F32)


def bands_kernel(momentum, gradient, cols_hi, cols_lo, rows3, exact, rounded):
    high, low = split(mixed_of(momentum, gradient))
    high = stacked(high, WIDE * TILE)
    low = stacked(low, WIDE * TILE)
    narrow = dot(high, cols_hi[...]) + dot(low, cols_hi[...]) + dot(high, cols_lo[...])
    narrow = jnp.concatenate(
        [narrow[k * TILE : (k + 1) * TILE] for k in range(narrow.shape[0] // TILE)], axis=1
    )
    high, low = split(narrow)
    bands = dot(rows3[...], jnp.concatenate([high, low, high], axis=0))
    exact[...] = bands
    rounded[...] = bands.astype(BF16)


def restored(bands, back_rows3, back_hi, back_lo):
    high, low = split(bands)
    tall = dot(back_rows3[...], jnp.concatenate([high, low, high], axis=0))
    high, low = split(stacked(tall, WIDE * BAND))
    return dot(high, back_hi[...]) + dot(low, back_hi[...]) + dot(high, back_lo[...])


def residual_kernel(momentum, gradient, bands, back_rows3, back_hi, back_lo, out):
    mixed = mixed_of(momentum, gradient)
    low = restored(bands[...], back_rows3, back_hi, back_lo)
    wide = WIDE * TILE
    for k in range(mixed.shape[1] // wide):
        cut = slice(k * wide, (k + 1) * wide)
        out[0, :, cut] = mixed[:, cut] - low[k * TILE : (k + 1) * TILE]


def soft_sign(update):
    return update * lax.rsqrt(update * update + soft_width)


def direction_kernel(total, back_rows3, back_hi, back_lo, out):
    sign = soft_sign(restored(total[...], back_rows3, back_hi, back_lo))
    wide = WIDE * TILE
    for k in range(out.shape[1] // wide):
        out[:, k * wide : (k + 1) * wide] = sign[k * TILE : (k + 1) * TILE]


def forward_kernel(parts, first, own, other, back_rows, back_cols, *refs):
    groups = len(parts)
    refs = list(refs)
    bands = [refs.pop(0) for _ in range(groups)]
    weights = [[refs.pop(0) for _ in range(n)] for n in parts]
    outs = [refs.pop(0) for _ in range(2 * groups)]
    tall, fresh, total = refs
    wide = WIDE * TILE
    steps = own.shape[1] // wide
    start = first[0]

    for g in range(groups):
        spread = dot(back_rows[...], bands[g][...]).astype(BF16)
        for k in range(steps):
            tall[k] = spread[:, k * WIDE * BAND : (k + 1) * WIDE * BAND]

        def renew(k, slot, g=g):
            cut = pl.ds(pl.multiple_of(k * wide, wide), wide)
            sign = soft_sign(dot(tall[k], back_cols[...]))
            row = 0
            for ref in weights[g]:
                rows = ref.shape[0]
                for r in range(0, rows, TILE):
                    new = ref[r : r + TILE, cut].astype(F32) - step_rate * sign[row : row + TILE]
                    spot_ = lax.rem(start + row // TILE, 4) * TILE
                    fresh[slot, pl.ds(pl.multiple_of(spot_, TILE), TILE), :] = new.astype(BF16)
                    row += TILE

        def multiply(k, slot):
            cut = pl.ds(pl.multiple_of(k * wide, wide), wide)
            rows = own.shape[0]
            for n, ref in enumerate((own, other)):
                total[n * rows : (n + 1) * rows] += lax.dot_general(
                    ref[:, cut], fresh[slot], NT, preferred_element_type=F32
                )

        total[...] = jnp.zeros_like(total)
        renew(0, 0)

        @pl.loop(0, steps // 2)
        def _(pair):
            k = pair * 2
            multiply(k, 0)
            renew(k + 1, 1)
            multiply(k + 1, 1)
            renew(lax.rem(k + 2, steps), 0)

        rows = own.shape[0]
        outs[2 * g][...] = total[:rows].astype(BF16)
        outs[2 * g + 1][...] = total[rows:].astype(BF16)


def weave_kernel(where, *refs):
    mine, theirs, out, held = refs[:4], refs[4:8], refs[8], refs[9]
    core, my_start, their_start = where[0], where[1], where[2]
    for g in range(4):
        held[core, lax.rem(my_start + g, 4)] = mine[g][...]
        held[1 - core, lax.rem(their_start + g, 4)] = theirs[g][...]
    for y in range(4):
        for z in range(4):
            left = held[0, z, :, y * TILE : (y + 1) * TILE]
            right = held[1, y, :, z * TILE : (z + 1) * TILE]
            j = (y * 4 + z) * 2 * TILE
            out[:, j : j + 2 * TILE] = jnp.concatenate([left, right], axis=1)


def on_device(momentum, gradient, weight, activations):
    cosines = cosine_rows()
    high, low = halves(cosines)
    eye = np.eye(WIDE)
    cols_hi, cols_lo = (np.kron(eye, np.asarray(h, np.float32).T).astype(jnp.bfloat16) for h in (high, low))
    rows3 = np.concatenate([high, high, low], axis=1)
    back_rows3 = np.concatenate([high.T, high.T, low.T], axis=1)
    back_hi, back_lo = cols_hi.T, cols_lo.T
    back_rows = np.kron(np.eye(4), np.asarray(high, np.float32).T).astype(jnp.bfloat16)
    width = weight.shape[1]
    narrow = width // TILE * BAND
    rows = weight.shape[0]
    tokens = activations.shape[0]

    core = lax.axis_index("fsdp") % 2
    y = lax.axis_index("fsdp") // 8
    z = lax.axis_index("fsdp") // 2 % 4
    first = jnp.where(core == 0, y, z).astype(jnp.int32)
    second = jnp.where(core == 0, z, y).astype(jnp.int32)

    shape = jax.ShapeDtypeStruct
    exact, rounded = call(
        bands_kernel,
        (shape((BAND, narrow), F32), shape((BAND, narrow), BF16)),
        (momentum, gradient, cols_hi, cols_lo, rows3),
    )

    ahead, behind, across = (fetch(weight, along(0, s)) for s in (1, -1, 2))
    line = jnp.concatenate([weight, ahead, across, behind], axis=0)

    total = rounded.astype(F32)
    for part in [fetch(rounded, along_x(s)) for s in (1, -1, 2)]:
        total = total + part.astype(F32)
    sent = total.astype(BF16)
    total = sent.astype(F32) + fetch(sent, far_z).astype(F32)

    new_momentum = call(
        residual_kernel,
        shape(momentum.shape, F32),
        (momentum, gradient, exact, back_rows3, back_hi, back_lo),
    )
    other = fetch(activations, sibling)

    sent = total.astype(BF16)
    ahead, behind, across = (fetch(sent, along(0, s)) for s in (1, -1, 2))
    band_line = jnp.concatenate([sent, ahead, across, behind], axis=0)
    bands = [band_line] + [fetch(band_line, along(1, s)) for s in (1, 2, -1)]

    next_line = fetch(line, along(1, 1))
    last_line = fetch(line, along(1, -1))
    half = line.shape[0] // 2
    far_a = fetch(next_line[:half], along(1, 1))
    far_b = fetch(last_line[half:], along(1, -1))
    lines = [[line], [next_line], [far_a, far_b], [last_line]]

    direction = call(
        direction_kernel,
        shape((rows, width), F32),
        (total, back_rows3, back_hi, back_lo),
    )

    def forward(order):
        parts = [len(lines[g]) for g in order]
        inputs = [first[None], activations, other, back_rows, back_hi]
        inputs += [bands[g] for g in order]
        for g in order:
            inputs += lines[g]
        block = shape((tokens, 4 * rows), BF16)
        return call(
            lambda *refs: forward_kernel(parts, *refs),
            tuple([block] * (2 * len(order))),
            inputs,
            (
                pltpu.VMEM((width // (WIDE * TILE), 4 * rows, WIDE * BAND), BF16),
                pltpu.VMEM((2, 4 * rows, WIDE * TILE), BF16),
                pltpu.VMEM((2 * tokens, 4 * rows), F32),
            ),
            limit=40,
            flops=len(order) * 2 * 2 * tokens * 4 * rows * width,
            smem=1,
        )

    mine, theirs = [None] * 4, [None] * 4
    for order in ([0], [1, 3, 2]):
        result = forward(order)
        for n, g in enumerate(order):
            mine[g] = result[2 * n]
            theirs[g] = fetch(result[2 * n + 1], sibling)
    where = jnp.stack([core.astype(jnp.int32), second, first])
    projected = call(
        weave_kernel,
        shape((tokens, 32 * rows), BF16),
        (where, *mine, *theirs),
        (pltpu.VMEM((2, 4, tokens, 4 * rows), BF16),),
        smem=1,
    )
    return (new_momentum, direction, projected)


def solution(mesh):
    return jax.shard_map(
        on_device,
        mesh=mesh,
        in_specs=(
            P("rep", "fsdp", None),
            P("rep", "fsdp", None),
            P("fsdp", None),
            P(("rep", "fsdp"), None),
        ),
        out_specs=(P("rep", "fsdp", None), P("fsdp", None), P(("rep", "fsdp"), None)),
        check_vma=False,
    )
```

time: 186 us -> 144 us (0.77)
  waiting for transfers between devices: 104 us -> 50.6 us
  starting transfers between devices: 0.04 us -> 42.1 us
  blocking collectives: 40.7 us -> 0 us
  Pallas kernels: 0 us -> 35 us
  matrix products: 23.4 us -> 0 us
  between operations: 14.1 us -> 0.84 us
  local copies, waits for them, and re-layouts: 3.7 us -> 14.7 us
    all_gather x1 -> x0, waiting for transfers between devices: 104 us -> none  [on_device(): lax.all_gather(new_weight, 'fsdp', axis=0, tiled=True)]
    ppermute x0 -> x22, waiting for transfers between devices: none -> 50.6 us  [fetch(): lax.ppermute(value, AXES, [(place(*source(*spot(i))), i) for i in range(2...]
    ppermute x0 -> x22, starting transfers between devices: none -> 42.1 us  [fetch(): lax.ppermute(value, AXES, [(place(*source(*spot(i))), i) for i in range(2...]
    all_gather x1 -> x0, blocking collectives: 40.7 us -> none  [on_device(): lax.all_gather(bands.astype(jnp.bfloat16), 'rep', axis=0, tiled=True)]
    pallas_call x0 -> x6, Pallas kernels: none -> 35 us  [call(): pl.pallas_call(kernel, out_shape=out_shape, in_specs=specs, out_specs=jax...]
    dot_general x7 -> x0, matrix products: 23.4 us -> none  [the longest x1 13.6 us: forward_rows(): lax.dot_general(activations, rows, (((1,), (1,)), ((), ())), preferred_el...]
    unnamed x7 -> x61, local copies, waits for them, and re-layouts: 2.4 us -> 12.4 us
    slice x0 -> x2, local copies, waits for them, and re-layouts: none -> 2.28 us  [the longest x1 1.14 us: on_device(): far_b = fetch(last_line[half:], along(1, -1))]
  transfers between devices with their start and end apart: 1 -> 22, of which waited for: 1 -> 13; matrix products, arithmetic and copies ran while one was open for 2% -> 3% of each run, Pallas kernels for 0% -> 8%
where the time goes in v1:
time: 144 us
  waiting for transfers between devices  50.6 us (35%)
  starting transfers between devices  42.1 us (29%)
  Pallas kernels  35 us (24%)
  local copies, waits for them, and re-layouts  14.7 us (10%)
    ppermute x22, waiting for transfers between devices, fetch(): lax.ppermute(value, AXES, [(place(*source(*spot(i))), i) for i in range(2...  50.6 us
    ppermute x22, starting transfers between devices, fetch(): lax.ppermute(value, AXES, [(place(*source(*spot(i))), i) for i in range(2...  42.1 us
    pallas_call x6, Pallas kernels, call(): pl.pallas_call(kernel, out_shape=out_shape, in_specs=specs, out_specs=jax...  35 us
    unnamed x61, local copies, waits for them, and re-layouts  12.4 us
  transfers between devices with their start and end apart: 22, of which 13 were waited for; matrix products, arithmetic and copies ran while one was open for 3% of the time, Pallas kernels for 8%

profile of v1, /device:TPU:1, one launch (start us, length us, event | category | flops | bytes accessed | tf_op | source)
XLA Modules:
  0.0 143.9 jit_solution(4360789819529095522)
XLA Ops:
  0.6 6.5 %collective-permute-start.8 = (bf16[64,4096]{1,0:T(8,128)(2,1)}, bf16[64,4096]{1,0:T(8,128)(2,1)S(1)}, u32[]{:S(2)}, u32[]{:S(2)}) collective-permute-start(bf16[64,4096]{1,0:T(8,128)(2,1)} %param.13), channel_id=1, source_target_pairs={{8,0},{3,1},{10,2},{5,3},{12,4},{7,5},{14,6},{129,7},{16,8},{11,9}... | collective-permute-start | bytes 1572872 | tf_op jit(solution)/shard_map/ppermute | solution.py:61
  9.4 4.1 %collective-permute-done.8 = bf16[64,4096]{1,0:T(8,128)(2,1)S(1)} collective-permute-done((bf16[64,4096]{1,0:T(8,128)(2,1)}, bf16[64,4096]{1,0:T(8,128)(2,1)S(1)}, u32[]{:S(2)}, u32[]{:S(2)}) %collective-permute-start.8) | collective-permute-done | bytes 524320 | tf_op jit(solution)/shard_map/ppermute | solution.py:61
  13.6 5.6 %collective-permute-done.9 = bf16[64,4096]{1,0:T(8,128)(2,1)S(1)} collective-permute-done((bf16[64,4096]{1,0:T(8,128)(2,1)}, bf16[64,4096]{1,0:T(8,128)(2,1)S(1)}, u32[]{:S(2)}, u32[]{:S(2)}) %collective-permute-start.9) | collective-permute-done | bytes 524320 | tf_op jit(solution)/shard_map/ppermute | solution.py:61
  20.7 2.5 %collective-permute-start.14 = (bf16[256,4096]{1,0:T(8,128)(2,1)S(1)}, bf16[256,4096]{1,0:T(8,128)(2,1)S(1)}, u32[]{:S(2)}, u32[]{:S(2)}) collective-permute-start(bf16[256,4096]{1,0:T(8,128)(2,1)S(1)} %constant_dynamic-update-slice_fusion.refs_6_), channel_id=1, source_target_pairs={{2,0},{9,1},{4,2},{11,3},{6,4},{13,5},{128,6},{15,7},{10,8},{17,9}... | collective-permute-start | bytes 6291464 | tf_op jit(solution)/shard_map/ppermute | solution.py:61
  23.2 23.0 %collective-permute-done.14.refs_8_ = bf16[256,4096]{1,0:T(8,128)(2,1)S(1)} collective-permute-done((bf16[256,4096]{1,0:T(8,128)(2,1)S(1)}, bf16[256,4096]{1,0:T(8,128)(2,1)S(1)}, u32[]{:S(2)}, u32[]{:S(2)}) %collective-permute-start.14) | collective-permute-done | bytes 2097184 | tf_op jit(solution)/shard_map/ppermute | solution.py:61
  47.3 3.4 %collective-permute-start.16 = (bf16[128,4096]{1,0:T(8,128)(2,1)}, bf16[128,4096]{1,0:T(8,128)(2,1)}, u32[]{:S(2)}, u32[]{:S(2)}) collective-permute-start(bf16[128,4096]{1,0:T(8,128)(2,1)} %slice.8), channel_id=1, source_target_pairs={{2,0},{9,1},{4,2},{11,3},{6,4},{13,5},{128,6},{15,7},{10,8},{17,9}... | collective-permute-start | bytes 3145736 | tf_op jit(solution)/shard_map/ppermute | solution.py:61
  52.7 2.5 %collective-permute-start = (bf16[16,1024]{1,0:T(8,128)(2,1)S(1)}, bf16[16,1024]{1,0:T(8,128)(2,1)S(1)}, u32[]{:S(2)}, u32[]{:S(2)}) collective-permute-start(bf16[16,1024]{1,0:T(8,128)(2,1)S(1)} %get-tuple-element.14), channel_id=1, source_target_pairs={{32,0},{33,1},{34,2},{35,3},{36,4},{37,5},{38,6},{39,7},{40,8},{41... | collective-permute-start | bytes 98312 | tf_op jit(solution)/shard_map/ppermute | solution.py:61
  56.3 2.0 %collective-permute-start.2 = (bf16[16,1024]{1,0:T(8,128)(2,1)S(1)}, bf16[16,1024]{1,0:T(8,128)(2,1)S(1)}, u32[]{:S(2)}, u32[]{:S(2)}) collective-permute-start(bf16[16,1024]{1,0:T(8,128)(2,1)S(1)} %get-tuple-element.14), channel_id=1, source_target_pairs={{64,0},{65,1},{66,2},{67,3},{68,4},{69,5},{70,6},{71,7},{72,8},{73... | collective-permute-start | bytes 98312 | tf_op jit(solution)/shard_map/ppermute | solution.py:61
  60.6 4.7 %collective-permute-start.3 = (bf16[16,1024]{1,0:T(8,128)(2,1)S(1)}, bf16[16,1024]{1,0:T(8,128)(2,1)S(1)}, u32[]{:S(2)}, u32[]{:S(2)}) collective-permute-start(bf16[16,1024]{1,0:T(8,128)(2,1)S(1)} %add_convert_fusion), channel_id=1, source_target_pairs={{128,0},{129,1},{130,2},{131,3},{132,4},{133,5},{134,6},{135,7},{1... | collective-permute-start | bytes 98312 | tf_op jit(solution)/shard_map/ppermute | solution.py:61
  65.3 2.5 %collective-permute-done.3 = bf16[16,1024]{1,0:T(8,128)(2,1)S(1)} collective-permute-done((bf16[16,1024]{1,0:T(8,128)(2,1)S(1)}, bf16[16,1024]{1,0:T(8,128)(2,1)S(1)}, u32[]{:S(2)}, u32[]{:S(2)}) %collective-permute-start.3) | collective-permute-done | bytes 32800 | tf_op jit(solution)/shard_map/ppermute | solution.py:61
  68.4 1.7 %collective-permute-start.5 = (bf16[16,1024]{1,0:T(8,128)(2,1)S(1)}, bf16[16,1024]{1,0:T(8,128)(2,1)S(1)}, u32[]{:S(2)}, u32[]{:S(2)}) collective-permute-start(bf16[16,1024]{1,0:T(8,128)(2,1)S(1)} %get-tuple-element.23), channel_id=1, source_target_pairs={{8,0},{3,1},{10,2},{5,3},{12,4},{7,5},{14,6},{129,7},{16,8},{11,9}... | collective-permute-start | bytes 98312 | tf_op jit(solution)/shard_map/ppermute | solution.py:61
  70.1 2.4 %collective-permute-start.6 = (bf16[16,1024]{1,0:T(8,128)(2,1)S(1)}, bf16[16,1024]{1,0:T(8,128)(2,1)S(1)}, u32[]{:S(2)}, u32[]{:S(2)}) collective-permute-start(bf16[16,1024]{1,0:T(8,128)(2,1)S(1)} %get-tuple-element.23), channel_id=1, source_target_pairs={{16,0},{5,1},{18,2},{135,3},{20,4},{129,5},{22,6},{3,7},{24,8},{13... | collective-permute-start | bytes 98312 | tf_op jit(solution)/shard_map/ppermute | solution.py:61
  72.5 1.6 %collective-permute-done.6 = bf16[16,1024]{1,0:T(8,128)(2,1)S(1)} collective-permute-done((bf16[16,1024]{1,0:T(8,128)(2,1)S(1)}, bf16[16,1024]{1,0:T(8,128)(2,1)S(1)}, u32[]{:S(2)}, u32[]{:S(2)}) %collective-permute-start.6) | collective-permute-done | bytes 32800 | tf_op jit(solution)/shard_map/ppermute | solution.py:61
  74.1 2.3 %collective-permute-done.7 = bf16[16,1024]{1,0:T(8,128)(2,1)S(1)} collective-permute-done((bf16[16,1024]{1,0:T(8,128)(2,1)S(1)}, bf16[16,1024]{1,0:T(8,128)(2,1)S(1)}, u32[]{:S(2)}, u32[]{:S(2)}) %collective-permute-start.7) | collective-permute-done | bytes 32800 | tf_op jit(solution)/shard_map/ppermute | solution.py:61
  76.5 2.6 %collective-permute-start.11 = (bf16[64,1024]{1,0:T(8,128)(2,1)S(1)}, bf16[64,1024]{1,0:T(8,128)(2,1)S(1)}, u32[]{:S(2)}, u32[]{:S(2)}) collective-permute-start(bf16[64,1024]{1,0:T(8,128)(2,1)S(1)} %pad_maximum_fusion.refs_5_), channel_id=1, source_target_pairs={{2,0},{9,1},{4,2},{11,3},{6,4},{13,5},{128,6},{15,7},{10,8},{17,9}... | collective-permute-start | bytes 393224 | tf_op jit(solution)/shard_map/ppermute | solution.py:61
  79.1 2.5 %collective-permute-done.11.refs_5_ = bf16[64,1024]{1,0:T(8,128)(2,1)S(1)} collective-permute-done((bf16[64,1024]{1,0:T(8,128)(2,1)S(1)}, bf16[64,1024]{1,0:T(8,128)(2,1)S(1)}, u32[]{:S(2)}, u32[]{:S(2)}) %collective-permute-start.11) | collective-permute-done | bytes 131104 | tf_op jit(solution)/shard_map/ppermute | solution.py:61
  84.2 3.4 %collective-permute-done.13.refs_7_ = bf16[64,1024]{1,0:T(8,128)(2,1)} collective-permute-done((bf16[64,1024]{1,0:T(8,128)(2,1)S(1)}, bf16[64,1024]{1,0:T(8,128)(2,1)}, u32[]{:S(2)}, u32[]{:S(2)}) %collective-permute-start.13) | collective-permute-done | bytes 131104 | tf_op jit(solution)/shard_map/ppermute | solution.py:61
  87.7 2.2 %copy-done.1 = bf16[512,4096]{1,0:T(8,128)(2,1)S(1)} copy-done((bf16[512,4096]{1,0:T(8,128)(2,1)S(1)}, bf16[512,4096]{1,0:T(8,128)(2,1)}, u32[]{:S(2)}) %copy-start.1) | copy-done | bytes 4194328
  93.9 19.4 %shard_map.134 = (bf16[512,256]{1,0:T(8,128)(2,1)S(1)}, bf16[512,256]{1,0:T(8,128)(2,1)}, bf16[512,256]{1,0:T(8,128)(2,1)S(1)}, bf16[512,256]{1,0:T(8,128)(2,1)}...) custom-call(s32[1]{0:T(128)} %bitcast.2.refs_0_, bf16[512,4096]{1,0:T(8,128)(2,1)S(1)} %copy-done.1, ...), custom_call_target="tpu_custom_call" | custom-call | flops 6442450944 | bytes 15237124 | tf_op jit(solution)/shard_map/pallas_call | solution.py:91
  114.1 10.9 %collective-permute-start.19 = (bf16[512,256]{1,0:T(8,128)(2,1)}, bf16[512,256]{1,0:T(8,128)(2,1)}, u32[]{:S(2)}, u32[]{:S(2)}) collective-permute-start(bf16[512,256]{1,0:T(8,128)(2,1)} %get-tuple-element.20), channel_id=1, source_target_pairs={{1,0},{0,1},{3,2},{2,3},{5,4},{4,5},{7,6},{6,7},{9,8},{8,9},{11,10... | collective-permute-start | bytes 786440 | tf_op jit(solution)/shard_map/ppermute | solution.py:61
  125.5 8.1 %shard_map.133 = (bf16[512,256]{1,0:T(8,128)(2,1)S(1)}, bf16[512,256]{1,0:T(8,128)(2,1)}) custom-call(s32[1]{0:T(128)} %bitcast.2.refs_0_, bf16[512,4096]{1,0:T(8,128)(2,1)S(1)} %copy-done.1, bf16[512,4096]{1,0:T(8,128)(2,1)} %collective-permute-done.4.refs_2_, bf16[256,64]{1,0:T(8,128)(2,1)S(1)} %copy-done.22, bf16[128,512]{1,0:T(8,128)(2,1)S(1)} %copy-done.4, ...), custom_call_target="tpu_custom_call" | custom-call | flops 2147483648 | bytes 10780676 | tf_op jit(solution)/shard_map/pallas_call | solution.py:91
  136.3 1.7 %shard_map.131 = f32[1,64,4096]{2,1,0:T(8,128)} custom-call(f32[1,64,4096]{2,1,0:T(8,128)S(1)} %copy-done, bf16[1,64,4096]{2,1,0:T(8,128)(2,1)S(1)} %copy-done.3, f32[16,1024]{1,0:T(8,128)S(1)} %copy-done.25, bf16[64,48]{1,0:T(8,128)(2,1)S(1)} %copy-done.23, bf16[128,512]{1,0:T(8,128)(2,1)S(1)} %copy-done.4, bf16[128,512]{1,0:T(8,128)(2,1)S(1)} %copy-done.9), custom_call_target="tpu_custom_call" | custom-call | bytes 1906688 | tf_op jit(solution)/shard_map/pallas_call | solution.py:91
  138.8 1.7 %shard_map.132 = f32[64,4096]{1,0:T(8,128)} custom-call(f32[16,1024]{1,0:T(8,128)S(1)} %copy-done.18, bf16[64,48]{1,0:T(8,128)(2,1)S(1)} %copy-done.23, bf16[128,512]{1,0:T(8,128)(2,1)S(1)} %copy-done.4, bf16[128,512]{1,0:T(8,128)(2,1)S(1)} %copy-done.9), custom_call_target="tpu_custom_call" | custom-call | bytes 333824 | tf_op jit(solution)/shard_map/pallas_call | solution.py:91
  140.6 3.4 %shard_map.135 = bf16[512,2048]{1,0:T(8,128)(2,1)} custom-call(s32[3]{0:T(128)S(1)} %pad_add_fusion.where, bf16[512,256]{1,0:T(8,128)(2,1)S(1)} %copy-done.17, bf16[512,256]{1,0:T(8,128)(2,1)S(1)} %copy-done.11, bf16[512,256]{1,0:T(8,128)(2,1)S(1)} %copy-done.15, bf16[512,256]{1,0:T(8,128)(2,1)S(1)} %copy-done.13, ...), custom_call_target="tpu_custom_call" | custom-call | bytes 2097164 | tf_op jit(solution)/shard_map/pallas_call | solution.py:91
  (94 shorter events, 22.5 us)
Async XLA Ops:
  0.6 12.9 %collective-permute-start.8 = (bf16[64,4096]{1,0:T(8,128)(2,1)}, bf16[64,4096]{1,0:T(8,128)(2,1)S(1)}, u32[]{:S(2)}, u32[]{:S(2)}) collective-permute-start(bf16[64,4096]{1,0:T(8,128)(2,1)} %param.13), channel_id=1, source_target_pairs={{8,0},{3,1},{10,2},{5,3},{12,4},{7,5},{14,6},{129,7},{16,8},{11,9}... | collective-permute-start | bytes 1572872 | tf_op jit(solution)/shard_map/ppermute | solution.py:61
  7.1 12.1 %collective-permute-start.9 = (bf16[64,4096]{1,0:T(8,128)(2,1)}, bf16[64,4096]{1,0:T(8,128)(2,1)S(1)}, u32[]{:S(2)}, u32[]{:S(2)}) collective-permute-start(bf16[64,4096]{1,0:T(8,128)(2,1)} %param.13), channel_id=1, source_target_pairs={{16,0},{5,1},{18,2},{135,3},{20,4},{129,5},{22,6},{3,7},{24,8},{13... | collective-permute-start | bytes 1572872 | tf_op jit(solution)/shard_map/ppermute | solution.py:61
  8.3 12.3 %collective-permute-start.10 = (bf16[64,4096]{1,0:T(8,128)(2,1)}, bf16[64,4096]{1,0:T(8,128)(2,1)S(1)}, u32[]{:S(2)}, u32[]{:S(2)}) collective-permute-start(bf16[64,4096]{1,0:T(8,128)(2,1)} %param.13), channel_id=1, source_target_pairs={{24,0},{135,1},{26,2},{1,3},{28,4},{3,5},{30,6},{5,7},{0,8},{143,9... | collective-permute-start | bytes 1572872 | tf_op jit(solution)/shard_map/ppermute | solution.py:61
  8.3 79.4 %collective-permute-start.4 = (bf16[512,4096]{1,0:T(8,128)(2,1)}, bf16[512,4096]{1,0:T(8,128)(2,1)}, u32[]{:S(2)}, u32[]{:S(2)}) collective-permute-start(bf16[512,4096]{1,0:T(8,128)(2,1)} %refs_1_.3), channel_id=1, source_target_pairs={{1,0},{0,1},{3,2},{2,3},{5,4},{4,5},{7,6},{6,7},{9,8},{8,9},{11,10... | collective-permute-start | bytes 12582920 | tf_op jit(solution)/shard_map/ppermute | solution.py:61
  20.7 25.5 %collective-permute-start.14 = (bf16[256,4096]{1,0:T(8,128)(2,1)S(1)}, bf16[256,4096]{1,0:T(8,128)(2,1)S(1)}, u32[]{:S(2)}, u32[]{:S(2)}) collective-permute-start(bf16[256,4096]{1,0:T(8,128)(2,1)S(1)} %constant_dynamic-update-slice_fusion.refs_6_), channel_id=1, source_target_pairs={{2,0},{9,1},{4,2},{11,3},{6,4},{13,5},{128,6},{15,7},{10,8},{17,9}... | collective-permute-start | bytes 6291464 | tf_op jit(solution)/shard_map/ppermute | solution.py:61
  23.2 27.5 %collective-permute-start.15 = (bf16[256,4096]{1,0:T(8,128)(2,1)S(1)}, bf16[256,4096]{1,0:T(8,128)(2,1)S(1)}, u32[]{:S(2)}, u32[]{:S(2)}) collective-permute-start(bf16[256,4096]{1,0:T(8,128)(2,1)S(1)} %constant_dynamic-update-slice_fusion.refs_6_), channel_id=1, source_target_pairs={{134,0},{25,1},{0,2},{27,3},{2,4},{29,5},{4,6},{31,7},{142,8},{1,9... | collective-permute-start | bytes 6291464 | tf_op jit(solution)/shard_map/ppermute | solution.py:61
  47.3 40.3 %copy-start.4 = (bf16[128,512]{1,0:T(8,128)(2,1)S(1)}, bf16[128,512]{1,0:T(8,128)(2,1)}, u32[]{:S(2)}) copy-start(bf16[128,512]{1,0:T(8,128)(2,1)} %constant.67.clone.back_hi.refs_4_) | copy-start | bytes 393220
  47.3 40.3 %copy-start.21 = (bf16[256,64]{1,0:T(8,128)(2,1)S(1)}, bf16[256,64]{1,0:T(8,128)(2,1)}, u32[]{:S(2)}) copy-start(bf16[256,64]{1,0:T(8,128)(2,1)} %constant.69.clone.refs_3_) | copy-start | bytes 98308
  47.3 40.3 %collective-permute-start.16 = (bf16[128,4096]{1,0:T(8,128)(2,1)}, bf16[128,4096]{1,0:T(8,128)(2,1)}, u32[]{:S(2)}, u32[]{:S(2)}) collective-permute-start(bf16[128,4096]{1,0:T(8,128)(2,1)} %slice.8), channel_id=1, source_target_pairs={{2,0},{9,1},{4,2},{11,3},{6,4},{13,5},{128,6},{15,7},{10,8},{17,9}... | collective-permute-start | bytes 3145736 | tf_op jit(solution)/shard_map/ppermute | solution.py:61
  51.9 35.7 %collective-permute-start.17 = (bf16[128,4096]{1,0:T(8,128)(2,1)}, bf16[128,4096]{1,0:T(8,128)(2,1)}, u32[]{:S(2)}, u32[]{:S(2)}) collective-permute-start(bf16[128,4096]{1,0:T(8,128)(2,1)} %slice.9), channel_id=1, source_target_pairs={{134,0},{25,1},{0,2},{27,3},{2,4},{29,5},{4,6},{31,7},{142,8},{1,9... | collective-permute-start | bytes 3145736 | tf_op jit(solution)/shard_map/ppermute | solution.py:61
  52.7 3.5 %collective-permute-start = (bf16[16,1024]{1,0:T(8,128)(2,1)S(1)}, bf16[16,1024]{1,0:T(8,128)(2,1)S(1)}, u32[]{:S(2)}, u32[]{:S(2)}) collective-permute-start(bf16[16,1024]{1,0:T(8,128)(2,1)S(1)} %get-tuple-element.14), channel_id=1, source_target_pairs={{32,0},{33,1},{34,2},{35,3},{36,4},{37,5},{38,6},{39,7},{40,8},{41... | collective-permute-start | bytes 98312 | tf_op jit(solution)/shard_map/ppermute | solution.py:61
  55.2 4.0 %collective-permute-start.1 = (bf16[16,1024]{1,0:T(8,128)(2,1)S(1)}, bf16[16,1024]{1,0:T(8,128)(2,1)S(1)}, u32[]{:S(2)}, u32[]{:S(2)}) collective-permute-start(bf16[16,1024]{1,0:T(8,128)(2,1)S(1)} %get-tuple-element.14), channel_id=1, source_target_pairs={{96,0},{97,1},{98,2},{99,3},{100,4},{101,5},{102,6},{103,7},{104,8... | collective-permute-start | bytes 98312 | tf_op jit(solution)/shard_map/ppermute | solution.py:61
  56.3 4.3 %collective-permute-start.2 = (bf16[16,1024]{1,0:T(8,128)(2,1)S(1)}, bf16[16,1024]{1,0:T(8,128)(2,1)S(1)}, u32[]{:S(2)}, u32[]{:S(2)}) collective-permute-start(bf16[16,1024]{1,0:T(8,128)(2,1)S(1)} %get-tuple-element.14), channel_id=1, source_target_pairs={{64,0},{65,1},{66,2},{67,3},{68,4},{69,5},{70,6},{71,7},{72,8},{73... | collective-permute-start | bytes 98312 | tf_op jit(solution)/shard_map/ppermute | solution.py:61
  60.6 7.2 %collective-permute-start.3 = (bf16[16,1024]{1,0:T(8,128)(2,1)S(1)}, bf16[16,1024]{1,0:T(8,128)(2,1)S(1)}, u32[]{:S(2)}, u32[]{:S(2)}) collective-permute-start(bf16[16,1024]{1,0:T(8,128)(2,1)S(1)} %add_convert_fusion), channel_id=1, source_target_pairs={{128,0},{129,1},{130,2},{131,3},{132,4},{133,5},{134,6},{135,7},{1... | collective-permute-start | bytes 98312 | tf_op jit(solution)/shard_map/ppermute | solution.py:61
  68.4 4.1 %collective-permute-start.5 = (bf16[16,1024]{1,0:T(8,128)(2,1)S(1)}, bf16[16,1024]{1,0:T(8,128)(2,1)S(1)}, u32[]{:S(2)}, u32[]{:S(2)}) collective-permute-start(bf16[16,1024]{1,0:T(8,128)(2,1)S(1)} %get-tuple-element.23), channel_id=1, source_target_pairs={{8,0},{3,1},{10,2},{5,3},{12,4},{7,5},{14,6},{129,7},{16,8},{11,9}... | collective-permute-start | bytes 98312 | tf_op jit(solution)/shard_map/ppermute | solution.py:61
  70.1 4.1 %collective-permute-start.6 = (bf16[16,1024]{1,0:T(8,128)(2,1)S(1)}, bf16[16,1024]{1,0:T(8,128)(2,1)S(1)}, u32[]{:S(2)}, u32[]{:S(2)}) collective-permute-start(bf16[16,1024]{1,0:T(8,128)(2,1)S(1)} %get-tuple-element.23), channel_id=1, source_target_pairs={{16,0},{5,1},{18,2},{135,3},{20,4},{129,5},{22,6},{3,7},{24,8},{13... | collective-permute-start | bytes 98312 | tf_op jit(solution)/shard_map/ppermute | solution.py:61
  72.5 4.0 %collective-permute-start.7 = (bf16[16,1024]{1,0:T(8,128)(2,1)S(1)}, bf16[16,1024]{1,0:T(8,128)(2,1)S(1)}, u32[]{:S(2)}, u32[]{:S(2)}) collective-permute-start(bf16[16,1024]{1,0:T(8,128)(2,1)S(1)} %get-tuple-element.23), channel_id=1, source_target_pairs={{24,0},{135,1},{26,2},{1,3},{28,4},{3,5},{30,6},{5,7},{0,8},{143,9... | collective-permute-start | bytes 98312 | tf_op jit(solution)/shard_map/ppermute | solution.py:61
  76.5 5.1 %collective-permute-start.11 = (bf16[64,1024]{1,0:T(8,128)(2,1)S(1)}, bf16[64,1024]{1,0:T(8,128)(2,1)S(1)}, u32[]{:S(2)}, u32[]{:S(2)}) collective-permute-start(bf16[64,1024]{1,0:T(8,128)(2,1)S(1)} %pad_maximum_fusion.refs_5_), channel_id=1, source_target_pairs={{2,0},{9,1},{4,2},{11,3},{6,4},{13,5},{128,6},{15,7},{10,8},{17,9}... | collective-permute-start | bytes 393224 | tf_op jit(solution)/shard_map/ppermute | solution.py:61
  79.1 5.1 %collective-permute-start.12 = (bf16[64,1024]{1,0:T(8,128)(2,1)S(1)}, bf16[64,1024]{1,0:T(8,128)(2,1)}, u32[]{:S(2)}, u32[]{:S(2)}) collective-permute-start(bf16[64,1024]{1,0:T(8,128)(2,1)S(1)} %pad_maximum_fusion.refs_5_), channel_id=1, source_target_pairs={{134,0},{25,1},{0,2},{27,3},{2,4},{29,5},{4,6},{31,7},{142,8},{1,9... | collective-permute-start | bytes 393224 | tf_op jit(solution)/shard_map/ppermute | solution.py:61
  82.2 5.4 %collective-permute-start.13 = (bf16[64,1024]{1,0:T(8,128)(2,1)S(1)}, bf16[64,1024]{1,0:T(8,128)(2,1)}, u32[]{:S(2)}, u32[]{:S(2)}) collective-permute-start(bf16[64,1024]{1,0:T(8,128)(2,1)S(1)} %pad_maximum_fusion.refs_5_), channel_id=1, source_target_pairs={{4,0},{17,1},{134,2},{19,3},{128,4},{21,5},{2,6},{23,7},{12,8},{25... | collective-permute-start | bytes 393224 | tf_op jit(solution)/shard_map/ppermute | solution.py:61
  114.1 26.4 %collective-permute-start.19 = (bf16[512,256]{1,0:T(8,128)(2,1)}, bf16[512,256]{1,0:T(8,128)(2,1)}, u32[]{:S(2)}, u32[]{:S(2)}) collective-permute-start(bf16[512,256]{1,0:T(8,128)(2,1)} %get-tuple-element.20), channel_id=1, source_target_pairs={{1,0},{0,1},{3,2},{2,3},{5,4},{4,5},{7,6},{6,7},{9,8},{8,9},{11,10... | collective-permute-start | bytes 786440 | tf_op jit(solution)/shard_map/ppermute | solution.py:61
  125.0 15.5 %collective-permute-start.20 = (bf16[512,256]{1,0:T(8,128)(2,1)}, bf16[512,256]{1,0:T(8,128)(2,1)}, u32[]{:S(2)}, u32[]{:S(2)}) collective-permute-start(bf16[512,256]{1,0:T(8,128)(2,1)} %get-tuple-element.21), channel_id=1, source_target_pairs={{1,0},{0,1},{3,2},{2,3},{5,4},{4,5},{7,6},{6,7},{9,8},{8,9},{11,10... | collective-permute-start | bytes 786440 | tf_op jit(solution)/shard_map/ppermute | solution.py:61
  125.0 15.5 %collective-permute-start.21 = (bf16[512,256]{1,0:T(8,128)(2,1)}, bf16[512,256]{1,0:T(8,128)(2,1)}, u32[]{:S(2)}, u32[]{:S(2)}) collective-permute-start(bf16[512,256]{1,0:T(8,128)(2,1)} %get-tuple-element.22), channel_id=1, source_target_pairs={{1,0},{0,1},{3,2},{2,3},{5,4},{4,5},{7,6},{6,7},{9,8},{8,9},{11,10... | collective-permute-start | bytes 786440 | tf_op jit(solution)/shard_map/ppermute | solution.py:61
  134.3 6.2 %collective-permute-start.18 = (bf16[512,256]{1,0:T(8,128)(2,1)}, bf16[512,256]{1,0:T(8,128)(2,1)S(1)}, u32[]{:S(2)}, u32[]{:S(2)}) collective-permute-start(bf16[512,256]{1,0:T(8,128)(2,1)} %get-tuple-element.19), channel_id=1, source_target_pairs={{1,0},{0,1},{3,2},{2,3},{5,4},{4,5},{7,6},{6,7},{9,8},{8,9},{11,10... | collective-permute-start | bytes 786440 | tf_op jit(solution)/shard_map/ppermute | solution.py:61
  (27 other events, 326.0 us)

commit v2 on v1

--- a/solution.py
+++ b/solution.py
@@ -84,9 +84,11 @@
     return x, y, z, 1 - core
 
 
-def call(kernel, out_shape, inputs, scratch=(), limit=16, flops=0, smem=0):
+def call(kernel, out_shape, inputs, scratch=(), limit=16, flops=0, smem=0, kept=()):
     specs = [pl.BlockSpec(memory_space=pltpu.SMEM)] * smem
     specs += [pl.BlockSpec(memory_space=pltpu.VMEM)] * (len(inputs) - smem)
+    specs += [pl.BlockSpec(memory_space=pl.ANY)] * len(kept)
+    inputs = (*inputs, *kept)
     moved = sum(math.prod(v.shape) * v.dtype.itemsize for v in inputs)
     return pl.pallas_call(
         kernel,
@@ -150,68 +152,73 @@
         out[:, k * wide : (k + 1) * wide] = sign[k * TILE : (k + 1) * TILE]
 
 
-def forward_kernel(parts, first, own, other, back_rows, back_cols, *refs):
+def forward_kernel(parts, first, back_rows, back_cols, *refs):
     groups = len(parts)
     refs = list(refs)
     bands = [refs.pop(0) for _ in range(groups)]
+    tokens = [refs.pop(0) for _ in range(2)]
     weights = [[refs.pop(0) for _ in range(n)] for n in parts]
     outs = [refs.pop(0) for _ in range(2 * groups)]
-    tall, fresh, total = refs
+    kept, raw, *fresh, token_sem, raw_sem = refs
     wide = WIDE * TILE
-    steps = own.shape[1] // wide
+    rows, width = kept.shape[1:]
     start = first[0]
 
+    pieces = []
     for g in range(groups):
-        spread = dot(back_rows[...], bands[g][...]).astype(BF16)
-        for k in range(steps):
-            tall[k] = spread[:, k * WIDE * BAND : (k + 1) * WIDE * BAND]
-
-        def renew(k, slot, g=g):
-            cut = pl.ds(pl.multiple_of(k * wide, wide), wide)
-            sign = soft_sign(dot(tall[k], back_cols[...]))
-            row = 0
-            for ref in weights[g]:
-                rows = ref.shape[0]
-                for r in range(0, rows, TILE):
-                    new = ref[r : r + TILE, cut].astype(F32) - step_rate * sign[row : row + TILE]
-                    spot_ = lax.rem(start + row // TILE, 4) * TILE
-                    fresh[slot, pl.ds(pl.multiple_of(spot_, TILE), TILE), :] = new.astype(BF16)
-                    row += TILE
-
-        def multiply(k, slot):
-            cut = pl.ds(pl.multiple_of(k * wide, wide), wide)
-            rows = own.shape[0]
-            for n, ref in enumerate((own, other)):
-                total[n * rows : (n + 1) * rows] += lax.dot_general(
-                    ref[:, cut], fresh[slot], NT, preferred_element_type=F32
-                )
-
-        total[...] = jnp.zeros_like(total)
-        renew(0, 0)
-
-        @pl.loop(0, steps // 2)
-        def _(pair):
-            k = pair * 2
-            multiply(k, 0)
-            renew(k + 1, 1)
-            multiply(k + 1, 1)
-            renew(lax.rem(k + 2, steps), 0)
-
-        rows = own.shape[0]
-        outs[2 * g][...] = total[:rows].astype(BF16)
-        outs[2 * g + 1][...] = total[rows:].astype(BF16)
+        found = []
+        for ref in weights[g]:
+            found += [(ref, r) for r in range(0, ref.shape[0], TILE)]
+        pieces.append(found)
+    raw_copy = {}
+    for g in range(groups):
+        for f, (ref, r) in enumerate(pieces[g]):
+            raw_copy[g, f] = pltpu.make_async_copy(ref.at[r : r + TILE], raw.at[g, f], raw_sem.at[g, f])
+    per = tokens[0].shape[0] // rows
+    token_copy = [
+        pltpu.make_async_copy(tokens[t // per].at[pl.ds(t % per * rows, rows)], kept.at[t], token_sem.at[t])
+        for t in range(4)
+    ]
+    for f in range(4):
+        raw_copy[0, f].start()
+    for copy in token_copy:
+        copy.start()
+    for g in range(1, groups):
+        for f in range(4):
+            raw_copy[g, f].start()
+
+    def renew(g, f):
+        raw_copy[g, f].wait()
+        tall = dot(back_rows[...], bands[g][f * BAND : (f + 1) * BAND]).astype(BF16)
+        sign = soft_sign(dot(stacked(tall, WIDE * BAND), back_cols[...]))
+        at = pl.ds(pl.multiple_of(lax.rem(start + f, 4) * TILE, TILE), TILE)
+        for k in range(width // wide):
+            cut = slice(k * wide, (k + 1) * wide)
+            new = raw[g, f, :, cut].astype(F32) - step_rate * sign[k * TILE : (k + 1) * TILE]
+            fresh[g % 2][at, cut] = new.astype(BF16)
+
+    for f in range(4):
+        renew(0, f)
+    for g in range(groups):
+        for t in range(4):
+            if g == 0:
+                token_copy[t].wait()
+            product = lax.dot_general(kept[t], fresh[g % 2][...], NT, preferred_element_type=F32)
+            outs[2 * g + t // per][t % per * rows : (t % per + 1) * rows] = product.astype(BF16)
+            if g + 1 < groups:
+                renew(g + 1, t)
 
 
 def weave_kernel(where, *refs):
     mine, theirs, out, held = refs[:4], refs[4:8], refs[8], refs[9]
     core, my_start, their_start = where[0], where[1], where[2]
     for g in range(4):
-        held[core, lax.rem(my_start + g, 4)] = mine[g][...]
-        held[1 - core, lax.rem(their_start + g, 4)] = theirs[g][...]
+        held[1 - core, lax.rem(my_start + g, 4)] = mine[g][...]
+        held[core, lax.rem(their_start + g, 4)] = theirs[g][...]
     for y in range(4):
         for z in range(4):
-            left = held[0, z, :, y * TILE : (y + 1) * TILE]
-            right = held[1, y, :, z * TILE : (z + 1) * TILE]
+            left = held[0, y, :, z * TILE : (z + 1) * TILE]
+            right = held[1, z, :, y * TILE : (y + 1) * TILE]
             j = (y * 4 + z) * 2 * TILE
             out[:, j : j + 2 * TILE] = jnp.concatenate([left, right], axis=1)
 
@@ -224,7 +231,7 @@
     rows3 = np.concatenate([high, high, low], axis=1)
     back_rows3 = np.concatenate([high.T, high.T, low.T], axis=1)
     back_hi, back_lo = cols_hi.T, cols_lo.T
-    back_rows = np.kron(np.eye(4), np.asarray(high, np.float32).T).astype(jnp.bfloat16)
+    back_rows = high.T
     width = weight.shape[1]
     narrow = width // TILE * BAND
     rows = weight.shape[0]
@@ -243,13 +250,19 @@
         (momentum, gradient, cols_hi, cols_lo, rows3),
     )
 
-    ahead, behind, across = (fetch(weight, along(0, s)) for s in (1, -1, 2))
-    line = jnp.concatenate([weight, ahead, across, behind], axis=0)
-
-    total = rounded.astype(F32)
-    for part in [fetch(rounded, along_x(s)) for s in (1, -1, 2)]:
-        total = total + part.astype(F32)
+    def after(value, *others):
+        return lax.optimization_barrier((value, *others))[0]
+
+    swapped = fetch(weight, sibling)
+    swapped = after(swapped, rounded)
+    ahead, behind, across = (fetch(swapped, along(0, s)) for s in (1, -1, 2))
+
+    total = rounded.astype(F32) + fetch(rounded, along_x(1)).astype(F32)
+    total = total + fetch(total.astype(BF16), along_x(2)).astype(F32)
     sent = total.astype(BF16)
+    other = fetch(after(activations, sent), sibling)
+    line = jnp.concatenate([swapped, ahead, across, behind], axis=0)
+    line = after(line, sent)
     total = sent.astype(F32) + fetch(sent, far_z).astype(F32)
 
     new_momentum = call(
@@ -257,12 +270,15 @@
         shape(momentum.shape, F32),
         (momentum, gradient, exact, back_rows3, back_hi, back_lo),
     )
-    other = fetch(activations, sibling)
-
-    sent = total.astype(BF16)
-    ahead, behind, across = (fetch(sent, along(0, s)) for s in (1, -1, 2))
-    band_line = jnp.concatenate([sent, ahead, across, behind], axis=0)
-    bands = [band_line] + [fetch(band_line, along(1, s)) for s in (1, 2, -1)]
+
+    def gather(value):
+        pair = jnp.concatenate([value, fetch(value, along(0, 1))], axis=0)
+        return pair, fetch(pair, along(0, 2))
+
+    band_line = jnp.concatenate(gather(total.astype(BF16)), axis=0)
+    near, far = gather(fetch(band_line, sibling))
+    blocks = jnp.concatenate([near, far], axis=0).reshape(4, 4, BAND, narrow)
+    bands = [blocks[:, g].reshape(4 * BAND, narrow) for g in range(4)]
 
     next_line = fetch(line, along(1, 1))
     last_line = fetch(line, along(1, -1))
@@ -279,27 +295,29 @@
 
     def forward(order):
         parts = [len(lines[g]) for g in order]
-        inputs = [first[None], activations, other, back_rows, back_hi]
-        inputs += [bands[g] for g in order]
-        for g in order:
-            inputs += lines[g]
+        inputs = [first[None], back_rows, back_hi] + [bands[g] for g in order]
+        kept = [activations, other] + [line for g in order for line in lines[g]]
         block = shape((tokens, 4 * rows), BF16)
         return call(
             lambda *refs: forward_kernel(parts, *refs),
             tuple([block] * (2 * len(order))),
             inputs,
             (
-                pltpu.VMEM((width // (WIDE * TILE), 4 * rows, WIDE * BAND), BF16),
-                pltpu.VMEM((2, 4 * rows, WIDE * TILE), BF16),
-                pltpu.VMEM((2 * tokens, 4 * rows), F32),
+                pltpu.VMEM((4, tokens // 2, width), BF16),
+                pltpu.VMEM((len(order), 4, rows, width), BF16),
+                pltpu.VMEM((4 * rows, width), BF16),
+                pltpu.VMEM((4 * rows, width), BF16),
+                pltpu.SemaphoreType.DMA((4,)),
+                pltpu.SemaphoreType.DMA((len(order), 4)),
             ),
-            limit=40,
+            limit=48,
             flops=len(order) * 2 * 2 * tokens * 4 * rows * width,
             smem=1,
+            kept=kept,
         )
 
     mine, theirs = [None] * 4, [None] * 4
-    for order in ([0], [1, 3, 2]):
+    for order in ([0], [1, 3], [2]):
         result = forward(order)
         for n, g in enumerate(order):
             mine[g] = result[2 * n]

time: 144 us -> 149 us (1.035); the launches traced: 144 us -> 146 us
  starting transfers between devices: 42.1 us -> 60.6 us
  waiting for transfers between devices: 50.6 us -> 35.7 us
  local copies, waits for them, and re-layouts: 14.7 us -> 9.19 us
  Pallas kernels: 35 us -> 37.4 us
  other arithmetic: 0.75 us -> 2.62 us
    ppermute x22 -> x21, starting transfers between devices: 42.1 us -> 60.6 us  [fetch(): lax.ppermute(value, AXES, [(place(*source(*spot(i))), i) for i in range(2...]
    ppermute x22 -> x21, waiting for transfers between devices: 50.6 us -> 35.7 us  [fetch(): lax.ppermute(value, AXES, [(place(*source(*spot(i))), i) for i in range(2...]
    unnamed x61 -> x48, local copies, waits for them, and re-layouts: 12.4 us -> 6.95 us
    pallas_call x6 -> x7, Pallas kernels: 35 us -> 37.4 us  [call(): pl.pallas_call(kernel, out_shape=out_shape, in_specs=specs, out_specs=jax...]
    concatenate x1 -> x5, other arithmetic: 0.01 us -> 1.89 us  [the longest x1 0.98 us: on_device(): blocks = jnp.concatenate([near, far], axis=0).reshape(4, 4, BAND, narrow)]
  transfers between devices with their start and end apart: 22 -> 21, of which waited for: 13 -> 12; matrix products, arithmetic and copies ran while one was open for 3% -> 3% of each run, Pallas kernels for 8% -> 23%
where the time goes in v2:
time: 149 us; the launch traced here: 146 us
  starting transfers between devices  60.6 us (41%)
  Pallas kernels  37.4 us (25%)
  waiting for transfers between devices  35.7 us (24%)
  local copies, waits for them, and re-layouts  9.19 us (6%)
  other arithmetic  2.62 us (2%)
    ppermute x21, starting transfers between devices, fetch(): lax.ppermute(value, AXES, [(place(*source(*spot(i))), i) for i in range(2...  60.6 us
    pallas_call x7, Pallas kernels, call(): pl.pallas_call(kernel, out_shape=out_shape, in_specs=specs, out_specs=jax...  37.4 us
    ppermute x21, waiting for transfers between devices, fetch(): lax.ppermute(value, AXES, [(place(*source(*spot(i))), i) for i in range(2...  35.7 us
    unnamed x48, local copies, waits for them, and re-layouts  6.95 us
  transfers between devices with their start and end apart: 21, of which 12 were waited for; matrix products, arithmetic and copies ran while one was open for 3% of the time, Pallas kernels for 23%

profile of v2, /device:TPU:1, one launch (start us, length us, event | category | flops | bytes accessed | tf_op | source)
XLA Modules:
  0.0 146.4 jit_solution(5751981377136541443)
XLA Ops:
  6.2 3.4 %collective-permute-start = (bf16[16,1024]{1,0:T(8,128)(2,1)S(1)}, bf16[16,1024]{1,0:T(8,128)(2,1)S(1)}, u32[]{:S(2)}, u32[]{:S(2)}) collective-permute-start(bf16[16,1024]{1,0:T(8,128)(2,1)S(1)} %get-tuple-element.17), channel_id=1, source_target_pairs={{32,0},{33,1},{34,2},{35,3},{36,4},{37,5},{38,6},{39,7},{40,8},{41... | collective-permute-start | bytes 98312 | tf_op jit(solution)/shard_map/ppermute | solution.py:61
  10.6 2.1 %collective-permute-start.1 = (bf16[16,1024]{1,0:T(8,128)(2,1)S(1)}, bf16[16,1024]{1,0:T(8,128)(2,1)S(1)}, u32[]{:S(2)}, u32[]{:S(2)}) collective-permute-start(bf16[16,1024]{1,0:T(8,128)(2,1)S(1)} %fusion), channel_id=1, source_target_pairs={{64,0},{65,1},{66,2},{67,3},{68,4},{69,5},{70,6},{71,7},{72,8},{73... | collective-permute-start | bytes 98312 | tf_op jit(solution)/shard_map/ppermute | solution.py:61
  12.6 2.3 %collective-permute-done.1 = bf16[16,1024]{1,0:T(8,128)(2,1)S(1)} collective-permute-done((bf16[16,1024]{1,0:T(8,128)(2,1)S(1)}, bf16[16,1024]{1,0:T(8,128)(2,1)S(1)}, u32[]{:S(2)}, u32[]{:S(2)}) %collective-permute-start.1) | collective-permute-done | bytes 32800 | tf_op jit(solution)/shard_map/ppermute | solution.py:61
  14.9 4.1 %collective-permute-start.8 = (bf16[512,4096]{1,0:T(8,128)(2,1)}, bf16[512,4096]{1,0:T(8,128)(2,1)}, u32[]{:S(2)}, u32[]{:S(2)}) collective-permute-start(bf16[512,4096]{1,0:T(8,128)(2,1)} %refs_4_.3), channel_id=1, source_target_pairs={{1,0},{0,1},{3,2},{2,3},{5,4},{4,5},{7,6},{6,7},{9,8},{8,9},{11,10... | collective-permute-start | bytes 12582920 | tf_op jit(solution)/shard_map/ppermute | solution.py:61
  19.1 7.3 %collective-permute-done.9 = bf16[64,4096]{1,0:T(8,128)(2,1)S(1)} collective-permute-done((bf16[64,4096]{1,0:T(8,128)(2,1)}, bf16[64,4096]{1,0:T(8,128)(2,1)S(1)}, u32[]{:S(2)}, u32[]{:S(2)}) %collective-permute-start.9) | collective-permute-done | bytes 524320 | tf_op jit(solution)/shard_map/ppermute | solution.py:61
  26.7 5.1 %collective-permute-start.11 = (bf16[64,4096]{1,0:T(8,128)(2,1)S(1)}, bf16[64,4096]{1,0:T(8,128)(2,1)S(1)}, u32[]{:S(2)}, u32[]{:S(2)}) collective-permute-start(bf16[64,4096]{1,0:T(8,128)(2,1)S(1)} %collective-permute-done.9), channel_id=1, source_target_pairs={{16,0},{5,1},{18,2},{135,3},{20,4},{129,5},{22,6},{3,7},{24,8},{13... | collective-permute-start | bytes 1572872 | tf_op jit(solution)/shard_map/ppermute | solution.py:61
  31.8 5.7 %collective-permute-done.12 = bf16[64,4096]{1,0:T(8,128)(2,1)S(1)} collective-permute-done((bf16[64,4096]{1,0:T(8,128)(2,1)S(1)}, bf16[64,4096]{1,0:T(8,128)(2,1)S(1)}, u32[]{:S(2)}, u32[]{:S(2)}) %collective-permute-start.12) | collective-permute-done | bytes 524320 | tf_op jit(solution)/shard_map/ppermute | solution.py:61
  38.0 5.6 %collective-permute-done.10 = bf16[64,4096]{1,0:T(8,128)(2,1)S(1)} collective-permute-done((bf16[64,4096]{1,0:T(8,128)(2,1)S(1)}, bf16[64,4096]{1,0:T(8,128)(2,1)S(1)}, u32[]{:S(2)}, u32[]{:S(2)}) %collective-permute-start.10) | collective-permute-done | bytes 524320 | tf_op jit(solution)/shard_map/ppermute | solution.py:61
  43.8 2.8 %collective-permute-start.13 = (bf16[256,4096]{1,0:T(8,128)(2,1)S(1)}, bf16[256,4096]{1,0:T(8,128)(2,1)S(1)}, u32[]{:S(2)}, u32[]{:S(2)}) collective-permute-start(bf16[256,4096]{1,0:T(8,128)(2,1)S(1)} %pad_maximum_fusion.refs_6_), channel_id=1, source_target_pairs={{2,0},{9,1},{4,2},{11,3},{6,4},{13,5},{128,6},{15,7},{10,8},{17,9}... | collective-permute-start | bytes 6291464 | tf_op jit(solution)/shard_map/ppermute | solution.py:61
  46.6 3.3 %collective-permute-start.2 = (bf16[16,1024]{1,0:T(8,128)(2,1)S(1)}, bf16[16,1024]{1,0:T(8,128)(2,1)S(1)}, u32[]{:S(2)}, u32[]{:S(2)}) collective-permute-start(bf16[16,1024]{1,0:T(8,128)(2,1)S(1)} %add_convert_fusion), channel_id=1, source_target_pairs={{128,0},{129,1},{130,2},{131,3},{132,4},{133,5},{134,6},{135,7},{1... | collective-permute-start | bytes 98312 | tf_op jit(solution)/shard_map/ppermute | solution.py:61
  49.9 3.7 %collective-permute-done.2 = bf16[16,1024]{1,0:T(8,128)(2,1)S(1)} collective-permute-done((bf16[16,1024]{1,0:T(8,128)(2,1)S(1)}, bf16[16,1024]{1,0:T(8,128)(2,1)S(1)}, u32[]{:S(2)}, u32[]{:S(2)}) %collective-permute-start.2) | collective-permute-done | bytes 32800 | tf_op jit(solution)/shard_map/ppermute | solution.py:61
  54.3 3.4 %collective-permute-start.3 = (bf16[16,1024]{1,0:T(8,128)(2,1)S(1)}, bf16[16,1024]{1,0:T(8,128)(2,1)S(1)}, u32[]{:S(2)}, u32[]{:S(2)}) collective-permute-start(bf16[16,1024]{1,0:T(8,128)(2,1)S(1)} %get-tuple-element.33), channel_id=1, source_target_pairs={{8,0},{3,1},{10,2},{5,3},{12,4},{7,5},{14,6},{129,7},{16,8},{11,9}... | collective-permute-start | bytes 98312 | tf_op jit(solution)/shard_map/ppermute | solution.py:61
  58.9 2.6 %collective-permute-start.4 = (bf16[32,1024]{1,0:T(8,128)(2,1)S(1)}, bf16[32,1024]{1,0:T(8,128)(2,1)S(1)}, u32[]{:S(2)}, u32[]{:S(2)}) collective-permute-start(bf16[32,1024]{1,0:T(8,128)(2,1)S(1)} %pad_maximum_fusion.4), channel_id=1, source_target_pairs={{16,0},{5,1},{18,2},{135,3},{20,4},{129,5},{22,6},{3,7},{24,8},{13... | collective-permute-start | bytes 196616 | tf_op jit(solution)/shard_map/ppermute | solution.py:61
  61.5 2.5 %collective-permute-done.4 = bf16[32,1024]{1,0:T(8,128)(2,1)S(1)} collective-permute-done((bf16[32,1024]{1,0:T(8,128)(2,1)S(1)}, bf16[32,1024]{1,0:T(8,128)(2,1)S(1)}, u32[]{:S(2)}, u32[]{:S(2)}) %collective-permute-start.4) | collective-permute-done | bytes 65568 | tf_op jit(solution)/shard_map/ppermute | solution.py:61
  64.0 24.5 %collective-permute-start.5 = (bf16[64,1024]{1,0:T(8,128)(2,1)S(1)}, bf16[64,1024]{1,0:T(8,128)(2,1)S(1)}, u32[]{:S(2)}, u32[]{:S(2)}) collective-permute-start(bf16[64,1024]{1,0:T(8,128)(2,1)S(1)} %pad_maximum_fusion.3), channel_id=1, source_target_pairs={{1,0},{0,1},{3,2},{2,3},{5,4},{4,5},{7,6},{6,7},{9,8},{8,9},{11,10... | collective-permute-start | bytes 393224 | tf_op jit(solution)/shard_map/ppermute | solution.py:61
  89.5 4.1 %collective-permute-done.6 = bf16[64,1024]{1,0:T(8,128)(2,1)S(1)} collective-permute-done((bf16[64,1024]{1,0:T(8,128)(2,1)S(1)}, bf16[64,1024]{1,0:T(8,128)(2,1)S(1)}, u32[]{:S(2)}, u32[]{:S(2)}) %collective-permute-start.6) | collective-permute-done | bytes 131104 | tf_op jit(solution)/shard_map/ppermute | solution.py:61
  95.4 2.9 %collective-permute-start.15 = (bf16[128,4096]{1,0:T(8,128)(2,1)}, bf16[128,4096]{1,0:T(8,128)(2,1)S(1)}, u32[]{:S(2)}, u32[]{:S(2)}) collective-permute-start(bf16[128,4096]{1,0:T(8,128)(2,1)} %slice.28), channel_id=1, source_target_pairs={{2,0},{9,1},{4,2},{11,3},{6,4},{13,5},{128,6},{15,7},{10,8},{17,9}... | collective-permute-start | bytes 3145736 | tf_op jit(solution)/shard_map/ppermute | solution.py:61
  101.8 8.0 %shard_map.133 = (bf16[512,256]{1,0:T(8,128)(2,1)S(1)}, bf16[512,256]{1,0:T(8,128)(2,1)}) custom-call(s32[1]{0:T(128)} %bitcast.2.refs_0_, bf16[64,16]{1,0:T(8,128)(2,1)S(1)} %copy-done.20, bf16[128,512]{1,0:T(8,128)(2,1)S(1)} %copy-done.2, bf16[64,1024]{1,0:T(8,128)(2,1)S(1)} %bitcast.17, bf16[512,4096]{1,0:T(8,128)(2,1)} %refs_4_.3, ...), custom_call_target="tpu_custom_call" | custom-call | flops 2147483648 | bytes 10749956 | tf_op jit(solution)/shard_map/pallas_call | solution.py:93
  109.9 5.1 %collective-permute-start.17 = (bf16[512,256]{1,0:T(8,128)(2,1)}, bf16[512,256]{1,0:T(8,128)(2,1)S(1)}, u32[]{:S(2)}, u32[]{:S(2)}) collective-permute-start(bf16[512,256]{1,0:T(8,128)(2,1)} %get-tuple-element.25), channel_id=1, source_target_pairs={{1,0},{0,1},{3,2},{2,3},{5,4},{4,5},{7,6},{6,7},{9,8},{8,9},{11,10... | collective-permute-start | bytes 786440 | tf_op jit(solution)/shard_map/ppermute | solution.py:61
  115.0 12.5 %shard_map.134 = (bf16[512,256]{1,0:T(8,128)(2,1)S(1)}, bf16[512,256]{1,0:T(8,128)(2,1)}, bf16[512,256]{1,0:T(8,128)(2,1)S(1)}, bf16[512,256]{1,0:T(8,128)(2,1)}) custom-call(s32[1]{0:T(128)} %bitcast.2.refs_0_, bf16[64,16]{1,0:T(8,128)(2,1)S(1)} %copy-done.20, bf16[128,512]{1,0:T(8,128)(2,1)S(1)} %copy-done.2, bf16[64,1024]{1,0:T(8,128)(2,1)S(1)} %bitcast.19, ...), custom_call_target="tpu_custom_call" | custom-call | flops 4294967296 | bytes 12978180 | tf_op jit(solution)/shard_map/pallas_call | solution.py:93
  127.9 9.6 %shard_map.135 = (bf16[512,256]{1,0:T(8,128)(2,1)S(1)}, bf16[512,256]{1,0:T(8,128)(2,1)}) custom-call(s32[1]{0:T(128)} %bitcast.2.refs_0_, bf16[64,16]{1,0:T(8,128)(2,1)S(1)} %copy-done.20, bf16[128,512]{1,0:T(8,128)(2,1)S(1)} %copy-done.2, bf16[64,1024]{1,0:T(8,128)(2,1)S(1)} %bitcast.16, bf16[512,4096]{1,0:T(8,128)(2,1)} %refs_4_.3, ...), custom_call_target="tpu_custom_call" | custom-call | flops 2147483648 | bytes 10749956 | tf_op jit(solution)/shard_map/pallas_call | solution.py:93
  139.6 1.7 %shard_map.131 = f32[1,64,4096]{2,1,0:T(8,128)} custom-call(f32[1,64,4096]{2,1,0:T(8,128)S(1)} %copy-done.1, bf16[1,64,4096]{2,1,0:T(8,128)(2,1)S(1)} %copy-done.4, f32[16,1024]{1,0:T(8,128)S(1)} %copy-done.22, bf16[64,48]{1,0:T(8,128)(2,1)S(1)} %copy-done.19, bf16[128,512]{1,0:T(8,128)(2,1)S(1)} %copy-done.2, bf16[128,512]{1,0:T(8,128)(2,1)S(1)} %copy-done.9), custom_call_target="tpu_custom_call" | custom-call | bytes 1906688 | tf_op jit(solution)/shard_map/pallas_call | solution.py:93
  141.4 1.7 %shard_map.132 = f32[64,4096]{1,0:T(8,128)} custom-call(f32[16,1024]{1,0:T(8,128)S(1)} %copy-done.16, bf16[64,48]{1,0:T(8,128)(2,1)S(1)} %copy-done.19, bf16[128,512]{1,0:T(8,128)(2,1)S(1)} %copy-done.2, bf16[128,512]{1,0:T(8,128)(2,1)S(1)} %copy-done.9), custom_call_target="tpu_custom_call" | custom-call | bytes 333824 | tf_op jit(solution)/shard_map/pallas_call | solution.py:93
  143.1 3.3 %shard_map.136 = bf16[512,2048]{1,0:T(8,128)(2,1)} custom-call(s32[3]{0:T(128)S(1)} %pad_add_fusion.where, bf16[512,256]{1,0:T(8,128)(2,1)S(1)} %get-tuple-element.21.refs_0_, bf16[512,256]{1,0:T(8,128)(2,1)S(1)} %copy-done.11, bf16[512,256]{1,0:T(8,128)(2,1)S(1)} %copy-done.15, bf16[512,256]{1,0:T(8,128)(2,1)S(1)} %copy-done.13, ...), custom_call_target="tpu_custom_call" | custom-call | bytes 2097164 | tf_op jit(solution)/shard_map/pallas_call | solution.py:93
  (85 shorter events, 18.5 us)
Async XLA Ops:
  6.2 31.8 %copy-start.21 = (f32[16,1024]{1,0:T(8,128)}, f32[16,1024]{1,0:T(8,128)S(1)}, u32[]{:S(2)}) copy-start(f32[16,1024]{1,0:T(8,128)S(1)} %get-tuple-element.16.bands) | copy-start | bytes 196612
  6.2 4.4 %collective-permute-start = (bf16[16,1024]{1,0:T(8,128)(2,1)S(1)}, bf16[16,1024]{1,0:T(8,128)(2,1)S(1)}, u32[]{:S(2)}, u32[]{:S(2)}) collective-permute-start(bf16[16,1024]{1,0:T(8,128)(2,1)S(1)} %get-tuple-element.17), channel_id=1, source_target_pairs={{32,0},{33,1},{34,2},{35,3},{36,4},{37,5},{38,6},{39,7},{40,8},{41... | collective-permute-start | bytes 98312 | tf_op jit(solution)/shard_map/ppermute | solution.py:61
  10.6 4.4 %collective-permute-start.1 = (bf16[16,1024]{1,0:T(8,128)(2,1)S(1)}, bf16[16,1024]{1,0:T(8,128)(2,1)S(1)}, u32[]{:S(2)}, u32[]{:S(2)}) collective-permute-start(bf16[16,1024]{1,0:T(8,128)(2,1)S(1)} %fusion), channel_id=1, source_target_pairs={{64,0},{65,1},{66,2},{67,3},{68,4},{69,5},{70,6},{71,7},{72,8},{73... | collective-permute-start | bytes 98312 | tf_op jit(solution)/shard_map/ppermute | solution.py:61
  14.9 86.9 %collective-permute-start.8 = (bf16[512,4096]{1,0:T(8,128)(2,1)}, bf16[512,4096]{1,0:T(8,128)(2,1)}, u32[]{:S(2)}, u32[]{:S(2)}) collective-permute-start(bf16[512,4096]{1,0:T(8,128)(2,1)} %refs_4_.3), channel_id=1, source_target_pairs={{1,0},{0,1},{3,2},{2,3},{5,4},{4,5},{7,6},{6,7},{9,8},{8,9},{11,10... | collective-permute-start | bytes 12582920 | tf_op jit(solution)/shard_map/ppermute | solution.py:61
  19.0 7.4 %collective-permute-start.9 = (bf16[64,4096]{1,0:T(8,128)(2,1)}, bf16[64,4096]{1,0:T(8,128)(2,1)S(1)}, u32[]{:S(2)}, u32[]{:S(2)}) collective-permute-start(bf16[64,4096]{1,0:T(8,128)(2,1)} %param.13), channel_id=1, source_target_pairs={{1,0},{0,1},{3,2},{2,3},{5,4},{4,5},{7,6},{6,7},{9,8},{8,9},{11,10... | collective-permute-start | bytes 1572872 | tf_op jit(solution)/shard_map/ppermute | solution.py:61
  26.4 11.1 %collective-permute-start.12 = (bf16[64,4096]{1,0:T(8,128)(2,1)S(1)}, bf16[64,4096]{1,0:T(8,128)(2,1)S(1)}, u32[]{:S(2)}, u32[]{:S(2)}) collective-permute-start(bf16[64,4096]{1,0:T(8,128)(2,1)S(1)} %collective-permute-done.9), channel_id=1, source_target_pairs={{24,0},{135,1},{26,2},{1,3},{28,4},{3,5},{30,6},{5,7},{0,8},{143,9... | collective-permute-start | bytes 1572872 | tf_op jit(solution)/shard_map/ppermute | solution.py:61
  26.7 11.3 %collective-permute-start.11 = (bf16[64,4096]{1,0:T(8,128)(2,1)S(1)}, bf16[64,4096]{1,0:T(8,128)(2,1)S(1)}, u32[]{:S(2)}, u32[]{:S(2)}) collective-permute-start(bf16[64,4096]{1,0:T(8,128)(2,1)S(1)} %collective-permute-done.9), channel_id=1, source_target_pairs={{16,0},{5,1},{18,2},{135,3},{20,4},{129,5},{22,6},{3,7},{24,8},{13... | collective-permute-start | bytes 1572872 | tf_op jit(solution)/shard_map/ppermute | solution.py:61
  31.8 11.8 %collective-permute-start.10 = (bf16[64,4096]{1,0:T(8,128)(2,1)S(1)}, bf16[64,4096]{1,0:T(8,128)(2,1)S(1)}, u32[]{:S(2)}, u32[]{:S(2)}) collective-permute-start(bf16[64,4096]{1,0:T(8,128)(2,1)S(1)} %collective-permute-done.9), channel_id=1, source_target_pairs={{8,0},{3,1},{10,2},{5,3},{12,4},{7,5},{14,6},{129,7},{16,8},{11,9}... | collective-permute-start | bytes 1572872 | tf_op jit(solution)/shard_map/ppermute | solution.py:61
  43.8 58.0 %copy-start.2 = (bf16[128,512]{1,0:T(8,128)(2,1)S(1)}, bf16[128,512]{1,0:T(8,128)(2,1)}, u32[]{:S(2)}) copy-start(bf16[128,512]{1,0:T(8,128)(2,1)} %constant.67.clone.back_hi.refs_2_) | copy-start | bytes 393220
  43.8 58.0 %copy-start.20 = (bf16[64,16]{1,0:T(8,128)(2,1)S(1)}, bf16[64,16]{1,0:T(8,128)(2,1)}, u32[]{:S(2)}) copy-start(bf16[64,16]{1,0:T(8,128)(2,1)} %constant.69.clone.refs_1_) | copy-start | bytes 6148
  43.8 50.5 %collective-permute-start.13 = (bf16[256,4096]{1,0:T(8,128)(2,1)S(1)}, bf16[256,4096]{1,0:T(8,128)(2,1)S(1)}, u32[]{:S(2)}, u32[]{:S(2)}) collective-permute-start(bf16[256,4096]{1,0:T(8,128)(2,1)S(1)} %pad_maximum_fusion.refs_6_), channel_id=1, source_target_pairs={{2,0},{9,1},{4,2},{11,3},{6,4},{13,5},{128,6},{15,7},{10,8},{17,9}... | collective-permute-start | bytes 6291464 | tf_op jit(solution)/shard_map/ppermute | solution.py:61
  46.6 51.8 %collective-permute-start.14 = (bf16[256,4096]{1,0:T(8,128)(2,1)S(1)}, bf16[256,4096]{1,0:T(8,128)(2,1)S(1)}, u32[]{:S(2)}, u32[]{:S(2)}) collective-permute-start(bf16[256,4096]{1,0:T(8,128)(2,1)S(1)} %pad_maximum_fusion.refs_6_), channel_id=1, source_target_pairs={{134,0},{25,1},{0,2},{27,3},{2,4},{29,5},{4,6},{31,7},{142,8},{1,9... | collective-permute-start | bytes 6291464 | tf_op jit(solution)/shard_map/ppermute | solution.py:61
  46.6 7.0 %collective-permute-start.2 = (bf16[16,1024]{1,0:T(8,128)(2,1)S(1)}, bf16[16,1024]{1,0:T(8,128)(2,1)S(1)}, u32[]{:S(2)}, u32[]{:S(2)}) collective-permute-start(bf16[16,1024]{1,0:T(8,128)(2,1)S(1)} %add_convert_fusion), channel_id=1, source_target_pairs={{128,0},{129,1},{130,2},{131,3},{132,4},{133,5},{134,6},{135,7},{1... | collective-permute-start | bytes 98312 | tf_op jit(solution)/shard_map/ppermute | solution.py:61
  54.3 4.6 %collective-permute-start.3 = (bf16[16,1024]{1,0:T(8,128)(2,1)S(1)}, bf16[16,1024]{1,0:T(8,128)(2,1)S(1)}, u32[]{:S(2)}, u32[]{:S(2)}) collective-permute-start(bf16[16,1024]{1,0:T(8,128)(2,1)S(1)} %get-tuple-element.33), channel_id=1, source_target_pairs={{8,0},{3,1},{10,2},{5,3},{12,4},{7,5},{14,6},{129,7},{16,8},{11,9}... | collective-permute-start | bytes 98312 | tf_op jit(solution)/shard_map/ppermute | solution.py:61
  58.9 5.1 %collective-permute-start.4 = (bf16[32,1024]{1,0:T(8,128)(2,1)S(1)}, bf16[32,1024]{1,0:T(8,128)(2,1)S(1)}, u32[]{:S(2)}, u32[]{:S(2)}) collective-permute-start(bf16[32,1024]{1,0:T(8,128)(2,1)S(1)} %pad_maximum_fusion.4), channel_id=1, source_target_pairs={{16,0},{5,1},{18,2},{135,3},{20,4},{129,5},{22,6},{3,7},{24,8},{13... | collective-permute-start | bytes 196616 | tf_op jit(solution)/shard_map/ppermute | solution.py:61
  64.0 25.5 %collective-permute-start.5 = (bf16[64,1024]{1,0:T(8,128)(2,1)S(1)}, bf16[64,1024]{1,0:T(8,128)(2,1)S(1)}, u32[]{:S(2)}, u32[]{:S(2)}) collective-permute-start(bf16[64,1024]{1,0:T(8,128)(2,1)S(1)} %pad_maximum_fusion.3), channel_id=1, source_target_pairs={{1,0},{0,1},{3,2},{2,3},{5,4},{4,5},{7,6},{6,7},{9,8},{8,9},{11,10... | collective-permute-start | bytes 393224 | tf_op jit(solution)/shard_map/ppermute | solution.py:61
  89.5 4.1 %collective-permute-start.6 = (bf16[64,1024]{1,0:T(8,128)(2,1)S(1)}, bf16[64,1024]{1,0:T(8,128)(2,1)S(1)}, u32[]{:S(2)}, u32[]{:S(2)}) collective-permute-start(bf16[64,1024]{1,0:T(8,128)(2,1)S(1)} %collective-permute-done.5), channel_id=1, source_target_pairs={{8,0},{3,1},{10,2},{5,3},{12,4},{7,5},{14,6},{129,7},{16,8},{11,9}... | collective-permute-start | bytes 393224 | tf_op jit(solution)/shard_map/ppermute | solution.py:61
  94.3 6.4 %collective-permute-start.7 = (bf16[128,1024]{1,0:T(8,128)(2,1)}, bf16[128,1024]{1,0:T(8,128)(2,1)}, u32[]{:S(2)}, u32[]{:S(2)}) collective-permute-start(bf16[128,1024]{1,0:T(8,128)(2,1)} %pad_maximum_fusion.2), channel_id=1, source_target_pairs={{16,0},{5,1},{18,2},{135,3},{20,4},{129,5},{22,6},{3,7},{24,8},{13... | collective-permute-start | bytes 786440 | tf_op jit(solution)/shard_map/ppermute | solution.py:61
  95.4 32.4 %collective-permute-start.15 = (bf16[128,4096]{1,0:T(8,128)(2,1)}, bf16[128,4096]{1,0:T(8,128)(2,1)S(1)}, u32[]{:S(2)}, u32[]{:S(2)}) collective-permute-start(bf16[128,4096]{1,0:T(8,128)(2,1)} %slice.28), channel_id=1, source_target_pairs={{2,0},{9,1},{4,2},{11,3},{6,4},{13,5},{128,6},{15,7},{10,8},{17,9}... | collective-permute-start | bytes 3145736 | tf_op jit(solution)/shard_map/ppermute | solution.py:61
  100.0 27.8 %collective-permute-start.16 = (bf16[128,4096]{1,0:T(8,128)(2,1)}, bf16[128,4096]{1,0:T(8,128)(2,1)}, u32[]{:S(2)}, u32[]{:S(2)}) collective-permute-start(bf16[128,4096]{1,0:T(8,128)(2,1)} %slice.29), channel_id=1, source_target_pairs={{134,0},{25,1},{0,2},{27,3},{2,4},{29,5},{4,6},{31,7},{142,8},{1,9... | collective-permute-start | bytes 3145736 | tf_op jit(solution)/shard_map/ppermute | solution.py:61
  109.9 33.2 %collective-permute-start.17 = (bf16[512,256]{1,0:T(8,128)(2,1)}, bf16[512,256]{1,0:T(8,128)(2,1)S(1)}, u32[]{:S(2)}, u32[]{:S(2)}) collective-permute-start(bf16[512,256]{1,0:T(8,128)(2,1)} %get-tuple-element.25), channel_id=1, source_target_pairs={{1,0},{0,1},{3,2},{2,3},{5,4},{4,5},{7,6},{6,7},{9,8},{8,9},{11,10... | collective-permute-start | bytes 786440 | tf_op jit(solution)/shard_map/ppermute | solution.py:61
  127.5 15.6 %collective-permute-start.18 = (bf16[512,256]{1,0:T(8,128)(2,1)}, bf16[512,256]{1,0:T(8,128)(2,1)}, u32[]{:S(2)}, u32[]{:S(2)}) collective-permute-start(bf16[512,256]{1,0:T(8,128)(2,1)} %get-tuple-element.26), channel_id=1, source_target_pairs={{1,0},{0,1},{3,2},{2,3},{5,4},{4,5},{7,6},{6,7},{9,8},{8,9},{11,10... | collective-permute-start | bytes 786440 | tf_op jit(solution)/shard_map/ppermute | solution.py:61
  138.2 4.8 %collective-permute-start.19 = (bf16[512,256]{1,0:T(8,128)(2,1)}, bf16[512,256]{1,0:T(8,128)(2,1)S(1)}, u32[]{:S(2)}, u32[]{:S(2)}) collective-permute-start(bf16[512,256]{1,0:T(8,128)(2,1)} %get-tuple-element.27), channel_id=1, source_target_pairs={{1,0},{0,1},{3,2},{2,3},{5,4},{4,5},{7,6},{6,7},{9,8},{8,9},{11,10... | collective-permute-start | bytes 786440 | tf_op jit(solution)/shard_map/ppermute | solution.py:61
  138.7 4.4 %collective-permute-start.20 = (bf16[512,256]{1,0:T(8,128)(2,1)}, bf16[512,256]{1,0:T(8,128)(2,1)}, u32[]{:S(2)}, u32[]{:S(2)}) collective-permute-start(bf16[512,256]{1,0:T(8,128)(2,1)} %get-tuple-element.28), channel_id=1, source_target_pairs={{1,0},{0,1},{3,2},{2,3},{5,4},{4,5},{7,6},{6,7},{9,8},{8,9},{11,10... | collective-permute-start | bytes 786440 | tf_op jit(solution)/shard_map/ppermute | solution.py:61
  (21 other events, 130.2 us)

commit v3 on v2

--- a/solution.py
+++ b/solution.py
@@ -76,6 +76,10 @@
     return lambda x, y, z, core: (x + step, y, z, core)
 
 
+def pair_x(x, y, z, core):
+    return x ^ 1, y, z, core
+
+
 def far_z(x, y, z, core):
     return x, y, z + 4, core
 
@@ -84,23 +88,45 @@
     return x, y, z, 1 - core
 
 
-def call(kernel, out_shape, inputs, scratch=(), limit=16, flops=0, smem=0, kept=()):
+def call(kernel, out_shape, inputs, scratch=(), limit=16, flops=0, smem=0, kept=(), resident=()):
     specs = [pl.BlockSpec(memory_space=pltpu.SMEM)] * smem
-    specs += [pl.BlockSpec(memory_space=pltpu.VMEM)] * (len(inputs) - smem)
-    specs += [pl.BlockSpec(memory_space=pl.ANY)] * len(kept)
-    inputs = (*inputs, *kept)
+    specs += [pl.BlockSpec(memory_space=pltpu.VMEM)] * (len(inputs) - smem + len(resident))
+    specs += [pl.BlockSpec(memory_space=pltpu.HBM)] * len(kept)
+    resident = [pltpu.with_memory_space_constraint(v, pltpu.VMEM) for v in resident]
+    kept = [pltpu.with_memory_space_constraint(v, pltpu.HBM) for v in kept]
+    inputs = (*inputs, *resident, *kept)
     moved = sum(math.prod(v.shape) * v.dtype.itemsize for v in inputs)
     return pl.pallas_call(
         kernel,
         out_shape=out_shape,
         in_specs=specs,
-        out_specs=jax.tree.map(lambda _: pl.BlockSpec(memory_space=pltpu.VMEM), out_shape),
+        out_specs=jax.tree.map(
+            lambda _: pl.BlockSpec(memory_space=pltpu.VMEM),
+            out_shape,
+            is_leaf=lambda v: not isinstance(v, tuple),
+        ),
         scratch_shapes=list(scratch),
         compiler_params=pltpu.CompilerParams(vmem_limit_bytes=limit << 20),
         cost_estimate=pl.CostEstimate(flops=flops, bytes_accessed=moved, transcendentals=0),
     )(*inputs)
 
 
+def stay_kernel(source, out, sem):
+    copy = pltpu.make_async_copy(source, out, sem)
+    copy.start()
+    copy.wait()
+
+
+def stay(value):
+    return call(
+        stay_kernel,
+        pltpu.VMEM(value.shape, value.dtype),
+        (),
+        (pltpu.SemaphoreType.DMA,),
+        kept=(value,),
+    )
+
+
 def stacked(value, wide):
     return jnp.concatenate(
         [value[:, k * wide : (k + 1) * wide] for k in range(value.shape[1] // wide)], axis=0
@@ -111,16 +137,29 @@
     return momentum_decay * momentum[0] + gradient[0].astype(F32)
 
 
-def bands_kernel(momentum, gradient, cols_hi, cols_lo, rows3, exact, rounded):
-    high, low = split(mixed_of(momentum, gradient))
-    high = stacked(high, WIDE * TILE)
-    low = stacked(low, WIDE * TILE)
-    narrow = dot(high, cols_hi[...]) + dot(low, cols_hi[...]) + dot(high, cols_lo[...])
-    narrow = jnp.concatenate(
-        [narrow[k * TILE : (k + 1) * TILE] for k in range(narrow.shape[0] // TILE)], axis=1
-    )
-    high, low = split(narrow)
-    bands = dot(rows3[...], jnp.concatenate([high, low, high], axis=0))
+def bands_kernel(momentum, gradient, cols, rows3, exact, rounded, m, g, c, r, sems):
+    wide = WIDE * TILE
+    steps = momentum.shape[2] // wide
+    copies = [pltpu.make_async_copy(cols, c, sems.at[2 * steps])]
+    copies += [pltpu.make_async_copy(rows3, r, sems.at[2 * steps + 1])]
+    for k in range(steps):
+        cut = pl.ds(k * wide, wide)
+        copies += [
+            pltpu.make_async_copy(momentum.at[0, :, cut], m.at[k], sems.at[2 * k]),
+            pltpu.make_async_copy(gradient.at[0, :, cut], g.at[k], sems.at[2 * k + 1]),
+        ]
+    for copy in copies:
+        copy.start()
+    copies[0].wait()
+    narrow = []
+    for k in range(steps):
+        copies[2 * k + 2].wait()
+        copies[2 * k + 3].wait()
+        high, low = split(momentum_decay * m[k] + g[k].astype(F32))
+        narrow.append(dot(high, c[:wide]) + dot(low, c[:wide]) + dot(high, c[wide:]))
+    copies[1].wait()
+    high, low = split(jnp.concatenate(narrow, axis=1))
+    bands = dot(r[...], jnp.concatenate([high, low, high], axis=0))
     exact[...] = bands
     rounded[...] = bands.astype(BF16)
 
@@ -159,9 +198,10 @@
     tokens = [refs.pop(0) for _ in range(2)]
     weights = [[refs.pop(0) for _ in range(n)] for n in parts]
     outs = [refs.pop(0) for _ in range(2 * groups)]
-    kept, raw, *fresh, token_sem, raw_sem = refs
+    raw, *fresh, raw_sem = refs
     wide = WIDE * TILE
-    rows, width = kept.shape[1:]
+    rows, width = fresh[0].shape
+    per = tokens[0].shape[0] // rows
     start = first[0]
 
     pieces = []
@@ -174,21 +214,11 @@
     for g in range(groups):
         for f, (ref, r) in enumerate(pieces[g]):
             raw_copy[g, f] = pltpu.make_async_copy(ref.at[r : r + TILE], raw.at[g, f], raw_sem.at[g, f])
-    per = tokens[0].shape[0] // rows
-    token_copy = [
-        pltpu.make_async_copy(tokens[t // per].at[pl.ds(t % per * rows, rows)], kept.at[t], token_sem.at[t])
-        for t in range(4)
-    ]
-    for f in range(4):
-        raw_copy[0, f].start()
-    for copy in token_copy:
-        copy.start()
-    for g in range(1, groups):
+    for g in range(groups):
         for f in range(4):
             raw_copy[g, f].start()
 
     def renew(g, f):
-        raw_copy[g, f].wait()
         tall = dot(back_rows[...], bands[g][f * BAND : (f + 1) * BAND]).astype(BF16)
         sign = soft_sign(dot(stacked(tall, WIDE * BAND), back_cols[...]))
         at = pl.ds(pl.multiple_of(lax.rem(start + f, 4) * TILE, TILE), TILE)
@@ -198,13 +228,16 @@
             fresh[g % 2][at, cut] = new.astype(BF16)
 
     for f in range(4):
+        raw_copy[0, f].wait()
         renew(0, f)
     for g in range(groups):
+        if g + 1 < groups:
+            for f in range(4):
+                raw_copy[g + 1, f].wait()
         for t in range(4):
-            if g == 0:
-                token_copy[t].wait()
-            product = lax.dot_general(kept[t], fresh[g % 2][...], NT, preferred_element_type=F32)
-            outs[2 * g + t // per][t % per * rows : (t % per + 1) * rows] = product.astype(BF16)
+            cut = slice(t % per * rows, (t % per + 1) * rows)
+            product = lax.dot_general(tokens[t // per][cut], fresh[g % 2][...], NT, preferred_element_type=F32)
+            outs[2 * g + t // per][cut] = product.astype(BF16)
             if g + 1 < groups:
                 renew(g + 1, t)
 
@@ -244,26 +277,36 @@
     second = jnp.where(core == 0, z, y).astype(jnp.int32)
 
     shape = jax.ShapeDtypeStruct
+    steps = width // (WIDE * TILE)
     exact, rounded = call(
         bands_kernel,
         (shape((BAND, narrow), F32), shape((BAND, narrow), BF16)),
-        (momentum, gradient, cols_hi, cols_lo, rows3),
+        (),
+        (
+            pltpu.VMEM((steps, rows, WIDE * TILE), F32),
+            pltpu.VMEM((steps, rows, WIDE * TILE), BF16),
+            pltpu.VMEM((2 * WIDE * TILE, WIDE * BAND), BF16),
+            pltpu.VMEM(rows3.shape, BF16),
+            pltpu.SemaphoreType.DMA((2 * steps + 2,)),
+        ),
+        kept=(momentum, gradient, np.concatenate([cols_hi, cols_lo], axis=0), rows3),
     )
 
     def after(value, *others):
         return lax.optimization_barrier((value, *others))[0]
 
     swapped = fetch(weight, sibling)
+    other = fetch(after(activations, swapped), sibling)
     swapped = after(swapped, rounded)
     ahead, behind, across = (fetch(swapped, along(0, s)) for s in (1, -1, 2))
 
-    total = rounded.astype(F32) + fetch(rounded, along_x(1)).astype(F32)
-    total = total + fetch(total.astype(BF16), along_x(2)).astype(F32)
-    sent = total.astype(BF16)
-    other = fetch(after(activations, sent), sibling)
-    line = jnp.concatenate([swapped, ahead, across, behind], axis=0)
-    line = after(line, sent)
-    total = sent.astype(F32) + fetch(sent, far_z).astype(F32)
+    def join(value, source):
+        return value.astype(F32) + fetch(value, source).astype(F32)
+
+    sent = join(rounded, far_z).astype(BF16)
+    total = join(join(sent, pair_x).astype(BF16), along_x(2))
+    own = stay(after(activations, sent))
+    other = stay(other)
 
     new_momentum = call(
         residual_kernel,
@@ -280,12 +323,12 @@
     blocks = jnp.concatenate([near, far], axis=0).reshape(4, 4, BAND, narrow)
     bands = [blocks[:, g].reshape(4 * BAND, narrow) for g in range(4)]
 
-    next_line = fetch(line, along(1, 1))
-    last_line = fetch(line, along(1, -1))
-    half = line.shape[0] // 2
-    far_a = fetch(next_line[:half], along(1, 1))
-    far_b = fetch(last_line[half:], along(1, -1))
-    lines = [[line], [next_line], [far_a, far_b], [last_line]]
+    early = after(jnp.concatenate([swapped, ahead], axis=0), sent)
+    late = after(jnp.concatenate([across, behind], axis=0), new_momentum)
+    next_early, last_early = fetch(early, along(1, 1)), fetch(early, along(1, -1))
+    next_late, last_late = fetch(late, along(1, 1)), fetch(late, along(1, -1))
+    far_early, far_late = fetch(next_early, along(1, 1)), fetch(last_late, along(1, -1))
+    lines = [[early, late], [next_early, next_late], [far_early, far_late], [last_early, last_late]]
 
     direction = call(
         direction_kernel,
@@ -296,24 +339,23 @@
     def forward(order):
         parts = [len(lines[g]) for g in order]
         inputs = [first[None], back_rows, back_hi] + [bands[g] for g in order]
-        kept = [activations, other] + [line for g in order for line in lines[g]]
+        kept = [line for g in order for line in lines[g]]
         block = shape((tokens, 4 * rows), BF16)
         return call(
             lambda *refs: forward_kernel(parts, *refs),
             tuple([block] * (2 * len(order))),
             inputs,
             (
-                pltpu.VMEM((4, tokens // 2, width), BF16),
                 pltpu.VMEM((len(order), 4, rows, width), BF16),
                 pltpu.VMEM((4 * rows, width), BF16),
                 pltpu.VMEM((4 * rows, width), BF16),
-                pltpu.SemaphoreType.DMA((4,)),
                 pltpu.SemaphoreType.DMA((len(order), 4)),
             ),
-            limit=48,
+            limit=24,
             flops=len(order) * 2 * 2 * tokens * 4 * rows * width,
             smem=1,
             kept=kept,
+            resident=(own, other),
         )
 
     mine, theirs = [None] * 4, [None] * 4

time: 149 us -> 107 us (0.72); the launches traced: 146 us -> 107 us
  starting transfers between devices: 60.6 us -> 45.3 us
  waiting for transfers between devices: 35.7 us -> 26.5 us
  local copies, waits for them, and re-layouts: 9.19 us -> 0.08 us
  Pallas kernels: 37.4 us -> 33 us
    ppermute x21 -> x23, starting transfers between devices: 60.6 us -> 45.3 us  [fetch(): lax.ppermute(value, AXES, [(place(*source(*spot(i))), i) for i in range(2...]
    ppermute x21 -> x23, waiting for transfers between devices: 35.7 us -> 26.5 us  [fetch(): lax.ppermute(value, AXES, [(place(*source(*spot(i))), i) for i in range(2...]
    unnamed x48 -> x14, local copies, waits for them, and re-layouts: 6.95 us -> 0.04 us
    pallas_call x7 -> x9, Pallas kernels: 37.4 us -> 33 us  [call(): pl.pallas_call(kernel, out_shape=out_shape, in_specs=specs, out_specs=jax...]
    slice x2 -> x0, local copies, waits for them, and re-layouts: 2.2 us -> none  [the longest x1 1.1 us: on_device(): far_a = fetch(next_line[:half], along(1, 1))]
  transfers between devices with their start and end apart: 21 -> 23, of which waited for: 12 -> 9; matrix products, arithmetic and copies ran while one was open for 3% -> 1% of each run, Pallas kernels for 23% -> 28%
where the time goes in v3:
time: 107 us
  starting transfers between devices  45.3 us (42%)
  Pallas kernels  33 us (31%)
  waiting for transfers between devices  26.5 us (25%)
  other arithmetic  1.33 us (1%)
    ppermute x23, starting transfers between devices, fetch(): lax.ppermute(value, AXES, [(place(*source(*spot(i))), i) for i in range(2...  45.3 us
    pallas_call x9, Pallas kernels, call(): pl.pallas_call(kernel, out_shape=out_shape, in_specs=specs, out_specs=jax...  33 us
    ppermute x23, waiting for transfers between devices, fetch(): lax.ppermute(value, AXES, [(place(*source(*spot(i))), i) for i in range(2...  26.5 us
  transfers between devices with their start and end apart: 23, of which 9 were waited for; matrix products, arithmetic and copies ran while one was open for 1% of the time, Pallas kernels for 28%

profile of v3, /device:TPU:1, one launch (start us, length us, event | category | flops | bytes accessed | tf_op | source)
XLA Modules:
  0.0 107.1 jit_solution(4318413530379963133)
XLA Ops:
  0.7 3.3 %collective-permute-start.8 = (bf16[64,4096]{1,0:T(8,128)(2,1)}, bf16[64,4096]{1,0:T(8,128)(2,1)S(1)}, u32[]{:S(2)}, u32[]{:S(2)}) collective-permute-start(bf16[64,4096]{1,0:T(8,128)(2,1)} %param.12), channel_id=1, source_target_pairs={{1,0},{0,1},{3,2},{2,3},{5,4},{4,5},{7,6},{6,7},{9,8},{8,9},{11,10... | collective-permute-start | bytes 1572872 | tf_op jit(solution)/shard_map/ppermute | solution.py:61
  4.0 1.7 %collective-permute-done.8 = bf16[64,4096]{1,0:T(8,128)(2,1)S(1)} collective-permute-done((bf16[64,4096]{1,0:T(8,128)(2,1)}, bf16[64,4096]{1,0:T(8,128)(2,1)S(1)}, u32[]{:S(2)}, u32[]{:S(2)}) %collective-permute-start.8) | collective-permute-done | bytes 524320 | tf_op jit(solution)/shard_map/ppermute | solution.py:61
  6.1 3.0 %shard_map.121 = (f32[16,1024]{1,0:T(8,128)S(1)}, bf16[16,1024]{1,0:T(8,128)(2,1)S(1)}) custom-call(f32[1,64,4096]{2,1,0:T(8,128)} %momentum.3, bf16[1,64,4096]{2,1,0:T(8,128)(2,1)} %gradient.3, bf16[1024,128]{1,0:T(8,128)(2,1)} %constant.61.clone.cols, bf16[16,192]{1,0:T(8,128)(2,1)} %constant.62.clone.rows3), custom_call_target="tpu_custom_call" | custom-call | bytes 1841152 | tf_op jit(solution)/shard_map/pallas_call | solution.py:99
  9.2 5.3 %collective-permute-start = (bf16[16,1024]{1,0:T(8,128)(2,1)S(1)}, bf16[16,1024]{1,0:T(8,128)(2,1)S(1)}, u32[]{:S(2)}, u32[]{:S(2)}) collective-permute-start(bf16[16,1024]{1,0:T(8,128)(2,1)S(1)} %get-tuple-element.19), channel_id=1, source_target_pairs={{128,0},{129,1},{130,2},{131,3},{132,4},{133,5},{134,6},{135,7},{1... | collective-permute-start | bytes 98312 | tf_op jit(solution)/shard_map/ppermute | solution.py:61
  17.4 3.8 %collective-permute-start.10 = (bf16[64,4096]{1,0:T(8,128)(2,1)S(1)}, bf16[64,4096]{1,0:T(8,128)(2,1)S(1)}, u32[]{:S(2)}, u32[]{:S(2)}) collective-permute-start(bf16[64,4096]{1,0:T(8,128)(2,1)S(1)} %collective-permute-done.8), channel_id=1, source_target_pairs={{8,0},{3,1},{10,2},{5,3},{12,4},{7,5},{14,6},{129,7},{16,8},{11,9}... | collective-permute-start | bytes 1572872 | tf_op jit(solution)/shard_map/ppermute | solution.py:61
  21.2 2.5 %collective-permute-start.2 = (bf16[16,1024]{1,0:T(8,128)(2,1)S(1)}, bf16[16,1024]{1,0:T(8,128)(2,1)S(1)}, u32[]{:S(2)}, u32[]{:S(2)}) collective-permute-start(bf16[16,1024]{1,0:T(8,128)(2,1)S(1)} %add_convert_fusion), channel_id=1, source_target_pairs={{64,0},{65,1},{66,2},{67,3},{68,4},{69,5},{70,6},{71,7},{72,8},{73... | collective-permute-start | bytes 98312 | tf_op jit(solution)/shard_map/ppermute | solution.py:61
  23.7 1.8 %collective-permute-done.2 = bf16[16,1024]{1,0:T(8,128)(2,1)S(1)} collective-permute-done((bf16[16,1024]{1,0:T(8,128)(2,1)S(1)}, bf16[16,1024]{1,0:T(8,128)(2,1)S(1)}, u32[]{:S(2)}, u32[]{:S(2)}) %collective-permute-start.2) | collective-permute-done | bytes 32800 | tf_op jit(solution)/shard_map/ppermute | solution.py:61
  28.9 1.9 %collective-permute-start.11 = (bf16[64,4096]{1,0:T(8,128)(2,1)S(1)}, bf16[64,4096]{1,0:T(8,128)(2,1)S(1)}, u32[]{:S(2)}, u32[]{:S(2)}) collective-permute-start(bf16[64,4096]{1,0:T(8,128)(2,1)S(1)} %collective-permute-done.8), channel_id=1, source_target_pairs={{16,0},{5,1},{18,2},{135,3},{20,4},{129,5},{22,6},{3,7},{24,8},{13... | collective-permute-start | bytes 1572872 | tf_op jit(solution)/shard_map/ppermute | solution.py:61
  32.2 6.2 %collective-permute-done.12 = bf16[64,4096]{1,0:T(8,128)(2,1)S(1)} collective-permute-done((bf16[64,4096]{1,0:T(8,128)(2,1)S(1)}, bf16[64,4096]{1,0:T(8,128)(2,1)S(1)}, u32[]{:S(2)}, u32[]{:S(2)}) %collective-permute-start.12) | collective-permute-done | bytes 524320 | tf_op jit(solution)/shard_map/ppermute | solution.py:61
  39.5 2.8 %collective-permute-start.13 = (bf16[128,4096]{1,0:T(8,128)(2,1)S(1)}, bf16[128,4096]{1,0:T(8,128)(2,1)}, u32[]{:S(2)}, u32[]{:S(2)}) collective-permute-start(bf16[128,4096]{1,0:T(8,128)(2,1)S(1)} %pad_maximum_fusion.refs_6_), channel_id=1, source_target_pairs={{2,0},{9,1},{4,2},{11,3},{6,4},{13,5},{128,6},{15,7},{10,8},{17,9}... | collective-permute-start | bytes 3145736 | tf_op jit(solution)/shard_map/ppermute | solution.py:61
  42.2 11.3 %collective-permute-start.5 = (bf16[64,1024]{1,0:T(8,128)(2,1)S(1)}, bf16[64,1024]{1,0:T(8,128)(2,1)S(1)}, u32[]{:S(2)}, u32[]{:S(2)}) collective-permute-start(bf16[64,1024]{1,0:T(8,128)(2,1)S(1)} %pad_maximum_fusion.4), channel_id=1, source_target_pairs={{1,0},{0,1},{3,2},{2,3},{5,4},{4,5},{7,6},{6,7},{9,8},{8,9},{11,10... | collective-permute-start | bytes 393224 | tf_op jit(solution)/shard_map/ppermute | solution.py:61
  54.6 3.0 %collective-permute-start.6 = (bf16[64,1024]{1,0:T(8,128)(2,1)S(1)}, bf16[64,1024]{1,0:T(8,128)(2,1)S(1)}, u32[]{:S(2)}, u32[]{:S(2)}) collective-permute-start(bf16[64,1024]{1,0:T(8,128)(2,1)S(1)} %collective-permute-done.5), channel_id=1, source_target_pairs={{8,0},{3,1},{10,2},{5,3},{12,4},{7,5},{14,6},{129,7},{16,8},{11,9}... | collective-permute-start | bytes 393224 | tf_op jit(solution)/shard_map/ppermute | solution.py:61
  57.5 3.4 %collective-permute-done.6 = bf16[64,1024]{1,0:T(8,128)(2,1)S(1)} collective-permute-done((bf16[64,1024]{1,0:T(8,128)(2,1)S(1)}, bf16[64,1024]{1,0:T(8,128)(2,1)S(1)}, u32[]{:S(2)}, u32[]{:S(2)}) %collective-permute-start.6) | collective-permute-done | bytes 131104 | tf_op jit(solution)/shard_map/ppermute | solution.py:61
  60.9 2.6 %collective-permute-start.7 = (bf16[128,1024]{1,0:T(8,128)(2,1)S(1)}, bf16[128,1024]{1,0:T(8,128)(2,1)S(1)}, u32[]{:S(2)}, u32[]{:S(2)}) collective-permute-start(bf16[128,1024]{1,0:T(8,128)(2,1)S(1)} %pad_maximum_fusion.3), channel_id=1, source_target_pairs={{16,0},{5,1},{18,2},{135,3},{20,4},{129,5},{22,6},{3,7},{24,8},{13... | collective-permute-start | bytes 786440 | tf_op jit(solution)/shard_map/ppermute | solution.py:61
  63.5 6.8 %collective-permute-done.7 = bf16[128,1024]{1,0:T(8,128)(2,1)S(1)} collective-permute-done((bf16[128,1024]{1,0:T(8,128)(2,1)S(1)}, bf16[128,1024]{1,0:T(8,128)(2,1)S(1)}, u32[]{:S(2)}, u32[]{:S(2)}) %collective-permute-start.7) | collective-permute-done | bytes 262176 | tf_op jit(solution)/shard_map/ppermute | solution.py:61
  70.4 2.7 %collective-permute-start.17 = (bf16[128,4096]{1,0:T(8,128)(2,1)}, bf16[128,4096]{1,0:T(8,128)(2,1)}, u32[]{:S(2)}, u32[]{:S(2)}) collective-permute-start(bf16[128,4096]{1,0:T(8,128)(2,1)} %collective-permute-done.13.refs_7_), channel_id=1, source_target_pairs={{2,0},{9,1},{4,2},{11,3},{6,4},{13,5},{128,6},{15,7},{10,8},{17,9}... | collective-permute-start | bytes 3145736 | tf_op jit(solution)/shard_map/ppermute | solution.py:61
  73.1 2.2 %shard_map.124.refs_4_.refs_5_ = bf16[512,4096]{1,0:T(8,128)(2,1)S(1)} custom-call(bf16[512,4096]{1,0:T(8,128)(2,1)} %source), custom_call_target="tpu_custom_call" | custom-call | bytes 4194304 | tf_op jit(solution)/shard_map/pallas_call | solution.py:99
  75.4 2.2 %shard_map.125.refs_5_.refs_6_ = bf16[512,4096]{1,0:T(8,128)(2,1)S(1)} custom-call(bf16[512,4096]{1,0:T(8,128)(2,1)} %collective-permute-done.9.source), custom_call_target="tpu_custom_call" | custom-call | bytes 4194304 | tf_op jit(solution)/shard_map/pallas_call | solution.py:99
  77.6 5.4 %shard_map.126 = (bf16[512,256]{1,0:T(8,128)(2,1)S(1)}, bf16[512,256]{1,0:T(8,128)(2,1)S(1)}) custom-call(s32[1]{0:T(128)} %bitcast.2.refs_0_, bf16[64,16]{1,0:T(8,128)(2,1)S(1)} %copy-done.5, bf16[128,512]{1,0:T(8,128)(2,1)S(1)} %copy-done.1, bf16[64,1024]{1,0:T(8,128)(2,1)S(1)} %bitcast.17, bf16[512,4096]{1,0:T(8,128)(2,1)S(1)} %shard_map.124.refs_4_.refs_5_, ...), custom_call_target="tpu_custom_call" | custom-call | flops 2147483648 | bytes 10749956 | tf_op jit(solution)/shard_map/pallas_call | solution.py:99
  83.9 1.7 %collective-permute-done.15.refs_9_ = bf16[128,4096]{1,0:T(8,128)(2,1)} collective-permute-done((bf16[128,4096]{1,0:T(8,128)(2,1)S(1)}, bf16[128,4096]{1,0:T(8,128)(2,1)}, u32[]{:S(2)}, u32[]{:S(2)}) %collective-permute-start.15) | collective-permute-done | bytes 1048608 | tf_op jit(solution)/shard_map/ppermute | solution.py:61
  85.6 8.7 %shard_map.127 = (bf16[512,256]{1,0:T(8,128)(2,1)S(1)}, bf16[512,256]{1,0:T(8,128)(2,1)S(1)}, bf16[512,256]{1,0:T(8,128)(2,1)S(1)}, bf16[512,256]{1,0:T(8,128)(2,1)S(1)}) custom-call(s32[1]{0:T(128)} %bitcast.2.refs_0_, bf16[64,16]{1,0:T(8,128)(2,1)S(1)} %copy-done.5, bf16[128,512]{1,0:T(8,128)(2,1)S(1)} %copy-done.1, bf16[64,1024]{1,0:T(8,128)(2,1)S(1)} %bitcast.19, ...), custom_call_target="tpu_custom_call" | custom-call | flops 4294967296 | bytes 12978180 | tf_op jit(solution)/shard_map/pallas_call | solution.py:99
  94.5 2.1 %collective-permute-done.18.refs_7_ = bf16[128,4096]{1,0:T(8,128)(2,1)} collective-permute-done((bf16[128,4096]{1,0:T(8,128)(2,1)}, bf16[128,4096]{1,0:T(8,128)(2,1)}, u32[]{:S(2)}, u32[]{:S(2)}) %collective-permute-start.18) | collective-permute-done | bytes 1048608 | tf_op jit(solution)/shard_map/ppermute | solution.py:61
  96.6 5.4 %shard_map.128 = (bf16[512,256]{1,0:T(8,128)(2,1)S(1)}, bf16[512,256]{1,0:T(8,128)(2,1)S(1)}) custom-call(s32[1]{0:T(128)} %bitcast.2.refs_0_, bf16[64,16]{1,0:T(8,128)(2,1)S(1)} %copy-done.5, bf16[128,512]{1,0:T(8,128)(2,1)S(1)} %copy-done.1, bf16[64,1024]{1,0:T(8,128)(2,1)S(1)} %bitcast.16, bf16[512,4096]{1,0:T(8,128)(2,1)S(1)} %shard_map.124.refs_4_.refs_5_, ...), custom_call_target="tpu_custom_call" | custom-call | flops 2147483648 | bytes 10749956 | tf_op jit(solution)/shard_map/pallas_call | solution.py:99
  104.3 2.8 %shard_map.129 = bf16[512,2048]{1,0:T(8,128)(2,1)} custom-call(s32[3]{0:T(128)S(1)} %pad_add_fusion.where, bf16[512,256]{1,0:T(8,128)(2,1)S(1)} %get-tuple-element.25.refs_0_, bf16[512,256]{1,0:T(8,128)(2,1)S(1)} %get-tuple-element.26.refs_1_, bf16[512,256]{1,0:T(8,128)(2,1)S(1)} %get-tuple-element.27.refs_2_, ...), custom_call_target="tpu_custom_call" | custom-call | bytes 2097164 | tf_op jit(solution)/shard_map/pallas_call | solution.py:99
  (56 shorter events, 13.6 us)
Async XLA Ops:
  0.7 5.1 %collective-permute-start.8 = (bf16[64,4096]{1,0:T(8,128)(2,1)}, bf16[64,4096]{1,0:T(8,128)(2,1)S(1)}, u32[]{:S(2)}, u32[]{:S(2)}) collective-permute-start(bf16[64,4096]{1,0:T(8,128)(2,1)} %param.12), channel_id=1, source_target_pairs={{1,0},{0,1},{3,2},{2,3},{5,4},{4,5},{7,6},{6,7},{9,8},{8,9},{11,10... | collective-permute-start | bytes 1572872 | tf_op jit(solution)/shard_map/ppermute | solution.py:61
  5.8 69.6 %collective-permute-start.9 = (bf16[512,4096]{1,0:T(8,128)(2,1)}, bf16[512,4096]{1,0:T(8,128)(2,1)}, u32[]{:S(2)}, u32[]{:S(2)}) collective-permute-start(bf16[512,4096]{1,0:T(8,128)(2,1)} %source), channel_id=1, source_target_pairs={{1,0},{0,1},{3,2},{2,3},{5,4},{4,5},{7,6},{6,7},{9,8},{8,9},{11,10... | collective-permute-start | bytes 12582920 | tf_op jit(solution)/shard_map/ppermute | solution.py:61
  9.2 6.9 %collective-permute-start = (bf16[16,1024]{1,0:T(8,128)(2,1)S(1)}, bf16[16,1024]{1,0:T(8,128)(2,1)S(1)}, u32[]{:S(2)}, u32[]{:S(2)}) collective-permute-start(bf16[16,1024]{1,0:T(8,128)(2,1)S(1)} %get-tuple-element.19), channel_id=1, source_target_pairs={{128,0},{129,1},{130,2},{131,3},{132,4},{133,5},{134,6},{135,7},{1... | collective-permute-start | bytes 98312 | tf_op jit(solution)/shard_map/ppermute | solution.py:61
  16.1 5.1 %collective-permute-start.1 = (bf16[16,1024]{1,0:T(8,128)(2,1)S(1)}, bf16[16,1024]{1,0:T(8,128)(2,1)S(1)}, u32[]{:S(2)}, u32[]{:S(2)}) collective-permute-start(bf16[16,1024]{1,0:T(8,128)(2,1)S(1)} %add_convert_fusion.1), channel_id=1, source_target_pairs={{32,0},{33,1},{34,2},{35,3},{36,4},{37,5},{38,6},{39,7},{40,8},{41... | collective-permute-start | bytes 98312 | tf_op jit(solution)/shard_map/ppermute | solution.py:61
  17.4 14.6 %collective-permute-start.10 = (bf16[64,4096]{1,0:T(8,128)(2,1)S(1)}, bf16[64,4096]{1,0:T(8,128)(2,1)S(1)}, u32[]{:S(2)}, u32[]{:S(2)}) collective-permute-start(bf16[64,4096]{1,0:T(8,128)(2,1)S(1)} %collective-permute-done.8), channel_id=1, source_target_pairs={{8,0},{3,1},{10,2},{5,3},{12,4},{7,5},{14,6},{129,7},{16,8},{11,9}... | collective-permute-start | bytes 1572872 | tf_op jit(solution)/shard_map/ppermute | solution.py:61
  21.2 4.4 %collective-permute-start.2 = (bf16[16,1024]{1,0:T(8,128)(2,1)S(1)}, bf16[16,1024]{1,0:T(8,128)(2,1)S(1)}, u32[]{:S(2)}, u32[]{:S(2)}) collective-permute-start(bf16[16,1024]{1,0:T(8,128)(2,1)S(1)} %add_convert_fusion), channel_id=1, source_target_pairs={{64,0},{65,1},{66,2},{67,3},{68,4},{69,5},{70,6},{71,7},{72,8},{73... | collective-permute-start | bytes 98312 | tf_op jit(solution)/shard_map/ppermute | solution.py:61
  25.5 5.2 %collective-permute-start.3 = (bf16[16,1024]{1,0:T(8,128)(2,1)S(1)}, bf16[16,1024]{1,0:T(8,128)(2,1)S(1)}, u32[]{:S(2)}, u32[]{:S(2)}) collective-permute-start(bf16[16,1024]{1,0:T(8,128)(2,1)S(1)} %get-tuple-element.37), channel_id=1, source_target_pairs={{8,0},{3,1},{10,2},{5,3},{12,4},{7,5},{14,6},{129,7},{16,8},{11,9}... | collective-permute-start | bytes 98312 | tf_op jit(solution)/shard_map/ppermute | solution.py:61
  28.8 9.5 %collective-permute-start.12 = (bf16[64,4096]{1,0:T(8,128)(2,1)S(1)}, bf16[64,4096]{1,0:T(8,128)(2,1)S(1)}, u32[]{:S(2)}, u32[]{:S(2)}) collective-permute-start(bf16[64,4096]{1,0:T(8,128)(2,1)S(1)} %collective-permute-done.8), channel_id=1, source_target_pairs={{24,0},{135,1},{26,2},{1,3},{28,4},{3,5},{30,6},{5,7},{0,8},{143,9... | collective-permute-start | bytes 1572872 | tf_op jit(solution)/shard_map/ppermute | solution.py:61
  28.9 9.5 %collective-permute-start.11 = (bf16[64,4096]{1,0:T(8,128)(2,1)S(1)}, bf16[64,4096]{1,0:T(8,128)(2,1)S(1)}, u32[]{:S(2)}, u32[]{:S(2)}) collective-permute-start(bf16[64,4096]{1,0:T(8,128)(2,1)S(1)} %collective-permute-done.8), channel_id=1, source_target_pairs={{16,0},{5,1},{18,2},{135,3},{20,4},{129,5},{22,6},{3,7},{24,8},{13... | collective-permute-start | bytes 1572872 | tf_op jit(solution)/shard_map/ppermute | solution.py:61
  30.7 11.5 %collective-permute-start.4 = (bf16[32,1024]{1,0:T(8,128)(2,1)S(1)}, bf16[32,1024]{1,0:T(8,128)(2,1)S(1)}, u32[]{:S(2)}, u32[]{:S(2)}) collective-permute-start(bf16[32,1024]{1,0:T(8,128)(2,1)S(1)} %pad_maximum_fusion.5), channel_id=1, source_target_pairs={{16,0},{5,1},{18,2},{135,3},{20,4},{129,5},{22,6},{3,7},{24,8},{13... | collective-permute-start | bytes 196616 | tf_op jit(solution)/shard_map/ppermute | solution.py:61
  32.1 43.1 %copy-start.6 = (bf16[128,4096]{1,0:T(8,128)(2,1)}, bf16[128,4096]{1,0:T(8,128)(2,1)S(1)}, u32[]{:S(2)}) copy-start(bf16[128,4096]{1,0:T(8,128)(2,1)S(1)} %pad_maximum_fusion.refs_6_) | copy-start | bytes 3145732
  39.5 30.9 %collective-permute-start.13 = (bf16[128,4096]{1,0:T(8,128)(2,1)S(1)}, bf16[128,4096]{1,0:T(8,128)(2,1)}, u32[]{:S(2)}, u32[]{:S(2)}) collective-permute-start(bf16[128,4096]{1,0:T(8,128)(2,1)S(1)} %pad_maximum_fusion.refs_6_), channel_id=1, source_target_pairs={{2,0},{9,1},{4,2},{11,3},{6,4},{13,5},{128,6},{15,7},{10,8},{17,9}... | collective-permute-start | bytes 3145736 | tf_op jit(solution)/shard_map/ppermute | solution.py:61
  42.2 30.9 %collective-permute-start.16 = (bf16[128,4096]{1,0:T(8,128)(2,1)}, bf16[128,4096]{1,0:T(8,128)(2,1)}, u32[]{:S(2)}, u32[]{:S(2)}) collective-permute-start(bf16[128,4096]{1,0:T(8,128)(2,1)} %pad_maximum_fusion.1.refs_7_), channel_id=1, source_target_pairs={{134,0},{25,1},{0,2},{27,3},{2,4},{29,5},{4,6},{31,7},{142,8},{1,9... | collective-permute-start | bytes 3145736 | tf_op jit(solution)/shard_map/ppermute | solution.py:61
  42.2 12.3 %collective-permute-start.5 = (bf16[64,1024]{1,0:T(8,128)(2,1)S(1)}, bf16[64,1024]{1,0:T(8,128)(2,1)S(1)}, u32[]{:S(2)}, u32[]{:S(2)}) collective-permute-start(bf16[64,1024]{1,0:T(8,128)(2,1)S(1)} %pad_maximum_fusion.4), channel_id=1, source_target_pairs={{1,0},{0,1},{3,2},{2,3},{5,4},{4,5},{7,6},{6,7},{9,8},{8,9},{11,10... | collective-permute-start | bytes 393224 | tf_op jit(solution)/shard_map/ppermute | solution.py:61
  54.6 6.3 %collective-permute-start.6 = (bf16[64,1024]{1,0:T(8,128)(2,1)S(1)}, bf16[64,1024]{1,0:T(8,128)(2,1)S(1)}, u32[]{:S(2)}, u32[]{:S(2)}) collective-permute-start(bf16[64,1024]{1,0:T(8,128)(2,1)S(1)} %collective-permute-done.5), channel_id=1, source_target_pairs={{8,0},{3,1},{10,2},{5,3},{12,4},{7,5},{14,6},{129,7},{16,8},{11,9}... | collective-permute-start | bytes 393224 | tf_op jit(solution)/shard_map/ppermute | solution.py:61
  60.9 9.5 %collective-permute-start.7 = (bf16[128,1024]{1,0:T(8,128)(2,1)S(1)}, bf16[128,1024]{1,0:T(8,128)(2,1)S(1)}, u32[]{:S(2)}, u32[]{:S(2)}) collective-permute-start(bf16[128,1024]{1,0:T(8,128)(2,1)S(1)} %pad_maximum_fusion.3), channel_id=1, source_target_pairs={{16,0},{5,1},{18,2},{135,3},{20,4},{129,5},{22,6},{3,7},{24,8},{13... | collective-permute-start | bytes 786440 | tf_op jit(solution)/shard_map/ppermute | solution.py:61
  63.5 20.4 %collective-permute-start.14 = (bf16[128,4096]{1,0:T(8,128)(2,1)}, bf16[128,4096]{1,0:T(8,128)(2,1)}, u32[]{:S(2)}, u32[]{:S(2)}) collective-permute-start(bf16[128,4096]{1,0:T(8,128)(2,1)} %pad_maximum_fusion.1.refs_7_), channel_id=1, source_target_pairs={{2,0},{9,1},{4,2},{11,3},{6,4},{13,5},{128,6},{15,7},{10,8},{17,9}... | collective-permute-start | bytes 3145736 | tf_op jit(solution)/shard_map/ppermute | solution.py:61
  70.4 15.3 %collective-permute-start.15 = (bf16[128,4096]{1,0:T(8,128)(2,1)S(1)}, bf16[128,4096]{1,0:T(8,128)(2,1)}, u32[]{:S(2)}, u32[]{:S(2)}) collective-permute-start(bf16[128,4096]{1,0:T(8,128)(2,1)S(1)} %pad_maximum_fusion.refs_6_), channel_id=1, source_target_pairs={{134,0},{25,1},{0,2},{27,3},{2,4},{29,5},{4,6},{31,7},{142,8},{1,9... | collective-permute-start | bytes 3145736 | tf_op jit(solution)/shard_map/ppermute | solution.py:61
  70.4 24.1 %collective-permute-start.17 = (bf16[128,4096]{1,0:T(8,128)(2,1)}, bf16[128,4096]{1,0:T(8,128)(2,1)}, u32[]{:S(2)}, u32[]{:S(2)}) collective-permute-start(bf16[128,4096]{1,0:T(8,128)(2,1)} %collective-permute-done.13.refs_7_), channel_id=1, source_target_pairs={{2,0},{9,1},{4,2},{11,3},{6,4},{13,5},{128,6},{15,7},{10,8},{17,9}... | collective-permute-start | bytes 3145736 | tf_op jit(solution)/shard_map/ppermute | solution.py:61
  73.1 23.5 %collective-permute-start.18 = (bf16[128,4096]{1,0:T(8,128)(2,1)}, bf16[128,4096]{1,0:T(8,128)(2,1)}, u32[]{:S(2)}, u32[]{:S(2)}) collective-permute-start(bf16[128,4096]{1,0:T(8,128)(2,1)} %collective-permute-done.16.refs_10_), channel_id=1, source_target_pairs={{134,0},{25,1},{0,2},{27,3},{2,4},{29,5},{4,6},{31,7},{142,8},{1,9... | collective-permute-start | bytes 3145736 | tf_op jit(solution)/shard_map/ppermute | solution.py:61
  83.0 21.3 %collective-permute-start.19 = (bf16[512,256]{1,0:T(8,128)(2,1)S(1)}, bf16[512,256]{1,0:T(8,128)(2,1)S(1)}, u32[]{:S(2)}, u32[]{:S(2)}) collective-permute-start(bf16[512,256]{1,0:T(8,128)(2,1)S(1)} %get-tuple-element.29), channel_id=1, source_target_pairs={{1,0},{0,1},{3,2},{2,3},{5,4},{4,5},{7,6},{6,7},{9,8},{8,9},{11,10... | collective-permute-start | bytes 786440 | tf_op jit(solution)/shard_map/ppermute | solution.py:61
  94.4 9.9 %collective-permute-start.20 = (bf16[512,256]{1,0:T(8,128)(2,1)S(1)}, bf16[512,256]{1,0:T(8,128)(2,1)S(1)}, u32[]{:S(2)}, u32[]{:S(2)}) collective-permute-start(bf16[512,256]{1,0:T(8,128)(2,1)S(1)} %get-tuple-element.30), channel_id=1, source_target_pairs={{1,0},{0,1},{3,2},{2,3},{5,4},{4,5},{7,6},{6,7},{9,8},{8,9},{11,10... | collective-permute-start | bytes 786440 | tf_op jit(solution)/shard_map/ppermute | solution.py:61
  102.0 2.3 %collective-permute-start.21 = (bf16[512,256]{1,0:T(8,128)(2,1)S(1)}, bf16[512,256]{1,0:T(8,128)(2,1)S(1)}, u32[]{:S(2)}, u32[]{:S(2)}) collective-permute-start(bf16[512,256]{1,0:T(8,128)(2,1)S(1)} %get-tuple-element.31), channel_id=1, source_target_pairs={{1,0},{0,1},{3,2},{2,3},{5,4},{4,5},{7,6},{6,7},{9,8},{8,9},{11,10... | collective-permute-start | bytes 786440 | tf_op jit(solution)/shard_map/ppermute | solution.py:61
  102.1 2.2 %collective-permute-start.22 = (bf16[512,256]{1,0:T(8,128)(2,1)S(1)}, bf16[512,256]{1,0:T(8,128)(2,1)S(1)}, u32[]{:S(2)}, u32[]{:S(2)}) collective-permute-start(bf16[512,256]{1,0:T(8,128)(2,1)S(1)} %get-tuple-element.32), channel_id=1, source_target_pairs={{1,0},{0,1},{3,2},{2,3},{5,4},{4,5},{7,6},{6,7},{9,8},{8,9},{11,10... | collective-permute-start | bytes 786440 | tf_op jit(solution)/shard_map/ppermute | solution.py:61
  (6 other events, 134.9 us)

commit v4 on v3

--- a/solution.py
+++ b/solution.py
@@ -191,55 +191,81 @@
         out[:, k * wide : (k + 1) * wide] = sign[k * TILE : (k + 1) * TILE]
 
 
+def row_copies(weights, raw, sems):
+    copies = []
+    for g, refs in enumerate(weights):
+        pieces = [(ref, r) for ref in refs for r in range(0, ref.shape[0], TILE)]
+        copies.append(
+            [
+                pltpu.make_async_copy(ref.at[r : r + TILE], raw.at[g, f], sems.at[g, f])
+                for f, (ref, r) in enumerate(pieces)
+            ]
+        )
+        for copy in copies[g]:
+            copy.start()
+    return copies
+
+
+def rows_at(start, f):
+    return pl.ds(pl.multiple_of(lax.rem(start + f, 4) * TILE, TILE), TILE)
+
+
+def products(tokens, fresh, outs, t):
+    rows = fresh.shape[0]
+    per = tokens[0].shape[0] // rows
+    cut = slice(t % per * rows, (t % per + 1) * rows)
+    product = lax.dot_general(tokens[t // per][cut], fresh[...], NT, preferred_element_type=F32)
+    outs[t // per][cut] = product.astype(BF16)
+
+
 def forward_kernel(parts, first, back_rows, back_cols, *refs):
     groups = len(parts)
     refs = list(refs)
-    bands = [refs.pop(0) for _ in range(groups)]
+    bands = [refs.pop(0) for _ in range(groups + 1)]
     tokens = [refs.pop(0) for _ in range(2)]
     weights = [[refs.pop(0) for _ in range(n)] for n in parts]
     outs = [refs.pop(0) for _ in range(2 * groups)]
-    raw, *fresh, raw_sem = refs
+    step, raw, *fresh, sems = refs
     wide = WIDE * TILE
-    rows, width = fresh[0].shape
-    per = tokens[0].shape[0] // rows
+    width = step.shape[1]
     start = first[0]
-
-    pieces = []
-    for g in range(groups):
-        found = []
-        for ref in weights[g]:
-            found += [(ref, r) for r in range(0, ref.shape[0], TILE)]
-        pieces.append(found)
-    raw_copy = {}
-    for g in range(groups):
-        for f, (ref, r) in enumerate(pieces[g]):
-            raw_copy[g, f] = pltpu.make_async_copy(ref.at[r : r + TILE], raw.at[g, f], raw_sem.at[g, f])
-    for g in range(groups):
-        for f in range(4):
-            raw_copy[g, f].start()
+    copies = row_copies(weights, raw, sems)
 
     def renew(g, f):
         tall = dot(back_rows[...], bands[g][f * BAND : (f + 1) * BAND]).astype(BF16)
-        sign = soft_sign(dot(stacked(tall, WIDE * BAND), back_cols[...]))
-        at = pl.ds(pl.multiple_of(lax.rem(start + f, 4) * TILE, TILE), TILE)
+        sign = step_rate * soft_sign(dot(stacked(tall, WIDE * BAND), back_cols[...]))
+        at = rows_at(start, f)
         for k in range(width // wide):
             cut = slice(k * wide, (k + 1) * wide)
-            new = raw[g, f, :, cut].astype(F32) - step_rate * sign[k * TILE : (k + 1) * TILE]
-            fresh[g % 2][at, cut] = new.astype(BF16)
+            part = sign[k * TILE : (k + 1) * TILE]
+            if g == groups:
+                step[at, cut] = part.astype(BF16)
+            else:
+                fresh[g % 2][at, cut] = (raw[g, f, :, cut].astype(F32) - part).astype(BF16)
 
     for f in range(4):
-        raw_copy[0, f].wait()
+        copies[0][f].wait()
         renew(0, f)
     for g in range(groups):
         if g + 1 < groups:
             for f in range(4):
-                raw_copy[g + 1, f].wait()
+                copies[g + 1][f].wait()
         for t in range(4):
-            cut = slice(t % per * rows, (t % per + 1) * rows)
-            product = lax.dot_general(tokens[t // per][cut], fresh[g % 2][...], NT, preferred_element_type=F32)
-            outs[2 * g + t // per][cut] = product.astype(BF16)
-            if g + 1 < groups:
-                renew(g + 1, t)
+            products(tokens, fresh[g % 2], outs[2 * g : 2 * g + 2], t)
+            renew(g + 1, t)
+
+
+def last_kernel(parts, first, own, other, step, *refs):
+    refs = list(refs)
+    weights = [refs.pop(0) for _ in range(parts)]
+    out_own, out_other, raw, fresh, sems = refs
+    copies = row_copies([weights], raw, sems)[0]
+    for f in range(4):
+        copies[f].wait()
+        at = rows_at(first[0], f)
+        fresh[at] = (raw[0, f].astype(F32) - step[at].astype(F32)).astype(BF16)
+    for t in range(4):
+        products((own, other), fresh, (out_own, out_other), t)
 
 
 def weave_kernel(where, *refs):
@@ -296,74 +322,84 @@
         return lax.optimization_barrier((value, *others))[0]
 
     swapped = fetch(weight, sibling)
-    other = fetch(after(activations, swapped), sibling)
     swapped = after(swapped, rounded)
     ahead, behind, across = (fetch(swapped, along(0, s)) for s in (1, -1, 2))
 
     def join(value, source):
         return value.astype(F32) + fetch(value, source).astype(F32)
 
-    sent = join(rounded, far_z).astype(BF16)
-    total = join(join(sent, pair_x).astype(BF16), along_x(2))
-    own = stay(after(activations, sent))
-    other = stay(other)
+    sent = join(after(rounded, swapped), far_z).astype(BF16)
+    other = fetch(after(activations, sent), sibling)
+    second_sum = join(after(sent, ahead, behind), pair_x).astype(BF16)
+    total = join(after(second_sum, across), along_x(2))
+    own, other = stay(after(activations, sent)), stay(other)
 
     new_momentum = call(
         residual_kernel,
         shape(momentum.shape, F32),
         (momentum, gradient, exact, back_rows3, back_hi, back_lo),
     )
-
-    def gather(value):
-        pair = jnp.concatenate([value, fetch(value, along(0, 1))], axis=0)
-        return pair, fetch(pair, along(0, 2))
-
-    band_line = jnp.concatenate(gather(total.astype(BF16)), axis=0)
-    near, far = gather(fetch(band_line, sibling))
-    blocks = jnp.concatenate([near, far], axis=0).reshape(4, 4, BAND, narrow)
-    bands = [blocks[:, g].reshape(4 * BAND, narrow) for g in range(4)]
+    direction = call(
+        direction_kernel,
+        shape((rows, width), F32),
+        (total, back_rows3, back_hi, back_lo),
+    )
 
     early = after(jnp.concatenate([swapped, ahead], axis=0), sent)
-    late = after(jnp.concatenate([across, behind], axis=0), new_momentum)
+    late = jnp.concatenate([across, behind], axis=0)
     next_early, last_early = fetch(early, along(1, 1)), fetch(early, along(1, -1))
     next_late, last_late = fetch(late, along(1, 1)), fetch(late, along(1, -1))
     far_early, far_late = fetch(next_early, along(1, 1)), fetch(last_late, along(1, -1))
     lines = [[early, late], [next_early, next_late], [far_early, far_late], [last_early, last_late]]
 
-    direction = call(
-        direction_kernel,
-        shape((rows, width), F32),
-        (total, back_rows3, back_hi, back_lo),
-    )
-
-    def forward(order):
-        parts = [len(lines[g]) for g in order]
-        inputs = [first[None], back_rows, back_hi] + [bands[g] for g in order]
-        kept = [line for g in order for line in lines[g]]
-        block = shape((tokens, 4 * rows), BF16)
-        return call(
-            lambda *refs: forward_kernel(parts, *refs),
-            tuple([block] * (2 * len(order))),
-            inputs,
-            (
-                pltpu.VMEM((len(order), 4, rows, width), BF16),
-                pltpu.VMEM((4 * rows, width), BF16),
-                pltpu.VMEM((4 * rows, width), BF16),
-                pltpu.SemaphoreType.DMA((len(order), 4)),
-            ),
-            limit=24,
-            flops=len(order) * 2 * 2 * tokens * 4 * rows * width,
-            smem=1,
-            kept=kept,
-            resident=(own, other),
-        )
-
+    def gather(value, *others):
+        pair = jnp.concatenate([value, fetch(value, along(0, 1))], axis=0)
+        return jnp.concatenate([pair, fetch(after(pair, *others), along(0, 2))], axis=0)
+
+    band_line = gather(after(total.astype(BF16), late, new_momentum, own, other))
+    band_line = fetch(after(band_line, next_early, last_early, direction), sibling)
+    blocks = gather(band_line, next_late, last_late).reshape(4, 4, BAND, narrow)
+    bands = [blocks[:, g].reshape(4 * BAND, narrow) for g in range(4)]
+
+    block = shape((tokens, 4 * rows), BF16)
+    step = pltpu.VMEM((4 * rows, width), BF16)
+    order = [0, 3, 1]
+    parts = [len(lines[g]) for g in order]
+    *results, step = call(
+        lambda *refs: forward_kernel(parts, *refs),
+        (*[block] * 6, step),
+        [first[None], back_rows, back_hi] + [bands[g] for g in order + [2]],
+        (
+            pltpu.VMEM((3, 4, rows, width), BF16),
+            pltpu.VMEM((4 * rows, width), BF16),
+            pltpu.VMEM((4 * rows, width), BF16),
+            pltpu.SemaphoreType.DMA((3, 4)),
+        ),
+        limit=24,
+        flops=3 * 2 * 2 * tokens * 4 * rows * width,
+        smem=1,
+        kept=[line for g in order for line in lines[g]],
+        resident=(own, other),
+    )
+    results += call(
+        lambda *refs: last_kernel(len(lines[2]), *refs),
+        (block, block),
+        [first[None]],
+        (
+            pltpu.VMEM((1, 4, rows, width), BF16),
+            pltpu.VMEM((4 * rows, width), BF16),
+            pltpu.SemaphoreType.DMA((1, 4)),
+        ),
+        limit=24,
+        flops=2 * 2 * tokens * 4 * rows * width,
+        smem=1,
+        kept=lines[2],
+        resident=(own, other, step),
+    )
     mine, theirs = [None] * 4, [None] * 4
-    for order in ([0], [1, 3], [2]):
-        result = forward(order)
-        for n, g in enumerate(order):
-            mine[g] = result[2 * n]
-            theirs[g] = fetch(result[2 * n + 1], sibling)
+    for n, g in enumerate(order + [2]):
+        mine[g] = results[2 * n]
+        theirs[g] = fetch(results[2 * n + 1], sibling)
     where = jnp.stack([core.astype(jnp.int32), second, first])
     projected = call(
         weave_kernel,

time: 107 us -> 114 us (1.065)
  the two profiles are of different devices: /device:TPU:1 before, /device:TPU:25 now
where the time goes in v4:
time: 114 us
  starting transfers between devices  52.3 us (46%)
  Pallas kernels  30.4 us (27%)
  waiting for transfers between devices  19.7 us (17%)
  local copies, waits for them, and re-layouts  10.5 us (9%)
    ppermute x23, starting transfers between devices, fetch(): lax.ppermute(value, AXES, [(place(*source(*spot(i))), i) for i in range(2...  52.3 us
    pallas_call x8, Pallas kernels, call(): pl.pallas_call(kernel, out_shape=out_shape, in_specs=specs, out_specs=jax...  30.4 us
    ppermute x23, waiting for transfers between devices, fetch(): lax.ppermute(value, AXES, [(place(*source(*spot(i))), i) for i in range(2...  19.7 us
    unnamed x35, local copies, waits for them, and re-layouts  10.5 us
  transfers between devices with their start and end apart: 23, of which 13 were waited for; matrix products, arithmetic and copies ran while one was open for 0% of the time, Pallas kernels for 24%

profile of v4, /device:TPU:25, one launch (start us, length us, event | category | flops | bytes accessed | tf_op | source)
XLA Modules:
  0.0 114.2 jit_solution(4678791383337488550)
XLA Ops:
  1.4 3.0 %shard_map.121 = (f32[16,1024]{1,0:T(8,128)S(1)}, bf16[16,1024]{1,0:T(8,128)(2,1)S(1)}) custom-call(f32[1,64,4096]{2,1,0:T(8,128)} %momentum.3, bf16[1,64,4096]{2,1,0:T(8,128)(2,1)} %gradient.3, bf16[1024,128]{1,0:T(8,128)(2,1)} %constant.61.clone.cols, bf16[16,192]{1,0:T(8,128)(2,1)} %constant.62.clone.rows3), custom_call_target="tpu_custom_call" | custom-call | bytes 1841152 | tf_op jit(solution)/shard_map/pallas_call | solution.py:99
  4.5 7.0 %collective-permute-start.1 = (bf16[16,1024]{1,0:T(8,128)(2,1)S(1)}, bf16[16,1024]{1,0:T(8,128)(2,1)S(1)}, u32[]{:S(2)}, u32[]{:S(2)}) collective-permute-start(bf16[16,1024]{1,0:T(8,128)(2,1)S(1)} %get-tuple-element.26), channel_id=1, source_target_pairs={{128,0},{129,1},{130,2},{131,3},{132,4},{133,5},{134,6},{135,7},{1... | collective-permute-start | bytes 98312 | tf_op jit(solution)/shard_map/ppermute | solution.py:61
  14.1 4.1 %collective-permute-start.2 = (bf16[64,4096]{1,0:T(8,128)(2,1)S(1)}, bf16[64,4096]{1,0:T(8,128)(2,1)S(1)}, u32[]{:S(2)}, u32[]{:S(2)}) collective-permute-start(bf16[64,4096]{1,0:T(8,128)(2,1)S(1)} %collective-permute-done), channel_id=1, source_target_pairs={{8,0},{3,1},{10,2},{5,3},{12,4},{7,5},{14,6},{129,7},{16,8},{11,9}... | collective-permute-start | bytes 1572872 | tf_op jit(solution)/shard_map/ppermute | solution.py:61
  20.0 4.2 %collective-permute-done.2 = bf16[64,4096]{1,0:T(8,128)(2,1)S(1)} collective-permute-done((bf16[64,4096]{1,0:T(8,128)(2,1)S(1)}, bf16[64,4096]{1,0:T(8,128)(2,1)S(1)}, u32[]{:S(2)}, u32[]{:S(2)}) %collective-permute-start.2) | collective-permute-done | bytes 524320 | tf_op jit(solution)/shard_map/ppermute | solution.py:61
  24.9 2.2 %collective-permute-start.11 = (bf16[128,4096]{1,0:T(8,128)(2,1)S(1)}, bf16[128,4096]{1,0:T(8,128)(2,1)S(1)}, u32[]{:S(2)}, u32[]{:S(2)}) collective-permute-start(bf16[128,4096]{1,0:T(8,128)(2,1)S(1)} %pad_maximum_fusion.refs_9_), channel_id=1, source_target_pairs={{134,0},{25,1},{0,2},{27,3},{2,4},{29,5},{4,6},{31,7},{142,8},{1,9... | collective-permute-start | bytes 3145736 | tf_op jit(solution)/shard_map/ppermute | solution.py:61
  30.4 2.9 %collective-permute-start.6 = (bf16[16,1024]{1,0:T(8,128)(2,1)S(1)}, bf16[16,1024]{1,0:T(8,128)(2,1)S(1)}, u32[]{:S(2)}, u32[]{:S(2)}) collective-permute-start(bf16[16,1024]{1,0:T(8,128)(2,1)S(1)} %add_convert_fusion), channel_id=1, source_target_pairs={{64,0},{65,1},{66,2},{67,3},{68,4},{69,5},{70,6},{71,7},{72,8},{73... | collective-permute-start | bytes 98312 | tf_op jit(solution)/shard_map/ppermute | solution.py:61
  37.8 2.2 %shard_map.124.refs_7_.refs_1_ = bf16[512,4096]{1,0:T(8,128)(2,1)S(1)} custom-call(bf16[512,4096]{1,0:T(8,128)(2,1)} %source), custom_call_target="tpu_custom_call" | custom-call | bytes 4194304 | tf_op jit(solution)/shard_map/pallas_call | solution.py:99
  40.0 2.0 %copy-done = bf16[512,4096]{1,0:T(8,128)(2,1)} copy-done((bf16[512,4096]{1,0:T(8,128)(2,1)}, bf16[512,4096]{1,0:T(8,128)(2,1)S(1)}, u32[]{:S(2)}) %copy-start) | copy-done | bytes 4194328
  42.0 2.0 %copy-done.12 = bf16[512,4096]{1,0:T(8,128)(2,1)} copy-done((bf16[512,4096]{1,0:T(8,128)(2,1)}, bf16[512,4096]{1,0:T(8,128)(2,1)S(1)}, u32[]{:S(2)}) %copy-start.12) | copy-done | bytes 4194328
  44.0 2.2 %shard_map.125.refs_8_.refs_2_ = bf16[512,4096]{1,0:T(8,128)(2,1)S(1)} custom-call(bf16[512,4096]{1,0:T(8,128)(2,1)} %copy-done.12), custom_call_target="tpu_custom_call" | custom-call | bytes 4194304 | tf_op jit(solution)/shard_map/pallas_call | solution.py:99
  46.3 2.0 %copy-done.3 = bf16[512,4096]{1,0:T(8,128)(2,1)} copy-done((bf16[512,4096]{1,0:T(8,128)(2,1)}, bf16[512,4096]{1,0:T(8,128)(2,1)S(1)}, u32[]{:S(2)}) %copy-start.3) | copy-done | bytes 4194328
  48.3 3.1 %collective-permute-start.8 = (bf16[16,1024]{1,0:T(8,128)(2,1)S(1)}, bf16[16,1024]{1,0:T(8,128)(2,1)S(1)}, u32[]{:S(2)}, u32[]{:S(2)}) collective-permute-start(bf16[16,1024]{1,0:T(8,128)(2,1)S(1)} %get-tuple-element.30), channel_id=1, source_target_pairs={{8,0},{3,1},{10,2},{5,3},{12,4},{7,5},{14,6},{129,7},{16,8},{11,9}... | collective-permute-start | bytes 98312 | tf_op jit(solution)/shard_map/ppermute | solution.py:61
  51.4 2.8 %collective-permute-done.8 = bf16[16,1024]{1,0:T(8,128)(2,1)S(1)} collective-permute-done((bf16[16,1024]{1,0:T(8,128)(2,1)S(1)}, bf16[16,1024]{1,0:T(8,128)(2,1)S(1)}, u32[]{:S(2)}, u32[]{:S(2)}) %collective-permute-start.8) | collective-permute-done | bytes 32800 | tf_op jit(solution)/shard_map/ppermute | solution.py:61
  58.8 10.4 %collective-permute-start.12 = (bf16[64,1024]{1,0:T(8,128)(2,1)S(1)}, bf16[64,1024]{1,0:T(8,128)(2,1)S(1)}, u32[]{:S(2)}, u32[]{:S(2)}) collective-permute-start(bf16[64,1024]{1,0:T(8,128)(2,1)S(1)} %pad_maximum_fusion.3), channel_id=1, source_target_pairs={{1,0},{0,1},{3,2},{2,3},{5,4},{4,5},{7,6},{6,7},{9,8},{8,9},{11,10... | collective-permute-start | bytes 393224 | tf_op jit(solution)/shard_map/ppermute | solution.py:61
  70.2 2.9 %collective-permute-start.13 = (bf16[64,1024]{1,0:T(8,128)(2,1)S(1)}, bf16[64,1024]{1,0:T(8,128)(2,1)S(1)}, u32[]{:S(2)}, u32[]{:S(2)}) collective-permute-start(bf16[64,1024]{1,0:T(8,128)(2,1)S(1)} %collective-permute-done.12), channel_id=1, source_target_pairs={{8,0},{3,1},{10,2},{5,3},{12,4},{7,5},{14,6},{129,7},{16,8},{11,9}... | collective-permute-start | bytes 393224 | tf_op jit(solution)/shard_map/ppermute | solution.py:61
  75.1 2.4 %collective-permute-start.16 = (bf16[128,1024]{1,0:T(8,128)(2,1)S(1)}, bf16[128,1024]{1,0:T(8,128)(2,1)S(1)}, u32[]{:S(2)}, u32[]{:S(2)}) collective-permute-start(bf16[128,1024]{1,0:T(8,128)(2,1)S(1)} %pad_maximum_fusion.2), channel_id=1, source_target_pairs={{16,0},{5,1},{18,2},{135,3},{20,4},{129,5},{22,6},{3,7},{24,8},{13... | collective-permute-start | bytes 786440 | tf_op jit(solution)/shard_map/ppermute | solution.py:61
  77.5 2.7 %collective-permute-start.18 = (bf16[128,4096]{1,0:T(8,128)(2,1)}, bf16[128,4096]{1,0:T(8,128)(2,1)}, u32[]{:S(2)}, u32[]{:S(2)}) collective-permute-start(bf16[128,4096]{1,0:T(8,128)(2,1)} %collective-permute-done.15.refs_12_), channel_id=1, source_target_pairs={{134,0},{25,1},{0,2},{27,3},{2,4},{29,5},{4,6},{31,7},{142,8},{1,9... | collective-permute-start | bytes 3145736 | tf_op jit(solution)/shard_map/ppermute | solution.py:61
  80.2 3.0 %collective-permute-done.16 = bf16[128,1024]{1,0:T(8,128)(2,1)S(1)} collective-permute-done((bf16[128,1024]{1,0:T(8,128)(2,1)S(1)}, bf16[128,1024]{1,0:T(8,128)(2,1)S(1)}, u32[]{:S(2)}, u32[]{:S(2)}) %collective-permute-start.16) | collective-permute-done | bytes 262176 | tf_op jit(solution)/shard_map/ppermute | solution.py:61
  83.3 2.2 %copy-done.1 = bf16[512,4096]{1,0:T(8,128)(2,1)S(1)} copy-done((bf16[512,4096]{1,0:T(8,128)(2,1)S(1)}, bf16[512,4096]{1,0:T(8,128)(2,1)}, u32[]{:S(2)}) %copy-start.1) | copy-done | bytes 4194328
  85.5 2.2 %copy-done.4 = bf16[512,4096]{1,0:T(8,128)(2,1)S(1)} copy-done((bf16[512,4096]{1,0:T(8,128)(2,1)S(1)}, bf16[512,4096]{1,0:T(8,128)(2,1)}, u32[]{:S(2)}) %copy-start.4) | copy-done | bytes 4194328
  87.7 12.8 %shard_map.126 = (bf16[512,256]{1,0:T(8,128)(2,1)S(1)}, bf16[512,256]{1,0:T(8,128)(2,1)S(1)}, bf16[512,256]{1,0:T(8,128)(2,1)S(1)}, bf16[512,256]{1,0:T(8,128)(2...) custom-call(s32[1]{0:T(128)} %bitcast.2.refs_0_, ...), custom_call_target="tpu_custom_call" | custom-call | flops 6442450944 | bytes 15337476 | tf_op jit(solution)/shard_map/pallas_call | solution.py:99
  100.5 4.4 %collective-permute-start.19 = (bf16[512,256]{1,0:T(8,128)(2,1)S(1)}, bf16[512,256]{1,0:T(8,128)(2,1)S(1)}, u32[]{:S(2)}, u32[]{:S(2)}) collective-permute-start(bf16[512,256]{1,0:T(8,128)(2,1)S(1)} %get-tuple-element.39), channel_id=1, source_target_pairs={{1,0},{0,1},{3,2},{2,3},{5,4},{4,5},{7,6},{6,7},{9,8},{8,9},{11,10... | collective-permute-start | bytes 786440 | tf_op jit(solution)/shard_map/ppermute | solution.py:61
  105.4 4.0 %shard_map.127 = (bf16[512,256]{1,0:T(8,128)(2,1)S(1)}, bf16[512,256]{1,0:T(8,128)(2,1)S(1)}) custom-call(s32[1]{0:T(128)} %bitcast.2.refs_0_, bf16[512,4096]{1,0:T(8,128)(2,1)S(1)} %copy-done.2, bf16[512,4096]{1,0:T(8,128)(2,1)S(1)} %copy-done.5, bf16[256,4096]{1,0:T(8,128)(2,1)S(1)} %get-tuple-element.36.refs_3_, ...), custom_call_target="tpu_custom_call" | custom-call | flops 2147483648 | bytes 12582916 | tf_op jit(solution)/shard_map/pallas_call | solution.py:99
  111.4 2.8 %shard_map.128 = bf16[512,2048]{1,0:T(8,128)(2,1)} custom-call(s32[3]{0:T(128)S(1)} %pad_add_fusion.where, bf16[512,256]{1,0:T(8,128)(2,1)S(1)} %get-tuple-element.34.refs_0_, bf16[512,256]{1,0:T(8,128)(2,1)S(1)} %get-tuple-element.35.refs_1_, bf16[512,256]{1,0:T(8,128)(2,1)S(1)} %get-tuple-element.37.refs_2_, ...), custom_call_target="tpu_custom_call" | custom-call | bytes 2097164 | tf_op jit(solution)/shard_map/pallas_call | solution.py:99
  (76 shorter events, 23.7 us)
Async XLA Ops:
  0.6 3.8 %collective-permute-start = (bf16[64,4096]{1,0:T(8,128)(2,1)}, bf16[64,4096]{1,0:T(8,128)(2,1)S(1)}, u32[]{:S(2)}, u32[]{:S(2)}) collective-permute-start(bf16[64,4096]{1,0:T(8,128)(2,1)} %param.12), channel_id=1, source_target_pairs={{1,0},{0,1},{3,2},{2,3},{5,4},{4,5},{7,6},{6,7},{9,8},{8,9},{11,10... | collective-permute-start | bytes 1572872 | tf_op jit(solution)/shard_map/ppermute | solution.py:61
  4.5 8.7 %collective-permute-start.1 = (bf16[16,1024]{1,0:T(8,128)(2,1)S(1)}, bf16[16,1024]{1,0:T(8,128)(2,1)S(1)}, u32[]{:S(2)}, u32[]{:S(2)}) collective-permute-start(bf16[16,1024]{1,0:T(8,128)(2,1)S(1)} %get-tuple-element.26), channel_id=1, source_target_pairs={{128,0},{129,1},{130,2},{131,3},{132,4},{133,5},{134,6},{135,7},{1... | collective-permute-start | bytes 98312 | tf_op jit(solution)/shard_map/ppermute | solution.py:61
  13.3 28.7 %collective-permute-start.7 = (bf16[512,4096]{1,0:T(8,128)(2,1)}, bf16[512,4096]{1,0:T(8,128)(2,1)S(1)}, u32[]{:S(2)}, u32[]{:S(2)}) collective-permute-start(bf16[512,4096]{1,0:T(8,128)(2,1)} %source), channel_id=1, source_target_pairs={{1,0},{0,1},{3,2},{2,3},{5,4},{4,5},{7,6},{6,7},{9,8},{8,9},{11,10... | collective-permute-start | bytes 12582920 | tf_op jit(solution)/shard_map/ppermute | solution.py:61
  14.1 10.2 %collective-permute-start.2 = (bf16[64,4096]{1,0:T(8,128)(2,1)S(1)}, bf16[64,4096]{1,0:T(8,128)(2,1)S(1)}, u32[]{:S(2)}, u32[]{:S(2)}) collective-permute-start(bf16[64,4096]{1,0:T(8,128)(2,1)S(1)} %collective-permute-done), channel_id=1, source_target_pairs={{8,0},{3,1},{10,2},{5,3},{12,4},{7,5},{14,6},{129,7},{16,8},{11,9}... | collective-permute-start | bytes 1572872 | tf_op jit(solution)/shard_map/ppermute | solution.py:61
  18.1 9.5 %collective-permute-start.3 = (bf16[64,4096]{1,0:T(8,128)(2,1)S(1)}, bf16[64,4096]{1,0:T(8,128)(2,1)S(1)}, u32[]{:S(2)}, u32[]{:S(2)}) collective-permute-start(bf16[64,4096]{1,0:T(8,128)(2,1)S(1)} %collective-permute-done), channel_id=1, source_target_pairs={{24,0},{135,1},{26,2},{1,3},{28,4},{3,5},{30,6},{5,7},{0,8},{143,9... | collective-permute-start | bytes 1572872 | tf_op jit(solution)/shard_map/ppermute | solution.py:61
  18.1 11.7 %collective-permute-start.5 = (bf16[64,4096]{1,0:T(8,128)(2,1)S(1)}, bf16[64,4096]{1,0:T(8,128)(2,1)S(1)}, u32[]{:S(2)}, u32[]{:S(2)}) collective-permute-start(bf16[64,4096]{1,0:T(8,128)(2,1)S(1)} %collective-permute-done), channel_id=1, source_target_pairs={{16,0},{5,1},{18,2},{135,3},{20,4},{129,5},{22,6},{3,7},{24,8},{13... | collective-permute-start | bytes 1572872 | tf_op jit(solution)/shard_map/ppermute | solution.py:61
  24.3 34.4 %collective-permute-start.10 = (bf16[128,4096]{1,0:T(8,128)(2,1)S(1)}, bf16[128,4096]{1,0:T(8,128)(2,1)}, u32[]{:S(2)}, u32[]{:S(2)}) collective-permute-start(bf16[128,4096]{1,0:T(8,128)(2,1)S(1)} %pad_maximum_fusion.refs_9_), channel_id=1, source_target_pairs={{2,0},{9,1},{4,2},{11,3},{6,4},{13,5},{128,6},{15,7},{10,8},{17,9}... | collective-permute-start | bytes 3145736 | tf_op jit(solution)/shard_map/ppermute | solution.py:61
  24.9 33.9 %collective-permute-start.11 = (bf16[128,4096]{1,0:T(8,128)(2,1)S(1)}, bf16[128,4096]{1,0:T(8,128)(2,1)S(1)}, u32[]{:S(2)}, u32[]{:S(2)}) collective-permute-start(bf16[128,4096]{1,0:T(8,128)(2,1)S(1)} %pad_maximum_fusion.refs_9_), channel_id=1, source_target_pairs={{134,0},{25,1},{0,2},{27,3},{2,4},{29,5},{4,6},{31,7},{142,8},{1,9... | collective-permute-start | bytes 3145736 | tf_op jit(solution)/shard_map/ppermute | solution.py:61
  27.7 2.8 %collective-permute-start.4 = (bf16[16,1024]{1,0:T(8,128)(2,1)S(1)}, bf16[16,1024]{1,0:T(8,128)(2,1)S(1)}, u32[]{:S(2)}, u32[]{:S(2)}) collective-permute-start(bf16[16,1024]{1,0:T(8,128)(2,1)S(1)} %add_convert_fusion.1), channel_id=1, source_target_pairs={{32,0},{33,1},{34,2},{35,3},{36,4},{37,5},{38,6},{39,7},{40,8},{41... | collective-permute-start | bytes 98312 | tf_op jit(solution)/shard_map/ppermute | solution.py:61
  30.4 4.4 %collective-permute-start.6 = (bf16[16,1024]{1,0:T(8,128)(2,1)S(1)}, bf16[16,1024]{1,0:T(8,128)(2,1)S(1)}, u32[]{:S(2)}, u32[]{:S(2)}) collective-permute-start(bf16[16,1024]{1,0:T(8,128)(2,1)S(1)} %add_convert_fusion), channel_id=1, source_target_pairs={{64,0},{65,1},{66,2},{67,3},{68,4},{69,5},{70,6},{71,7},{72,8},{73... | collective-permute-start | bytes 98312 | tf_op jit(solution)/shard_map/ppermute | solution.py:61
  33.4 41.7 %collective-permute-start.14 = (bf16[128,4096]{1,0:T(8,128)(2,1)S(1)}, bf16[128,4096]{1,0:T(8,128)(2,1)S(1)}, u32[]{:S(2)}, u32[]{:S(2)}) collective-permute-start(bf16[128,4096]{1,0:T(8,128)(2,1)S(1)} %constant_dynamic-update-slice_fusion.refs_10_), channel_id=1, source_target_pairs={{2,0},{9,1},{4,2},{11,3},{6,4},{13,5},{128,6},{15,7},{10,8},{17,9}... | collective-permute-start | bytes 3145736 | tf_op jit(solution)/shard_map/ppermute | solution.py:61
  34.8 40.3 %collective-permute-start.15 = (bf16[128,4096]{1,0:T(8,128)(2,1)S(1)}, bf16[128,4096]{1,0:T(8,128)(2,1)}, u32[]{:S(2)}, u32[]{:S(2)}) collective-permute-start(bf16[128,4096]{1,0:T(8,128)(2,1)S(1)} %constant_dynamic-update-slice_fusion.refs_10_), channel_id=1, source_target_pairs={{134,0},{25,1},{0,2},{27,3},{2,4},{29,5},{4,6},{31,7},{142,8},{1,9... | collective-permute-start | bytes 3145736 | tf_op jit(solution)/shard_map/ppermute | solution.py:61
  48.3 5.9 %collective-permute-start.8 = (bf16[16,1024]{1,0:T(8,128)(2,1)S(1)}, bf16[16,1024]{1,0:T(8,128)(2,1)S(1)}, u32[]{:S(2)}, u32[]{:S(2)}) collective-permute-start(bf16[16,1024]{1,0:T(8,128)(2,1)S(1)} %get-tuple-element.30), channel_id=1, source_target_pairs={{8,0},{3,1},{10,2},{5,3},{12,4},{7,5},{14,6},{129,7},{16,8},{11,9}... | collective-permute-start | bytes 98312 | tf_op jit(solution)/shard_map/ppermute | solution.py:61
  54.2 4.6 %collective-permute-start.9 = (bf16[32,1024]{1,0:T(8,128)(2,1)S(1)}, bf16[32,1024]{1,0:T(8,128)(2,1)S(1)}, u32[]{:S(2)}, u32[]{:S(2)}) collective-permute-start(bf16[32,1024]{1,0:T(8,128)(2,1)S(1)} %pad_maximum_fusion.4), channel_id=1, source_target_pairs={{16,0},{5,1},{18,2},{135,3},{20,4},{129,5},{22,6},{3,7},{24,8},{13... | collective-permute-start | bytes 196616 | tf_op jit(solution)/shard_map/ppermute | solution.py:61
  55.6 27.7 %copy-start.11 = (bf16[64,16]{1,0:T(8,128)(2,1)S(1)}, bf16[64,16]{1,0:T(8,128)(2,1)}, u32[]{:S(2)}) copy-start(bf16[64,16]{1,0:T(8,128)(2,1)} %constant.66.clone.refs_1_) | copy-start | bytes 6148
  58.8 11.4 %collective-permute-start.12 = (bf16[64,1024]{1,0:T(8,128)(2,1)S(1)}, bf16[64,1024]{1,0:T(8,128)(2,1)S(1)}, u32[]{:S(2)}, u32[]{:S(2)}) collective-permute-start(bf16[64,1024]{1,0:T(8,128)(2,1)S(1)} %pad_maximum_fusion.3), channel_id=1, source_target_pairs={{1,0},{0,1},{3,2},{2,3},{5,4},{4,5},{7,6},{6,7},{9,8},{8,9},{11,10... | collective-permute-start | bytes 393224 | tf_op jit(solution)/shard_map/ppermute | solution.py:61
  70.2 4.9 %collective-permute-start.13 = (bf16[64,1024]{1,0:T(8,128)(2,1)S(1)}, bf16[64,1024]{1,0:T(8,128)(2,1)S(1)}, u32[]{:S(2)}, u32[]{:S(2)}) collective-permute-start(bf16[64,1024]{1,0:T(8,128)(2,1)S(1)} %collective-permute-done.12), channel_id=1, source_target_pairs={{8,0},{3,1},{10,2},{5,3},{12,4},{7,5},{14,6},{129,7},{16,8},{11,9}... | collective-permute-start | bytes 393224 | tf_op jit(solution)/shard_map/ppermute | solution.py:61
  75.1 8.1 %collective-permute-start.16 = (bf16[128,1024]{1,0:T(8,128)(2,1)S(1)}, bf16[128,1024]{1,0:T(8,128)(2,1)S(1)}, u32[]{:S(2)}, u32[]{:S(2)}) collective-permute-start(bf16[128,1024]{1,0:T(8,128)(2,1)S(1)} %pad_maximum_fusion.2), channel_id=1, source_target_pairs={{16,0},{5,1},{18,2},{135,3},{20,4},{129,5},{22,6},{3,7},{24,8},{13... | collective-permute-start | bytes 786440 | tf_op jit(solution)/shard_map/ppermute | solution.py:61
  77.5 27.8 %collective-permute-start.17 = (bf16[128,4096]{1,0:T(8,128)(2,1)}, bf16[128,4096]{1,0:T(8,128)(2,1)}, u32[]{:S(2)}, u32[]{:S(2)}) collective-permute-start(bf16[128,4096]{1,0:T(8,128)(2,1)} %collective-permute-done.10.refs_13_), channel_id=1, source_target_pairs={{2,0},{9,1},{4,2},{11,3},{6,4},{13,5},{128,6},{15,7},{10,8},{17,9}... | collective-permute-start | bytes 3145736 | tf_op jit(solution)/shard_map/ppermute | solution.py:61
  77.5 27.8 %collective-permute-start.18 = (bf16[128,4096]{1,0:T(8,128)(2,1)}, bf16[128,4096]{1,0:T(8,128)(2,1)}, u32[]{:S(2)}, u32[]{:S(2)}) collective-permute-start(bf16[128,4096]{1,0:T(8,128)(2,1)} %collective-permute-done.15.refs_12_), channel_id=1, source_target_pairs={{134,0},{25,1},{0,2},{27,3},{2,4},{29,5},{4,6},{31,7},{142,8},{1,9... | collective-permute-start | bytes 3145736 | tf_op jit(solution)/shard_map/ppermute | solution.py:61
  100.5 9.5 %collective-permute-start.19 = (bf16[512,256]{1,0:T(8,128)(2,1)S(1)}, bf16[512,256]{1,0:T(8,128)(2,1)S(1)}, u32[]{:S(2)}, u32[]{:S(2)}) collective-permute-start(bf16[512,256]{1,0:T(8,128)(2,1)S(1)} %get-tuple-element.39), channel_id=1, source_target_pairs={{1,0},{0,1},{3,2},{2,3},{5,4},{4,5},{7,6},{6,7},{9,8},{8,9},{11,10... | collective-permute-start | bytes 786440 | tf_op jit(solution)/shard_map/ppermute | solution.py:61
  105.0 5.1 %collective-permute-start.20 = (bf16[512,256]{1,0:T(8,128)(2,1)S(1)}, bf16[512,256]{1,0:T(8,128)(2,1)S(1)}, u32[]{:S(2)}, u32[]{:S(2)}) collective-permute-start(bf16[512,256]{1,0:T(8,128)(2,1)S(1)} %get-tuple-element.40), channel_id=1, source_target_pairs={{1,0},{0,1},{3,2},{2,3},{5,4},{4,5},{7,6},{6,7},{9,8},{8,9},{11,10... | collective-permute-start | bytes 786440 | tf_op jit(solution)/shard_map/ppermute | solution.py:61
  109.4 1.6 %collective-permute-start.21 = (bf16[512,256]{1,0:T(8,128)(2,1)S(1)}, bf16[512,256]{1,0:T(8,128)(2,1)S(1)}, u32[]{:S(2)}, u32[]{:S(2)}) collective-permute-start(bf16[512,256]{1,0:T(8,128)(2,1)S(1)} %get-tuple-element.41), channel_id=1, source_target_pairs={{1,0},{0,1},{3,2},{2,3},{5,4},{4,5},{7,6},{6,7},{9,8},{8,9},{11,10... | collective-permute-start | bytes 786440 | tf_op jit(solution)/shard_map/ppermute | solution.py:61
  109.6 1.8 %collective-permute-start.22 = (bf16[512,256]{1,0:T(8,128)(2,1)S(1)}, bf16[512,256]{1,0:T(8,128)(2,1)S(1)}, u32[]{:S(2)}, u32[]{:S(2)}) collective-permute-start(bf16[512,256]{1,0:T(8,128)(2,1)S(1)} %get-tuple-element.42), channel_id=1, source_target_pairs={{1,0},{0,1},{3,2},{2,3},{5,4},{4,5},{7,6},{6,7},{9,8},{8,9},{11,10... | collective-permute-start | bytes 786440 | tf_op jit(solution)/shard_map/ppermute | solution.py:61
  (16 other events, 201.5 us)

commit v5 on v4

--- a/solution.py
+++ b/solution.py
@@ -109,22 +109,6 @@
         compiler_params=pltpu.CompilerParams(vmem_limit_bytes=limit << 20),
         cost_estimate=pl.CostEstimate(flops=flops, bytes_accessed=moved, transcendentals=0),
     )(*inputs)
-
-
-def stay_kernel(source, out, sem):
-    copy = pltpu.make_async_copy(source, out, sem)
-    copy.start()
-    copy.wait()
-
-
-def stay(value):
-    return call(
-        stay_kernel,
-        pltpu.VMEM(value.shape, value.dtype),
-        (),
-        (pltpu.SemaphoreType.DMA,),
-        kept=(value,),
-    )
 
 
 def stacked(value, wide):
@@ -191,13 +175,13 @@
         out[:, k * wide : (k + 1) * wide] = sign[k * TILE : (k + 1) * TILE]
 
 
-def row_copies(weights, raw, sems):
+def row_copies(weights, raw, sems, base):
     copies = []
     for g, refs in enumerate(weights):
         pieces = [(ref, r) for ref in refs for r in range(0, ref.shape[0], TILE)]
         copies.append(
             [
-                pltpu.make_async_copy(ref.at[r : r + TILE], raw.at[g, f], sems.at[g, f])
+                pltpu.make_async_copy(ref.at[r : r + TILE], raw.at[base + g, f], sems.at[base + g, f])
                 for f, (ref, r) in enumerate(pieces)
             ]
         )
@@ -218,30 +202,45 @@
     outs[t // per][cut] = product.astype(BF16)
 
 
+def move_of(update):
+    update = update.astype(BF16)
+    return update * lax.rsqrt(update * update * BF16(1 / step_rate**2) + BF16(soft_width / step_rate**2))
+
+
 def forward_kernel(parts, first, back_rows, back_cols, *refs):
     groups = len(parts)
     refs = list(refs)
     bands = [refs.pop(0) for _ in range(groups + 1)]
-    tokens = [refs.pop(0) for _ in range(2)]
+    sources = [refs.pop(0) for _ in range(2)]
     weights = [[refs.pop(0) for _ in range(n)] for n in parts]
     outs = [refs.pop(0) for _ in range(2 * groups)]
-    step, raw, *fresh, sems = refs
+    step, own, other, raw, *fresh, sems, token_sems = refs
+    tokens = (own, other)
     wide = WIDE * TILE
-    width = step.shape[1]
+    rows, width = step.shape
+    per = own.shape[0] // rows
     start = first[0]
-    copies = row_copies(weights, raw, sems)
+    copies = row_copies(weights[:1], raw, sems, 0)
+    token_copies = []
+    for t in range(2 * per):
+        cut = pl.ds(t % per * rows, rows)
+        token_copies.append(
+            pltpu.make_async_copy(sources[t // per].at[cut], tokens[t // per].at[cut], token_sems.at[t])
+        )
+        token_copies[t].start()
+    copies += row_copies(weights[1:], raw, sems, 1)
 
     def renew(g, f):
         tall = dot(back_rows[...], bands[g][f * BAND : (f + 1) * BAND]).astype(BF16)
-        sign = step_rate * soft_sign(dot(stacked(tall, WIDE * BAND), back_cols[...]))
+        move = move_of(dot(stacked(tall, WIDE * BAND), back_cols[...]))
         at = rows_at(start, f)
         for k in range(width // wide):
             cut = slice(k * wide, (k + 1) * wide)
-            part = sign[k * TILE : (k + 1) * TILE]
+            part = move[k * TILE : (k + 1) * TILE]
             if g == groups:
-                step[at, cut] = part.astype(BF16)
+                step[at, cut] = part
             else:
-                fresh[g % 2][at, cut] = (raw[g, f, :, cut].astype(F32) - part).astype(BF16)
+                fresh[g % 2][at, cut] = raw[g, f, :, cut] - part
 
     for f in range(4):
         copies[0][f].wait()
@@ -251,6 +250,8 @@
             for f in range(4):
                 copies[g + 1][f].wait()
         for t in range(4):
+            if g == 0:
+                token_copies[t].wait()
             products(tokens, fresh[g % 2], outs[2 * g : 2 * g + 2], t)
             renew(g + 1, t)
 
@@ -259,11 +260,11 @@
     refs = list(refs)
     weights = [refs.pop(0) for _ in range(parts)]
     out_own, out_other, raw, fresh, sems = refs
-    copies = row_copies([weights], raw, sems)[0]
+    copies = row_copies([weights], raw, sems, 0)[0]
     for f in range(4):
         copies[f].wait()
         at = rows_at(first[0], f)
-        fresh[at] = (raw[0, f].astype(F32) - step[at].astype(F32)).astype(BF16)
+        fresh[at] = raw[0, f] - step[at]
     for t in range(4):
         products((own, other), fresh, (out_own, out_other), t)
 
@@ -322,6 +323,7 @@
         return lax.optimization_barrier((value, *others))[0]
 
     swapped = fetch(weight, sibling)
+    other = fetch(after(activations, swapped), sibling)
     swapped = after(swapped, rounded)
     ahead, behind, across = (fetch(swapped, along(0, s)) for s in (1, -1, 2))
 
@@ -329,10 +331,8 @@
         return value.astype(F32) + fetch(value, source).astype(F32)
 
     sent = join(after(rounded, swapped), far_z).astype(BF16)
-    other = fetch(after(activations, sent), sibling)
-    second_sum = join(after(sent, ahead, behind), pair_x).astype(BF16)
+    second_sum = join(after(sent, ahead, behind, other), pair_x).astype(BF16)
     total = join(after(second_sum, across), along_x(2))
-    own, other = stay(after(activations, sent)), stay(other)
 
     new_momentum = call(
         residual_kernel,
@@ -356,7 +356,7 @@
         pair = jnp.concatenate([value, fetch(value, along(0, 1))], axis=0)
         return jnp.concatenate([pair, fetch(after(pair, *others), along(0, 2))], axis=0)
 
-    band_line = gather(after(total.astype(BF16), late, new_momentum, own, other))
+    band_line = gather(after(total.astype(BF16), late, new_momentum))
     band_line = fetch(after(band_line, next_early, last_early, direction), sibling)
     blocks = gather(band_line, next_late, last_late).reshape(4, 4, BAND, narrow)
     bands = [blocks[:, g].reshape(4 * BAND, narrow) for g in range(4)]
@@ -365,21 +365,21 @@
     step = pltpu.VMEM((4 * rows, width), BF16)
     order = [0, 3, 1]
     parts = [len(lines[g]) for g in order]
-    *results, step = call(
+    *results, step, own, other = call(
         lambda *refs: forward_kernel(parts, *refs),
-        (*[block] * 6, step),
+        (*[block] * 6, step, *[pltpu.VMEM(activations.shape, BF16)] * 2),
         [first[None], back_rows, back_hi] + [bands[g] for g in order + [2]],
         (
             pltpu.VMEM((3, 4, rows, width), BF16),
             pltpu.VMEM((4 * rows, width), BF16),
             pltpu.VMEM((4 * rows, width), BF16),
             pltpu.SemaphoreType.DMA((3, 4)),
+            pltpu.SemaphoreType.DMA((4,)),
         ),
-        limit=24,
+        limit=40,
         flops=3 * 2 * 2 * tokens * 4 * rows * width,
         smem=1,
-        kept=[line for g in order for line in lines[g]],
-        resident=(own, other),
+        kept=[activations, other] + [line for g in order for line in lines[g]],
     )
     results += call(
         lambda *refs: last_kernel(len(lines[2]), *refs),

time: 114 us -> 99.8 us (0.88)
  the two profiles are of different devices: /device:TPU:25 before, /device:TPU:1 now
where the time goes in v5:
time: 99.8 us; the launch traced here: 99.7 us
  starting transfers between devices  38.7 us (39%)
  waiting for transfers between devices  31.8 us (32%)
  Pallas kernels  27.9 us (28%)
    ppermute x23, starting transfers between devices, fetch(): lax.ppermute(value, AXES, [(place(*source(*spot(i))), i) for i in range(2...  38.7 us
    ppermute x23, waiting for transfers between devices, fetch(): lax.ppermute(value, AXES, [(place(*source(*spot(i))), i) for i in range(2...  31.8 us
    pallas_call x6, Pallas kernels, call(): pl.pallas_call(kernel, out_shape=out_shape, in_specs=specs, out_specs=jax...  27.9 us
  transfers between devices with their start and end apart: 23, of which 12 were waited for; matrix products, arithmetic and copies ran while one was open for 0% of the time, Pallas kernels for 25%

profile of v5, /device:TPU:1, one launch (start us, length us, event | category | flops | bytes accessed | tf_op | source)
XLA Modules:
  0.0 99.7 jit_solution(11353205936632899355)
XLA Ops:
  0.6 3.3 %collective-permute-start = (bf16[64,4096]{1,0:T(8,128)(2,1)}, bf16[64,4096]{1,0:T(8,128)(2,1)S(1)}, u32[]{:S(2)}, u32[]{:S(2)}) collective-permute-start(bf16[64,4096]{1,0:T(8,128)(2,1)} %param.12), channel_id=1, source_target_pairs={{1,0},{0,1},{3,2},{2,3},{5,4},{4,5},{7,6},{6,7},{9,8},{8,9},{11,10... | collective-permute-start | bytes 1572872 | tf_op jit(solution)/shard_map/ppermute | solution.py:61
  4.0 1.7 %collective-permute-done = bf16[64,4096]{1,0:T(8,128)(2,1)S(1)} collective-permute-done((bf16[64,4096]{1,0:T(8,128)(2,1)}, bf16[64,4096]{1,0:T(8,128)(2,1)S(1)}, u32[]{:S(2)}, u32[]{:S(2)}) %collective-permute-start) | collective-permute-done | bytes 524320 | tf_op jit(solution)/shard_map/ppermute | solution.py:61
  6.1 3.0 %shard_map.121 = (f32[16,1024]{1,0:T(8,128)S(1)}, bf16[16,1024]{1,0:T(8,128)(2,1)S(1)}) custom-call(f32[1,64,4096]{2,1,0:T(8,128)} %momentum.3, bf16[1,64,4096]{2,1,0:T(8,128)(2,1)} %gradient.3, bf16[1024,128]{1,0:T(8,128)(2,1)} %constant.61.clone.cols, bf16[16,192]{1,0:T(8,128)(2,1)} %constant.62.clone.rows3), custom_call_target="tpu_custom_call" | custom-call | bytes 1841152 | tf_op jit(solution)/shard_map/pallas_call | solution.py:99
  9.1 3.9 %collective-permute-start.2 = (bf16[64,4096]{1,0:T(8,128)(2,1)S(1)}, bf16[64,4096]{1,0:T(8,128)(2,1)S(1)}, u32[]{:S(2)}, u32[]{:S(2)}) collective-permute-start(bf16[64,4096]{1,0:T(8,128)(2,1)S(1)} %collective-permute-done), channel_id=1, source_target_pairs={{8,0},{3,1},{10,2},{5,3},{12,4},{7,5},{14,6},{129,7},{16,8},{11,9}... | collective-permute-start | bytes 1572872 | tf_op jit(solution)/shard_map/ppermute | solution.py:61
  13.0 1.4 %collective-permute-start.1 = (bf16[16,1024]{1,0:T(8,128)(2,1)S(1)}, bf16[16,1024]{1,0:T(8,128)(2,1)S(1)}, u32[]{:S(2)}, u32[]{:S(2)}) collective-permute-start(bf16[16,1024]{1,0:T(8,128)(2,1)S(1)} %get-tuple-element.28), channel_id=1, source_target_pairs={{128,0},{129,1},{130,2},{131,3},{132,4},{133,5},{134,6},{135,7},{1... | collective-permute-start | bytes 98312 | tf_op jit(solution)/shard_map/ppermute | solution.py:61
  14.5 1.4 %collective-permute-start.3 = (bf16[64,4096]{1,0:T(8,128)(2,1)S(1)}, bf16[64,4096]{1,0:T(8,128)(2,1)S(1)}, u32[]{:S(2)}, u32[]{:S(2)}) collective-permute-start(bf16[64,4096]{1,0:T(8,128)(2,1)S(1)} %collective-permute-done), channel_id=1, source_target_pairs={{24,0},{135,1},{26,2},{1,3},{28,4},{3,5},{30,6},{5,7},{0,8},{143,9... | collective-permute-start | bytes 1572872 | tf_op jit(solution)/shard_map/ppermute | solution.py:61
  15.9 3.9 %collective-permute-done.1 = bf16[16,1024]{1,0:T(8,128)(2,1)S(1)} collective-permute-done((bf16[16,1024]{1,0:T(8,128)(2,1)S(1)}, bf16[16,1024]{1,0:T(8,128)(2,1)S(1)}, u32[]{:S(2)}, u32[]{:S(2)}) %collective-permute-start.1) | collective-permute-done | bytes 32800 | tf_op jit(solution)/shard_map/ppermute | solution.py:61
  20.2 3.3 %collective-permute-start.10 = (bf16[128,4096]{1,0:T(8,128)(2,1)S(1)}, bf16[128,4096]{1,0:T(8,128)(2,1)}, u32[]{:S(2)}, u32[]{:S(2)}) collective-permute-start(bf16[128,4096]{1,0:T(8,128)(2,1)S(1)} %pad_maximum_fusion.refs_9_), channel_id=1, source_target_pairs={{2,0},{9,1},{4,2},{11,3},{6,4},{13,5},{128,6},{15,7},{10,8},{17,9}... | collective-permute-start | bytes 3145736 | tf_op jit(solution)/shard_map/ppermute | solution.py:61
  23.5 4.6 %collective-permute-done.6 = bf16[64,4096]{1,0:T(8,128)(2,1)S(1)} collective-permute-done((bf16[64,4096]{1,0:T(8,128)(2,1)S(1)}, bf16[64,4096]{1,0:T(8,128)(2,1)S(1)}, u32[]{:S(2)}, u32[]{:S(2)}) %collective-permute-start.6) | collective-permute-done | bytes 524320 | tf_op jit(solution)/shard_map/ppermute | solution.py:61
  28.1 1.3 %collective-permute-start.5 = (bf16[16,1024]{1,0:T(8,128)(2,1)S(1)}, bf16[16,1024]{1,0:T(8,128)(2,1)S(1)}, u32[]{:S(2)}, u32[]{:S(2)}) collective-permute-start(bf16[16,1024]{1,0:T(8,128)(2,1)S(1)} %add_convert_fusion.1), channel_id=1, source_target_pairs={{32,0},{33,1},{34,2},{35,3},{36,4},{37,5},{38,6},{39,7},{40,8},{41... | collective-permute-start | bytes 98312 | tf_op jit(solution)/shard_map/ppermute | solution.py:61
  29.4 3.1 %collective-permute-start.14 = (bf16[128,4096]{1,0:T(8,128)(2,1)S(1)}, bf16[128,4096]{1,0:T(8,128)(2,1)S(1)}, u32[]{:S(2)}, u32[]{:S(2)}) collective-permute-start(bf16[128,4096]{1,0:T(8,128)(2,1)S(1)} %constant_dynamic-update-slice_fusion.refs_10_), channel_id=1, source_target_pairs={{2,0},{9,1},{4,2},{11,3},{6,4},{13,5},{128,6},{15,7},{10,8},{17,9}... | collective-permute-start | bytes 3145736 | tf_op jit(solution)/shard_map/ppermute | solution.py:61
  32.5 2.5 %collective-permute-start.7 = (bf16[16,1024]{1,0:T(8,128)(2,1)S(1)}, bf16[16,1024]{1,0:T(8,128)(2,1)S(1)}, u32[]{:S(2)}, u32[]{:S(2)}) collective-permute-start(bf16[16,1024]{1,0:T(8,128)(2,1)S(1)} %add_convert_fusion), channel_id=1, source_target_pairs={{64,0},{65,1},{66,2},{67,3},{68,4},{69,5},{70,6},{71,7},{72,8},{73... | collective-permute-start | bytes 98312 | tf_op jit(solution)/shard_map/ppermute | solution.py:61
  35.1 1.7 %shard_map.122 = f32[1,64,4096]{2,1,0:T(8,128)} custom-call(f32[1,64,4096]{2,1,0:T(8,128)S(1)} %copy-done, bf16[1,64,4096]{2,1,0:T(8,128)(2,1)S(1)} %copy-done.1, f32[16,1024]{1,0:T(8,128)S(1)} %get-tuple-element.25.bands, bf16[64,48]{1,0:T(8,128)(2,1)S(1)} %copy-done.4, bf16[128,512]{1,0:T(8,128)(2,1)S(1)} %copy-done.2, bf16[128,512]{1,0:T(8,128)(2,1)S(1)} %copy-done.3), custom_call_target="tpu_custom_call" | custom-call | bytes 1906688 | tf_op jit(solution)/shard_map/pallas_call | solution.py:99
  37.2 2.1 %collective-permute-start.8 = (bf16[16,1024]{1,0:T(8,128)(2,1)S(1)}, bf16[16,1024]{1,0:T(8,128)(2,1)S(1)}, u32[]{:S(2)}, u32[]{:S(2)}) collective-permute-start(bf16[16,1024]{1,0:T(8,128)(2,1)S(1)} %get-tuple-element.32), channel_id=1, source_target_pairs={{8,0},{3,1},{10,2},{5,3},{12,4},{7,5},{14,6},{129,7},{16,8},{11,9}... | collective-permute-start | bytes 98312 | tf_op jit(solution)/shard_map/ppermute | solution.py:61
  39.3 6.2 %collective-permute-done.8 = bf16[16,1024]{1,0:T(8,128)(2,1)S(1)} collective-permute-done((bf16[16,1024]{1,0:T(8,128)(2,1)S(1)}, bf16[16,1024]{1,0:T(8,128)(2,1)S(1)}, u32[]{:S(2)}, u32[]{:S(2)}) %collective-permute-start.8) | collective-permute-done | bytes 32800 | tf_op jit(solution)/shard_map/ppermute | solution.py:61
  46.8 1.7 %shard_map.123 = f32[64,4096]{1,0:T(8,128)} custom-call(f32[16,1024]{1,0:T(8,128)S(1)} %get-tuple-element.52.total, bf16[64,48]{1,0:T(8,128)(2,1)S(1)} %copy-done.4, bf16[128,512]{1,0:T(8,128)(2,1)S(1)} %copy-done.2, bf16[128,512]{1,0:T(8,128)(2,1)S(1)} %copy-done.3), custom_call_target="tpu_custom_call" | custom-call | bytes 333824 | tf_op jit(solution)/shard_map/pallas_call | solution.py:99
  48.4 3.1 %collective-permute-done.9 = bf16[32,1024]{1,0:T(8,128)(2,1)S(1)} collective-permute-done((bf16[32,1024]{1,0:T(8,128)(2,1)S(1)}, bf16[32,1024]{1,0:T(8,128)(2,1)S(1)}, u32[]{:S(2)}, u32[]{:S(2)}) %collective-permute-start.9) | collective-permute-done | bytes 65568 | tf_op jit(solution)/shard_map/ppermute | solution.py:61
  51.6 6.9 %collective-permute-start.12 = (bf16[64,1024]{1,0:T(8,128)(2,1)S(1)}, bf16[64,1024]{1,0:T(8,128)(2,1)S(1)}, u32[]{:S(2)}, u32[]{:S(2)}) collective-permute-start(bf16[64,1024]{1,0:T(8,128)(2,1)S(1)} %pad_maximum_fusion.3), channel_id=1, source_target_pairs={{1,0},{0,1},{3,2},{2,3},{5,4},{4,5},{7,6},{6,7},{9,8},{8,9},{11,10... | collective-permute-start | bytes 393224 | tf_op jit(solution)/shard_map/ppermute | solution.py:61
  60.2 3.6 %collective-permute-done.13 = bf16[64,1024]{1,0:T(8,128)(2,1)S(1)} collective-permute-done((bf16[64,1024]{1,0:T(8,128)(2,1)S(1)}, bf16[64,1024]{1,0:T(8,128)(2,1)S(1)}, u32[]{:S(2)}, u32[]{:S(2)}) %collective-permute-start.13) | collective-permute-done | bytes 131104 | tf_op jit(solution)/shard_map/ppermute | solution.py:61
  65.5 5.7 %collective-permute-done.16 = bf16[128,1024]{1,0:T(8,128)(2,1)S(1)} collective-permute-done((bf16[128,1024]{1,0:T(8,128)(2,1)S(1)}, bf16[128,1024]{1,0:T(8,128)(2,1)S(1)}, u32[]{:S(2)}, u32[]{:S(2)}) %collective-permute-start.16) | collective-permute-done | bytes 262176 | tf_op jit(solution)/shard_map/ppermute | solution.py:61
  71.3 14.8 %shard_map.124 = (bf16[512,256]{1,0:T(8,128)(2,1)S(1)}, bf16[512,256]{1,0:T(8,128)(2,1)S(1)}, bf16[512,256]{1,0:T(8,128)(2,1)S(1)}, bf16[512,256]{1,0:T(8,128)(2...) custom-call(s32[1]{0:T(128)} %bitcast.2.refs_0_, ...), custom_call_target="tpu_custom_call" | custom-call | flops 6442450944 | bytes 15337476 | tf_op jit(solution)/shard_map/pallas_call | solution.py:99
  86.0 4.5 %collective-permute-start.19 = (bf16[512,256]{1,0:T(8,128)(2,1)S(1)}, bf16[512,256]{1,0:T(8,128)(2,1)S(1)}, u32[]{:S(2)}, u32[]{:S(2)}) collective-permute-start(bf16[512,256]{1,0:T(8,128)(2,1)S(1)} %get-tuple-element.43), channel_id=1, source_target_pairs={{1,0},{0,1},{3,2},{2,3},{5,4},{4,5},{7,6},{6,7},{9,8},{8,9},{11,10... | collective-permute-start | bytes 786440 | tf_op jit(solution)/shard_map/ppermute | solution.py:61
  90.9 4.0 %shard_map.125 = (bf16[512,256]{1,0:T(8,128)(2,1)S(1)}, bf16[512,256]{1,0:T(8,128)(2,1)S(1)}) custom-call(s32[1]{0:T(128)} %bitcast.2.refs_0_, bf16[512,4096]{1,0:T(8,128)(2,1)S(1)} %get-tuple-element.38.refs_1_, bf16[512,4096]{1,0:T(8,128)(2,1)S(1)} %get-tuple-element.39.refs_2_, bf16[256,4096]{1,0:T(8,128)(2,1)S(1)} %get-tuple-element.40.refs_3_, ...), custom_call_target="tpu_custom_call" | custom-call | flops 2147483648 | bytes 12582916 | tf_op jit(solution)/shard_map/pallas_call | solution.py:99
  96.9 2.8 %shard_map.126 = bf16[512,2048]{1,0:T(8,128)(2,1)} custom-call(s32[3]{0:T(128)S(1)} %pad_add_fusion.where, bf16[512,256]{1,0:T(8,128)(2,1)S(1)} %get-tuple-element.36.refs_0_, bf16[512,256]{1,0:T(8,128)(2,1)S(1)} %get-tuple-element.37.refs_1_, bf16[512,256]{1,0:T(8,128)(2,1)S(1)} %get-tuple-element.41.refs_2_, ...), custom_call_target="tpu_custom_call" | custom-call | bytes 2097164 | tf_op jit(solution)/shard_map/pallas_call | solution.py:99
  (62 shorter events, 8.3 us)
Async XLA Ops:
  0.6 5.1 %collective-permute-start = (bf16[64,4096]{1,0:T(8,128)(2,1)}, bf16[64,4096]{1,0:T(8,128)(2,1)S(1)}, u32[]{:S(2)}, u32[]{:S(2)}) collective-permute-start(bf16[64,4096]{1,0:T(8,128)(2,1)} %param.12), channel_id=1, source_target_pairs={{1,0},{0,1},{3,2},{2,3},{5,4},{4,5},{7,6},{6,7},{9,8},{8,9},{11,10... | collective-permute-start | bytes 1572872 | tf_op jit(solution)/shard_map/ppermute | solution.py:61
  5.7 22.4 %collective-permute-start.4 = (bf16[512,4096]{1,0:T(8,128)(2,1)}, bf16[512,4096]{1,0:T(8,128)(2,1)S(1)}, u32[]{:S(2)}, u32[]{:S(2)}) collective-permute-start(bf16[512,4096]{1,0:T(8,128)(2,1)} %refs_7_.1), channel_id=1, source_target_pairs={{1,0},{0,1},{3,2},{2,3},{5,4},{4,5},{7,6},{6,7},{9,8},{8,9},{11,10... | collective-permute-start | bytes 12582920 | tf_op jit(solution)/shard_map/ppermute | solution.py:61
  9.1 11.0 %collective-permute-start.2 = (bf16[64,4096]{1,0:T(8,128)(2,1)S(1)}, bf16[64,4096]{1,0:T(8,128)(2,1)S(1)}, u32[]{:S(2)}, u32[]{:S(2)}) collective-permute-start(bf16[64,4096]{1,0:T(8,128)(2,1)S(1)} %collective-permute-done), channel_id=1, source_target_pairs={{8,0},{3,1},{10,2},{5,3},{12,4},{7,5},{14,6},{129,7},{16,8},{11,9}... | collective-permute-start | bytes 1572872 | tf_op jit(solution)/shard_map/ppermute | solution.py:61
  13.0 6.7 %collective-permute-start.1 = (bf16[16,1024]{1,0:T(8,128)(2,1)S(1)}, bf16[16,1024]{1,0:T(8,128)(2,1)S(1)}, u32[]{:S(2)}, u32[]{:S(2)}) collective-permute-start(bf16[16,1024]{1,0:T(8,128)(2,1)S(1)} %get-tuple-element.28), channel_id=1, source_target_pairs={{128,0},{129,1},{130,2},{131,3},{132,4},{133,5},{134,6},{135,7},{1... | collective-permute-start | bytes 98312 | tf_op jit(solution)/shard_map/ppermute | solution.py:61
  14.5 13.6 %collective-permute-start.3 = (bf16[64,4096]{1,0:T(8,128)(2,1)S(1)}, bf16[64,4096]{1,0:T(8,128)(2,1)S(1)}, u32[]{:S(2)}, u32[]{:S(2)}) collective-permute-start(bf16[64,4096]{1,0:T(8,128)(2,1)S(1)} %collective-permute-done), channel_id=1, source_target_pairs={{24,0},{135,1},{26,2},{1,3},{28,4},{3,5},{30,6},{5,7},{0,8},{143,9... | collective-permute-start | bytes 1572872 | tf_op jit(solution)/shard_map/ppermute | solution.py:61
  15.9 12.2 %collective-permute-start.6 = (bf16[64,4096]{1,0:T(8,128)(2,1)S(1)}, bf16[64,4096]{1,0:T(8,128)(2,1)S(1)}, u32[]{:S(2)}, u32[]{:S(2)}) collective-permute-start(bf16[64,4096]{1,0:T(8,128)(2,1)S(1)} %collective-permute-done), channel_id=1, source_target_pairs={{16,0},{5,1},{18,2},{135,3},{20,4},{129,5},{22,6},{3,7},{24,8},{13... | collective-permute-start | bytes 1572872 | tf_op jit(solution)/shard_map/ppermute | solution.py:61
  20.2 31.4 %collective-permute-start.10 = (bf16[128,4096]{1,0:T(8,128)(2,1)S(1)}, bf16[128,4096]{1,0:T(8,128)(2,1)}, u32[]{:S(2)}, u32[]{:S(2)}) collective-permute-start(bf16[128,4096]{1,0:T(8,128)(2,1)S(1)} %pad_maximum_fusion.refs_9_), channel_id=1, source_target_pairs={{2,0},{9,1},{4,2},{11,3},{6,4},{13,5},{128,6},{15,7},{10,8},{17,9}... | collective-permute-start | bytes 3145736 | tf_op jit(solution)/shard_map/ppermute | solution.py:61
  23.5 28.1 %collective-permute-start.11 = (bf16[128,4096]{1,0:T(8,128)(2,1)S(1)}, bf16[128,4096]{1,0:T(8,128)(2,1)S(1)}, u32[]{:S(2)}, u32[]{:S(2)}) collective-permute-start(bf16[128,4096]{1,0:T(8,128)(2,1)S(1)} %pad_maximum_fusion.refs_9_), channel_id=1, source_target_pairs={{134,0},{25,1},{0,2},{27,3},{2,4},{29,5},{4,6},{31,7},{142,8},{1,9... | collective-permute-start | bytes 3145736 | tf_op jit(solution)/shard_map/ppermute | solution.py:61
  28.1 4.4 %collective-permute-start.5 = (bf16[16,1024]{1,0:T(8,128)(2,1)S(1)}, bf16[16,1024]{1,0:T(8,128)(2,1)S(1)}, u32[]{:S(2)}, u32[]{:S(2)}) collective-permute-start(bf16[16,1024]{1,0:T(8,128)(2,1)S(1)} %add_convert_fusion.1), channel_id=1, source_target_pairs={{32,0},{33,1},{34,2},{35,3},{36,4},{37,5},{38,6},{39,7},{40,8},{41... | collective-permute-start | bytes 98312 | tf_op jit(solution)/shard_map/ppermute | solution.py:61
  29.4 34.4 %collective-permute-start.14 = (bf16[128,4096]{1,0:T(8,128)(2,1)S(1)}, bf16[128,4096]{1,0:T(8,128)(2,1)S(1)}, u32[]{:S(2)}, u32[]{:S(2)}) collective-permute-start(bf16[128,4096]{1,0:T(8,128)(2,1)S(1)} %constant_dynamic-update-slice_fusion.refs_10_), channel_id=1, source_target_pairs={{2,0},{9,1},{4,2},{11,3},{6,4},{13,5},{128,6},{15,7},{10,8},{17,9}... | collective-permute-start | bytes 3145736 | tf_op jit(solution)/shard_map/ppermute | solution.py:61
  32.5 31.3 %collective-permute-start.15 = (bf16[128,4096]{1,0:T(8,128)(2,1)S(1)}, bf16[128,4096]{1,0:T(8,128)(2,1)}, u32[]{:S(2)}, u32[]{:S(2)}) collective-permute-start(bf16[128,4096]{1,0:T(8,128)(2,1)S(1)} %constant_dynamic-update-slice_fusion.refs_10_), channel_id=1, source_target_pairs={{134,0},{25,1},{0,2},{27,3},{2,4},{29,5},{4,6},{31,7},{142,8},{1,9... | collective-permute-start | bytes 3145736 | tf_op jit(solution)/shard_map/ppermute | solution.py:61
  32.5 4.7 %collective-permute-start.7 = (bf16[16,1024]{1,0:T(8,128)(2,1)S(1)}, bf16[16,1024]{1,0:T(8,128)(2,1)S(1)}, u32[]{:S(2)}, u32[]{:S(2)}) collective-permute-start(bf16[16,1024]{1,0:T(8,128)(2,1)S(1)} %add_convert_fusion), channel_id=1, source_target_pairs={{64,0},{65,1},{66,2},{67,3},{68,4},{69,5},{70,6},{71,7},{72,8},{73... | collective-permute-start | bytes 98312 | tf_op jit(solution)/shard_map/ppermute | solution.py:61
  37.2 8.3 %collective-permute-start.8 = (bf16[16,1024]{1,0:T(8,128)(2,1)S(1)}, bf16[16,1024]{1,0:T(8,128)(2,1)S(1)}, u32[]{:S(2)}, u32[]{:S(2)}) collective-permute-start(bf16[16,1024]{1,0:T(8,128)(2,1)S(1)} %get-tuple-element.32), channel_id=1, source_target_pairs={{8,0},{3,1},{10,2},{5,3},{12,4},{7,5},{14,6},{129,7},{16,8},{11,9}... | collective-permute-start | bytes 98312 | tf_op jit(solution)/shard_map/ppermute | solution.py:61
  45.5 6.0 %collective-permute-start.9 = (bf16[32,1024]{1,0:T(8,128)(2,1)S(1)}, bf16[32,1024]{1,0:T(8,128)(2,1)S(1)}, u32[]{:S(2)}, u32[]{:S(2)}) collective-permute-start(bf16[32,1024]{1,0:T(8,128)(2,1)S(1)} %pad_maximum_fusion.4), channel_id=1, source_target_pairs={{16,0},{5,1},{18,2},{135,3},{20,4},{129,5},{22,6},{3,7},{24,8},{13... | collective-permute-start | bytes 196616 | tf_op jit(solution)/shard_map/ppermute | solution.py:61
  46.8 24.5 %copy-start.5 = (bf16[64,16]{1,0:T(8,128)(2,1)S(1)}, bf16[64,16]{1,0:T(8,128)(2,1)}, u32[]{:S(2)}) copy-start(bf16[64,16]{1,0:T(8,128)(2,1)} %constant.66.clone.refs_1_) | copy-start | bytes 6148
  51.6 7.9 %collective-permute-start.12 = (bf16[64,1024]{1,0:T(8,128)(2,1)S(1)}, bf16[64,1024]{1,0:T(8,128)(2,1)S(1)}, u32[]{:S(2)}, u32[]{:S(2)}) collective-permute-start(bf16[64,1024]{1,0:T(8,128)(2,1)S(1)} %pad_maximum_fusion.3), channel_id=1, source_target_pairs={{1,0},{0,1},{3,2},{2,3},{5,4},{4,5},{7,6},{6,7},{9,8},{8,9},{11,10... | collective-permute-start | bytes 393224 | tf_op jit(solution)/shard_map/ppermute | solution.py:61
  59.5 4.3 %collective-permute-start.13 = (bf16[64,1024]{1,0:T(8,128)(2,1)S(1)}, bf16[64,1024]{1,0:T(8,128)(2,1)S(1)}, u32[]{:S(2)}, u32[]{:S(2)}) collective-permute-start(bf16[64,1024]{1,0:T(8,128)(2,1)S(1)} %collective-permute-done.12), channel_id=1, source_target_pairs={{8,0},{3,1},{10,2},{5,3},{12,4},{7,5},{14,6},{129,7},{16,8},{11,9}... | collective-permute-start | bytes 393224 | tf_op jit(solution)/shard_map/ppermute | solution.py:61
  63.8 7.4 %collective-permute-start.16 = (bf16[128,1024]{1,0:T(8,128)(2,1)S(1)}, bf16[128,1024]{1,0:T(8,128)(2,1)S(1)}, u32[]{:S(2)}, u32[]{:S(2)}) collective-permute-start(bf16[128,1024]{1,0:T(8,128)(2,1)S(1)} %pad_maximum_fusion.2), channel_id=1, source_target_pairs={{16,0},{5,1},{18,2},{135,3},{20,4},{129,5},{22,6},{3,7},{24,8},{13... | collective-permute-start | bytes 786440 | tf_op jit(solution)/shard_map/ppermute | solution.py:61
  63.9 27.0 %collective-permute-start.17 = (bf16[128,4096]{1,0:T(8,128)(2,1)}, bf16[128,4096]{1,0:T(8,128)(2,1)}, u32[]{:S(2)}, u32[]{:S(2)}) collective-permute-start(bf16[128,4096]{1,0:T(8,128)(2,1)} %collective-permute-done.10.refs_13_), channel_id=1, source_target_pairs={{2,0},{9,1},{4,2},{11,3},{6,4},{13,5},{128,6},{15,7},{10,8},{17,9}... | collective-permute-start | bytes 3145736 | tf_op jit(solution)/shard_map/ppermute | solution.py:61
  65.2 25.7 %collective-permute-start.18 = (bf16[128,4096]{1,0:T(8,128)(2,1)}, bf16[128,4096]{1,0:T(8,128)(2,1)}, u32[]{:S(2)}, u32[]{:S(2)}) collective-permute-start(bf16[128,4096]{1,0:T(8,128)(2,1)} %collective-permute-done.15.refs_12_), channel_id=1, source_target_pairs={{134,0},{25,1},{0,2},{27,3},{2,4},{29,5},{4,6},{31,7},{142,8},{1,9... | collective-permute-start | bytes 3145736 | tf_op jit(solution)/shard_map/ppermute | solution.py:61
  86.0 9.6 %collective-permute-start.19 = (bf16[512,256]{1,0:T(8,128)(2,1)S(1)}, bf16[512,256]{1,0:T(8,128)(2,1)S(1)}, u32[]{:S(2)}, u32[]{:S(2)}) collective-permute-start(bf16[512,256]{1,0:T(8,128)(2,1)S(1)} %get-tuple-element.43), channel_id=1, source_target_pairs={{1,0},{0,1},{3,2},{2,3},{5,4},{4,5},{7,6},{6,7},{9,8},{8,9},{11,10... | collective-permute-start | bytes 786440 | tf_op jit(solution)/shard_map/ppermute | solution.py:61
  90.5 5.1 %collective-permute-start.20 = (bf16[512,256]{1,0:T(8,128)(2,1)S(1)}, bf16[512,256]{1,0:T(8,128)(2,1)S(1)}, u32[]{:S(2)}, u32[]{:S(2)}) collective-permute-start(bf16[512,256]{1,0:T(8,128)(2,1)S(1)} %get-tuple-element.44), channel_id=1, source_target_pairs={{1,0},{0,1},{3,2},{2,3},{5,4},{4,5},{7,6},{6,7},{9,8},{8,9},{11,10... | collective-permute-start | bytes 786440 | tf_op jit(solution)/shard_map/ppermute | solution.py:61
  94.9 1.6 %collective-permute-start.21 = (bf16[512,256]{1,0:T(8,128)(2,1)S(1)}, bf16[512,256]{1,0:T(8,128)(2,1)S(1)}, u32[]{:S(2)}, u32[]{:S(2)}) collective-permute-start(bf16[512,256]{1,0:T(8,128)(2,1)S(1)} %get-tuple-element.45), channel_id=1, source_target_pairs={{1,0},{0,1},{3,2},{2,3},{5,4},{4,5},{7,6},{6,7},{9,8},{8,9},{11,10... | collective-permute-start | bytes 786440 | tf_op jit(solution)/shard_map/ppermute | solution.py:61
  95.2 1.8 %collective-permute-start.22 = (bf16[512,256]{1,0:T(8,128)(2,1)S(1)}, bf16[512,256]{1,0:T(8,128)(2,1)S(1)}, u32[]{:S(2)}, u32[]{:S(2)}) collective-permute-start(bf16[512,256]{1,0:T(8,128)(2,1)S(1)} %get-tuple-element.46), channel_id=1, source_target_pairs={{1,0},{0,1},{3,2},{2,3},{5,4},{4,5},{7,6},{6,7},{9,8},{8,9},{11,10... | collective-permute-start | bytes 786440 | tf_op jit(solution)/shard_map/ppermute | solution.py:61
  (10 other events, 134.9 us)

commit v6 on v5

--- a/solution.py
+++ b/solution.py
@@ -207,27 +207,30 @@
     return update * lax.rsqrt(update * update * BF16(1 / step_rate**2) + BF16(soft_width / step_rate**2))
 
 
-def forward_kernel(parts, first, back_rows, back_cols, *refs):
+def forward_kernel(parts, load, extra, first, back_rows, back_cols, *refs):
     groups = len(parts)
     refs = list(refs)
-    bands = [refs.pop(0) for _ in range(groups + 1)]
+    bands = [refs.pop(0) for _ in range(groups + extra)]
     sources = [refs.pop(0) for _ in range(2)]
     weights = [[refs.pop(0) for _ in range(n)] for n in parts]
     outs = [refs.pop(0) for _ in range(2 * groups)]
-    step, own, other, raw, *fresh, sems, token_sems = refs
-    tokens = (own, other)
+    tokens = [refs.pop(0) for _ in range(2)] if load else sources
+    step = refs.pop(0) if extra else None
+    token_sems = refs.pop() if load else None
+    raw, *fresh, sems = refs
     wide = WIDE * TILE
-    rows, width = step.shape
-    per = own.shape[0] // rows
+    rows, width = fresh[0].shape
+    per = tokens[0].shape[0] // rows
     start = first[0]
     copies = row_copies(weights[:1], raw, sems, 0)
     token_copies = []
-    for t in range(2 * per):
-        cut = pl.ds(t % per * rows, rows)
-        token_copies.append(
-            pltpu.make_async_copy(sources[t // per].at[cut], tokens[t // per].at[cut], token_sems.at[t])
-        )
-        token_copies[t].start()
+    if load:
+        for t in range(2 * per):
+            cut = pl.ds(t % per * rows, rows)
+            token_copies.append(
+                pltpu.make_async_copy(sources[t // per].at[cut], tokens[t // per].at[cut], token_sems.at[t])
+            )
+            token_copies[t].start()
     copies += row_copies(weights[1:], raw, sems, 1)
 
     def renew(g, f):
@@ -250,10 +253,11 @@
             for f in range(4):
                 copies[g + 1][f].wait()
         for t in range(4):
-            if g == 0:
+            if g == 0 and load:
                 token_copies[t].wait()
             products(tokens, fresh[g % 2], outs[2 * g : 2 * g + 2], t)
-            renew(g + 1, t)
+            if g + 1 < groups + extra:
+                renew(g + 1, t)
 
 
 def last_kernel(parts, first, own, other, step, *refs):
@@ -323,8 +327,8 @@
         return lax.optimization_barrier((value, *others))[0]
 
     swapped = fetch(weight, sibling)
+    swapped = after(swapped, rounded)
     other = fetch(after(activations, swapped), sibling)
-    swapped = after(swapped, rounded)
     ahead, behind, across = (fetch(swapped, along(0, s)) for s in (1, -1, 2))
 
     def join(value, source):
@@ -332,62 +336,71 @@
 
     sent = join(after(rounded, swapped), far_z).astype(BF16)
     second_sum = join(after(sent, ahead, behind, other), pair_x).astype(BF16)
-    total = join(after(second_sum, across), along_x(2))
-
+    total = join(second_sum, along_x(2))
+
+    early = after(jnp.concatenate([swapped, ahead], axis=0), sent)
+    late = jnp.concatenate([across, behind], axis=0)
+    next_early, last_early = fetch(early, along(1, 1)), fetch(early, along(1, -1))
+    def gather(value):
+        return jnp.concatenate([value] + [fetch(value, along(0, s)) for s in (1, 2, -1)], axis=0)
+
+    band_line = gather(after(total.astype(BF16), late))
+    late = after(late, band_line)
+    next_late, last_late = fetch(late, along(1, 1)), fetch(late, along(1, -1))
+    band_line = fetch(after(band_line, next_early, last_early), sibling)
+    blocks = gather(band_line).reshape(4, 4, BAND, narrow)
+    far_early = fetch(after(next_early, blocks), along(1, 1))
+    lines = [[early, late], [next_early, next_late], [far_early], [last_early, last_late]]
+    bands = [blocks[:, g].reshape(4 * BAND, narrow) for g in range(4)]
+
+    block = shape((tokens, 4 * rows), BF16)
+    held = pltpu.VMEM(activations.shape, BF16)
+    rows_like = pltpu.VMEM((4 * rows, width), BF16)
+
+    def forward(order, more=()):
+        parts, load = [len(lines[g]) for g in order], not more
+        count = len(order)
+        return call(
+            lambda *refs: forward_kernel(parts, load, len(more), *refs),
+            (*[block] * (2 * count), *([held] * 2 if load else []), *[rows_like] * len(more)),
+            [first[None], back_rows, back_hi] + [bands[g] for g in (*order, *more)],
+            (
+                pltpu.VMEM((count, 4, rows, width), BF16),
+                rows_like,
+                rows_like,
+                pltpu.SemaphoreType.DMA((count, 4)),
+                *([pltpu.SemaphoreType.DMA((4,))] if load else []),
+            ),
+            limit=32,
+            flops=count * 2 * 2 * tokens * 4 * rows * width,
+            smem=1,
+            resident=() if load else (own, other),
+            kept=([activations, other] if load else []) + [line for g in order for line in lines[g]],
+        )
+
+    *results, own, other = forward([0])
+    first_out = results[0]
+    lines[2].append(fetch(after(last_late, first_out), along(1, -1)))
     new_momentum = call(
         residual_kernel,
         shape(momentum.shape, F32),
-        (momentum, gradient, exact, back_rows3, back_hi, back_lo),
+        (momentum, gradient, after(exact, first_out), back_rows3, back_hi, back_lo),
     )
     direction = call(
         direction_kernel,
         shape((rows, width), F32),
-        (total, back_rows3, back_hi, back_lo),
-    )
-
-    early = after(jnp.concatenate([swapped, ahead], axis=0), sent)
-    late = jnp.concatenate([across, behind], axis=0)
-    next_early, last_early = fetch(early, along(1, 1)), fetch(early, along(1, -1))
-    next_late, last_late = fetch(late, along(1, 1)), fetch(late, along(1, -1))
-    far_early, far_late = fetch(next_early, along(1, 1)), fetch(last_late, along(1, -1))
-    lines = [[early, late], [next_early, next_late], [far_early, far_late], [last_early, last_late]]
-
-    def gather(value, *others):
-        pair = jnp.concatenate([value, fetch(value, along(0, 1))], axis=0)
-        return jnp.concatenate([pair, fetch(after(pair, *others), along(0, 2))], axis=0)
-
-    band_line = gather(after(total.astype(BF16), late, new_momentum))
-    band_line = fetch(after(band_line, next_early, last_early, direction), sibling)
-    blocks = gather(band_line, next_late, last_late).reshape(4, 4, BAND, narrow)
-    bands = [blocks[:, g].reshape(4 * BAND, narrow) for g in range(4)]
-
-    block = shape((tokens, 4 * rows), BF16)
-    step = pltpu.VMEM((4 * rows, width), BF16)
-    order = [0, 3, 1]
-    parts = [len(lines[g]) for g in order]
-    *results, step, own, other = call(
-        lambda *refs: forward_kernel(parts, *refs),
-        (*[block] * 6, step, *[pltpu.VMEM(activations.shape, BF16)] * 2),
-        [first[None], back_rows, back_hi] + [bands[g] for g in order + [2]],
-        (
-            pltpu.VMEM((3, 4, rows, width), BF16),
-            pltpu.VMEM((4 * rows, width), BF16),
-            pltpu.VMEM((4 * rows, width), BF16),
-            pltpu.SemaphoreType.DMA((3, 4)),
-            pltpu.SemaphoreType.DMA((4,)),
-        ),
-        limit=40,
-        flops=3 * 2 * 2 * tokens * 4 * rows * width,
-        smem=1,
-        kept=[activations, other] + [line for g in order for line in lines[g]],
-    )
+        (after(total, first_out), back_rows3, back_hi, back_lo),
+    )
+    *more, step = forward([3, 1], [2])
+    results += more
+    lines[2][0] = after(lines[2][0], direction, new_momentum)
     results += call(
         lambda *refs: last_kernel(len(lines[2]), *refs),
         (block, block),
         [first[None]],
         (
             pltpu.VMEM((1, 4, rows, width), BF16),
-            pltpu.VMEM((4 * rows, width), BF16),
+            rows_like,
             pltpu.SemaphoreType.DMA((1, 4)),
         ),
         limit=24,
@@ -397,7 +410,7 @@
         resident=(own, other, step),
     )
     mine, theirs = [None] * 4, [None] * 4
-    for n, g in enumerate(order + [2]):
+    for n, g in enumerate((0, 3, 1, 2)):
         mine[g] = results[2 * n]
         theirs[g] = fetch(results[2 * n + 1], sibling)
     where = jnp.stack([core.astype(jnp.int32), second, first])

time: 99.8 us -> 101 us (1.012)
  waiting for transfers between devices: 31.8 us -> 13.8 us
  starting transfers between devices: 38.7 us -> 50.7 us
  local copies, waits for them, and re-layouts: 0.17 us -> 4.06 us
  Pallas kernels: 27.9 us -> 30.9 us
    ppermute x23 -> x25, waiting for transfers between devices: 31.8 us -> 13.8 us  [fetch(): lax.ppermute(value, AXES, [(place(*source(*spot(i))), i) for i in range(2...]
    ppermute x23 -> x25, starting transfers between devices: 38.7 us -> 50.7 us  [fetch(): lax.ppermute(value, AXES, [(place(*source(*spot(i))), i) for i in range(2...]
    unnamed x23 -> x28, local copies, waits for them, and re-layouts: 0.09 us -> 3.19 us
    pallas_call x6 -> x7, Pallas kernels: 27.9 us -> 30.9 us  [call(): pl.pallas_call(kernel, out_shape=out_shape, in_specs=specs, out_specs=jax...]
  transfers between devices with their start and end apart: 23 -> 25, of which waited for: 12 -> 10; matrix products, arithmetic and copies ran while one was open for 0% -> 2% of each run, Pallas kernels for 25% -> 28%
where the time goes in v6:
time: 101 us
  starting transfers between devices  50.7 us (50%)
  Pallas kernels  30.9 us (31%)
  waiting for transfers between devices  13.8 us (14%)
  local copies, waits for them, and re-layouts  4.06 us (4%)
    ppermute x25, starting transfers between devices, fetch(): lax.ppermute(value, AXES, [(place(*source(*spot(i))), i) for i in range(2...  50.7 us
    pallas_call x7, Pallas kernels, call(): pl.pallas_call(kernel, out_shape=out_shape, in_specs=specs, out_specs=jax...  30.9 us
    ppermute x25, waiting for transfers between devices, fetch(): lax.ppermute(value, AXES, [(place(*source(*spot(i))), i) for i in range(2...  13.8 us
    unnamed x28, local copies, waits for them, and re-layouts  3.19 us
  transfers between devices with their start and end apart: 25, of which 10 were waited for; matrix products, arithmetic and copies ran while one was open for 2% of the time, Pallas kernels for 28%

profile of v6, /device:TPU:1, one launch (start us, length us, event | category | flops | bytes accessed | tf_op | source)
XLA Modules:
  0.0 100.6 jit_solution(4549676774816861369)
XLA Ops:
  0.6 3.3 %collective-permute-start = (bf16[64,4096]{1,0:T(8,128)(2,1)}, bf16[64,4096]{1,0:T(8,128)(2,1)S(1)}, u32[]{:S(2)}, u32[]{:S(2)}) collective-permute-start(bf16[64,4096]{1,0:T(8,128)(2,1)} %param.12), channel_id=1, source_target_pairs={{1,0},{0,1},{3,2},{2,3},{5,4},{4,5},{7,6},{6,7},{9,8},{8,9},{11,10... | collective-permute-start | bytes 1572872 | tf_op jit(solution)/shard_map/ppermute | solution.py:61
  4.0 3.0 %shard_map.121 = (f32[16,1024]{1,0:T(8,128)S(1)}, bf16[16,1024]{1,0:T(8,128)(2,1)S(1)}) custom-call(f32[1,64,4096]{2,1,0:T(8,128)} %momentum.3, bf16[1,64,4096]{2,1,0:T(8,128)(2,1)} %gradient.3, bf16[1024,128]{1,0:T(8,128)(2,1)} %constant.61.clone.cols, bf16[16,192]{1,0:T(8,128)(2,1)} %constant.62.clone.rows3), custom_call_target="tpu_custom_call" | custom-call | bytes 1841152 | tf_op jit(solution)/shard_map/pallas_call | solution.py:99
  7.1 3.9 %collective-permute-start.2 = (bf16[64,4096]{1,0:T(8,128)(2,1)S(1)}, bf16[64,4096]{1,0:T(8,128)(2,1)S(1)}, u32[]{:S(2)}, u32[]{:S(2)}) collective-permute-start(bf16[64,4096]{1,0:T(8,128)(2,1)S(1)} %collective-permute-done), channel_id=1, source_target_pairs={{8,0},{3,1},{10,2},{5,3},{12,4},{7,5},{14,6},{129,7},{16,8},{11,9}... | collective-permute-start | bytes 1572872 | tf_op jit(solution)/shard_map/ppermute | solution.py:61
  13.8 4.0 %collective-permute-done.1 = bf16[16,1024]{1,0:T(8,128)(2,1)S(1)} collective-permute-done((bf16[16,1024]{1,0:T(8,128)(2,1)S(1)}, bf16[16,1024]{1,0:T(8,128)(2,1)S(1)}, u32[]{:S(2)}, u32[]{:S(2)}) %collective-permute-start.1) | collective-permute-done | bytes 32800 | tf_op jit(solution)/shard_map/ppermute | solution.py:61
  18.2 3.3 %collective-permute-start.11 = (bf16[128,4096]{1,0:T(8,128)(2,1)S(1)}, bf16[128,4096]{1,0:T(8,128)(2,1)}, u32[]{:S(2)}, u32[]{:S(2)}) collective-permute-start(bf16[128,4096]{1,0:T(8,128)(2,1)S(1)} %pad_maximum_fusion.refs_6_), channel_id=1, source_target_pairs={{2,0},{9,1},{4,2},{11,3},{6,4},{13,5},{128,6},{15,7},{10,8},{17,9}... | collective-permute-start | bytes 3145736 | tf_op jit(solution)/shard_map/ppermute | solution.py:61
  21.5 1.6 %collective-permute-done.3 = bf16[64,4096]{1,0:T(8,128)(2,1)S(1)} collective-permute-done((bf16[64,4096]{1,0:T(8,128)(2,1)S(1)}, bf16[64,4096]{1,0:T(8,128)(2,1)S(1)}, u32[]{:S(2)}, u32[]{:S(2)}) %collective-permute-start.3) | collective-permute-done | bytes 524320 | tf_op jit(solution)/shard_map/ppermute | solution.py:61
  26.6 2.8 %collective-permute-start.6 = (bf16[16,1024]{1,0:T(8,128)(2,1)S(1)}, bf16[16,1024]{1,0:T(8,128)(2,1)S(1)}, u32[]{:S(2)}, u32[]{:S(2)}) collective-permute-start(bf16[16,1024]{1,0:T(8,128)(2,1)S(1)} %add_convert_fusion), channel_id=1, source_target_pairs={{64,0},{65,1},{66,2},{67,3},{68,4},{69,5},{70,6},{71,7},{72,8},{73... | collective-permute-start | bytes 98312 | tf_op jit(solution)/shard_map/ppermute | solution.py:61
  31.3 2.2 %collective-permute-start.8 = (bf16[16,1024]{1,0:T(8,128)(2,1)S(1)}, bf16[16,1024]{1,0:T(8,128)(2,1)S(1)}, u32[]{:S(2)}, u32[]{:S(2)}) collective-permute-start(bf16[16,1024]{1,0:T(8,128)(2,1)S(1)} %get-tuple-element.35), channel_id=1, source_target_pairs={{8,0},{3,1},{10,2},{5,3},{12,4},{7,5},{14,6},{129,7},{16,8},{11,9}... | collective-permute-start | bytes 98312 | tf_op jit(solution)/shard_map/ppermute | solution.py:61
  33.6 4.3 %collective-permute-start.9 = (bf16[16,1024]{1,0:T(8,128)(2,1)S(1)}, bf16[16,1024]{1,0:T(8,128)(2,1)S(1)}, u32[]{:S(2)}, u32[]{:S(2)}) collective-permute-start(bf16[16,1024]{1,0:T(8,128)(2,1)S(1)} %get-tuple-element.35), channel_id=1, source_target_pairs={{16,0},{5,1},{18,2},{135,3},{20,4},{129,5},{22,6},{3,7},{24,8},{13... | collective-permute-start | bytes 98312 | tf_op jit(solution)/shard_map/ppermute | solution.py:61
  37.9 2.3 %collective-permute-start.10 = (bf16[16,1024]{1,0:T(8,128)(2,1)S(1)}, bf16[16,1024]{1,0:T(8,128)(2,1)S(1)}, u32[]{:S(2)}, u32[]{:S(2)}) collective-permute-start(bf16[16,1024]{1,0:T(8,128)(2,1)S(1)} %get-tuple-element.35), channel_id=1, source_target_pairs={{24,0},{135,1},{26,2},{1,3},{28,4},{3,5},{30,6},{5,7},{0,8},{143,9... | collective-permute-start | bytes 98312 | tf_op jit(solution)/shard_map/ppermute | solution.py:61
  40.2 1.6 %collective-permute-done.10 = bf16[16,1024]{1,0:T(8,128)(2,1)S(1)} collective-permute-done((bf16[16,1024]{1,0:T(8,128)(2,1)S(1)}, bf16[16,1024]{1,0:T(8,128)(2,1)S(1)}, u32[]{:S(2)}, u32[]{:S(2)}) %collective-permute-start.10) | collective-permute-done | bytes 32800 | tf_op jit(solution)/shard_map/ppermute | solution.py:61
  41.8 5.0 %collective-permute-start.17 = (bf16[128,4096]{1,0:T(8,128)(2,1)}, bf16[128,4096]{1,0:T(8,128)(2,1)}, u32[]{:S(2)}, u32[]{:S(2)}) collective-permute-start(bf16[128,4096]{1,0:T(8,128)(2,1)} %constant_dynamic-update-slice_fusion.refs_7_), channel_id=1, source_target_pairs={{134,0},{25,1},{0,2},{27,3},{2,4},{29,5},{4,6},{31,7},{142,8},{1,9... | collective-permute-start | bytes 3145736 | tf_op jit(solution)/shard_map/ppermute | solution.py:61
  46.8 4.1 %collective-permute-start.13 = (bf16[64,1024]{1,0:T(8,128)(2,1)S(1)}, bf16[64,1024]{1,0:T(8,128)(2,1)S(1)}, u32[]{:S(2)}, u32[]{:S(2)}) collective-permute-start(bf16[64,1024]{1,0:T(8,128)(2,1)S(1)} %constant_dynamic-update-slice_fusion.2), channel_id=1, source_target_pairs={{1,0},{0,1},{3,2},{2,3},{5,4},{4,5},{7,6},{6,7},{9,8},{8,9},{11,10... | collective-permute-start | bytes 393224 | tf_op jit(solution)/shard_map/ppermute | solution.py:61
  51.9 3.9 %collective-permute-start.16 = (bf16[64,1024]{1,0:T(8,128)(2,1)S(1)}, bf16[64,1024]{1,0:T(8,128)(2,1)S(1)}, u32[]{:S(2)}, u32[]{:S(2)}) collective-permute-start(bf16[64,1024]{1,0:T(8,128)(2,1)S(1)} %collective-permute-done.13), channel_id=1, source_target_pairs={{24,0},{135,1},{26,2},{1,3},{28,4},{3,5},{30,6},{5,7},{0,8},{143,9... | collective-permute-start | bytes 393224 | tf_op jit(solution)/shard_map/ppermute | solution.py:61
  56.0 2.1 %collective-permute-start.14 = (bf16[64,1024]{1,0:T(8,128)(2,1)S(1)}, bf16[64,1024]{1,0:T(8,128)(2,1)S(1)}, u32[]{:S(2)}, u32[]{:S(2)}) collective-permute-start(bf16[64,1024]{1,0:T(8,128)(2,1)S(1)} %collective-permute-done.13), channel_id=1, source_target_pairs={{8,0},{3,1},{10,2},{5,3},{12,4},{7,5},{14,6},{129,7},{16,8},{11,9}... | collective-permute-start | bytes 393224 | tf_op jit(solution)/shard_map/ppermute | solution.py:61
  58.1 1.7 %collective-permute-start.18 = (bf16[128,4096]{1,0:T(8,128)(2,1)}, bf16[128,4096]{1,0:T(8,128)(2,1)S(1)}, u32[]{:S(2)}, u32[]{:S(2)}) collective-permute-start(bf16[128,4096]{1,0:T(8,128)(2,1)} %constant_dynamic-update-slice_fusion.refs_7_), channel_id=1, source_target_pairs={{2,0},{9,1},{4,2},{11,3},{6,4},{13,5},{128,6},{15,7},{10,8},{17,9}... | collective-permute-start | bytes 3145736 | tf_op jit(solution)/shard_map/ppermute | solution.py:61
  61.7 2.2 %collective-permute-start.19 = (bf16[128,4096]{1,0:T(8,128)(2,1)}, bf16[128,4096]{1,0:T(8,128)(2,1)S(1)}, u32[]{:S(2)}, u32[]{:S(2)}) collective-permute-start(bf16[128,4096]{1,0:T(8,128)(2,1)} %collective-permute-done.11.refs_10_), channel_id=1, source_target_pairs={{2,0},{9,1},{4,2},{11,3},{6,4},{13,5},{128,6},{15,7},{10,8},{17,9}... | collective-permute-start | bytes 3145736 | tf_op jit(solution)/shard_map/ppermute | solution.py:61
  64.1 9.0 %shard_map.122 = (bf16[512,256]{1,0:T(8,128)(2,1)S(1)}, bf16[512,256]{1,0:T(8,128)(2,1)S(1)}, bf16[512,4096]{1,0:T(8,128)(2,1)S(1)}, bf16[512,4096]{1,0:T(8,128)(2,1)S(1)}) custom-call(s32[1]{0:T(128)} %bitcast.refs_0_, bf16[64,16]{1,0:T(8,128)(2,1)S(1)} %copy-done.5, bf16[128,512]{1,0:T(8,128)(2,1)S(1)} %copy-done.2, bf16[64,1024]{1,0:T(8,128)(2,1)S(1)} %bitcast.14, ...), custom_call_target="tpu_custom_call" | custom-call | flops 2147483648 | bytes 10749956 | tf_op jit(solution)/shard_map/pallas_call | solution.py:99
  73.2 1.6 %shard_map.123 = f32[1,64,4096]{2,1,0:T(8,128)} custom-call(f32[1,64,4096]{2,1,0:T(8,128)S(1)} %copy-done, bf16[1,64,4096]{2,1,0:T(8,128)(2,1)S(1)} %copy-done.1, f32[16,1024]{1,0:T(8,128)S(1)} %get-tuple-element.40.bands, bf16[64,48]{1,0:T(8,128)(2,1)S(1)} %copy-done.4, bf16[128,512]{1,0:T(8,128)(2,1)S(1)} %copy-done.2, bf16[128,512]{1,0:T(8,128)(2,1)S(1)} %copy-done.3), custom_call_target="tpu_custom_call" | custom-call | bytes 1906688 | tf_op jit(solution)/shard_map/pallas_call | solution.py:99
  74.9 1.7 %shard_map.124 = f32[64,4096]{1,0:T(8,128)} custom-call(f32[16,1024]{1,0:T(8,128)S(1)} %get-tuple-element.41.total, bf16[64,48]{1,0:T(8,128)(2,1)S(1)} %copy-done.4, bf16[128,512]{1,0:T(8,128)(2,1)S(1)} %copy-done.2, bf16[128,512]{1,0:T(8,128)(2,1)S(1)} %copy-done.3), custom_call_target="tpu_custom_call" | custom-call | bytes 333824 | tf_op jit(solution)/shard_map/pallas_call | solution.py:99
  76.5 3.7 %collective-permute-start.21 = (bf16[512,256]{1,0:T(8,128)(2,1)S(1)}, bf16[512,256]{1,0:T(8,128)(2,1)S(1)}, u32[]{:S(2)}, u32[]{:S(2)}) collective-permute-start(bf16[512,256]{1,0:T(8,128)(2,1)S(1)} %get-tuple-element.51), channel_id=1, source_target_pairs={{1,0},{0,1},{3,2},{2,3},{5,4},{4,5},{7,6},{6,7},{9,8},{8,9},{11,10... | collective-permute-start | bytes 786440 | tf_op jit(solution)/shard_map/ppermute | solution.py:61
  81.3 8.9 %shard_map.125 = (bf16[512,256]{1,0:T(8,128)(2,1)S(1)}, bf16[512,256]{1,0:T(8,128)(2,1)S(1)}, bf16[512,256]{1,0:T(8,128)(2,1)S(1)}, bf16[512,256]{1,0:T(8,128)(2,1)S(1)}, bf16[256,4096]{1,0:T(8,128)(2,1)S(1)}) custom-call(s32[1]{0:T(128)} %bitcast.refs_0_, bf16[64,16]{1,0:T(8,128)(2,1)S(1)} %copy-done.5, bf16[128,512]{1,0:T(8,128)(2,1)S(1)} %copy-done.2, ...), custom_call_target="tpu_custom_call" | custom-call | flops 4294967296 | bytes 13109252 | tf_op jit(solution)/shard_map/pallas_call | solution.py:99
  92.1 3.9 %shard_map.126 = (bf16[512,256]{1,0:T(8,128)(2,1)S(1)}, bf16[512,256]{1,0:T(8,128)(2,1)S(1)}) custom-call(s32[1]{0:T(128)} %bitcast.refs_0_, bf16[512,4096]{1,0:T(8,128)(2,1)S(1)} %get-tuple-element.42.refs_6_.refs_1_, bf16[512,4096]{1,0:T(8,128)(2,1)S(1)} %get-tuple-element.43.refs_7_.refs_2_, bf16[256,4096]{1,0:T(8,128)(2,1)S(1)} %get-tuple-element.45.refs_3_, ...), custom_call_target="tpu_custom_call" | custom-call | flops 2147483648 | bytes 12582916 | tf_op jit(solution)/shard_map/pallas_call | solution.py:99
  97.9 2.8 %shard_map.127 = bf16[512,2048]{1,0:T(8,128)(2,1)} custom-call(s32[3]{0:T(128)S(1)} %pad_add_fusion.where, bf16[512,256]{1,0:T(8,128)(2,1)S(1)} %get-tuple-element.39.refs_0_, bf16[512,256]{1,0:T(8,128)(2,1)S(1)} %get-tuple-element.44.refs_1_, bf16[512,256]{1,0:T(8,128)(2,1)S(1)} %get-tuple-element.49.refs_2_, ...), custom_call_target="tpu_custom_call" | custom-call | bytes 2097164 | tf_op jit(solution)/shard_map/pallas_call | solution.py:99
  (70 shorter events, 16.7 us)
Async XLA Ops:
  0.6 6.4 %collective-permute-start = (bf16[64,4096]{1,0:T(8,128)(2,1)}, bf16[64,4096]{1,0:T(8,128)(2,1)S(1)}, u32[]{:S(2)}, u32[]{:S(2)}) collective-permute-start(bf16[64,4096]{1,0:T(8,128)(2,1)} %param.12), channel_id=1, source_target_pairs={{1,0},{0,1},{3,2},{2,3},{5,4},{4,5},{7,6},{6,7},{9,8},{8,9},{11,10... | collective-permute-start | bytes 1572872 | tf_op jit(solution)/shard_map/ppermute | solution.py:61
  7.0 16.1 %collective-permute-start.4 = (bf16[512,4096]{1,0:T(8,128)(2,1)}, bf16[512,4096]{1,0:T(8,128)(2,1)S(1)}, u32[]{:S(2)}, u32[]{:S(2)}) collective-permute-start(bf16[512,4096]{1,0:T(8,128)(2,1)} %refs_4_.1), channel_id=1, source_target_pairs={{1,0},{0,1},{3,2},{2,3},{5,4},{4,5},{7,6},{6,7},{9,8},{8,9},{11,10... | collective-permute-start | bytes 12582920 | tf_op jit(solution)/shard_map/ppermute | solution.py:61
  7.1 11.0 %collective-permute-start.2 = (bf16[64,4096]{1,0:T(8,128)(2,1)S(1)}, bf16[64,4096]{1,0:T(8,128)(2,1)S(1)}, u32[]{:S(2)}, u32[]{:S(2)}) collective-permute-start(bf16[64,4096]{1,0:T(8,128)(2,1)S(1)} %collective-permute-done), channel_id=1, source_target_pairs={{8,0},{3,1},{10,2},{5,3},{12,4},{7,5},{14,6},{129,7},{16,8},{11,9}... | collective-permute-start | bytes 1572872 | tf_op jit(solution)/shard_map/ppermute | solution.py:61
  11.0 6.8 %collective-permute-start.1 = (bf16[16,1024]{1,0:T(8,128)(2,1)S(1)}, bf16[16,1024]{1,0:T(8,128)(2,1)S(1)}, u32[]{:S(2)}, u32[]{:S(2)}) collective-permute-start(bf16[16,1024]{1,0:T(8,128)(2,1)S(1)} %get-tuple-element.32), channel_id=1, source_target_pairs={{128,0},{129,1},{130,2},{131,3},{132,4},{133,5},{134,6},{135,7},{1... | collective-permute-start | bytes 98312 | tf_op jit(solution)/shard_map/ppermute | solution.py:61
  12.5 10.6 %collective-permute-start.3 = (bf16[64,4096]{1,0:T(8,128)(2,1)S(1)}, bf16[64,4096]{1,0:T(8,128)(2,1)S(1)}, u32[]{:S(2)}, u32[]{:S(2)}) collective-permute-start(bf16[64,4096]{1,0:T(8,128)(2,1)S(1)} %collective-permute-done), channel_id=1, source_target_pairs={{24,0},{135,1},{26,2},{1,3},{28,4},{3,5},{30,6},{5,7},{0,8},{143,9... | collective-permute-start | bytes 1572872 | tf_op jit(solution)/shard_map/ppermute | solution.py:61
  13.8 11.9 %collective-permute-start.7 = (bf16[64,4096]{1,0:T(8,128)(2,1)S(1)}, bf16[64,4096]{1,0:T(8,128)(2,1)S(1)}, u32[]{:S(2)}, u32[]{:S(2)}) collective-permute-start(bf16[64,4096]{1,0:T(8,128)(2,1)S(1)} %collective-permute-done), channel_id=1, source_target_pairs={{16,0},{5,1},{18,2},{135,3},{20,4},{129,5},{22,6},{3,7},{24,8},{13... | collective-permute-start | bytes 1572872 | tf_op jit(solution)/shard_map/ppermute | solution.py:61
  18.2 28.6 %collective-permute-start.11 = (bf16[128,4096]{1,0:T(8,128)(2,1)S(1)}, bf16[128,4096]{1,0:T(8,128)(2,1)}, u32[]{:S(2)}, u32[]{:S(2)}) collective-permute-start(bf16[128,4096]{1,0:T(8,128)(2,1)S(1)} %pad_maximum_fusion.refs_6_), channel_id=1, source_target_pairs={{2,0},{9,1},{4,2},{11,3},{6,4},{13,5},{128,6},{15,7},{10,8},{17,9}... | collective-permute-start | bytes 3145736 | tf_op jit(solution)/shard_map/ppermute | solution.py:61
  21.5 25.3 %collective-permute-start.12 = (bf16[128,4096]{1,0:T(8,128)(2,1)S(1)}, bf16[128,4096]{1,0:T(8,128)(2,1)S(1)}, u32[]{:S(2)}, u32[]{:S(2)}) collective-permute-start(bf16[128,4096]{1,0:T(8,128)(2,1)S(1)} %pad_maximum_fusion.refs_6_), channel_id=1, source_target_pairs={{134,0},{25,1},{0,2},{27,3},{2,4},{29,5},{4,6},{31,7},{142,8},{1,9... | collective-permute-start | bytes 3145736 | tf_op jit(solution)/shard_map/ppermute | solution.py:61
  23.1 3.6 %collective-permute-start.5 = (bf16[16,1024]{1,0:T(8,128)(2,1)S(1)}, bf16[16,1024]{1,0:T(8,128)(2,1)S(1)}, u32[]{:S(2)}, u32[]{:S(2)}) collective-permute-start(bf16[16,1024]{1,0:T(8,128)(2,1)S(1)} %add_convert_fusion.1), channel_id=1, source_target_pairs={{32,0},{33,1},{34,2},{35,3},{36,4},{37,5},{38,6},{39,7},{40,8},{41... | collective-permute-start | bytes 98312 | tf_op jit(solution)/shard_map/ppermute | solution.py:61
  26.6 4.7 %collective-permute-start.6 = (bf16[16,1024]{1,0:T(8,128)(2,1)S(1)}, bf16[16,1024]{1,0:T(8,128)(2,1)S(1)}, u32[]{:S(2)}, u32[]{:S(2)}) collective-permute-start(bf16[16,1024]{1,0:T(8,128)(2,1)S(1)} %add_convert_fusion), channel_id=1, source_target_pairs={{64,0},{65,1},{66,2},{67,3},{68,4},{69,5},{70,6},{71,7},{72,8},{73... | collective-permute-start | bytes 98312 | tf_op jit(solution)/shard_map/ppermute | solution.py:61
  31.3 8.9 %collective-permute-start.8 = (bf16[16,1024]{1,0:T(8,128)(2,1)S(1)}, bf16[16,1024]{1,0:T(8,128)(2,1)S(1)}, u32[]{:S(2)}, u32[]{:S(2)}) collective-permute-start(bf16[16,1024]{1,0:T(8,128)(2,1)S(1)} %get-tuple-element.35), channel_id=1, source_target_pairs={{8,0},{3,1},{10,2},{5,3},{12,4},{7,5},{14,6},{129,7},{16,8},{11,9}... | collective-permute-start | bytes 98312 | tf_op jit(solution)/shard_map/ppermute | solution.py:61
  33.6 6.7 %collective-permute-start.9 = (bf16[16,1024]{1,0:T(8,128)(2,1)S(1)}, bf16[16,1024]{1,0:T(8,128)(2,1)S(1)}, u32[]{:S(2)}, u32[]{:S(2)}) collective-permute-start(bf16[16,1024]{1,0:T(8,128)(2,1)S(1)} %get-tuple-element.35), channel_id=1, source_target_pairs={{16,0},{5,1},{18,2},{135,3},{20,4},{129,5},{22,6},{3,7},{24,8},{13... | collective-permute-start | bytes 98312 | tf_op jit(solution)/shard_map/ppermute | solution.py:61
  37.9 4.0 %collective-permute-start.10 = (bf16[16,1024]{1,0:T(8,128)(2,1)S(1)}, bf16[16,1024]{1,0:T(8,128)(2,1)S(1)}, u32[]{:S(2)}, u32[]{:S(2)}) collective-permute-start(bf16[16,1024]{1,0:T(8,128)(2,1)S(1)} %get-tuple-element.35), channel_id=1, source_target_pairs={{24,0},{135,1},{26,2},{1,3},{28,4},{3,5},{30,6},{5,7},{0,8},{143,9... | collective-permute-start | bytes 98312 | tf_op jit(solution)/shard_map/ppermute | solution.py:61
  41.8 31.3 %collective-permute-start.17 = (bf16[128,4096]{1,0:T(8,128)(2,1)}, bf16[128,4096]{1,0:T(8,128)(2,1)}, u32[]{:S(2)}, u32[]{:S(2)}) collective-permute-start(bf16[128,4096]{1,0:T(8,128)(2,1)} %constant_dynamic-update-slice_fusion.refs_7_), channel_id=1, source_target_pairs={{134,0},{25,1},{0,2},{27,3},{2,4},{29,5},{4,6},{31,7},{142,8},{1,9... | collective-permute-start | bytes 3145736 | tf_op jit(solution)/shard_map/ppermute | solution.py:61
  46.8 5.0 %collective-permute-start.13 = (bf16[64,1024]{1,0:T(8,128)(2,1)S(1)}, bf16[64,1024]{1,0:T(8,128)(2,1)S(1)}, u32[]{:S(2)}, u32[]{:S(2)}) collective-permute-start(bf16[64,1024]{1,0:T(8,128)(2,1)S(1)} %constant_dynamic-update-slice_fusion.2), channel_id=1, source_target_pairs={{1,0},{0,1},{3,2},{2,3},{5,4},{4,5},{7,6},{6,7},{9,8},{8,9},{11,10... | collective-permute-start | bytes 393224 | tf_op jit(solution)/shard_map/ppermute | solution.py:61
  51.9 8.0 %collective-permute-start.16 = (bf16[64,1024]{1,0:T(8,128)(2,1)S(1)}, bf16[64,1024]{1,0:T(8,128)(2,1)S(1)}, u32[]{:S(2)}, u32[]{:S(2)}) collective-permute-start(bf16[64,1024]{1,0:T(8,128)(2,1)S(1)} %collective-permute-done.13), channel_id=1, source_target_pairs={{24,0},{135,1},{26,2},{1,3},{28,4},{3,5},{30,6},{5,7},{0,8},{143,9... | collective-permute-start | bytes 393224 | tf_op jit(solution)/shard_map/ppermute | solution.py:61
  55.7 5.2 %collective-permute-start.15 = (bf16[64,1024]{1,0:T(8,128)(2,1)S(1)}, bf16[64,1024]{1,0:T(8,128)(2,1)S(1)}, u32[]{:S(2)}, u32[]{:S(2)}) collective-permute-start(bf16[64,1024]{1,0:T(8,128)(2,1)S(1)} %collective-permute-done.13), channel_id=1, source_target_pairs={{16,0},{5,1},{18,2},{135,3},{20,4},{129,5},{22,6},{3,7},{24,8},{13... | collective-permute-start | bytes 393224 | tf_op jit(solution)/shard_map/ppermute | solution.py:61
  56.0 5.7 %collective-permute-start.14 = (bf16[64,1024]{1,0:T(8,128)(2,1)S(1)}, bf16[64,1024]{1,0:T(8,128)(2,1)S(1)}, u32[]{:S(2)}, u32[]{:S(2)}) collective-permute-start(bf16[64,1024]{1,0:T(8,128)(2,1)S(1)} %collective-permute-done.13), channel_id=1, source_target_pairs={{8,0},{3,1},{10,2},{5,3},{12,4},{7,5},{14,6},{129,7},{16,8},{11,9}... | collective-permute-start | bytes 393224 | tf_op jit(solution)/shard_map/ppermute | solution.py:61
  58.1 22.2 %collective-permute-start.18 = (bf16[128,4096]{1,0:T(8,128)(2,1)}, bf16[128,4096]{1,0:T(8,128)(2,1)S(1)}, u32[]{:S(2)}, u32[]{:S(2)}) collective-permute-start(bf16[128,4096]{1,0:T(8,128)(2,1)} %constant_dynamic-update-slice_fusion.refs_7_), channel_id=1, source_target_pairs={{2,0},{9,1},{4,2},{11,3},{6,4},{13,5},{128,6},{15,7},{10,8},{17,9}... | collective-permute-start | bytes 3145736 | tf_op jit(solution)/shard_map/ppermute | solution.py:61
  61.7 29.0 %collective-permute-start.19 = (bf16[128,4096]{1,0:T(8,128)(2,1)}, bf16[128,4096]{1,0:T(8,128)(2,1)S(1)}, u32[]{:S(2)}, u32[]{:S(2)}) collective-permute-start(bf16[128,4096]{1,0:T(8,128)(2,1)} %collective-permute-done.11.refs_10_), channel_id=1, source_target_pairs={{2,0},{9,1},{4,2},{11,3},{6,4},{13,5},{128,6},{15,7},{10,8},{17,9}... | collective-permute-start | bytes 3145736 | tf_op jit(solution)/shard_map/ppermute | solution.py:61
  73.1 17.6 %collective-permute-start.20 = (bf16[128,4096]{1,0:T(8,128)(2,1)}, bf16[128,4096]{1,0:T(8,128)(2,1)S(1)}, u32[]{:S(2)}, u32[]{:S(2)}) collective-permute-start(bf16[128,4096]{1,0:T(8,128)(2,1)} %collective-permute-done.17.refs_9_), channel_id=1, source_target_pairs={{134,0},{25,1},{0,2},{27,3},{2,4},{29,5},{4,6},{31,7},{142,8},{1,9... | collective-permute-start | bytes 3145736 | tf_op jit(solution)/shard_map/ppermute | solution.py:61
  76.5 20.2 %collective-permute-start.21 = (bf16[512,256]{1,0:T(8,128)(2,1)S(1)}, bf16[512,256]{1,0:T(8,128)(2,1)S(1)}, u32[]{:S(2)}, u32[]{:S(2)}) collective-permute-start(bf16[512,256]{1,0:T(8,128)(2,1)S(1)} %get-tuple-element.51), channel_id=1, source_target_pairs={{1,0},{0,1},{3,2},{2,3},{5,4},{4,5},{7,6},{6,7},{9,8},{8,9},{11,10... | collective-permute-start | bytes 786440 | tf_op jit(solution)/shard_map/ppermute | solution.py:61
  90.1 6.7 %collective-permute-start.22 = (bf16[512,256]{1,0:T(8,128)(2,1)S(1)}, bf16[512,256]{1,0:T(8,128)(2,1)S(1)}, u32[]{:S(2)}, u32[]{:S(2)}) collective-permute-start(bf16[512,256]{1,0:T(8,128)(2,1)S(1)} %get-tuple-element.52), channel_id=1, source_target_pairs={{1,0},{0,1},{3,2},{2,3},{5,4},{4,5},{7,6},{6,7},{9,8},{8,9},{11,10... | collective-permute-start | bytes 786440 | tf_op jit(solution)/shard_map/ppermute | solution.py:61
  90.2 6.5 %collective-permute-start.24 = (bf16[512,256]{1,0:T(8,128)(2,1)S(1)}, bf16[512,256]{1,0:T(8,128)(2,1)S(1)}, u32[]{:S(2)}, u32[]{:S(2)}) collective-permute-start(bf16[512,256]{1,0:T(8,128)(2,1)S(1)} %get-tuple-element.54), channel_id=1, source_target_pairs={{1,0},{0,1},{3,2},{2,3},{5,4},{4,5},{7,6},{6,7},{9,8},{8,9},{11,10... | collective-permute-start | bytes 786440 | tf_op jit(solution)/shard_map/ppermute | solution.py:61
  (13 other events, 178.5 us)

commit v7 on v6

--- a/solution.py
+++ b/solution.py
@@ -338,7 +338,7 @@
     second_sum = join(after(sent, ahead, behind, other), pair_x).astype(BF16)
     total = join(second_sum, along_x(2))
 
-    early = after(jnp.concatenate([swapped, ahead], axis=0), sent)
+    early = after(jnp.concatenate([swapped, ahead], axis=0), second_sum)
     late = jnp.concatenate([across, behind], axis=0)
     next_early, last_early = fetch(early, along(1, 1)), fetch(early, along(1, -1))
     def gather(value):
@@ -347,8 +347,8 @@
     band_line = gather(after(total.astype(BF16), late))
     late = after(late, band_line)
     next_late, last_late = fetch(late, along(1, 1)), fetch(late, along(1, -1))
-    band_line = fetch(after(band_line, next_early, last_early), sibling)
-    blocks = gather(band_line).reshape(4, 4, BAND, narrow)
+    band_line = fetch(band_line, sibling)
+    blocks = gather(after(band_line, next_early, last_early)).reshape(4, 4, BAND, narrow)
     far_early = fetch(after(next_early, blocks), along(1, 1))
     lines = [[early, late], [next_early, next_late], [far_early], [last_early, last_late]]
     bands = [blocks[:, g].reshape(4 * BAND, narrow) for g in range(4)]
@@ -381,18 +381,19 @@
     *results, own, other = forward([0])
     first_out = results[0]
     lines[2].append(fetch(after(last_late, first_out), along(1, -1)))
+    *more, step = forward([3, 1], [2])
+    results += more
+    second_out = more[0]
     new_momentum = call(
         residual_kernel,
         shape(momentum.shape, F32),
-        (momentum, gradient, after(exact, first_out), back_rows3, back_hi, back_lo),
+        (momentum, gradient, after(exact, second_out), back_rows3, back_hi, back_lo),
     )
     direction = call(
         direction_kernel,
         shape((rows, width), F32),
-        (after(total, first_out), back_rows3, back_hi, back_lo),
-    )
-    *more, step = forward([3, 1], [2])
-    results += more
+        (after(total, second_out), back_rows3, back_hi, back_lo),
+    )
     lines[2][0] = after(lines[2][0], direction, new_momentum)
     results += call(
         lambda *refs: last_kernel(len(lines[2]), *refs),

time: 101 us -> 102 us (level)
  waiting for transfers between devices: 13.8 us -> 21.1 us
  starting transfers between devices: 50.7 us -> 45.7 us
  local copies, waits for them, and re-layouts: 4.06 us -> 2.46 us
    ppermute x25, waiting for transfers between devices: 13.8 us -> 21.1 us  [fetch(): lax.ppermute(value, AXES, [(place(*source(*spot(i))), i) for i in range(2...]
    ppermute x25, starting transfers between devices: 50.7 us -> 45.7 us  [fetch(): lax.ppermute(value, AXES, [(place(*source(*spot(i))), i) for i in range(2...]
    unnamed x28 -> x32, local copies, waits for them, and re-layouts: 3.19 us -> 2.38 us
  transfers between devices with their start and end apart: 25 -> 25, of which waited for: 10 -> 11; matrix products, arithmetic and copies ran while one was open for 2% -> 0% of each run, Pallas kernels for 28% -> 28%
where the time goes in v7:
time: 102 us; the launch traced here: 101 us
  starting transfers between devices  45.7 us (45%)
  Pallas kernels  31 us (30%)
  waiting for transfers between devices  21.1 us (21%)
  local copies, waits for them, and re-layouts  2.46 us (2%)
    ppermute x25, starting transfers between devices, fetch(): lax.ppermute(value, AXES, [(place(*source(*spot(i))), i) for i in range(2...  45.7 us
    pallas_call x7, Pallas kernels, call(): pl.pallas_call(kernel, out_shape=out_shape, in_specs=specs, out_specs=jax...  31 us
    ppermute x25, waiting for transfers between devices, fetch(): lax.ppermute(value, AXES, [(place(*source(*spot(i))), i) for i in range(2...  21.1 us
    unnamed x32, local copies, waits for them, and re-layouts  2.38 us
  transfers between devices with their start and end apart: 25, of which 11 were waited for; matrix products, arithmetic and copies ran while one was open for 0% of the time, Pallas kernels for 28%

profile of v7, /device:TPU:1, one launch (start us, length us, event | category | flops | bytes accessed | tf_op | source)
XLA Modules:
  0.0 101.3 jit_solution(15825072019139928828)
XLA Ops:
  0.6 3.3 %collective-permute-start = (bf16[64,4096]{1,0:T(8,128)(2,1)}, bf16[64,4096]{1,0:T(8,128)(2,1)S(1)}, u32[]{:S(2)}, u32[]{:S(2)}) collective-permute-start(bf16[64,4096]{1,0:T(8,128)(2,1)} %param.12), channel_id=1, source_target_pairs={{1,0},{0,1},{3,2},{2,3},{5,4},{4,5},{7,6},{6,7},{9,8},{8,9},{11,10... | collective-permute-start | bytes 1572872 | tf_op jit(solution)/shard_map/ppermute | solution.py:61
  4.0 3.0 %shard_map.121 = (f32[16,1024]{1,0:T(8,128)S(1)}, bf16[16,1024]{1,0:T(8,128)(2,1)S(1)}) custom-call(f32[1,64,4096]{2,1,0:T(8,128)} %momentum.3, bf16[1,64,4096]{2,1,0:T(8,128)(2,1)} %gradient.3, bf16[1024,128]{1,0:T(8,128)(2,1)} %constant.61.clone.cols, bf16[16,192]{1,0:T(8,128)(2,1)} %constant.62.clone.rows3), custom_call_target="tpu_custom_call" | custom-call | bytes 1841152 | tf_op jit(solution)/shard_map/pallas_call | solution.py:99
  7.1 3.9 %collective-permute-start.2 = (bf16[64,4096]{1,0:T(8,128)(2,1)S(1)}, bf16[64,4096]{1,0:T(8,128)(2,1)S(1)}, u32[]{:S(2)}, u32[]{:S(2)}) collective-permute-start(bf16[64,4096]{1,0:T(8,128)(2,1)S(1)} %collective-permute-done), channel_id=1, source_target_pairs={{8,0},{3,1},{10,2},{5,3},{12,4},{7,5},{14,6},{129,7},{16,8},{11,9}... | collective-permute-start | bytes 1572872 | tf_op jit(solution)/shard_map/ppermute | solution.py:61
  13.8 4.0 %collective-permute-done.1 = bf16[16,1024]{1,0:T(8,128)(2,1)S(1)} collective-permute-done((bf16[16,1024]{1,0:T(8,128)(2,1)S(1)}, bf16[16,1024]{1,0:T(8,128)(2,1)S(1)}, u32[]{:S(2)}, u32[]{:S(2)}) %collective-permute-start.1) | collective-permute-done | bytes 32800 | tf_op jit(solution)/shard_map/ppermute | solution.py:61
  18.2 4.9 %collective-permute-done.3 = bf16[64,4096]{1,0:T(8,128)(2,1)S(1)} collective-permute-done((bf16[64,4096]{1,0:T(8,128)(2,1)S(1)}, bf16[64,4096]{1,0:T(8,128)(2,1)S(1)}, u32[]{:S(2)}, u32[]{:S(2)}) %collective-permute-start.3) | collective-permute-done | bytes 524320 | tf_op jit(solution)/shard_map/ppermute | solution.py:61
  24.4 1.8 %collective-permute-done.5 = bf16[16,1024]{1,0:T(8,128)(2,1)S(1)} collective-permute-done((bf16[16,1024]{1,0:T(8,128)(2,1)S(1)}, bf16[16,1024]{1,0:T(8,128)(2,1)S(1)}, u32[]{:S(2)}, u32[]{:S(2)}) %collective-permute-start.5) | collective-permute-done | bytes 32800 | tf_op jit(solution)/shard_map/ppermute | solution.py:61
  26.1 2.8 %collective-permute-start.6 = (bf16[16,1024]{1,0:T(8,128)(2,1)S(1)}, bf16[16,1024]{1,0:T(8,128)(2,1)S(1)}, u32[]{:S(2)}, u32[]{:S(2)}) collective-permute-start(bf16[16,1024]{1,0:T(8,128)(2,1)S(1)} %add_convert_fusion), channel_id=1, source_target_pairs={{64,0},{65,1},{66,2},{67,3},{68,4},{69,5},{70,6},{71,7},{72,8},{73... | collective-permute-start | bytes 98312 | tf_op jit(solution)/shard_map/ppermute | solution.py:61
  29.0 2.0 %collective-permute-start.12 = (bf16[128,4096]{1,0:T(8,128)(2,1)S(1)}, bf16[128,4096]{1,0:T(8,128)(2,1)S(1)}, u32[]{:S(2)}, u32[]{:S(2)}) collective-permute-start(bf16[128,4096]{1,0:T(8,128)(2,1)S(1)} %pad_maximum_fusion.refs_6_), channel_id=1, source_target_pairs={{2,0},{9,1},{4,2},{11,3},{6,4},{13,5},{128,6},{15,7},{10,8},{17,9}... | collective-permute-start | bytes 3145736 | tf_op jit(solution)/shard_map/ppermute | solution.py:61
  31.1 2.0 %collective-permute-start.8 = (bf16[16,1024]{1,0:T(8,128)(2,1)S(1)}, bf16[16,1024]{1,0:T(8,128)(2,1)S(1)}, u32[]{:S(2)}, u32[]{:S(2)}) collective-permute-start(bf16[16,1024]{1,0:T(8,128)(2,1)S(1)} %get-tuple-element.35), channel_id=1, source_target_pairs={{8,0},{3,1},{10,2},{5,3},{12,4},{7,5},{14,6},{129,7},{16,8},{11,9}... | collective-permute-start | bytes 98312 | tf_op jit(solution)/shard_map/ppermute | solution.py:61
  33.1 4.7 %collective-permute-start.9 = (bf16[16,1024]{1,0:T(8,128)(2,1)S(1)}, bf16[16,1024]{1,0:T(8,128)(2,1)S(1)}, u32[]{:S(2)}, u32[]{:S(2)}) collective-permute-start(bf16[16,1024]{1,0:T(8,128)(2,1)S(1)} %get-tuple-element.35), channel_id=1, source_target_pairs={{16,0},{5,1},{18,2},{135,3},{20,4},{129,5},{22,6},{3,7},{24,8},{13... | collective-permute-start | bytes 98312 | tf_op jit(solution)/shard_map/ppermute | solution.py:61
  38.8 2.9 %collective-permute-done.10 = bf16[16,1024]{1,0:T(8,128)(2,1)S(1)} collective-permute-done((bf16[16,1024]{1,0:T(8,128)(2,1)S(1)}, bf16[16,1024]{1,0:T(8,128)(2,1)S(1)}, u32[]{:S(2)}, u32[]{:S(2)}) %collective-permute-start.10) | collective-permute-done | bytes 32800 | tf_op jit(solution)/shard_map/ppermute | solution.py:61
  42.5 7.2 %collective-permute-start.11 = (bf16[64,1024]{1,0:T(8,128)(2,1)S(1)}, bf16[64,1024]{1,0:T(8,128)(2,1)S(1)}, u32[]{:S(2)}, u32[]{:S(2)}) collective-permute-start(bf16[64,1024]{1,0:T(8,128)(2,1)S(1)} %constant_dynamic-update-slice_fusion.2), channel_id=1, source_target_pairs={{1,0},{0,1},{3,2},{2,3},{5,4},{4,5},{7,6},{6,7},{9,8},{8,9},{11,10... | collective-permute-start | bytes 393224 | tf_op jit(solution)/shard_map/ppermute | solution.py:61
  51.7 2.3 %collective-permute-start.15 = (bf16[64,1024]{1,0:T(8,128)(2,1)S(1)}, bf16[64,1024]{1,0:T(8,128)(2,1)S(1)}, u32[]{:S(2)}, u32[]{:S(2)}) collective-permute-start(bf16[64,1024]{1,0:T(8,128)(2,1)S(1)} %collective-permute-done.11), channel_id=1, source_target_pairs={{16,0},{5,1},{18,2},{135,3},{20,4},{129,5},{22,6},{3,7},{24,8},{13... | collective-permute-start | bytes 393224 | tf_op jit(solution)/shard_map/ppermute | solution.py:61
  54.0 1.7 %collective-permute-start.14 = (bf16[64,1024]{1,0:T(8,128)(2,1)S(1)}, bf16[64,1024]{1,0:T(8,128)(2,1)S(1)}, u32[]{:S(2)}, u32[]{:S(2)}) collective-permute-start(bf16[64,1024]{1,0:T(8,128)(2,1)S(1)} %collective-permute-done.11), channel_id=1, source_target_pairs={{8,0},{3,1},{10,2},{5,3},{12,4},{7,5},{14,6},{129,7},{16,8},{11,9}... | collective-permute-start | bytes 393224 | tf_op jit(solution)/shard_map/ppermute | solution.py:61
  55.7 1.7 %collective-permute-start.18 = (bf16[128,4096]{1,0:T(8,128)(2,1)S(1)}, bf16[128,4096]{1,0:T(8,128)(2,1)S(1)}, u32[]{:S(2)}, u32[]{:S(2)}) collective-permute-start(bf16[128,4096]{1,0:T(8,128)(2,1)S(1)} %constant_dynamic-update-slice_fusion.refs_7_), channel_id=1, source_target_pairs={{2,0},{9,1},{4,2},{11,3},{6,4},{13,5},{128,6},{15,7},{10,8},{17,9}... | collective-permute-start | bytes 3145736 | tf_op jit(solution)/shard_map/ppermute | solution.py:61
  58.3 1.9 %collective-permute-start.19 = (bf16[128,4096]{1,0:T(8,128)(2,1)}, bf16[128,4096]{1,0:T(8,128)(2,1)S(1)}, u32[]{:S(2)}, u32[]{:S(2)}) collective-permute-start(bf16[128,4096]{1,0:T(8,128)(2,1)} %copy-done.11), channel_id=1, source_target_pairs={{2,0},{9,1},{4,2},{11,3},{6,4},{13,5},{128,6},{15,7},{10,8},{17,9}... | collective-permute-start | bytes 3145736 | tf_op jit(solution)/shard_map/ppermute | solution.py:61
  60.2 8.9 %shard_map.122 = (bf16[512,256]{1,0:T(8,128)(2,1)S(1)}, bf16[512,256]{1,0:T(8,128)(2,1)S(1)}, bf16[512,4096]{1,0:T(8,128)(2,1)S(1)}, bf16[512,4096]{1,0:T(8,128)(2,1)S(1)}) custom-call(s32[1]{0:T(128)} %bitcast.refs_0_, bf16[64,16]{1,0:T(8,128)(2,1)S(1)} %copy-done.5, bf16[128,512]{1,0:T(8,128)(2,1)S(1)} %copy-done.2, bf16[64,1024]{1,0:T(8,128)(2,1)S(1)} %bitcast.8, ...), custom_call_target="tpu_custom_call" | custom-call | flops 2147483648 | bytes 10749956 | tf_op jit(solution)/shard_map/pallas_call | solution.py:99
  69.2 3.3 %collective-permute-done.18.refs_11_ = bf16[128,4096]{1,0:T(8,128)(2,1)S(1)} collective-permute-done((bf16[128,4096]{1,0:T(8,128)(2,1)S(1)}, bf16[128,4096]{1,0:T(8,128)(2,1)S(1)}, u32[]{:S(2)}, u32[]{:S(2)}) %collective-permute-start.18) | collective-permute-done | bytes 1048608 | tf_op jit(solution)/shard_map/ppermute | solution.py:61
  73.5 9.0 %shard_map.123 = (bf16[512,256]{1,0:T(8,128)(2,1)S(1)}, bf16[512,256]{1,0:T(8,128)(2,1)S(1)}, bf16[512,256]{1,0:T(8,128)(2,1)S(1)}, bf16[512,256]{1,0:T(8,128)(2,1)S(1)}, bf16[256,4096]{1,0:T(8,128)(2,1)S(1)}) custom-call(s32[1]{0:T(128)} %bitcast.refs_0_, bf16[64,16]{1,0:T(8,128)(2,1)S(1)} %copy-done.5, bf16[128,512]{1,0:T(8,128)(2,1)S(1)} %copy-done.2, ...), custom_call_target="tpu_custom_call" | custom-call | flops 4294967296 | bytes 13109252 | tf_op jit(solution)/shard_map/pallas_call | solution.py:99
  82.5 1.7 %shard_map.124 = f32[1,64,4096]{2,1,0:T(8,128)} custom-call(f32[1,64,4096]{2,1,0:T(8,128)S(1)} %copy-done, bf16[1,64,4096]{2,1,0:T(8,128)(2,1)S(1)} %copy-done.1, f32[16,1024]{1,0:T(8,128)S(1)} %get-tuple-element.42.bands, bf16[64,48]{1,0:T(8,128)(2,1)S(1)} %copy-done.4, bf16[128,512]{1,0:T(8,128)(2,1)S(1)} %copy-done.2, bf16[128,512]{1,0:T(8,128)(2,1)S(1)} %copy-done.3), custom_call_target="tpu_custom_call" | custom-call | bytes 1906688 | tf_op jit(solution)/shard_map/pallas_call | solution.py:99
  84.1 1.7 %shard_map.125 = f32[64,4096]{1,0:T(8,128)} custom-call(f32[16,1024]{1,0:T(8,128)S(1)} %get-tuple-element.43.total, bf16[64,48]{1,0:T(8,128)(2,1)S(1)} %copy-done.4, bf16[128,512]{1,0:T(8,128)(2,1)S(1)} %copy-done.2, bf16[128,512]{1,0:T(8,128)(2,1)S(1)} %copy-done.3), custom_call_target="tpu_custom_call" | custom-call | bytes 333824 | tf_op jit(solution)/shard_map/pallas_call | solution.py:99
  85.8 5.3 %collective-permute-start.21 = (bf16[512,256]{1,0:T(8,128)(2,1)S(1)}, bf16[512,256]{1,0:T(8,128)(2,1)S(1)}, u32[]{:S(2)}, u32[]{:S(2)}) collective-permute-start(bf16[512,256]{1,0:T(8,128)(2,1)S(1)} %get-tuple-element.51), channel_id=1, source_target_pairs={{1,0},{0,1},{3,2},{2,3},{5,4},{4,5},{7,6},{6,7},{9,8},{8,9},{11,10... | collective-permute-start | bytes 786440 | tf_op jit(solution)/shard_map/ppermute | solution.py:61
  93.0 3.9 %shard_map.126 = (bf16[512,256]{1,0:T(8,128)(2,1)S(1)}, bf16[512,256]{1,0:T(8,128)(2,1)S(1)}) custom-call(s32[1]{0:T(128)} %bitcast.refs_0_, bf16[512,4096]{1,0:T(8,128)(2,1)S(1)} %get-tuple-element.39.refs_6_.refs_1_, bf16[512,4096]{1,0:T(8,128)(2,1)S(1)} %get-tuple-element.40.refs_7_.refs_2_, bf16[256,4096]{1,0:T(8,128)(2,1)S(1)} %get-tuple-element.46.refs_3_, ...), custom_call_target="tpu_custom_call" | custom-call | flops 2147483648 | bytes 12582916 | tf_op jit(solution)/shard_map/pallas_call | solution.py:99
  98.5 2.8 %shard_map.127 = bf16[512,2048]{1,0:T(8,128)(2,1)} custom-call(s32[3]{0:T(128)S(1)} %pad_add_fusion.where, bf16[512,256]{1,0:T(8,128)(2,1)S(1)} %get-tuple-element.44.refs_0_, bf16[512,256]{1,0:T(8,128)(2,1)S(1)} %get-tuple-element.45.refs_1_, bf16[512,256]{1,0:T(8,128)(2,1)S(1)} %get-tuple-element.50.refs_2_, ...), custom_call_target="tpu_custom_call" | custom-call | bytes 2097164 | tf_op jit(solution)/shard_map/pallas_call | solution.py:99
  (74 shorter events, 13.6 us)
Async XLA Ops:
  0.6 6.4 %collective-permute-start = (bf16[64,4096]{1,0:T(8,128)(2,1)}, bf16[64,4096]{1,0:T(8,128)(2,1)S(1)}, u32[]{:S(2)}, u32[]{:S(2)}) collective-permute-start(bf16[64,4096]{1,0:T(8,128)(2,1)} %param.12), channel_id=1, source_target_pairs={{1,0},{0,1},{3,2},{2,3},{5,4},{4,5},{7,6},{6,7},{9,8},{8,9},{11,10... | collective-permute-start | bytes 1572872 | tf_op jit(solution)/shard_map/ppermute | solution.py:61
  7.0 16.1 %collective-permute-start.4 = (bf16[512,4096]{1,0:T(8,128)(2,1)}, bf16[512,4096]{1,0:T(8,128)(2,1)S(1)}, u32[]{:S(2)}, u32[]{:S(2)}) collective-permute-start(bf16[512,4096]{1,0:T(8,128)(2,1)} %refs_4_.1), channel_id=1, source_target_pairs={{1,0},{0,1},{3,2},{2,3},{5,4},{4,5},{7,6},{6,7},{9,8},{8,9},{11,10... | collective-permute-start | bytes 12582920 | tf_op jit(solution)/shard_map/ppermute | solution.py:61
  7.1 11.0 %collective-permute-start.2 = (bf16[64,4096]{1,0:T(8,128)(2,1)S(1)}, bf16[64,4096]{1,0:T(8,128)(2,1)S(1)}, u32[]{:S(2)}, u32[]{:S(2)}) collective-permute-start(bf16[64,4096]{1,0:T(8,128)(2,1)S(1)} %collective-permute-done), channel_id=1, source_target_pairs={{8,0},{3,1},{10,2},{5,3},{12,4},{7,5},{14,6},{129,7},{16,8},{11,9}... | collective-permute-start | bytes 1572872 | tf_op jit(solution)/shard_map/ppermute | solution.py:61
  11.0 6.8 %collective-permute-start.1 = (bf16[16,1024]{1,0:T(8,128)(2,1)S(1)}, bf16[16,1024]{1,0:T(8,128)(2,1)S(1)}, u32[]{:S(2)}, u32[]{:S(2)}) collective-permute-start(bf16[16,1024]{1,0:T(8,128)(2,1)S(1)} %get-tuple-element.32), channel_id=1, source_target_pairs={{128,0},{129,1},{130,2},{131,3},{132,4},{133,5},{134,6},{135,7},{1... | collective-permute-start | bytes 98312 | tf_op jit(solution)/shard_map/ppermute | solution.py:61
  12.5 10.6 %collective-permute-start.3 = (bf16[64,4096]{1,0:T(8,128)(2,1)S(1)}, bf16[64,4096]{1,0:T(8,128)(2,1)S(1)}, u32[]{:S(2)}, u32[]{:S(2)}) collective-permute-start(bf16[64,4096]{1,0:T(8,128)(2,1)S(1)} %collective-permute-done), channel_id=1, source_target_pairs={{24,0},{135,1},{26,2},{1,3},{28,4},{3,5},{30,6},{5,7},{0,8},{143,9... | collective-permute-start | bytes 1572872 | tf_op jit(solution)/shard_map/ppermute | solution.py:61
  13.8 10.4 %collective-permute-start.7 = (bf16[64,4096]{1,0:T(8,128)(2,1)S(1)}, bf16[64,4096]{1,0:T(8,128)(2,1)S(1)}, u32[]{:S(2)}, u32[]{:S(2)}) collective-permute-start(bf16[64,4096]{1,0:T(8,128)(2,1)S(1)} %collective-permute-done), channel_id=1, source_target_pairs={{16,0},{5,1},{18,2},{135,3},{20,4},{129,5},{22,6},{3,7},{24,8},{13... | collective-permute-start | bytes 1572872 | tf_op jit(solution)/shard_map/ppermute | solution.py:61
  23.1 3.1 %collective-permute-start.5 = (bf16[16,1024]{1,0:T(8,128)(2,1)S(1)}, bf16[16,1024]{1,0:T(8,128)(2,1)S(1)}, u32[]{:S(2)}, u32[]{:S(2)}) collective-permute-start(bf16[16,1024]{1,0:T(8,128)(2,1)S(1)} %add_convert_fusion.1), channel_id=1, source_target_pairs={{32,0},{33,1},{34,2},{35,3},{36,4},{37,5},{38,6},{39,7},{40,8},{41... | collective-permute-start | bytes 98312 | tf_op jit(solution)/shard_map/ppermute | solution.py:61
  26.1 4.9 %collective-permute-start.6 = (bf16[16,1024]{1,0:T(8,128)(2,1)S(1)}, bf16[16,1024]{1,0:T(8,128)(2,1)S(1)}, u32[]{:S(2)}, u32[]{:S(2)}) collective-permute-start(bf16[16,1024]{1,0:T(8,128)(2,1)S(1)} %add_convert_fusion), channel_id=1, source_target_pairs={{64,0},{65,1},{66,2},{67,3},{68,4},{69,5},{70,6},{71,7},{72,8},{73... | collective-permute-start | bytes 98312 | tf_op jit(solution)/shard_map/ppermute | solution.py:61
  29.0 21.7 %collective-permute-start.12 = (bf16[128,4096]{1,0:T(8,128)(2,1)S(1)}, bf16[128,4096]{1,0:T(8,128)(2,1)S(1)}, u32[]{:S(2)}, u32[]{:S(2)}) collective-permute-start(bf16[128,4096]{1,0:T(8,128)(2,1)S(1)} %pad_maximum_fusion.refs_6_), channel_id=1, source_target_pairs={{2,0},{9,1},{4,2},{11,3},{6,4},{13,5},{128,6},{15,7},{10,8},{17,9}... | collective-permute-start | bytes 3145736 | tf_op jit(solution)/shard_map/ppermute | solution.py:61
  31.0 19.6 %collective-permute-start.13 = (bf16[128,4096]{1,0:T(8,128)(2,1)S(1)}, bf16[128,4096]{1,0:T(8,128)(2,1)S(1)}, u32[]{:S(2)}, u32[]{:S(2)}) collective-permute-start(bf16[128,4096]{1,0:T(8,128)(2,1)S(1)} %pad_maximum_fusion.refs_6_), channel_id=1, source_target_pairs={{134,0},{25,1},{0,2},{27,3},{2,4},{29,5},{4,6},{31,7},{142,8},{1,9... | collective-permute-start | bytes 3145736 | tf_op jit(solution)/shard_map/ppermute | solution.py:61
  31.1 6.7 %collective-permute-start.8 = (bf16[16,1024]{1,0:T(8,128)(2,1)S(1)}, bf16[16,1024]{1,0:T(8,128)(2,1)S(1)}, u32[]{:S(2)}, u32[]{:S(2)}) collective-permute-start(bf16[16,1024]{1,0:T(8,128)(2,1)S(1)} %get-tuple-element.35), channel_id=1, source_target_pairs={{8,0},{3,1},{10,2},{5,3},{12,4},{7,5},{14,6},{129,7},{16,8},{11,9}... | collective-permute-start | bytes 98312 | tf_op jit(solution)/shard_map/ppermute | solution.py:61
  33.1 5.7 %collective-permute-start.9 = (bf16[16,1024]{1,0:T(8,128)(2,1)S(1)}, bf16[16,1024]{1,0:T(8,128)(2,1)S(1)}, u32[]{:S(2)}, u32[]{:S(2)}) collective-permute-start(bf16[16,1024]{1,0:T(8,128)(2,1)S(1)} %get-tuple-element.35), channel_id=1, source_target_pairs={{16,0},{5,1},{18,2},{135,3},{20,4},{129,5},{22,6},{3,7},{24,8},{13... | collective-permute-start | bytes 98312 | tf_op jit(solution)/shard_map/ppermute | solution.py:61
  37.8 4.0 %collective-permute-start.10 = (bf16[16,1024]{1,0:T(8,128)(2,1)S(1)}, bf16[16,1024]{1,0:T(8,128)(2,1)S(1)}, u32[]{:S(2)}, u32[]{:S(2)}) collective-permute-start(bf16[16,1024]{1,0:T(8,128)(2,1)S(1)} %get-tuple-element.35), channel_id=1, source_target_pairs={{24,0},{135,1},{26,2},{1,3},{28,4},{3,5},{30,6},{5,7},{0,8},{143,9... | collective-permute-start | bytes 98312 | tf_op jit(solution)/shard_map/ppermute | solution.py:61
  41.8 27.3 %collective-permute-start.17 = (bf16[128,4096]{1,0:T(8,128)(2,1)S(1)}, bf16[128,4096]{1,0:T(8,128)(2,1)}, u32[]{:S(2)}, u32[]{:S(2)}) collective-permute-start(bf16[128,4096]{1,0:T(8,128)(2,1)S(1)} %constant_dynamic-update-slice_fusion.refs_7_), channel_id=1, source_target_pairs={{134,0},{25,1},{0,2},{27,3},{2,4},{29,5},{4,6},{31,7},{142,8},{1,9... | collective-permute-start | bytes 3145736 | tf_op jit(solution)/shard_map/ppermute | solution.py:61
  42.5 8.2 %collective-permute-start.11 = (bf16[64,1024]{1,0:T(8,128)(2,1)S(1)}, bf16[64,1024]{1,0:T(8,128)(2,1)S(1)}, u32[]{:S(2)}, u32[]{:S(2)}) collective-permute-start(bf16[64,1024]{1,0:T(8,128)(2,1)S(1)} %constant_dynamic-update-slice_fusion.2), channel_id=1, source_target_pairs={{1,0},{0,1},{3,2},{2,3},{5,4},{4,5},{7,6},{6,7},{9,8},{8,9},{11,10... | collective-permute-start | bytes 393224 | tf_op jit(solution)/shard_map/ppermute | solution.py:61
  50.7 7.2 %collective-permute-start.16 = (bf16[64,1024]{1,0:T(8,128)(2,1)S(1)}, bf16[64,1024]{1,0:T(8,128)(2,1)S(1)}, u32[]{:S(2)}, u32[]{:S(2)}) collective-permute-start(bf16[64,1024]{1,0:T(8,128)(2,1)S(1)} %collective-permute-done.11), channel_id=1, source_target_pairs={{24,0},{135,1},{26,2},{1,3},{28,4},{3,5},{30,6},{5,7},{0,8},{143,9... | collective-permute-start | bytes 393224 | tf_op jit(solution)/shard_map/ppermute | solution.py:61
  51.7 6.2 %collective-permute-start.15 = (bf16[64,1024]{1,0:T(8,128)(2,1)S(1)}, bf16[64,1024]{1,0:T(8,128)(2,1)S(1)}, u32[]{:S(2)}, u32[]{:S(2)}) collective-permute-start(bf16[64,1024]{1,0:T(8,128)(2,1)S(1)} %collective-permute-done.11), channel_id=1, source_target_pairs={{16,0},{5,1},{18,2},{135,3},{20,4},{129,5},{22,6},{3,7},{24,8},{13... | collective-permute-start | bytes 393224 | tf_op jit(solution)/shard_map/ppermute | solution.py:61
  54.0 4.2 %collective-permute-start.14 = (bf16[64,1024]{1,0:T(8,128)(2,1)S(1)}, bf16[64,1024]{1,0:T(8,128)(2,1)S(1)}, u32[]{:S(2)}, u32[]{:S(2)}) collective-permute-start(bf16[64,1024]{1,0:T(8,128)(2,1)S(1)} %collective-permute-done.11), channel_id=1, source_target_pairs={{8,0},{3,1},{10,2},{5,3},{12,4},{7,5},{14,6},{129,7},{16,8},{11,9}... | collective-permute-start | bytes 393224 | tf_op jit(solution)/shard_map/ppermute | solution.py:61
  55.7 16.8 %collective-permute-start.18 = (bf16[128,4096]{1,0:T(8,128)(2,1)S(1)}, bf16[128,4096]{1,0:T(8,128)(2,1)S(1)}, u32[]{:S(2)}, u32[]{:S(2)}) collective-permute-start(bf16[128,4096]{1,0:T(8,128)(2,1)S(1)} %constant_dynamic-update-slice_fusion.refs_7_), channel_id=1, source_target_pairs={{2,0},{9,1},{4,2},{11,3},{6,4},{13,5},{128,6},{15,7},{10,8},{17,9}... | collective-permute-start | bytes 3145736 | tf_op jit(solution)/shard_map/ppermute | solution.py:61
  58.3 33.4 %collective-permute-start.19 = (bf16[128,4096]{1,0:T(8,128)(2,1)}, bf16[128,4096]{1,0:T(8,128)(2,1)S(1)}, u32[]{:S(2)}, u32[]{:S(2)}) collective-permute-start(bf16[128,4096]{1,0:T(8,128)(2,1)} %copy-done.11), channel_id=1, source_target_pairs={{2,0},{9,1},{4,2},{11,3},{6,4},{13,5},{128,6},{15,7},{10,8},{17,9}... | collective-permute-start | bytes 3145736 | tf_op jit(solution)/shard_map/ppermute | solution.py:61
  69.1 22.5 %collective-permute-start.20 = (bf16[128,4096]{1,0:T(8,128)(2,1)}, bf16[128,4096]{1,0:T(8,128)(2,1)S(1)}, u32[]{:S(2)}, u32[]{:S(2)}) collective-permute-start(bf16[128,4096]{1,0:T(8,128)(2,1)} %collective-permute-done.17.refs_9_), channel_id=1, source_target_pairs={{134,0},{25,1},{0,2},{27,3},{2,4},{29,5},{4,6},{31,7},{142,8},{1,9... | collective-permute-start | bytes 3145736 | tf_op jit(solution)/shard_map/ppermute | solution.py:61
  85.8 11.5 %collective-permute-start.21 = (bf16[512,256]{1,0:T(8,128)(2,1)S(1)}, bf16[512,256]{1,0:T(8,128)(2,1)S(1)}, u32[]{:S(2)}, u32[]{:S(2)}) collective-permute-start(bf16[512,256]{1,0:T(8,128)(2,1)S(1)} %get-tuple-element.51), channel_id=1, source_target_pairs={{1,0},{0,1},{3,2},{2,3},{5,4},{4,5},{7,6},{6,7},{9,8},{8,9},{11,10... | collective-permute-start | bytes 786440 | tf_op jit(solution)/shard_map/ppermute | solution.py:61
  91.1 6.2 %collective-permute-start.22 = (bf16[512,256]{1,0:T(8,128)(2,1)S(1)}, bf16[512,256]{1,0:T(8,128)(2,1)S(1)}, u32[]{:S(2)}, u32[]{:S(2)}) collective-permute-start(bf16[512,256]{1,0:T(8,128)(2,1)S(1)} %get-tuple-element.52), channel_id=1, source_target_pairs={{1,0},{0,1},{3,2},{2,3},{5,4},{4,5},{7,6},{6,7},{9,8},{8,9},{11,10... | collective-permute-start | bytes 786440 | tf_op jit(solution)/shard_map/ppermute | solution.py:61
  91.1 6.2 %collective-permute-start.24 = (bf16[512,256]{1,0:T(8,128)(2,1)S(1)}, bf16[512,256]{1,0:T(8,128)(2,1)S(1)}, u32[]{:S(2)}, u32[]{:S(2)}) collective-permute-start(bf16[512,256]{1,0:T(8,128)(2,1)S(1)} %get-tuple-element.54), channel_id=1, source_target_pairs={{1,0},{0,1},{3,2},{2,3},{5,4},{4,5},{7,6},{6,7},{9,8},{8,9},{11,10... | collective-permute-start | bytes 786440 | tf_op jit(solution)/shard_map/ppermute | solution.py:61
  (15 other events, 196.1 us)

commit v8 on v7

--- a/solution.py
+++ b/solution.py
@@ -327,19 +327,25 @@
         return lax.optimization_barrier((value, *others))[0]
 
     swapped = fetch(weight, sibling)
-    swapped = after(swapped, rounded)
-    other = fetch(after(activations, swapped), sibling)
-    ahead, behind, across = (fetch(swapped, along(0, s)) for s in (1, -1, 2))
+    other = fetch(after(activations, swapped, rounded), sibling)
+    ahead, behind = (fetch(swapped, along(0, s)) for s in (1, -1))
+    across = [fetch(ahead[: rows // 2], along(0, 1)), fetch(behind[rows // 2 :], along(0, -1))]
+
+    new_momentum = call(
+        residual_kernel,
+        shape(momentum.shape, F32),
+        (momentum, gradient, exact, back_rows3, back_hi, back_lo),
+    )
 
     def join(value, source):
         return value.astype(F32) + fetch(value, source).astype(F32)
 
     sent = join(after(rounded, swapped), far_z).astype(BF16)
-    second_sum = join(after(sent, ahead, behind, other), pair_x).astype(BF16)
+    second_sum = join(after(sent, ahead, behind, other, new_momentum), pair_x).astype(BF16)
     total = join(second_sum, along_x(2))
 
     early = after(jnp.concatenate([swapped, ahead], axis=0), second_sum)
-    late = jnp.concatenate([across, behind], axis=0)
+    late = jnp.concatenate([*across, behind], axis=0)
     next_early, last_early = fetch(early, along(1, 1)), fetch(early, along(1, -1))
     def gather(value):
         return jnp.concatenate([value] + [fetch(value, along(0, s)) for s in (1, 2, -1)], axis=0)
@@ -348,9 +354,14 @@
     late = after(late, band_line)
     next_late, last_late = fetch(late, along(1, 1)), fetch(late, along(1, -1))
     band_line = fetch(band_line, sibling)
-    blocks = gather(after(band_line, next_early, last_early)).reshape(4, 4, BAND, narrow)
+    direction = call(
+        direction_kernel,
+        shape((rows, width), F32),
+        (total, back_rows3, back_hi, back_lo),
+    )
+    blocks = gather(after(band_line, next_early, last_early, direction)).reshape(4, 4, BAND, narrow)
     far_early = fetch(after(next_early, blocks), along(1, 1))
-    lines = [[early, late], [next_early, next_late], [far_early], [last_early, last_late]]
+    lines = [[early, late], [next_early, next_late], [far_early, fetch(last_late, along(1, -1))], [last_early, last_late]]
     bands = [blocks[:, g].reshape(4 * BAND, narrow) for g in range(4)]
 
     block = shape((tokens, 4 * rows), BF16)
@@ -379,22 +390,8 @@
         )
 
     *results, own, other = forward([0])
-    first_out = results[0]
-    lines[2].append(fetch(after(last_late, first_out), along(1, -1)))
     *more, step = forward([3, 1], [2])
     results += more
-    second_out = more[0]
-    new_momentum = call(
-        residual_kernel,
-        shape(momentum.shape, F32),
-        (momentum, gradient, after(exact, second_out), back_rows3, back_hi, back_lo),
-    )
-    direction = call(
-        direction_kernel,
-        shape((rows, width), F32),
-        (after(total, second_out), back_rows3, back_hi, back_lo),
-    )
-    lines[2][0] = after(lines[2][0], direction, new_momentum)
     results += call(
         lambda *refs: last_kernel(len(lines[2]), *refs),
         (block, block),

time: 102 us -> 99.9 us (0.979)
  starting transfers between devices: 45.7 us -> 39.1 us
  local copies, waits for them, and re-layouts: 2.46 us -> 4.95 us
  waiting for transfers between devices: 21.1 us -> 23.3 us
    ppermute x25 -> x26, starting transfers between devices: 45.7 us -> 39.1 us  [fetch(): lax.ppermute(value, AXES, [(place(*source(*spot(i))), i) for i in range(2...]
    ppermute x25 -> x26, waiting for transfers between devices: 21.1 us -> 23.3 us  [fetch(): lax.ppermute(value, AXES, [(place(*source(*spot(i))), i) for i in range(2...]
    unnamed x32 -> x25, local copies, waits for them, and re-layouts: 2.38 us -> 4.04 us
  transfers between devices with their start and end apart: 25 -> 26, of which waited for: 11 -> 9; matrix products, arithmetic and copies ran while one was open for 0% -> 3% of each run, Pallas kernels for 28% -> 29%
where the time goes in v8:
time: 99.9 us; the launch traced here: 99.7 us
  starting transfers between devices  39.1 us (39%)
  Pallas kernels  31.2 us (31%)
  waiting for transfers between devices  23.3 us (23%)
  local copies, waits for them, and re-layouts  4.95 us (5%)
    ppermute x26, starting transfers between devices, fetch(): lax.ppermute(value, AXES, [(place(*source(*spot(i))), i) for i in range(2...  39.1 us
    pallas_call x7, Pallas kernels, call(): pl.pallas_call(kernel, out_shape=out_shape, in_specs=specs, out_specs=jax...  31.2 us
    ppermute x26, waiting for transfers between devices, fetch(): lax.ppermute(value, AXES, [(place(*source(*spot(i))), i) for i in range(2...  23.3 us
    unnamed x25, local copies, waits for them, and re-layouts  4.04 us
  transfers between devices with their start and end apart: 26, of which 9 were waited for; matrix products, arithmetic and copies ran while one was open for 3% of the time, Pallas kernels for 29%

profile of v8, /device:TPU:1, one launch (start us, length us, event | category | flops | bytes accessed | tf_op | source)
XLA Modules:
  0.0 99.7 jit_solution(9345078322964645496)
XLA Ops:
  0.7 3.3 %collective-permute-start = (bf16[64,4096]{1,0:T(8,128)(2,1)}, bf16[64,4096]{1,0:T(8,128)(2,1)S(1)}, u32[]{:S(2)}, u32[]{:S(2)}) collective-permute-start(bf16[64,4096]{1,0:T(8,128)(2,1)} %param.12), channel_id=1, source_target_pairs={{1,0},{0,1},{3,2},{2,3},{5,4},{4,5},{7,6},{6,7},{9,8},{8,9},{11,10... | collective-permute-start | bytes 1572872 | tf_op jit(solution)/shard_map/ppermute | solution.py:61
  4.0 3.0 %shard_map.121 = (f32[16,1024]{1,0:T(8,128)S(1)}, bf16[16,1024]{1,0:T(8,128)(2,1)S(1)}) custom-call(f32[1,64,4096]{2,1,0:T(8,128)} %momentum.3, bf16[1,64,4096]{2,1,0:T(8,128)(2,1)} %gradient.3, bf16[1024,128]{1,0:T(8,128)(2,1)} %constant.61.clone.cols, bf16[16,192]{1,0:T(8,128)(2,1)} %constant.62.clone.rows3), custom_call_target="tpu_custom_call" | custom-call | bytes 1841152 | tf_op jit(solution)/shard_map/pallas_call | solution.py:99
  7.2 3.8 %collective-permute-start.2 = (bf16[64,4096]{1,0:T(8,128)(2,1)S(1)}, bf16[64,4096]{1,0:T(8,128)(2,1)S(1)}, u32[]{:S(2)}, u32[]{:S(2)}) collective-permute-start(bf16[64,4096]{1,0:T(8,128)(2,1)S(1)} %collective-permute-done), channel_id=1, source_target_pairs={{8,0},{3,1},{10,2},{5,3},{12,4},{7,5},{14,6},{129,7},{16,8},{11,9}... | collective-permute-start | bytes 1572872 | tf_op jit(solution)/shard_map/ppermute | solution.py:61
  11.1 2.8 %collective-permute-start.1 = (bf16[16,1024]{1,0:T(8,128)(2,1)S(1)}, bf16[16,1024]{1,0:T(8,128)(2,1)S(1)}, u32[]{:S(2)}, u32[]{:S(2)}) collective-permute-start(bf16[16,1024]{1,0:T(8,128)(2,1)S(1)} %get-tuple-element.26), channel_id=1, source_target_pairs={{128,0},{129,1},{130,2},{131,3},{132,4},{133,5},{134,6},{135,7},{1... | collective-permute-start | bytes 98312 | tf_op jit(solution)/shard_map/ppermute | solution.py:61
  16.4 1.6 %shard_map.122 = f32[1,64,4096]{2,1,0:T(8,128)} custom-call(f32[1,64,4096]{2,1,0:T(8,128)S(1)} %copy-done, bf16[1,64,4096]{2,1,0:T(8,128)(2,1)S(1)} %copy-done.1, f32[16,1024]{1,0:T(8,128)S(1)} %get-tuple-element.24.bands, bf16[64,48]{1,0:T(8,128)(2,1)S(1)} %copy-done.5, bf16[128,512]{1,0:T(8,128)(2,1)S(1)} %copy-done.2, bf16[128,512]{1,0:T(8,128)(2,1)S(1)} %copy-done.4), custom_call_target="tpu_custom_call" | custom-call | bytes 1906688 | tf_op jit(solution)/shard_map/pallas_call | solution.py:99
  18.1 3.5 %collective-permute-done.1 = bf16[16,1024]{1,0:T(8,128)(2,1)S(1)} collective-permute-done((bf16[16,1024]{1,0:T(8,128)(2,1)S(1)}, bf16[16,1024]{1,0:T(8,128)(2,1)S(1)}, u32[]{:S(2)}, u32[]{:S(2)}) %collective-permute-start.1) | collective-permute-done | bytes 32800 | tf_op jit(solution)/shard_map/ppermute | solution.py:61
  23.3 3.5 %collective-permute-done.7 = bf16[32,4096]{1,0:T(8,128)(2,1)S(1)} collective-permute-done((bf16[32,4096]{1,0:T(8,128)(2,1)S(1)}, bf16[32,4096]{1,0:T(8,128)(2,1)S(1)}, u32[]{:S(2)}, u32[]{:S(2)}) %collective-permute-start.7) | collective-permute-done | bytes 262176 | tf_op jit(solution)/shard_map/ppermute | solution.py:61
  30.7 2.8 %collective-permute-start.6 = (bf16[16,1024]{1,0:T(8,128)(2,1)S(1)}, bf16[16,1024]{1,0:T(8,128)(2,1)S(1)}, u32[]{:S(2)}, u32[]{:S(2)}) collective-permute-start(bf16[16,1024]{1,0:T(8,128)(2,1)S(1)} %add_convert_fusion), channel_id=1, source_target_pairs={{64,0},{65,1},{66,2},{67,3},{68,4},{69,5},{70,6},{71,7},{72,8},{73... | collective-permute-start | bytes 98312 | tf_op jit(solution)/shard_map/ppermute | solution.py:61
  34.4 2.7 %collective-permute-start.13 = (bf16[128,4096]{1,0:T(8,128)(2,1)S(1)}, bf16[128,4096]{1,0:T(8,128)(2,1)}, u32[]{:S(2)}, u32[]{:S(2)}) collective-permute-start(bf16[128,4096]{1,0:T(8,128)(2,1)S(1)} %pad_maximum_fusion.refs_6_), channel_id=1, source_target_pairs={{2,0},{9,1},{4,2},{11,3},{6,4},{13,5},{128,6},{15,7},{10,8},{17,9}... | collective-permute-start | bytes 3145736 | tf_op jit(solution)/shard_map/ppermute | solution.py:61
  37.1 1.4 %collective-permute-start.9 = (bf16[16,1024]{1,0:T(8,128)(2,1)S(1)}, bf16[16,1024]{1,0:T(8,128)(2,1)S(1)}, u32[]{:S(2)}, u32[]{:S(2)}) collective-permute-start(bf16[16,1024]{1,0:T(8,128)(2,1)S(1)} %get-tuple-element.29), channel_id=1, source_target_pairs={{8,0},{3,1},{10,2},{5,3},{12,4},{7,5},{14,6},{129,7},{16,8},{11,9}... | collective-permute-start | bytes 98312 | tf_op jit(solution)/shard_map/ppermute | solution.py:61
  38.5 1.4 %collective-permute-start.11 = (bf16[16,1024]{1,0:T(8,128)(2,1)S(1)}, bf16[16,1024]{1,0:T(8,128)(2,1)S(1)}, u32[]{:S(2)}, u32[]{:S(2)}) collective-permute-start(bf16[16,1024]{1,0:T(8,128)(2,1)S(1)} %get-tuple-element.29), channel_id=1, source_target_pairs={{24,0},{135,1},{26,2},{1,3},{28,4},{3,5},{30,6},{5,7},{0,8},{143,9... | collective-permute-start | bytes 98312 | tf_op jit(solution)/shard_map/ppermute | solution.py:61
  40.7 2.2 %collective-permute-done.10 = bf16[16,1024]{1,0:T(8,128)(2,1)S(1)} collective-permute-done((bf16[16,1024]{1,0:T(8,128)(2,1)S(1)}, bf16[16,1024]{1,0:T(8,128)(2,1)S(1)}, u32[]{:S(2)}, u32[]{:S(2)}) %collective-permute-start.10) | collective-permute-done | bytes 32800 | tf_op jit(solution)/shard_map/ppermute | solution.py:61
  43.8 2.1 %collective-permute-start.19 = (bf16[128,4096]{1,0:T(8,128)(2,1)}, bf16[128,4096]{1,0:T(8,128)(2,1)}, u32[]{:S(2)}, u32[]{:S(2)}) collective-permute-start(bf16[128,4096]{1,0:T(8,128)(2,1)} %constant_dynamic-update-slice_fusion.refs_7_), channel_id=1, source_target_pairs={{2,0},{9,1},{4,2},{11,3},{6,4},{13,5},{128,6},{15,7},{10,8},{17,9}... | collective-permute-start | bytes 3145736 | tf_op jit(solution)/shard_map/ppermute | solution.py:61
  45.9 5.7 %collective-permute-start.12 = (bf16[64,1024]{1,0:T(8,128)(2,1)S(1)}, bf16[64,1024]{1,0:T(8,128)(2,1)S(1)}, u32[]{:S(2)}, u32[]{:S(2)}) collective-permute-start(bf16[64,1024]{1,0:T(8,128)(2,1)S(1)} %constant_dynamic-update-slice_fusion.3), channel_id=1, source_target_pairs={{1,0},{0,1},{3,2},{2,3},{5,4},{4,5},{7,6},{6,7},{9,8},{8,9},{11,10... | collective-permute-start | bytes 393224 | tf_op jit(solution)/shard_map/ppermute | solution.py:61
  51.7 1.7 %shard_map.123 = f32[64,4096]{1,0:T(8,128)} custom-call(f32[16,1024]{1,0:T(8,128)S(1)} %get-tuple-element.50.total, bf16[64,48]{1,0:T(8,128)(2,1)S(1)} %copy-done.5, bf16[128,512]{1,0:T(8,128)(2,1)S(1)} %copy-done.2, bf16[128,512]{1,0:T(8,128)(2,1)S(1)} %copy-done.4), custom_call_target="tpu_custom_call" | custom-call | bytes 333824 | tf_op jit(solution)/shard_map/pallas_call | solution.py:99
  53.5 2.8 %collective-permute-start.16 = (bf16[64,1024]{1,0:T(8,128)(2,1)S(1)}, bf16[64,1024]{1,0:T(8,128)(2,1)S(1)}, u32[]{:S(2)}, u32[]{:S(2)}) collective-permute-start(bf16[64,1024]{1,0:T(8,128)(2,1)S(1)} %collective-permute-done.12), channel_id=1, source_target_pairs={{16,0},{5,1},{18,2},{135,3},{20,4},{129,5},{22,6},{3,7},{24,8},{13... | collective-permute-start | bytes 393224 | tf_op jit(solution)/shard_map/ppermute | solution.py:61
  56.6 10.5 %collective-permute-done.18.refs_9_ = bf16[128,4096]{1,0:T(8,128)(2,1)} collective-permute-done((bf16[128,4096]{1,0:T(8,128)(2,1)}, bf16[128,4096]{1,0:T(8,128)(2,1)}, u32[]{:S(2)}, u32[]{:S(2)}) %collective-permute-start.18) | collective-permute-done | bytes 1048608 | tf_op jit(solution)/shard_map/ppermute | solution.py:61
  67.2 2.7 %collective-permute-start.20 = (bf16[128,4096]{1,0:T(8,128)(2,1)}, bf16[128,4096]{1,0:T(8,128)(2,1)}, u32[]{:S(2)}, u32[]{:S(2)}) collective-permute-start(bf16[128,4096]{1,0:T(8,128)(2,1)} %collective-permute-done.13.refs_10_), channel_id=1, source_target_pairs={{2,0},{9,1},{4,2},{11,3},{6,4},{13,5},{128,6},{15,7},{10,8},{17,9}... | collective-permute-start | bytes 3145736 | tf_op jit(solution)/shard_map/ppermute | solution.py:61
  70.0 8.9 %shard_map.124 = (bf16[512,256]{1,0:T(8,128)(2,1)S(1)}, bf16[512,256]{1,0:T(8,128)(2,1)S(1)}, bf16[512,4096]{1,0:T(8,128)(2,1)S(1)}, bf16[512,4096]{1,0:T(8,128)(2,1)S(1)}) custom-call(s32[1]{0:T(128)} %bitcast.2.refs_0_, bf16[64,16]{1,0:T(8,128)(2,1)S(1)} %copy-done.6, bf16[128,512]{1,0:T(8,128)(2,1)S(1)} %copy-done.3, bf16[64,1024]{1,0:T(8,128)(2,1)S(1)} %bitcast.16, ...), custom_call_target="tpu_custom_call" | custom-call | flops 2147483648 | bytes 10749956 | tf_op jit(solution)/shard_map/pallas_call | solution.py:99
  78.9 2.5 %collective-permute-start.22 = (bf16[512,256]{1,0:T(8,128)(2,1)S(1)}, bf16[512,256]{1,0:T(8,128)(2,1)S(1)}, u32[]{:S(2)}, u32[]{:S(2)}) collective-permute-start(bf16[512,256]{1,0:T(8,128)(2,1)S(1)} %get-tuple-element.41), channel_id=1, source_target_pairs={{1,0},{0,1},{3,2},{2,3},{5,4},{4,5},{7,6},{6,7},{9,8},{8,9},{11,10... | collective-permute-start | bytes 786440 | tf_op jit(solution)/shard_map/ppermute | solution.py:61
  81.5 9.2 %shard_map.125 = (bf16[512,256]{1,0:T(8,128)(2,1)S(1)}, bf16[512,256]{1,0:T(8,128)(2,1)S(1)}, bf16[512,256]{1,0:T(8,128)(2,1)S(1)}, bf16[512,256]{1,0:T(8,128)(2,1)S(1)}, bf16[256,4096]{1,0:T(8,128)(2,1)S(1)}) custom-call(s32[1]{0:T(128)} %bitcast.2.refs_0_, bf16[64,16]{1,0:T(8,128)(2,1)S(1)} %copy-done.6, bf16[128,512]{1,0:T(8,128)(2,1)S(1)} %copy-done.3, ...), custom_call_target="tpu_custom_call" | custom-call | flops 4294967296 | bytes 13109252 | tf_op jit(solution)/shard_map/pallas_call | solution.py:99
  91.3 4.0 %shard_map.126 = (bf16[512,256]{1,0:T(8,128)(2,1)S(1)}, bf16[512,256]{1,0:T(8,128)(2,1)S(1)}) custom-call(s32[1]{0:T(128)} %bitcast.2.refs_0_, bf16[512,4096]{1,0:T(8,128)(2,1)S(1)} %get-tuple-element.34.refs_6_.refs_1_, bf16[512,4096]{1,0:T(8,128)(2,1)S(1)} %get-tuple-element.35.refs_7_.refs_2_, bf16[256,4096]{1,0:T(8,128)(2,1)S(1)} %get-tuple-element.37.refs_3_, ...), custom_call_target="tpu_custom_call" | custom-call | flops 2147483648 | bytes 12582916 | tf_op jit(solution)/shard_map/pallas_call | solution.py:99
  95.6 1.3 %collective-permute-done.24.refs_6_ = bf16[512,256]{1,0:T(8,128)(2,1)S(1)} collective-permute-done((bf16[512,256]{1,0:T(8,128)(2,1)S(1)}, bf16[512,256]{1,0:T(8,128)(2,1)S(1)}, u32[]{:S(2)}, u32[]{:S(2)}) %collective-permute-start.24) | collective-permute-done | bytes 262176 | tf_op jit(solution)/shard_map/ppermute | solution.py:61
  96.9 2.8 %shard_map.127 = bf16[512,2048]{1,0:T(8,128)(2,1)} custom-call(s32[3]{0:T(128)S(1)} %pad_add_fusion.where, bf16[512,256]{1,0:T(8,128)(2,1)S(1)} %get-tuple-element.33.refs_0_, bf16[512,256]{1,0:T(8,128)(2,1)S(1)} %get-tuple-element.36.refs_1_, bf16[512,256]{1,0:T(8,128)(2,1)S(1)} %get-tuple-element.39.refs_2_, ...), custom_call_target="tpu_custom_call" | custom-call | bytes 2097164 | tf_op jit(solution)/shard_map/pallas_call | solution.py:99
  (71 shorter events, 12.2 us)
Async XLA Ops:
  0.7 6.4 %collective-permute-start = (bf16[64,4096]{1,0:T(8,128)(2,1)}, bf16[64,4096]{1,0:T(8,128)(2,1)S(1)}, u32[]{:S(2)}, u32[]{:S(2)}) collective-permute-start(bf16[64,4096]{1,0:T(8,128)(2,1)} %param.12), channel_id=1, source_target_pairs={{1,0},{0,1},{3,2},{2,3},{5,4},{4,5},{7,6},{6,7},{9,8},{8,9},{11,10... | collective-permute-start | bytes 1572872 | tf_op jit(solution)/shard_map/ppermute | solution.py:61
  7.0 20.6 %collective-permute-start.4 = (bf16[512,4096]{1,0:T(8,128)(2,1)}, bf16[512,4096]{1,0:T(8,128)(2,1)S(1)}, u32[]{:S(2)}, u32[]{:S(2)}) collective-permute-start(bf16[512,4096]{1,0:T(8,128)(2,1)} %refs_4_.1), channel_id=1, source_target_pairs={{1,0},{0,1},{3,2},{2,3},{5,4},{4,5},{7,6},{6,7},{9,8},{8,9},{11,10... | collective-permute-start | bytes 12582920 | tf_op jit(solution)/shard_map/ppermute | solution.py:61
  7.2 14.3 %collective-permute-start.2 = (bf16[64,4096]{1,0:T(8,128)(2,1)S(1)}, bf16[64,4096]{1,0:T(8,128)(2,1)S(1)}, u32[]{:S(2)}, u32[]{:S(2)}) collective-permute-start(bf16[64,4096]{1,0:T(8,128)(2,1)S(1)} %collective-permute-done), channel_id=1, source_target_pairs={{8,0},{3,1},{10,2},{5,3},{12,4},{7,5},{14,6},{129,7},{16,8},{11,9}... | collective-permute-start | bytes 1572872 | tf_op jit(solution)/shard_map/ppermute | solution.py:61
  11.1 11.0 %collective-permute-start.3 = (bf16[64,4096]{1,0:T(8,128)(2,1)S(1)}, bf16[64,4096]{1,0:T(8,128)(2,1)S(1)}, u32[]{:S(2)}, u32[]{:S(2)}) collective-permute-start(bf16[64,4096]{1,0:T(8,128)(2,1)S(1)} %collective-permute-done), channel_id=1, source_target_pairs={{24,0},{135,1},{26,2},{1,3},{28,4},{3,5},{30,6},{5,7},{0,8},{143,9... | collective-permute-start | bytes 1572872 | tf_op jit(solution)/shard_map/ppermute | solution.py:61
  11.1 10.5 %collective-permute-start.1 = (bf16[16,1024]{1,0:T(8,128)(2,1)S(1)}, bf16[16,1024]{1,0:T(8,128)(2,1)S(1)}, u32[]{:S(2)}, u32[]{:S(2)}) collective-permute-start(bf16[16,1024]{1,0:T(8,128)(2,1)S(1)} %get-tuple-element.26), channel_id=1, source_target_pairs={{128,0},{129,1},{130,2},{131,3},{132,4},{133,5},{134,6},{135,7},{1... | collective-permute-start | bytes 98312 | tf_op jit(solution)/shard_map/ppermute | solution.py:61
  21.6 5.3 %collective-permute-start.7 = (bf16[32,4096]{1,0:T(8,128)(2,1)S(1)}, bf16[32,4096]{1,0:T(8,128)(2,1)S(1)}, u32[]{:S(2)}, u32[]{:S(2)}) collective-permute-start(bf16[32,4096]{1,0:T(8,128)(2,1)S(1)} %slice.24), channel_id=1, source_target_pairs={{8,0},{3,1},{10,2},{5,3},{12,4},{7,5},{14,6},{129,7},{16,8},{11,9}... | collective-permute-start | bytes 786440 | tf_op jit(solution)/shard_map/ppermute | solution.py:61
  22.1 6.8 %collective-permute-start.8 = (bf16[32,4096]{1,0:T(8,128)(2,1)S(1)}, bf16[32,4096]{1,0:T(8,128)(2,1)S(1)}, u32[]{:S(2)}, u32[]{:S(2)}) collective-permute-start(bf16[32,4096]{1,0:T(8,128)(2,1)S(1)} %slice.25), channel_id=1, source_target_pairs={{24,0},{135,1},{26,2},{1,3},{28,4},{3,5},{30,6},{5,7},{0,8},{143,9... | collective-permute-start | bytes 786440 | tf_op jit(solution)/shard_map/ppermute | solution.py:61
  30.7 6.4 %collective-permute-start.6 = (bf16[16,1024]{1,0:T(8,128)(2,1)S(1)}, bf16[16,1024]{1,0:T(8,128)(2,1)S(1)}, u32[]{:S(2)}, u32[]{:S(2)}) collective-permute-start(bf16[16,1024]{1,0:T(8,128)(2,1)S(1)} %add_convert_fusion), channel_id=1, source_target_pairs={{64,0},{65,1},{66,2},{67,3},{68,4},{69,5},{70,6},{71,7},{72,8},{73... | collective-permute-start | bytes 98312 | tf_op jit(solution)/shard_map/ppermute | solution.py:61
  34.4 19.0 %collective-permute-start.13 = (bf16[128,4096]{1,0:T(8,128)(2,1)S(1)}, bf16[128,4096]{1,0:T(8,128)(2,1)}, u32[]{:S(2)}, u32[]{:S(2)}) collective-permute-start(bf16[128,4096]{1,0:T(8,128)(2,1)S(1)} %pad_maximum_fusion.refs_6_), channel_id=1, source_target_pairs={{2,0},{9,1},{4,2},{11,3},{6,4},{13,5},{128,6},{15,7},{10,8},{17,9}... | collective-permute-start | bytes 3145736 | tf_op jit(solution)/shard_map/ppermute | solution.py:61
  37.1 16.2 %collective-permute-start.14 = (bf16[128,4096]{1,0:T(8,128)(2,1)S(1)}, bf16[128,4096]{1,0:T(8,128)(2,1)S(1)}, u32[]{:S(2)}, u32[]{:S(2)}) collective-permute-start(bf16[128,4096]{1,0:T(8,128)(2,1)S(1)} %pad_maximum_fusion.refs_6_), channel_id=1, source_target_pairs={{134,0},{25,1},{0,2},{27,3},{2,4},{29,5},{4,6},{31,7},{142,8},{1,9... | collective-permute-start | bytes 3145736 | tf_op jit(solution)/shard_map/ppermute | solution.py:61
  37.1 3.5 %collective-permute-start.9 = (bf16[16,1024]{1,0:T(8,128)(2,1)S(1)}, bf16[16,1024]{1,0:T(8,128)(2,1)S(1)}, u32[]{:S(2)}, u32[]{:S(2)}) collective-permute-start(bf16[16,1024]{1,0:T(8,128)(2,1)S(1)} %get-tuple-element.29), channel_id=1, source_target_pairs={{8,0},{3,1},{10,2},{5,3},{12,4},{7,5},{14,6},{129,7},{16,8},{11,9}... | collective-permute-start | bytes 98312 | tf_op jit(solution)/shard_map/ppermute | solution.py:61
  38.5 4.4 %collective-permute-start.10 = (bf16[16,1024]{1,0:T(8,128)(2,1)S(1)}, bf16[16,1024]{1,0:T(8,128)(2,1)S(1)}, u32[]{:S(2)}, u32[]{:S(2)}) collective-permute-start(bf16[16,1024]{1,0:T(8,128)(2,1)S(1)} %get-tuple-element.29), channel_id=1, source_target_pairs={{16,0},{5,1},{18,2},{135,3},{20,4},{129,5},{22,6},{3,7},{24,8},{13... | collective-permute-start | bytes 98312 | tf_op jit(solution)/shard_map/ppermute | solution.py:61
  38.5 4.7 %collective-permute-start.11 = (bf16[16,1024]{1,0:T(8,128)(2,1)S(1)}, bf16[16,1024]{1,0:T(8,128)(2,1)S(1)}, u32[]{:S(2)}, u32[]{:S(2)}) collective-permute-start(bf16[16,1024]{1,0:T(8,128)(2,1)S(1)} %get-tuple-element.29), channel_id=1, source_target_pairs={{24,0},{135,1},{26,2},{1,3},{28,4},{3,5},{30,6},{5,7},{0,8},{143,9... | collective-permute-start | bytes 98312 | tf_op jit(solution)/shard_map/ppermute | solution.py:61
  43.3 23.8 %collective-permute-start.18 = (bf16[128,4096]{1,0:T(8,128)(2,1)}, bf16[128,4096]{1,0:T(8,128)(2,1)}, u32[]{:S(2)}, u32[]{:S(2)}) collective-permute-start(bf16[128,4096]{1,0:T(8,128)(2,1)} %constant_dynamic-update-slice_fusion.refs_7_), channel_id=1, source_target_pairs={{134,0},{25,1},{0,2},{27,3},{2,4},{29,5},{4,6},{31,7},{142,8},{1,9... | collective-permute-start | bytes 3145736 | tf_op jit(solution)/shard_map/ppermute | solution.py:61
  43.8 37.7 %collective-permute-start.19 = (bf16[128,4096]{1,0:T(8,128)(2,1)}, bf16[128,4096]{1,0:T(8,128)(2,1)}, u32[]{:S(2)}, u32[]{:S(2)}) collective-permute-start(bf16[128,4096]{1,0:T(8,128)(2,1)} %constant_dynamic-update-slice_fusion.refs_7_), channel_id=1, source_target_pairs={{2,0},{9,1},{4,2},{11,3},{6,4},{13,5},{128,6},{15,7},{10,8},{17,9}... | collective-permute-start | bytes 3145736 | tf_op jit(solution)/shard_map/ppermute | solution.py:61
  45.9 7.4 %collective-permute-start.12 = (bf16[64,1024]{1,0:T(8,128)(2,1)S(1)}, bf16[64,1024]{1,0:T(8,128)(2,1)S(1)}, u32[]{:S(2)}, u32[]{:S(2)}) collective-permute-start(bf16[64,1024]{1,0:T(8,128)(2,1)S(1)} %constant_dynamic-update-slice_fusion.3), channel_id=1, source_target_pairs={{1,0},{0,1},{3,2},{2,3},{5,4},{4,5},{7,6},{6,7},{9,8},{8,9},{11,10... | collective-permute-start | bytes 393224 | tf_op jit(solution)/shard_map/ppermute | solution.py:61
  53.4 13.8 %collective-permute-start.17 = (bf16[64,1024]{1,0:T(8,128)(2,1)S(1)}, bf16[64,1024]{1,0:T(8,128)(2,1)S(1)}, u32[]{:S(2)}, u32[]{:S(2)}) collective-permute-start(bf16[64,1024]{1,0:T(8,128)(2,1)S(1)} %collective-permute-done.12), channel_id=1, source_target_pairs={{24,0},{135,1},{26,2},{1,3},{28,4},{3,5},{30,6},{5,7},{0,8},{143,9... | collective-permute-start | bytes 393224 | tf_op jit(solution)/shard_map/ppermute | solution.py:61
  53.5 13.7 %collective-permute-start.16 = (bf16[64,1024]{1,0:T(8,128)(2,1)S(1)}, bf16[64,1024]{1,0:T(8,128)(2,1)S(1)}, u32[]{:S(2)}, u32[]{:S(2)}) collective-permute-start(bf16[64,1024]{1,0:T(8,128)(2,1)S(1)} %collective-permute-done.12), channel_id=1, source_target_pairs={{16,0},{5,1},{18,2},{135,3},{20,4},{129,5},{22,6},{3,7},{24,8},{13... | collective-permute-start | bytes 393224 | tf_op jit(solution)/shard_map/ppermute | solution.py:61
  56.3 10.8 %collective-permute-start.15 = (bf16[64,1024]{1,0:T(8,128)(2,1)S(1)}, bf16[64,1024]{1,0:T(8,128)(2,1)S(1)}, u32[]{:S(2)}, u32[]{:S(2)}) collective-permute-start(bf16[64,1024]{1,0:T(8,128)(2,1)S(1)} %collective-permute-done.12), channel_id=1, source_target_pairs={{8,0},{3,1},{10,2},{5,3},{12,4},{7,5},{14,6},{129,7},{16,8},{11,9}... | collective-permute-start | bytes 393224 | tf_op jit(solution)/shard_map/ppermute | solution.py:61
  67.1 24.2 %collective-permute-start.21 = (bf16[128,4096]{1,0:T(8,128)(2,1)}, bf16[128,4096]{1,0:T(8,128)(2,1)}, u32[]{:S(2)}, u32[]{:S(2)}) collective-permute-start(bf16[128,4096]{1,0:T(8,128)(2,1)} %collective-permute-done.18.refs_9_), channel_id=1, source_target_pairs={{134,0},{25,1},{0,2},{27,3},{2,4},{29,5},{4,6},{31,7},{142,8},{1,9... | collective-permute-start | bytes 3145736 | tf_op jit(solution)/shard_map/ppermute | solution.py:61
  67.2 24.1 %collective-permute-start.20 = (bf16[128,4096]{1,0:T(8,128)(2,1)}, bf16[128,4096]{1,0:T(8,128)(2,1)}, u32[]{:S(2)}, u32[]{:S(2)}) collective-permute-start(bf16[128,4096]{1,0:T(8,128)(2,1)} %collective-permute-done.13.refs_10_), channel_id=1, source_target_pairs={{2,0},{9,1},{4,2},{11,3},{6,4},{13,5},{128,6},{15,7},{10,8},{17,9}... | collective-permute-start | bytes 3145736 | tf_op jit(solution)/shard_map/ppermute | solution.py:61
  78.9 16.6 %collective-permute-start.22 = (bf16[512,256]{1,0:T(8,128)(2,1)S(1)}, bf16[512,256]{1,0:T(8,128)(2,1)S(1)}, u32[]{:S(2)}, u32[]{:S(2)}) collective-permute-start(bf16[512,256]{1,0:T(8,128)(2,1)S(1)} %get-tuple-element.41), channel_id=1, source_target_pairs={{1,0},{0,1},{3,2},{2,3},{5,4},{4,5},{7,6},{6,7},{9,8},{8,9},{11,10... | collective-permute-start | bytes 786440 | tf_op jit(solution)/shard_map/ppermute | solution.py:61
  90.7 4.9 %collective-permute-start.23 = (bf16[512,256]{1,0:T(8,128)(2,1)S(1)}, bf16[512,256]{1,0:T(8,128)(2,1)S(1)}, u32[]{:S(2)}, u32[]{:S(2)}) collective-permute-start(bf16[512,256]{1,0:T(8,128)(2,1)S(1)} %get-tuple-element.42), channel_id=1, source_target_pairs={{1,0},{0,1},{3,2},{2,3},{5,4},{4,5},{7,6},{6,7},{9,8},{8,9},{11,10... | collective-permute-start | bytes 786440 | tf_op jit(solution)/shard_map/ppermute | solution.py:61
  90.8 4.7 %collective-permute-start.25 = (bf16[512,256]{1,0:T(8,128)(2,1)S(1)}, bf16[512,256]{1,0:T(8,128)(2,1)S(1)}, u32[]{:S(2)}, u32[]{:S(2)}) collective-permute-start(bf16[512,256]{1,0:T(8,128)(2,1)S(1)} %get-tuple-element.44), channel_id=1, source_target_pairs={{1,0},{0,1},{3,2},{2,3},{5,4},{4,5},{7,6},{6,7},{9,8},{8,9},{11,10... | collective-permute-start | bytes 786440 | tf_op jit(solution)/shard_map/ppermute | solution.py:61
  (12 other events, 207.8 us)

commit v9 on v3

--- a/solution.py
+++ b/solution.py
@@ -109,22 +109,6 @@
         compiler_params=pltpu.CompilerParams(vmem_limit_bytes=limit << 20),
         cost_estimate=pl.CostEstimate(flops=flops, bytes_accessed=moved, transcendentals=0),
     )(*inputs)
-
-
-def stay_kernel(source, out, sem):
-    copy = pltpu.make_async_copy(source, out, sem)
-    copy.start()
-    copy.wait()
-
-
-def stay(value):
-    return call(
-        stay_kernel,
-        pltpu.VMEM(value.shape, value.dtype),
-        (),
-        (pltpu.SemaphoreType.DMA,),
-        kept=(value,),
-    )
 
 
 def stacked(value, wide):
@@ -184,74 +168,64 @@
     return update * lax.rsqrt(update * update + soft_width)
 
 
-def direction_kernel(total, back_rows3, back_hi, back_lo, out):
+def update_kernel(total, weight, back_rows3, back_hi, back_lo, direction, new_weight):
     sign = soft_sign(restored(total[...], back_rows3, back_hi, back_lo))
     wide = WIDE * TILE
-    for k in range(out.shape[1] // wide):
-        out[:, k * wide : (k + 1) * wide] = sign[k * TILE : (k + 1) * TILE]
-
-
-def forward_kernel(parts, first, back_rows, back_cols, *refs):
-    groups = len(parts)
+    for k in range(direction.shape[1] // wide):
+        cut = slice(k * wide, (k + 1) * wide)
+        part = sign[k * TILE : (k + 1) * TILE]
+        direction[:, cut] = part
+        new_weight[:, cut] = (weight[:, cut].astype(F32) - step_rate * part).astype(BF16)
+
+
+def forward_kernel(pieces, load, first, *refs):
+    groups = len(pieces)
     refs = list(refs)
-    bands = [refs.pop(0) for _ in range(groups)]
-    tokens = [refs.pop(0) for _ in range(2)]
-    weights = [[refs.pop(0) for _ in range(n)] for n in parts]
+    sources = [refs.pop(0) for _ in range(2)]
+    weights = [refs.pop(0) for _ in range(1 + max(n for group in pieces for n, _ in group))]
     outs = [refs.pop(0) for _ in range(2 * groups)]
-    raw, *fresh, raw_sem = refs
-    wide = WIDE * TILE
-    rows, width = fresh[0].shape
+    tokens = [refs.pop(0) for _ in range(2)] if load else sources
+    fresh = [refs.pop(0) for _ in range(groups)]
+    sems, token_sems = refs
+    rows = fresh[0].shape[0]
     per = tokens[0].shape[0] // rows
-    start = first[0]
-
-    pieces = []
-    for g in range(groups):
-        found = []
-        for ref in weights[g]:
-            found += [(ref, r) for r in range(0, ref.shape[0], TILE)]
-        pieces.append(found)
-    raw_copy = {}
-    for g in range(groups):
-        for f, (ref, r) in enumerate(pieces[g]):
-            raw_copy[g, f] = pltpu.make_async_copy(ref.at[r : r + TILE], raw.at[g, f], raw_sem.at[g, f])
+    copies = []
+    for g, group in enumerate(pieces):
+        for f, (n, row) in enumerate(group):
+            at = pl.ds(pl.multiple_of(lax.rem(first[0] + f, 4) * TILE, TILE), TILE)
+            copies.append(
+                pltpu.make_async_copy(weights[n].at[pl.ds(row, TILE)], fresh[g].at[at], sems.at[g, f])
+            )
+    token_copies = []
+    if load:
+        for t in range(2 * per):
+            cut = pl.ds(t % per * rows, rows)
+            token_copies.append(
+                pltpu.make_async_copy(sources[t // per].at[cut], tokens[t // per].at[cut], token_sems.at[t])
+            )
+    for copy in copies[:4] + token_copies + copies[4:]:
+        copy.start()
     for g in range(groups):
         for f in range(4):
-            raw_copy[g, f].start()
-
-    def renew(g, f):
-        tall = dot(back_rows[...], bands[g][f * BAND : (f + 1) * BAND]).astype(BF16)
-        sign = soft_sign(dot(stacked(tall, WIDE * BAND), back_cols[...]))
-        at = pl.ds(pl.multiple_of(lax.rem(start + f, 4) * TILE, TILE), TILE)
-        for k in range(width // wide):
-            cut = slice(k * wide, (k + 1) * wide)
-            new = raw[g, f, :, cut].astype(F32) - step_rate * sign[k * TILE : (k + 1) * TILE]
-            fresh[g % 2][at, cut] = new.astype(BF16)
-
-    for f in range(4):
-        raw_copy[0, f].wait()
-        renew(0, f)
-    for g in range(groups):
-        if g + 1 < groups:
-            for f in range(4):
-                raw_copy[g + 1, f].wait()
-        for t in range(4):
+            copies[4 * g + f].wait()
+        for t in range(2 * per):
+            if g == 0 and load:
+                token_copies[t].wait()
             cut = slice(t % per * rows, (t % per + 1) * rows)
-            product = lax.dot_general(tokens[t // per][cut], fresh[g % 2][...], NT, preferred_element_type=F32)
+            product = lax.dot_general(tokens[t // per][cut], fresh[g][...], NT, preferred_element_type=F32)
             outs[2 * g + t // per][cut] = product.astype(BF16)
-            if g + 1 < groups:
-                renew(g + 1, t)
 
 
 def weave_kernel(where, *refs):
     mine, theirs, out, held = refs[:4], refs[4:8], refs[8], refs[9]
     core, my_start, their_start = where[0], where[1], where[2]
     for g in range(4):
-        held[1 - core, lax.rem(my_start + g, 4)] = mine[g][...]
-        held[core, lax.rem(their_start + g, 4)] = theirs[g][...]
+        held[core, lax.rem(my_start + g, 4)] = mine[g][...]
+        held[1 - core, lax.rem(their_start + g, 4)] = theirs[g][...]
     for y in range(4):
         for z in range(4):
-            left = held[0, y, :, z * TILE : (z + 1) * TILE]
-            right = held[1, z, :, y * TILE : (y + 1) * TILE]
+            left = held[0, z, :, y * TILE : (y + 1) * TILE]
+            right = held[1, y, :, z * TILE : (z + 1) * TILE]
             j = (y * 4 + z) * 2 * TILE
             out[:, j : j + 2 * TILE] = jnp.concatenate([left, right], axis=1)
 
@@ -295,75 +269,73 @@
     def after(value, *others):
         return lax.optimization_barrier((value, *others))[0]
 
-    swapped = fetch(weight, sibling)
-    other = fetch(after(activations, swapped), sibling)
-    swapped = after(swapped, rounded)
-    ahead, behind, across = (fetch(swapped, along(0, s)) for s in (1, -1, 2))
-
-    def join(value, source):
-        return value.astype(F32) + fetch(value, source).astype(F32)
-
-    sent = join(rounded, far_z).astype(BF16)
-    total = join(join(sent, pair_x).astype(BF16), along_x(2))
-    own = stay(after(activations, sent))
-    other = stay(other)
-
+    other = fetch(after(activations, rounded), sibling)
+
+    parts = [rounded.astype(F32)] + [fetch(rounded, along_x(n)).astype(F32) for n in (1, 2, -1)]
+    sent = ((parts[0] + parts[2]) + (parts[1] + parts[3])).astype(BF16)
     new_momentum = call(
         residual_kernel,
         shape(momentum.shape, F32),
         (momentum, gradient, exact, back_rows3, back_hi, back_lo),
     )
-
-    def gather(value):
-        pair = jnp.concatenate([value, fetch(value, along(0, 1))], axis=0)
-        return pair, fetch(pair, along(0, 2))
-
-    band_line = jnp.concatenate(gather(total.astype(BF16)), axis=0)
-    near, far = gather(fetch(band_line, sibling))
-    blocks = jnp.concatenate([near, far], axis=0).reshape(4, 4, BAND, narrow)
-    bands = [blocks[:, g].reshape(4 * BAND, narrow) for g in range(4)]
-
-    early = after(jnp.concatenate([swapped, ahead], axis=0), sent)
-    late = after(jnp.concatenate([across, behind], axis=0), new_momentum)
-    next_early, last_early = fetch(early, along(1, 1)), fetch(early, along(1, -1))
-    next_late, last_late = fetch(late, along(1, 1)), fetch(late, along(1, -1))
-    far_early, far_late = fetch(next_early, along(1, 1)), fetch(last_late, along(1, -1))
-    lines = [[early, late], [next_early, next_late], [far_early, far_late], [last_early, last_late]]
-
-    direction = call(
-        direction_kernel,
-        shape((rows, width), F32),
-        (total, back_rows3, back_hi, back_lo),
-    )
-
-    def forward(order):
-        parts = [len(lines[g]) for g in order]
-        inputs = [first[None], back_rows, back_hi] + [bands[g] for g in order]
-        kept = [line for g in order for line in lines[g]]
-        block = shape((tokens, 4 * rows), BF16)
+    total = sent.astype(F32) + fetch(sent, far_z).astype(F32)
+    direction, own = call(
+        update_kernel,
+        (shape((rows, width), F32), shape((rows, width), BF16)),
+        (after(total, new_momentum, other), weight, back_rows3, back_hi, back_lo),
+    )
+
+    ahead, behind = (fetch(own, along(0, n)) for n in (1, -1))
+    next_own, last_own = (fetch(own, along(1, n)) for n in (1, -1))
+    across = fetch(ahead, along(0, 1))
+    pair = jnp.concatenate([ahead, behind], axis=0)
+    next_pair, last_pair = (fetch(pair, along(1, n)) for n in (1, -1))
+    next_across, last_across = (fetch(across, along(1, n)) for n in (1, -1))
+    far_pair = fetch(next_pair, along(1, 1))
+    far_rest = fetch(jnp.concatenate([last_own, last_across], axis=0), along(1, -1))
+    lines = [
+        [(own, 0), (ahead, 0), (across, 0), (behind, 0)],
+        [(next_own, 0), (next_pair, 0), (next_across, 0), (next_pair, TILE)],
+        [(far_rest, 0), (far_pair, 0), (far_rest, TILE), (far_pair, TILE)],
+        [(last_own, 0), (last_pair, 0), (last_across, 0), (last_pair, TILE)],
+    ]
+
+    block = shape((tokens, 4 * rows), BF16)
+
+    def forward(order, load):
+        used, pieces = [], []
+        for g in order:
+            pieces.append([])
+            for value, row in lines[g]:
+                found = [n for n, v in enumerate(used) if v is value]
+                if not found:
+                    used.append(value)
+                pieces[-1].append((found[0] if found else len(used) - 1, row))
+        count = len(order)
+        held = pltpu.VMEM(activations.shape, BF16)
         return call(
-            lambda *refs: forward_kernel(parts, *refs),
-            tuple([block] * (2 * len(order))),
-            inputs,
+            lambda *refs: forward_kernel(pieces, load, *refs),
+            (*[block] * (2 * count), *([held] * 2 if load else [])),
+            [first[None]],
             (
-                pltpu.VMEM((len(order), 4, rows, width), BF16),
-                pltpu.VMEM((4 * rows, width), BF16),
-                pltpu.VMEM((4 * rows, width), BF16),
-                pltpu.SemaphoreType.DMA((len(order), 4)),
+                *[pltpu.VMEM((4 * rows, width), BF16)] * count,
+                pltpu.SemaphoreType.DMA((count, 4)),
+                pltpu.SemaphoreType.DMA((4,)),
             ),
             limit=24,
-            flops=len(order) * 2 * 2 * tokens * 4 * rows * width,
+            flops=count * 2 * 2 * tokens * 4 * rows * width,
             smem=1,
-            kept=kept,
-            resident=(own, other),
+            resident=() if load else (activations_in, other_in),
+            kept=([activations, other] if load else []) + used,
         )
 
+    *results, activations_in, other_in = forward([0], True)
+    results += forward([3, 1], False)
+    results += forward([2], False)
     mine, theirs = [None] * 4, [None] * 4
-    for order in ([0], [1, 3], [2]):
-        result = forward(order)
-        for n, g in enumerate(order):
-            mine[g] = result[2 * n]
-            theirs[g] = fetch(result[2 * n + 1], sibling)
+    for n, g in enumerate((0, 3, 1, 2)):
+        mine[g] = results[2 * n]
+        theirs[g] = fetch(results[2 * n + 1], sibling)
     where = jnp.stack([core.astype(jnp.int32), second, first])
     projected = call(
         weave_kernel,

time: 107 us -> 110 us (1.028)
  waiting for transfers between devices: 26.5 us -> 35 us
  starting transfers between devices: 45.3 us -> 37.3 us
  local copies, waits for them, and re-layouts: 0.08 us -> 6.55 us
  Pallas kernels: 33 us -> 28.6 us
    ppermute x23 -> x20, waiting for transfers between devices: 26.5 us -> 35 us  [fetch(): lax.ppermute(value, AXES, [(place(*source(*spot(i))), i) for i in range(2...]
    ppermute x23 -> x20, starting transfers between devices: 45.3 us -> 37.3 us  [fetch(): lax.ppermute(value, AXES, [(place(*source(*spot(i))), i) for i in range(2...]
    unnamed x14 -> x27, local copies, waits for them, and re-layouts: 0.04 us -> 5.65 us
    pallas_call x9 -> x7, Pallas kernels: 33 us -> 28.6 us  [call(): pl.pallas_call(kernel, out_shape=out_shape, in_specs=specs, out_specs=jax...]
  transfers between devices with their start and end apart: 23 -> 20, of which waited for: 9 -> 9; matrix products, arithmetic and copies ran while one was open for 1% -> 3% of each run, Pallas kernels for 28% -> 19%
where the time goes in v9:
time: 110 us
  starting transfers between devices  37.3 us (34%)
  waiting for transfers between devices  35 us (32%)
  Pallas kernels  28.6 us (26%)
  local copies, waits for them, and re-layouts  6.55 us (6%)
  other arithmetic  1.33 us (1%)
    ppermute x20, starting transfers between devices, fetch(): lax.ppermute(value, AXES, [(place(*source(*spot(i))), i) for i in range(2...  37.3 us
    ppermute x20, waiting for transfers between devices, fetch(): lax.ppermute(value, AXES, [(place(*source(*spot(i))), i) for i in range(2...  35 us
    pallas_call x7, Pallas kernels, call(): pl.pallas_call(kernel, out_shape=out_shape, in_specs=specs, out_specs=jax...  28.6 us
    unnamed x27, local copies, waits for them, and re-layouts  5.65 us
  transfers between devices with their start and end apart: 20, of which 9 were waited for; matrix products, arithmetic and copies ran while one was open for 3% of the time, Pallas kernels for 19%

profile of v9, /device:TPU:1, one launch (start us, length us, event | category | flops | bytes accessed | tf_op | source)
XLA Modules:
  0.0 109.6 jit_solution(6589298922704481311)
XLA Ops:
  0.6 3.1 %shard_map.112 = (f32[16,1024]{1,0:T(8,128)S(1)}, bf16[16,1024]{1,0:T(8,128)(2,1)S(1)}) custom-call(f32[1,64,4096]{2,1,0:T(8,128)} %momentum.3, bf16[1,64,4096]{2,1,0:T(8,128)(2,1)} %gradient.3, bf16[1024,128]{1,0:T(8,128)(2,1)} %constant.59.clone.cols, bf16[16,192]{1,0:T(8,128)(2,1)} %constant.60.clone.rows3), custom_call_target="tpu_custom_call" | custom-call | bytes 1841152 | tf_op jit(solution)/shard_map/pallas_call | solution.py:99
  3.8 3.3 %collective-permute-start.4 = (bf16[512,4096]{1,0:T(8,128)(2,1)}, bf16[512,4096]{1,0:T(8,128)(2,1)S(1)}, u32[]{:S(2)}, u32[]{:S(2)}) collective-permute-start(bf16[512,4096]{1,0:T(8,128)(2,1)} %refs_1_.1), channel_id=1, source_target_pairs={{1,0},{0,1},{3,2},{2,3},{5,4},{4,5},{7,6},{6,7},{9,8},{8,9},{11,10... | collective-permute-start | bytes 12582920 | tf_op jit(solution)/shard_map/ppermute | solution.py:61
  7.1 2.7 %collective-permute-start.1 = (bf16[16,1024]{1,0:T(8,128)(2,1)S(1)}, bf16[16,1024]{1,0:T(8,128)(2,1)S(1)}, u32[]{:S(2)}, u32[]{:S(2)}) collective-permute-start(bf16[16,1024]{1,0:T(8,128)(2,1)S(1)} %get-tuple-element.20), channel_id=1, source_target_pairs={{32,0},{33,1},{34,2},{35,3},{36,4},{37,5},{38,6},{39,7},{40,8},{41... | collective-permute-start | bytes 98312 | tf_op jit(solution)/shard_map/ppermute | solution.py:61
  9.8 1.3 %collective-permute-done.2 = bf16[16,1024]{1,0:T(8,128)(2,1)S(1)} collective-permute-done((bf16[16,1024]{1,0:T(8,128)(2,1)S(1)}, bf16[16,1024]{1,0:T(8,128)(2,1)S(1)}, u32[]{:S(2)}, u32[]{:S(2)}) %collective-permute-start.2) | collective-permute-done | bytes 32800 | tf_op jit(solution)/shard_map/ppermute | solution.py:61
  11.1 3.0 %collective-permute-done = bf16[16,1024]{1,0:T(8,128)(2,1)S(1)} collective-permute-done((bf16[16,1024]{1,0:T(8,128)(2,1)S(1)}, bf16[16,1024]{1,0:T(8,128)(2,1)S(1)}, u32[]{:S(2)}, u32[]{:S(2)}) %collective-permute-start) | collective-permute-done | bytes 32800 | tf_op jit(solution)/shard_map/ppermute | solution.py:61
  14.1 5.3 %collective-permute-start.3 = (bf16[16,1024]{1,0:T(8,128)(2,1)S(1)}, bf16[16,1024]{1,0:T(8,128)(2,1)S(1)}, u32[]{:S(2)}, u32[]{:S(2)}) collective-permute-start(bf16[16,1024]{1,0:T(8,128)(2,1)S(1)} %add_convert_fusion), channel_id=1, source_target_pairs={{128,0},{129,1},{130,2},{131,3},{132,4},{133,5},{134,6},{135,7},{1... | collective-permute-start | bytes 98312 | tf_op jit(solution)/shard_map/ppermute | solution.py:61
  24.1 1.7 %shard_map.113 = f32[1,64,4096]{2,1,0:T(8,128)} custom-call(f32[1,64,4096]{2,1,0:T(8,128)S(1)} %copy-done, bf16[1,64,4096]{2,1,0:T(8,128)(2,1)S(1)} %copy-done.1, f32[16,1024]{1,0:T(8,128)S(1)} %get-tuple-element.19.bands, bf16[64,48]{1,0:T(8,128)(2,1)S(1)} %copy-done.6, bf16[128,512]{1,0:T(8,128)(2,1)S(1)} %copy-done.3, bf16[128,512]{1,0:T(8,128)(2,1)S(1)} %copy-done.4), custom_call_target="tpu_custom_call" | custom-call | bytes 1906688 | tf_op jit(solution)/shard_map/pallas_call | solution.py:99
  25.8 2.2 %shard_map.114 = (f32[64,4096]{1,0:T(8,128)}, bf16[64,4096]{1,0:T(8,128)(2,1)S(1)}) custom-call(f32[16,1024]{1,0:T(8,128)S(1)} %convert_add_fusion.total, bf16[64,4096]{1,0:T(8,128)(2,1)S(1)} %copy-done.2, bf16[64,48]{1,0:T(8,128)(2,1)S(1)} %copy-done.6, bf16[128,512]{1,0:T(8,128)(2,1)S(1)} %copy-done.3, bf16[128,512]{1,0:T(8,128)(2,1)S(1)} %copy-done.4), custom_call_target="tpu_custom_call" | custom-call | bytes 858112 | tf_op jit(solution)/shard_map/pallas_call | solution.py:99
  28.1 1.5 %collective-permute-start.7 = (bf16[64,4096]{1,0:T(8,128)(2,1)S(1)}, bf16[64,4096]{1,0:T(8,128)(2,1)S(1)}, u32[]{:S(2)}, u32[]{:S(2)}) collective-permute-start(bf16[64,4096]{1,0:T(8,128)(2,1)S(1)} %get-tuple-element.24.refs_3_), channel_id=1, source_target_pairs={{24,0},{135,1},{26,2},{1,3},{28,4},{3,5},{30,6},{5,7},{0,8},{143,9... | collective-permute-start | bytes 1572872 | tf_op jit(solution)/shard_map/ppermute | solution.py:61
  29.5 6.9 %collective-permute-done.5.refs_4_ = bf16[64,4096]{1,0:T(8,128)(2,1)S(1)} collective-permute-done((bf16[64,4096]{1,0:T(8,128)(2,1)S(1)}, bf16[64,4096]{1,0:T(8,128)(2,1)S(1)}, u32[]{:S(2)}, u32[]{:S(2)}) %collective-permute-start.5) | collective-permute-done | bytes 524320 | tf_op jit(solution)/shard_map/ppermute | solution.py:61
  39.3 2.7 %collective-permute-start.12 = (bf16[128,4096]{1,0:T(8,128)(2,1)}, bf16[128,4096]{1,0:T(8,128)(2,1)}, u32[]{:S(2)}, u32[]{:S(2)}) collective-permute-start(bf16[128,4096]{1,0:T(8,128)(2,1)} %constant_dynamic-update-slice_fusion), channel_id=1, source_target_pairs={{2,0},{9,1},{4,2},{11,3},{6,4},{13,5},{128,6},{15,7},{10,8},{17,9}... | collective-permute-start | bytes 3145736 | tf_op jit(solution)/shard_map/ppermute | solution.py:61
  42.1 2.6 %collective-permute-done.6.refs_5_ = bf16[64,4096]{1,0:T(8,128)(2,1)S(1)} collective-permute-done((bf16[64,4096]{1,0:T(8,128)(2,1)S(1)}, bf16[64,4096]{1,0:T(8,128)(2,1)S(1)}, u32[]{:S(2)}, u32[]{:S(2)}) %collective-permute-start.6) | collective-permute-done | bytes 524320 | tf_op jit(solution)/shard_map/ppermute | solution.py:61
  44.7 1.3 %collective-permute-start.10 = (bf16[64,4096]{1,0:T(8,128)(2,1)S(1)}, bf16[64,4096]{1,0:T(8,128)(2,1)S(1)}, u32[]{:S(2)}, u32[]{:S(2)}) collective-permute-start(bf16[64,4096]{1,0:T(8,128)(2,1)S(1)} %collective-permute-done.6.refs_5_), channel_id=1, source_target_pairs={{134,0},{25,1},{0,2},{27,3},{2,4},{29,5},{4,6},{31,7},{142,8},{1,9... | collective-permute-start | bytes 1572872 | tf_op jit(solution)/shard_map/ppermute | solution.py:61
  47.3 4.3 %collective-permute-done.8.refs_3_ = bf16[64,4096]{1,0:T(8,128)(2,1)S(1)} collective-permute-done((bf16[64,4096]{1,0:T(8,128)(2,1)S(1)}, bf16[64,4096]{1,0:T(8,128)(2,1)S(1)}, u32[]{:S(2)}, u32[]{:S(2)}) %collective-permute-start.8) | collective-permute-done | bytes 524320 | tf_op jit(solution)/shard_map/ppermute | solution.py:61
  51.6 5.3 %collective-permute-done.10.refs_5_ = bf16[64,4096]{1,0:T(8,128)(2,1)S(1)} collective-permute-done((bf16[64,4096]{1,0:T(8,128)(2,1)S(1)}, bf16[64,4096]{1,0:T(8,128)(2,1)S(1)}, u32[]{:S(2)}, u32[]{:S(2)}) %collective-permute-start.10) | collective-permute-done | bytes 524320 | tf_op jit(solution)/shard_map/ppermute | solution.py:61
  58.1 1.6 %collective-permute-done.12.refs_7_ = bf16[128,4096]{1,0:T(8,128)(2,1)} collective-permute-done((bf16[128,4096]{1,0:T(8,128)(2,1)}, bf16[128,4096]{1,0:T(8,128)(2,1)}, u32[]{:S(2)}, u32[]{:S(2)}) %collective-permute-start.12) | collective-permute-done | bytes 1048608 | tf_op jit(solution)/shard_map/ppermute | solution.py:61
  59.7 3.1 %collective-permute-start.15 = (bf16[128,4096]{1,0:T(8,128)(2,1)}, bf16[128,4096]{1,0:T(8,128)(2,1)}, u32[]{:S(2)}, u32[]{:S(2)}) collective-permute-start(bf16[128,4096]{1,0:T(8,128)(2,1)} %collective-permute-done.12.refs_7_), channel_id=1, source_target_pairs={{2,0},{9,1},{4,2},{11,3},{6,4},{13,5},{128,6},{15,7},{10,8},{17,9}... | collective-permute-start | bytes 3145736 | tf_op jit(solution)/shard_map/ppermute | solution.py:61
  63.0 8.5 %shard_map.115 = (bf16[512,256]{1,0:T(8,128)(2,1)S(1)}, bf16[512,256]{1,0:T(8,128)(2,1)S(1)}, bf16[512,4096]{1,0:T(8,128)(2,1)S(1)}, bf16[512,4096]{1,0:T(8,128)(2,1)S(1)}) custom-call(s32[1]{0:T(128)} %bitcast.2.refs_0_, bf16[512,4096]{1,0:T(8,128)(2,1)} %refs_1_.1, bf16[512,4096]{1,0:T(8,128)(2,1)} %copy-done.7, bf16[64,4096]{1,0:T(8,128)(2,1)} %copy-done.5, ...), custom_call_target="tpu_custom_call" | custom-call | flops 2147483648 | bytes 10485764 | tf_op jit(solution)/shard_map/pallas_call | solution.py:99
  71.5 8.9 %collective-permute-done.11.refs_6_ = bf16[64,4096]{1,0:T(8,128)(2,1)} collective-permute-done((bf16[64,4096]{1,0:T(8,128)(2,1)S(1)}, bf16[64,4096]{1,0:T(8,128)(2,1)}, u32[]{:S(2)}, u32[]{:S(2)}) %collective-permute-start.11) | collective-permute-done | bytes 524320 | tf_op jit(solution)/shard_map/ppermute | solution.py:61
  80.4 8.5 %collective-permute-start.16 = (bf16[512,256]{1,0:T(8,128)(2,1)S(1)}, bf16[512,256]{1,0:T(8,128)(2,1)S(1)}, u32[]{:S(2)}, u32[]{:S(2)}) collective-permute-start(bf16[512,256]{1,0:T(8,128)(2,1)S(1)} %get-tuple-element.31), channel_id=1, source_target_pairs={{1,0},{0,1},{3,2},{2,3},{5,4},{4,5},{7,6},{6,7},{9,8},{8,9},{11,10... | collective-permute-start | bytes 786440 | tf_op jit(solution)/shard_map/ppermute | solution.py:61
  88.9 6.4 %shard_map.116 = (bf16[512,256]{1,0:T(8,128)(2,1)S(1)}, bf16[512,256]{1,0:T(8,128)(2,1)S(1)}, bf16[512,256]{1,0:T(8,128)(2,1)S(1)}, bf16[512,256]{1,0:T(8,128)(2,1)S(1)}) custom-call(s32[1]{0:T(128)} %bitcast.2.refs_0_, bf16[512,4096]{1,0:T(8,128)(2,1)S(1)} %get-tuple-element.26.refs_1_, bf16[512,4096]{1,0:T(8,128)(2,1)S(1)} %get-tuple-element.27.refs_2_, ...), custom_call_target="tpu_custom_call" | custom-call | flops 4294967296 | bytes 12582916 | tf_op jit(solution)/shard_map/pallas_call | solution.py:99
  95.3 5.7 %collective-permute-start.17 = (bf16[512,256]{1,0:T(8,128)(2,1)S(1)}, bf16[512,256]{1,0:T(8,128)(2,1)S(1)}, u32[]{:S(2)}, u32[]{:S(2)}) collective-permute-start(bf16[512,256]{1,0:T(8,128)(2,1)S(1)} %get-tuple-element.32), channel_id=1, source_target_pairs={{1,0},{0,1},{3,2},{2,3},{5,4},{4,5},{7,6},{6,7},{9,8},{8,9},{11,10... | collective-permute-start | bytes 786440 | tf_op jit(solution)/shard_map/ppermute | solution.py:61
  101.1 4.0 %shard_map.117 = (bf16[512,256]{1,0:T(8,128)(2,1)S(1)}, bf16[512,256]{1,0:T(8,128)(2,1)S(1)}) custom-call(s32[1]{0:T(128)} %bitcast.2.refs_0_, bf16[512,4096]{1,0:T(8,128)(2,1)S(1)} %get-tuple-element.26.refs_1_, bf16[512,4096]{1,0:T(8,128)(2,1)S(1)} %get-tuple-element.27.refs_2_, bf16[128,4096]{1,0:T(8,128)(2,1)} %collective-permute-done.14.refs_3_, ...), custom_call_target="tpu_custom_call" | custom-call | flops 2147483648 | bytes 10485764 | tf_op jit(solution)/shard_map/pallas_call | solution.py:99
  106.8 2.8 %shard_map.118 = bf16[512,2048]{1,0:T(8,128)(2,1)} custom-call(s32[3]{0:T(128)S(1)} %pad_add_fusion.where, bf16[512,256]{1,0:T(8,128)(2,1)S(1)} %get-tuple-element.25.refs_0_, bf16[512,256]{1,0:T(8,128)(2,1)S(1)} %get-tuple-element.28.refs_1_, bf16[512,256]{1,0:T(8,128)(2,1)S(1)} %get-tuple-element.29.refs_2_, ...), custom_call_target="tpu_custom_call" | custom-call | bytes 2097164 | tf_op jit(solution)/shard_map/pallas_call | solution.py:99
  (55 shorter events, 12.2 us)
Async XLA Ops:
  0.6 25.2 %copy-start.2 = (bf16[64,4096]{1,0:T(8,128)(2,1)S(1)}, bf16[64,4096]{1,0:T(8,128)(2,1)}, u32[]{:S(2)}) copy-start(bf16[64,4096]{1,0:T(8,128)(2,1)} %weight.1) | copy-start | bytes 1572868
  3.8 22.0 %collective-permute-start.4 = (bf16[512,4096]{1,0:T(8,128)(2,1)}, bf16[512,4096]{1,0:T(8,128)(2,1)S(1)}, u32[]{:S(2)}, u32[]{:S(2)}) collective-permute-start(bf16[512,4096]{1,0:T(8,128)(2,1)} %refs_1_.1), channel_id=1, source_target_pairs={{1,0},{0,1},{3,2},{2,3},{5,4},{4,5},{7,6},{6,7},{9,8},{8,9},{11,10... | collective-permute-start | bytes 12582920 | tf_op jit(solution)/shard_map/ppermute | solution.py:61
  7.1 4.0 %collective-permute-start.2 = (bf16[16,1024]{1,0:T(8,128)(2,1)S(1)}, bf16[16,1024]{1,0:T(8,128)(2,1)S(1)}, u32[]{:S(2)}, u32[]{:S(2)}) collective-permute-start(bf16[16,1024]{1,0:T(8,128)(2,1)S(1)} %get-tuple-element.20), channel_id=1, source_target_pairs={{96,0},{97,1},{98,2},{99,3},{100,4},{101,5},{102,6},{103,7},{104,8... | collective-permute-start | bytes 98312 | tf_op jit(solution)/shard_map/ppermute | solution.py:61
  7.1 4.0 %collective-permute-start.1 = (bf16[16,1024]{1,0:T(8,128)(2,1)S(1)}, bf16[16,1024]{1,0:T(8,128)(2,1)S(1)}, u32[]{:S(2)}, u32[]{:S(2)}) collective-permute-start(bf16[16,1024]{1,0:T(8,128)(2,1)S(1)} %get-tuple-element.20), channel_id=1, source_target_pairs={{32,0},{33,1},{34,2},{35,3},{36,4},{37,5},{38,6},{39,7},{40,8},{41... | collective-permute-start | bytes 98312 | tf_op jit(solution)/shard_map/ppermute | solution.py:61
  9.8 4.3 %collective-permute-start = (bf16[16,1024]{1,0:T(8,128)(2,1)S(1)}, bf16[16,1024]{1,0:T(8,128)(2,1)S(1)}, u32[]{:S(2)}, u32[]{:S(2)}) collective-permute-start(bf16[16,1024]{1,0:T(8,128)(2,1)S(1)} %get-tuple-element.20), channel_id=1, source_target_pairs={{64,0},{65,1},{66,2},{67,3},{68,4},{69,5},{70,6},{71,7},{72,8},{73... | collective-permute-start | bytes 98312 | tf_op jit(solution)/shard_map/ppermute | solution.py:61
  14.1 11.7 %collective-permute-start.3 = (bf16[16,1024]{1,0:T(8,128)(2,1)S(1)}, bf16[16,1024]{1,0:T(8,128)(2,1)S(1)}, u32[]{:S(2)}, u32[]{:S(2)}) collective-permute-start(bf16[16,1024]{1,0:T(8,128)(2,1)S(1)} %add_convert_fusion), channel_id=1, source_target_pairs={{128,0},{129,1},{130,2},{131,3},{132,4},{133,5},{134,6},{135,7},{1... | collective-permute-start | bytes 98312 | tf_op jit(solution)/shard_map/ppermute | solution.py:61
  25.8 33.9 %copy-start.7 = (bf16[512,4096]{1,0:T(8,128)(2,1)}, bf16[512,4096]{1,0:T(8,128)(2,1)S(1)}, u32[]{:S(2)}) copy-start(bf16[512,4096]{1,0:T(8,128)(2,1)S(1)} %collective-permute-done.4.refs_2_) | copy-start | bytes 12582916
  28.0 34.9 %copy-start.5 = (bf16[64,4096]{1,0:T(8,128)(2,1)}, bf16[64,4096]{1,0:T(8,128)(2,1)S(1)}, u32[]{:S(2)}) copy-start(bf16[64,4096]{1,0:T(8,128)(2,1)S(1)} %get-tuple-element.24.refs_3_) | copy-start | bytes 1572868
  28.1 8.3 %collective-permute-start.5 = (bf16[64,4096]{1,0:T(8,128)(2,1)S(1)}, bf16[64,4096]{1,0:T(8,128)(2,1)S(1)}, u32[]{:S(2)}, u32[]{:S(2)}) collective-permute-start(bf16[64,4096]{1,0:T(8,128)(2,1)S(1)} %get-tuple-element.24.refs_3_), channel_id=1, source_target_pairs={{8,0},{3,1},{10,2},{5,3},{12,4},{7,5},{14,6},{129,7},{16,8},{11,9}... | collective-permute-start | bytes 1572872 | tf_op jit(solution)/shard_map/ppermute | solution.py:61
  28.1 10.4 %collective-permute-start.7 = (bf16[64,4096]{1,0:T(8,128)(2,1)S(1)}, bf16[64,4096]{1,0:T(8,128)(2,1)S(1)}, u32[]{:S(2)}, u32[]{:S(2)}) collective-permute-start(bf16[64,4096]{1,0:T(8,128)(2,1)S(1)} %get-tuple-element.24.refs_3_), channel_id=1, source_target_pairs={{24,0},{135,1},{26,2},{1,3},{28,4},{3,5},{30,6},{5,7},{0,8},{143,9... | collective-permute-start | bytes 1572872 | tf_op jit(solution)/shard_map/ppermute | solution.py:61
  36.4 26.6 %copy-start.8 = (bf16[64,4096]{1,0:T(8,128)(2,1)}, bf16[64,4096]{1,0:T(8,128)(2,1)S(1)}, u32[]{:S(2)}) copy-start(bf16[64,4096]{1,0:T(8,128)(2,1)S(1)} %collective-permute-done.5.refs_4_) | copy-start | bytes 1572868
  36.4 8.3 %collective-permute-start.6 = (bf16[64,4096]{1,0:T(8,128)(2,1)S(1)}, bf16[64,4096]{1,0:T(8,128)(2,1)S(1)}, u32[]{:S(2)}, u32[]{:S(2)}) collective-permute-start(bf16[64,4096]{1,0:T(8,128)(2,1)S(1)} %collective-permute-done.5.refs_4_), channel_id=1, source_target_pairs={{8,0},{3,1},{10,2},{5,3},{12,4},{7,5},{14,6},{129,7},{16,8},{11,9}... | collective-permute-start | bytes 1572872 | tf_op jit(solution)/shard_map/ppermute | solution.py:61
  39.3 20.4 %collective-permute-start.12 = (bf16[128,4096]{1,0:T(8,128)(2,1)}, bf16[128,4096]{1,0:T(8,128)(2,1)}, u32[]{:S(2)}, u32[]{:S(2)}) collective-permute-start(bf16[128,4096]{1,0:T(8,128)(2,1)} %constant_dynamic-update-slice_fusion), channel_id=1, source_target_pairs={{2,0},{9,1},{4,2},{11,3},{6,4},{13,5},{128,6},{15,7},{10,8},{17,9}... | collective-permute-start | bytes 3145736 | tf_op jit(solution)/shard_map/ppermute | solution.py:61
  42.1 9.5 %collective-permute-start.8 = (bf16[64,4096]{1,0:T(8,128)(2,1)S(1)}, bf16[64,4096]{1,0:T(8,128)(2,1)S(1)}, u32[]{:S(2)}, u32[]{:S(2)}) collective-permute-start(bf16[64,4096]{1,0:T(8,128)(2,1)S(1)} %get-tuple-element.24.refs_3_), channel_id=1, source_target_pairs={{134,0},{25,1},{0,2},{27,3},{2,4},{29,5},{4,6},{31,7},{142,8},{1,9... | collective-permute-start | bytes 1572872 | tf_op jit(solution)/shard_map/ppermute | solution.py:61
  44.7 12.2 %collective-permute-start.10 = (bf16[64,4096]{1,0:T(8,128)(2,1)S(1)}, bf16[64,4096]{1,0:T(8,128)(2,1)S(1)}, u32[]{:S(2)}, u32[]{:S(2)}) collective-permute-start(bf16[64,4096]{1,0:T(8,128)(2,1)S(1)} %collective-permute-done.6.refs_5_), channel_id=1, source_target_pairs={{134,0},{25,1},{0,2},{27,3},{2,4},{29,5},{4,6},{31,7},{142,8},{1,9... | collective-permute-start | bytes 1572872 | tf_op jit(solution)/shard_map/ppermute | solution.py:61
  46.0 42.9 %collective-permute-start.9 = (bf16[128,4096]{1,0:T(8,128)(2,1)}, bf16[128,4096]{1,0:T(8,128)(2,1)}, u32[]{:S(2)}, u32[]{:S(2)}) collective-permute-start(bf16[128,4096]{1,0:T(8,128)(2,1)} %constant_dynamic-update-slice_fusion), channel_id=1, source_target_pairs={{134,0},{25,1},{0,2},{27,3},{2,4},{29,5},{4,6},{31,7},{142,8},{1,9... | collective-permute-start | bytes 3145736 | tf_op jit(solution)/shard_map/ppermute | solution.py:61
  58.1 43.0 %collective-permute-start.14 = (bf16[128,4096]{1,0:T(8,128)(2,1)}, bf16[128,4096]{1,0:T(8,128)(2,1)}, u32[]{:S(2)}, u32[]{:S(2)}) collective-permute-start(bf16[128,4096]{1,0:T(8,128)(2,1)} %pad_maximum_fusion), channel_id=1, source_target_pairs={{134,0},{25,1},{0,2},{27,3},{2,4},{29,5},{4,6},{31,7},{142,8},{1,9... | collective-permute-start | bytes 3145736 | tf_op jit(solution)/shard_map/ppermute | solution.py:61
  59.7 41.4 %collective-permute-start.15 = (bf16[128,4096]{1,0:T(8,128)(2,1)}, bf16[128,4096]{1,0:T(8,128)(2,1)}, u32[]{:S(2)}, u32[]{:S(2)}) collective-permute-start(bf16[128,4096]{1,0:T(8,128)(2,1)} %collective-permute-done.12.refs_7_), channel_id=1, source_target_pairs={{2,0},{9,1},{4,2},{11,3},{6,4},{13,5},{128,6},{15,7},{10,8},{17,9}... | collective-permute-start | bytes 3145736 | tf_op jit(solution)/shard_map/ppermute | solution.py:61
  62.9 17.6 %collective-permute-start.11 = (bf16[64,4096]{1,0:T(8,128)(2,1)S(1)}, bf16[64,4096]{1,0:T(8,128)(2,1)}, u32[]{:S(2)}, u32[]{:S(2)}) collective-permute-start(bf16[64,4096]{1,0:T(8,128)(2,1)S(1)} %get-tuple-element.24.refs_3_), channel_id=1, source_target_pairs={{2,0},{9,1},{4,2},{11,3},{6,4},{13,5},{128,6},{15,7},{10,8},{17,9}... | collective-permute-start | bytes 1572872 | tf_op jit(solution)/shard_map/ppermute | solution.py:61
  62.9 26.0 %collective-permute-start.13 = (bf16[64,4096]{1,0:T(8,128)(2,1)S(1)}, bf16[64,4096]{1,0:T(8,128)(2,1)}, u32[]{:S(2)}, u32[]{:S(2)}) collective-permute-start(bf16[64,4096]{1,0:T(8,128)(2,1)S(1)} %collective-permute-done.6.refs_5_), channel_id=1, source_target_pairs={{2,0},{9,1},{4,2},{11,3},{6,4},{13,5},{128,6},{15,7},{10,8},{17,9}... | collective-permute-start | bytes 1572872 | tf_op jit(solution)/shard_map/ppermute | solution.py:61
  80.4 25.3 %collective-permute-start.16 = (bf16[512,256]{1,0:T(8,128)(2,1)S(1)}, bf16[512,256]{1,0:T(8,128)(2,1)S(1)}, u32[]{:S(2)}, u32[]{:S(2)}) collective-permute-start(bf16[512,256]{1,0:T(8,128)(2,1)S(1)} %get-tuple-element.31), channel_id=1, source_target_pairs={{1,0},{0,1},{3,2},{2,3},{5,4},{4,5},{7,6},{6,7},{9,8},{8,9},{11,10... | collective-permute-start | bytes 786440 | tf_op jit(solution)/shard_map/ppermute | solution.py:61
  95.3 10.4 %collective-permute-start.17 = (bf16[512,256]{1,0:T(8,128)(2,1)S(1)}, bf16[512,256]{1,0:T(8,128)(2,1)S(1)}, u32[]{:S(2)}, u32[]{:S(2)}) collective-permute-start(bf16[512,256]{1,0:T(8,128)(2,1)S(1)} %get-tuple-element.32), channel_id=1, source_target_pairs={{1,0},{0,1},{3,2},{2,3},{5,4},{4,5},{7,6},{6,7},{9,8},{8,9},{11,10... | collective-permute-start | bytes 786440 | tf_op jit(solution)/shard_map/ppermute | solution.py:61
  101.0 4.7 %collective-permute-start.19 = (bf16[512,256]{1,0:T(8,128)(2,1)S(1)}, bf16[512,256]{1,0:T(8,128)(2,1)S(1)}, u32[]{:S(2)}, u32[]{:S(2)}) collective-permute-start(bf16[512,256]{1,0:T(8,128)(2,1)S(1)} %get-tuple-element.34), channel_id=1, source_target_pairs={{1,0},{0,1},{3,2},{2,3},{5,4},{4,5},{7,6},{6,7},{9,8},{8,9},{11,10... | collective-permute-start | bytes 786440 | tf_op jit(solution)/shard_map/ppermute | solution.py:61
  105.1 1.7 %collective-permute-start.18 = (bf16[512,256]{1,0:T(8,128)(2,1)S(1)}, bf16[512,256]{1,0:T(8,128)(2,1)S(1)}, u32[]{:S(2)}, u32[]{:S(2)}) collective-permute-start(bf16[512,256]{1,0:T(8,128)(2,1)S(1)} %get-tuple-element.33), channel_id=1, source_target_pairs={{1,0},{0,1},{3,2},{2,3},{5,4},{4,5},{7,6},{6,7},{9,8},{8,9},{11,10... | collective-permute-start | bytes 786440 | tf_op jit(solution)/shard_map/ppermute | solution.py:61
  (9 other events, 73.5 us)

commit v10 on v9

--- a/solution.py
+++ b/solution.py
@@ -88,13 +88,14 @@
     return x, y, z, 1 - core
 
 
-def call(kernel, out_shape, inputs, scratch=(), limit=16, flops=0, smem=0, kept=(), resident=()):
+def call(kernel, out_shape, inputs, scratch=(), limit=16, flops=0, smem=0, kept=(), resident=(), anywhere=()):
     specs = [pl.BlockSpec(memory_space=pltpu.SMEM)] * smem
     specs += [pl.BlockSpec(memory_space=pltpu.VMEM)] * (len(inputs) - smem + len(resident))
     specs += [pl.BlockSpec(memory_space=pltpu.HBM)] * len(kept)
+    specs += [pl.BlockSpec(memory_space=pl.ANY)] * len(anywhere)
     resident = [pltpu.with_memory_space_constraint(v, pltpu.VMEM) for v in resident]
     kept = [pltpu.with_memory_space_constraint(v, pltpu.HBM) for v in kept]
-    inputs = (*inputs, *resident, *kept)
+    inputs = (*inputs, *resident, *kept, *anywhere)
     moved = sum(math.prod(v.shape) * v.dtype.itemsize for v in inputs)
     return pl.pallas_call(
         kernel,
@@ -121,17 +122,25 @@
     return momentum_decay * momentum[0] + gradient[0].astype(F32)
 
 
-def bands_kernel(momentum, gradient, cols, rows3, exact, rounded, m, g, c, r, sems):
+def bands_kernel(
+    momentum, gradient, cols_in, rows3, back_rows3, weight_in, exact, rounded, mixed, cols, back, weight, g, r, sems
+):
     wide = WIDE * TILE
     steps = momentum.shape[2] // wide
-    copies = [pltpu.make_async_copy(cols, c, sems.at[2 * steps])]
-    copies += [pltpu.make_async_copy(rows3, r, sems.at[2 * steps + 1])]
+    copies = [
+        pltpu.make_async_copy(cols_in, cols, sems.at[2 * steps]),
+        pltpu.make_async_copy(rows3, r, sems.at[2 * steps + 1]),
+    ]
     for k in range(steps):
         cut = pl.ds(k * wide, wide)
         copies += [
-            pltpu.make_async_copy(momentum.at[0, :, cut], m.at[k], sems.at[2 * k]),
+            pltpu.make_async_copy(momentum.at[0, :, cut], mixed.at[k], sems.at[2 * k]),
             pltpu.make_async_copy(gradient.at[0, :, cut], g.at[k], sems.at[2 * k + 1]),
         ]
+    copies += [
+        pltpu.make_async_copy(back_rows3, back, sems.at[2 * steps + 2]),
+        pltpu.make_async_copy(weight_in, weight, sems.at[2 * steps + 3]),
+    ]
     for copy in copies:
         copy.start()
     copies[0].wait()
@@ -139,37 +148,44 @@
     for k in range(steps):
         copies[2 * k + 2].wait()
         copies[2 * k + 3].wait()
-        high, low = split(momentum_decay * m[k] + g[k].astype(F32))
-        narrow.append(dot(high, c[:wide]) + dot(low, c[:wide]) + dot(high, c[wide:]))
+        value = momentum_decay * mixed[k] + g[k].astype(F32)
+        mixed[k] = value
+        high, low = split(value)
+        narrow.append(dot(high, cols[:wide]) + dot(low, cols[:wide]) + dot(high, cols[wide:]))
     copies[1].wait()
     high, low = split(jnp.concatenate(narrow, axis=1))
     bands = dot(r[...], jnp.concatenate([high, low, high], axis=0))
     exact[...] = bands
     rounded[...] = bands.astype(BF16)
-
-
-def restored(bands, back_rows3, back_hi, back_lo):
+    for copy in copies[-2:]:
+        copy.wait()
+
+
+def restored(bands, back, cols):
+    wide = WIDE * TILE
     high, low = split(bands)
-    tall = dot(back_rows3[...], jnp.concatenate([high, low, high], axis=0))
+    tall = dot(back[...], jnp.concatenate([high, low, high], axis=0))
     high, low = split(stacked(tall, WIDE * BAND))
-    return dot(high, back_hi[...]) + dot(low, back_hi[...]) + dot(high, back_lo[...])
-
-
-def residual_kernel(momentum, gradient, bands, back_rows3, back_hi, back_lo, out):
-    mixed = mixed_of(momentum, gradient)
-    low = restored(bands[...], back_rows3, back_hi, back_lo)
+
+    def spread(a, b):
+        return lax.dot_general(a, b, NT, preferred_element_type=F32)
+
+    return spread(high, cols[:wide]) + spread(low, cols[:wide]) + spread(high, cols[wide:])
+
+
+def residual_kernel(bands, mixed, cols, back, out):
+    low = restored(bands[...], back, cols)
     wide = WIDE * TILE
-    for k in range(mixed.shape[1] // wide):
-        cut = slice(k * wide, (k + 1) * wide)
-        out[0, :, cut] = mixed[:, cut] - low[k * TILE : (k + 1) * TILE]
+    for k in range(mixed.shape[0]):
+        out[0, :, k * wide : (k + 1) * wide] = mixed[k] - low[k * TILE : (k + 1) * TILE]
 
 
 def soft_sign(update):
     return update * lax.rsqrt(update * update + soft_width)
 
 
-def update_kernel(total, weight, back_rows3, back_hi, back_lo, direction, new_weight):
-    sign = soft_sign(restored(total[...], back_rows3, back_hi, back_lo))
+def update_kernel(total, cols, back, weight, direction, new_weight):
+    sign = soft_sign(restored(total[...], back, cols))
     wide = WIDE * TILE
     for k in range(direction.shape[1] // wide):
         cut = slice(k * wide, (k + 1) * wide)
@@ -237,8 +253,6 @@
     cols_hi, cols_lo = (np.kron(eye, np.asarray(h, np.float32).T).astype(jnp.bfloat16) for h in (high, low))
     rows3 = np.concatenate([high, high, low], axis=1)
     back_rows3 = np.concatenate([high.T, high.T, low.T], axis=1)
-    back_hi, back_lo = cols_hi.T, cols_lo.T
-    back_rows = high.T
     width = weight.shape[1]
     narrow = width // TILE * BAND
     rows = weight.shape[0]
@@ -252,18 +266,24 @@
 
     shape = jax.ShapeDtypeStruct
     steps = width // (WIDE * TILE)
-    exact, rounded = call(
+    cols_in = np.concatenate([cols_hi, cols_lo], axis=0)
+    exact, rounded, mixed, cols, back, held_weight = call(
         bands_kernel,
-        (shape((BAND, narrow), F32), shape((BAND, narrow), BF16)),
+        (
+            shape((BAND, narrow), F32),
+            shape((BAND, narrow), BF16),
+            pltpu.VMEM((steps, rows, WIDE * TILE), F32),
+            pltpu.VMEM(cols_in.shape, BF16),
+            pltpu.VMEM(back_rows3.shape, BF16),
+            pltpu.VMEM(weight.shape, BF16),
+        ),
         (),
         (
-            pltpu.VMEM((steps, rows, WIDE * TILE), F32),
             pltpu.VMEM((steps, rows, WIDE * TILE), BF16),
-            pltpu.VMEM((2 * WIDE * TILE, WIDE * BAND), BF16),
             pltpu.VMEM(rows3.shape, BF16),
-            pltpu.SemaphoreType.DMA((2 * steps + 2,)),
+            pltpu.SemaphoreType.DMA((2 * steps + 4,)),
         ),
-        kept=(momentum, gradient, np.concatenate([cols_hi, cols_lo], axis=0), rows3),
+        kept=(momentum, gradient, cols_in, rows3, back_rows3, weight),
     )
 
     def after(value, *others):
@@ -273,30 +293,33 @@
 
     parts = [rounded.astype(F32)] + [fetch(rounded, along_x(n)).astype(F32) for n in (1, 2, -1)]
     sent = ((parts[0] + parts[2]) + (parts[1] + parts[3])).astype(BF16)
-    new_momentum = call(
-        residual_kernel,
-        shape(momentum.shape, F32),
-        (momentum, gradient, exact, back_rows3, back_hi, back_lo),
-    )
     total = sent.astype(F32) + fetch(sent, far_z).astype(F32)
     direction, own = call(
         update_kernel,
         (shape((rows, width), F32), shape((rows, width), BF16)),
-        (after(total, new_momentum, other), weight, back_rows3, back_hi, back_lo),
+        (after(total, other),),
+        resident=(cols, back, held_weight),
+    )
+    new_momentum = call(
+        residual_kernel,
+        shape(momentum.shape, F32),
+        (after(exact, own),),
+        resident=(mixed, cols, back),
     )
 
     ahead, behind = (fetch(own, along(0, n)) for n in (1, -1))
     next_own, last_own = (fetch(own, along(1, n)) for n in (1, -1))
+    pair = after(jnp.concatenate([ahead, behind], axis=0), next_own, last_own, new_momentum)
     across = fetch(ahead, along(0, 1))
-    pair = jnp.concatenate([ahead, behind], axis=0)
     next_pair, last_pair = (fetch(pair, along(1, n)) for n in (1, -1))
+    far_own = fetch(last_own, along(1, -1))
     next_across, last_across = (fetch(across, along(1, n)) for n in (1, -1))
-    far_pair = fetch(next_pair, along(1, 1))
-    far_rest = fetch(jnp.concatenate([last_own, last_across], axis=0), along(1, -1))
+    far_pair = fetch(after(next_pair, across, far_own), along(1, 1))
+    far_across = fetch(last_across, along(1, -1))
     lines = [
         [(own, 0), (ahead, 0), (across, 0), (behind, 0)],
         [(next_own, 0), (next_pair, 0), (next_across, 0), (next_pair, TILE)],
-        [(far_rest, 0), (far_pair, 0), (far_rest, TILE), (far_pair, TILE)],
+        [(far_own, 0), (far_pair, 0), (far_across, 0), (far_pair, TILE)],
         [(last_own, 0), (last_pair, 0), (last_across, 0), (last_pair, TILE)],
     ]
 
@@ -326,7 +349,8 @@
             flops=count * 2 * 2 * tokens * 4 * rows * width,
             smem=1,
             resident=() if load else (activations_in, other_in),
-            kept=([activations, other] if load else []) + used,
+            kept=[activations, other] if load else [],
+            anywhere=used,
         )
 
     *results, activations_in, other_in = forward([0], True)

time: 110 us -> 104 us (0.945)
  starting transfers between devices: 37.3 us -> 33.9 us
  local copies, waits for them, and re-layouts: 6.55 us -> 3.65 us
  waiting for transfers between devices: 35 us -> 37.5 us
  Pallas kernels: 28.6 us -> 27.3 us
    ppermute x20 -> x21, starting transfers between devices: 37.3 us -> 33.9 us  [fetch(): lax.ppermute(value, AXES, [(place(*source(*spot(i))), i) for i in range(2...]
    ppermute x20 -> x21, waiting for transfers between devices: 35 us -> 37.5 us  [fetch(): lax.ppermute(value, AXES, [(place(*source(*spot(i))), i) for i in range(2...]
    unnamed x27 -> x10, local copies, waits for them, and re-layouts: 5.65 us -> 3.65 us
    pallas_call x7, Pallas kernels: 28.6 us -> 27.3 us  [call(): pl.pallas_call(kernel, out_shape=out_shape, in_specs=specs, out_specs=jax...]
  transfers between devices with their start and end apart: 20 -> 21, of which waited for: 9 -> 11; matrix products, arithmetic and copies ran while one was open for 3% -> 1% of each run, Pallas kernels for 19% -> 19%
where the time goes in v10:
time: 104 us
  waiting for transfers between devices  37.5 us (36%)
  starting transfers between devices  33.9 us (33%)
  Pallas kernels  27.3 us (26%)
  local copies, waits for them, and re-layouts  3.65 us (4%)
  other arithmetic  1.15 us (1%)
    ppermute x21, waiting for transfers between devices, fetch(): lax.ppermute(value, AXES, [(place(*source(*spot(i))), i) for i in range(2...  37.5 us
    ppermute x21, starting transfers between devices, fetch(): lax.ppermute(value, AXES, [(place(*source(*spot(i))), i) for i in range(2...  33.9 us
    pallas_call x7, Pallas kernels, call(): pl.pallas_call(kernel, out_shape=out_shape, in_specs=specs, out_specs=jax...  27.3 us
    unnamed x10, local copies, waits for them, and re-layouts  3.65 us
  transfers between devices with their start and end apart: 21, of which 11 were waited for; matrix products, arithmetic and copies ran while one was open for 1% of the time, Pallas kernels for 19%

profile of v10, /device:TPU:1, one launch (start us, length us, event | category | flops | bytes accessed | tf_op | source)
XLA Modules:
  0.0 104.2 jit_solution(11528548896903225688)
XLA Ops:
  0.6 3.1 %shard_map.94 = (f32[16,1024]{1,0:T(8,128)S(1)}, bf16[16,1024]{1,0:T(8,128)(2,1)S(1)}, f32[8,64,512]{2,1,0:T(8,128)S(1)}, bf16[1024,128]{1,0:T(8,128)(2,1)S(1)},...) custom-call(f32[1,64,4096]{2,1,0:T(8,128)} %momentum.1, bf16[1,64,4096]{2,1,0:T(8,128)(2,1)} %gradient.1, ...), custom_call_target="tpu_custom_call" | custom-call | bytes 2371584 | tf_op jit(solution)/shard_map/pallas_call | solution.py:100
  3.7 3.3 %collective-permute-start.4 = (bf16[512,4096]{1,0:T(8,128)(2,1)}, bf16[512,4096]{1,0:T(8,128)(2,1)S(1)}, u32[]{:S(2)}, u32[]{:S(2)}) collective-permute-start(bf16[512,4096]{1,0:T(8,128)(2,1)} %refs_1_.1), channel_id=1, source_target_pairs={{1,0},{0,1},{3,2},{2,3},{5,4},{4,5},{7,6},{6,7},{9,8},{8,9},{11,10... | collective-permute-start | bytes 12582920 | tf_op jit(solution)/shard_map/ppermute | solution.py:61
  7.0 2.7 %collective-permute-start.1 = (bf16[16,1024]{1,0:T(8,128)(2,1)S(1)}, bf16[16,1024]{1,0:T(8,128)(2,1)S(1)}, u32[]{:S(2)}, u32[]{:S(2)}) collective-permute-start(bf16[16,1024]{1,0:T(8,128)(2,1)S(1)} %get-tuple-element.27), channel_id=1, source_target_pairs={{32,0},{33,1},{34,2},{35,3},{36,4},{37,5},{38,6},{39,7},{40,8},{41... | collective-permute-start | bytes 98312 | tf_op jit(solution)/shard_map/ppermute | solution.py:61
  11.0 3.0 %collective-permute-done = bf16[16,1024]{1,0:T(8,128)(2,1)S(1)} collective-permute-done((bf16[16,1024]{1,0:T(8,128)(2,1)S(1)}, bf16[16,1024]{1,0:T(8,128)(2,1)S(1)}, u32[]{:S(2)}, u32[]{:S(2)}) %collective-permute-start) | collective-permute-done | bytes 32800 | tf_op jit(solution)/shard_map/ppermute | solution.py:61
  14.0 5.3 %collective-permute-start.3 = (bf16[16,1024]{1,0:T(8,128)(2,1)S(1)}, bf16[16,1024]{1,0:T(8,128)(2,1)S(1)}, u32[]{:S(2)}, u32[]{:S(2)}) collective-permute-start(bf16[16,1024]{1,0:T(8,128)(2,1)S(1)} %add_convert_fusion), channel_id=1, source_target_pairs={{128,0},{129,1},{130,2},{131,3},{132,4},{133,5},{134,6},{135,7},{1... | collective-permute-start | bytes 98312 | tf_op jit(solution)/shard_map/ppermute | solution.py:61
  19.3 1.5 %collective-permute-done.3 = bf16[16,1024]{1,0:T(8,128)(2,1)S(1)} collective-permute-done((bf16[16,1024]{1,0:T(8,128)(2,1)S(1)}, bf16[16,1024]{1,0:T(8,128)(2,1)S(1)}, u32[]{:S(2)}, u32[]{:S(2)}) %collective-permute-start.3) | collective-permute-done | bytes 32800 | tf_op jit(solution)/shard_map/ppermute | solution.py:61
  20.8 1.9 %copy-done.4 = bf16[512,4096]{1,0:T(8,128)(2,1)} copy-done((bf16[512,4096]{1,0:T(8,128)(2,1)}, bf16[512,4096]{1,0:T(8,128)(2,1)S(1)}, u32[]{:S(2)}) %copy-start.4) | copy-done | bytes 4194328
  22.8 1.8 %shard_map.95 = (f32[64,4096]{1,0:T(8,128)}, bf16[64,4096]{1,0:T(8,128)(2,1)S(1)}) custom-call(f32[16,1024]{1,0:T(8,128)S(1)} %convert_add_fusion.total, bf16[1024,128]{1,0:T(8,128)(2,1)S(1)} %get-tuple-element.30.cols, bf16[64,48]{1,0:T(8,128)(2,1)S(1)} %get-tuple-element.31.back, bf16[64,4096]{1,0:T(8,128)(2,1)S(1)} %get-tuple-element.32.weight), custom_call_target="tpu_custom_call" | custom-call | bytes 858112 | tf_op jit(solution)/shard_map/pallas_call | solution.py:100
  24.5 3.8 %collective-permute-start.5 = (bf16[64,4096]{1,0:T(8,128)(2,1)S(1)}, bf16[64,4096]{1,0:T(8,128)(2,1)S(1)}, u32[]{:S(2)}, u32[]{:S(2)}) collective-permute-start(bf16[64,4096]{1,0:T(8,128)(2,1)S(1)} %get-tuple-element.33.refs_3_), channel_id=1, source_target_pairs={{8,0},{3,1},{10,2},{5,3},{12,4},{7,5},{14,6},{129,7},{16,8},{11,9}... | collective-permute-start | bytes 1572872 | tf_op jit(solution)/shard_map/ppermute | solution.py:61
  31.1 1.6 %shard_map.96 = f32[1,64,4096]{2,1,0:T(8,128)} custom-call(f32[16,1024]{1,0:T(8,128)S(1)} %get-tuple-element.34.bands, f32[8,64,512]{2,1,0:T(8,128)S(1)} %get-tuple-element.35.mixed, bf16[1024,128]{1,0:T(8,128)(2,1)S(1)} %get-tuple-element.30.cols, bf16[64,48]{1,0:T(8,128)(2,1)S(1)} %get-tuple-element.31.back), custom_call_target="tpu_custom_call" | custom-call | bytes 1382400 | tf_op jit(solution)/shard_map/pallas_call | solution.py:100
  32.8 1.7 %collective-permute-done.5.refs_4_ = bf16[64,4096]{1,0:T(8,128)(2,1)S(1)} collective-permute-done((bf16[64,4096]{1,0:T(8,128)(2,1)S(1)}, bf16[64,4096]{1,0:T(8,128)(2,1)S(1)}, u32[]{:S(2)}, u32[]{:S(2)}) %collective-permute-start.5) | collective-permute-done | bytes 524320 | tf_op jit(solution)/shard_map/ppermute | solution.py:61
  34.5 5.5 %collective-permute-done.7.refs_6_ = bf16[64,4096]{1,0:T(8,128)(2,1)S(1)} collective-permute-done((bf16[64,4096]{1,0:T(8,128)(2,1)S(1)}, bf16[64,4096]{1,0:T(8,128)(2,1)S(1)}, u32[]{:S(2)}, u32[]{:S(2)}) %collective-permute-start.7) | collective-permute-done | bytes 524320 | tf_op jit(solution)/shard_map/ppermute | solution.py:61
  42.7 3.4 %collective-permute-start.12 = (bf16[128,4096]{1,0:T(8,128)(2,1)}, bf16[128,4096]{1,0:T(8,128)(2,1)}, u32[]{:S(2)}, u32[]{:S(2)}) collective-permute-start(bf16[128,4096]{1,0:T(8,128)(2,1)} %pad_maximum_fusion), channel_id=1, source_target_pairs={{2,0},{9,1},{4,2},{11,3},{6,4},{13,5},{128,6},{15,7},{10,8},{17,9}... | collective-permute-start | bytes 3145736 | tf_op jit(solution)/shard_map/ppermute | solution.py:61
  46.2 2.9 %collective-permute-start.6 = (bf16[64,4096]{1,0:T(8,128)(2,1)S(1)}, bf16[64,4096]{1,0:T(8,128)(2,1)}, u32[]{:S(2)}, u32[]{:S(2)}) collective-permute-start(bf16[64,4096]{1,0:T(8,128)(2,1)S(1)} %collective-permute-done.5.refs_4_), channel_id=1, source_target_pairs={{8,0},{3,1},{10,2},{5,3},{12,4},{7,5},{14,6},{129,7},{16,8},{11,9}... | collective-permute-start | bytes 1572872 | tf_op jit(solution)/shard_map/ppermute | solution.py:61
  50.0 10.7 %collective-permute-done.6.refs_5_ = bf16[64,4096]{1,0:T(8,128)(2,1)} collective-permute-done((bf16[64,4096]{1,0:T(8,128)(2,1)S(1)}, bf16[64,4096]{1,0:T(8,128)(2,1)}, u32[]{:S(2)}, u32[]{:S(2)}) %collective-permute-start.6) | collective-permute-done | bytes 524320 | tf_op jit(solution)/shard_map/ppermute | solution.py:61
  60.7 3.1 %collective-permute-done.12.refs_7_ = bf16[128,4096]{1,0:T(8,128)(2,1)} collective-permute-done((bf16[128,4096]{1,0:T(8,128)(2,1)}, bf16[128,4096]{1,0:T(8,128)(2,1)}, u32[]{:S(2)}, u32[]{:S(2)}) %collective-permute-start.12) | collective-permute-done | bytes 1048608 | tf_op jit(solution)/shard_map/ppermute | solution.py:61
  63.8 3.4 %collective-permute-start.15 = (bf16[128,4096]{1,0:T(8,128)(2,1)}, bf16[128,4096]{1,0:T(8,128)(2,1)S(1)}, u32[]{:S(2)}, u32[]{:S(2)}) collective-permute-start(bf16[128,4096]{1,0:T(8,128)(2,1)} %collective-permute-done.12.refs_7_), channel_id=1, source_target_pairs={{2,0},{9,1},{4,2},{11,3},{6,4},{13,5},{128,6},{15,7},{10,8},{17,9}... | collective-permute-start | bytes 3145736 | tf_op jit(solution)/shard_map/ppermute | solution.py:61
  67.2 8.3 %collective-permute-done.11.refs_5_ = bf16[64,4096]{1,0:T(8,128)(2,1)} collective-permute-done((bf16[64,4096]{1,0:T(8,128)(2,1)}, bf16[64,4096]{1,0:T(8,128)(2,1)}, u32[]{:S(2)}, u32[]{:S(2)}) %collective-permute-start.11) | collective-permute-done | bytes 524320 | tf_op jit(solution)/shard_map/ppermute | solution.py:61
  75.6 7.7 %shard_map.97 = (bf16[512,256]{1,0:T(8,128)(2,1)S(1)}, bf16[512,256]{1,0:T(8,128)(2,1)}, bf16[512,4096]{1,0:T(8,128)(2,1)S(1)}, bf16[512,4096]{1,0:T(8,128)(2,1)S(1)}) custom-call(s32[1]{0:T(128)} %bitcast.2.refs_0_, bf16[512,4096]{1,0:T(8,128)(2,1)} %refs_1_.1, bf16[512,4096]{1,0:T(8,128)(2,1)} %copy-done.4, ...), custom_call_target="tpu_custom_call" | custom-call | flops 2147483648 | bytes 10485764 | tf_op jit(solution)/shard_map/pallas_call | solution.py:100
  83.3 3.6 %collective-permute-start.17 = (bf16[512,256]{1,0:T(8,128)(2,1)}, bf16[512,256]{1,0:T(8,128)(2,1)S(1)}, u32[]{:S(2)}, u32[]{:S(2)}) collective-permute-start(bf16[512,256]{1,0:T(8,128)(2,1)} %get-tuple-element.45), channel_id=1, source_target_pairs={{1,0},{0,1},{3,2},{2,3},{5,4},{4,5},{7,6},{6,7},{9,8},{8,9},{11,10... | collective-permute-start | bytes 786440 | tf_op jit(solution)/shard_map/ppermute | solution.py:61
  87.0 7.0 %shard_map.98 = (bf16[512,256]{1,0:T(8,128)(2,1)S(1)}, bf16[512,256]{1,0:T(8,128)(2,1)}, bf16[512,256]{1,0:T(8,128)(2,1)S(1)}, bf16[512,256]{1,0:T(8,128)(2,1)}) custom-call(s32[1]{0:T(128)} %bitcast.2.refs_0_, bf16[512,4096]{1,0:T(8,128)(2,1)S(1)} %get-tuple-element.38.refs_1_, bf16[512,4096]{1,0:T(8,128)(2,1)S(1)} %get-tuple-element.39.refs_2_, ...), custom_call_target="tpu_custom_call" | custom-call | flops 4294967296 | bytes 12582916 | tf_op jit(solution)/shard_map/pallas_call | solution.py:100
  94.0 2.0 %collective-permute-start.18 = (bf16[512,256]{1,0:T(8,128)(2,1)}, bf16[512,256]{1,0:T(8,128)(2,1)S(1)}, u32[]{:S(2)}, u32[]{:S(2)}) collective-permute-start(bf16[512,256]{1,0:T(8,128)(2,1)} %get-tuple-element.46), channel_id=1, source_target_pairs={{1,0},{0,1},{3,2},{2,3},{5,4},{4,5},{7,6},{6,7},{9,8},{8,9},{11,10... | collective-permute-start | bytes 786440 | tf_op jit(solution)/shard_map/ppermute | solution.py:61
  96.3 3.3 %shard_map.99 = (bf16[512,256]{1,0:T(8,128)(2,1)S(1)}, bf16[512,256]{1,0:T(8,128)(2,1)}) custom-call(s32[1]{0:T(128)} %bitcast.2.refs_0_, bf16[512,4096]{1,0:T(8,128)(2,1)S(1)} %get-tuple-element.38.refs_1_, bf16[512,4096]{1,0:T(8,128)(2,1)S(1)} %get-tuple-element.39.refs_2_, bf16[64,4096]{1,0:T(8,128)(2,1)S(1)} %collective-permute-done.14.refs_3_, ...), custom_call_target="tpu_custom_call" | custom-call | flops 2147483648 | bytes 10485764 | tf_op jit(solution)/shard_map/pallas_call | solution.py:100
  101.5 2.8 %shard_map.100 = bf16[512,2048]{1,0:T(8,128)(2,1)} custom-call(s32[3]{0:T(128)S(1)} %pad_add_fusion.where, bf16[512,256]{1,0:T(8,128)(2,1)S(1)} %get-tuple-element.37.refs_0_, bf16[512,256]{1,0:T(8,128)(2,1)S(1)} %get-tuple-element.41.refs_1_, bf16[512,256]{1,0:T(8,128)(2,1)S(1)} %get-tuple-element.43.refs_2_, ...), custom_call_target="tpu_custom_call" | custom-call | bytes 2097164 | tf_op jit(solution)/shard_map/pallas_call | solution.py:100
  (39 shorter events, 9.9 us)
Async XLA Ops:
  3.7 17.1 %collective-permute-start.4 = (bf16[512,4096]{1,0:T(8,128)(2,1)}, bf16[512,4096]{1,0:T(8,128)(2,1)S(1)}, u32[]{:S(2)}, u32[]{:S(2)}) collective-permute-start(bf16[512,4096]{1,0:T(8,128)(2,1)} %refs_1_.1), channel_id=1, source_target_pairs={{1,0},{0,1},{3,2},{2,3},{5,4},{4,5},{7,6},{6,7},{9,8},{8,9},{11,10... | collective-permute-start | bytes 12582920 | tf_op jit(solution)/shard_map/ppermute | solution.py:61
  7.0 4.0 %collective-permute-start.2 = (bf16[16,1024]{1,0:T(8,128)(2,1)S(1)}, bf16[16,1024]{1,0:T(8,128)(2,1)S(1)}, u32[]{:S(2)}, u32[]{:S(2)}) collective-permute-start(bf16[16,1024]{1,0:T(8,128)(2,1)S(1)} %get-tuple-element.27), channel_id=1, source_target_pairs={{96,0},{97,1},{98,2},{99,3},{100,4},{101,5},{102,6},{103,7},{104,8... | collective-permute-start | bytes 98312 | tf_op jit(solution)/shard_map/ppermute | solution.py:61
  7.0 4.0 %collective-permute-start.1 = (bf16[16,1024]{1,0:T(8,128)(2,1)S(1)}, bf16[16,1024]{1,0:T(8,128)(2,1)S(1)}, u32[]{:S(2)}, u32[]{:S(2)}) collective-permute-start(bf16[16,1024]{1,0:T(8,128)(2,1)S(1)} %get-tuple-element.27), channel_id=1, source_target_pairs={{32,0},{33,1},{34,2},{35,3},{36,4},{37,5},{38,6},{39,7},{40,8},{41... | collective-permute-start | bytes 98312 | tf_op jit(solution)/shard_map/ppermute | solution.py:61
  9.7 4.3 %collective-permute-start = (bf16[16,1024]{1,0:T(8,128)(2,1)S(1)}, bf16[16,1024]{1,0:T(8,128)(2,1)S(1)}, u32[]{:S(2)}, u32[]{:S(2)}) collective-permute-start(bf16[16,1024]{1,0:T(8,128)(2,1)S(1)} %get-tuple-element.27), channel_id=1, source_target_pairs={{64,0},{65,1},{66,2},{67,3},{68,4},{69,5},{70,6},{71,7},{72,8},{73... | collective-permute-start | bytes 98312 | tf_op jit(solution)/shard_map/ppermute | solution.py:61
  14.0 6.8 %collective-permute-start.3 = (bf16[16,1024]{1,0:T(8,128)(2,1)S(1)}, bf16[16,1024]{1,0:T(8,128)(2,1)S(1)}, u32[]{:S(2)}, u32[]{:S(2)}) collective-permute-start(bf16[16,1024]{1,0:T(8,128)(2,1)S(1)} %add_convert_fusion), channel_id=1, source_target_pairs={{128,0},{129,1},{130,2},{131,3},{132,4},{133,5},{134,6},{135,7},{1... | collective-permute-start | bytes 98312 | tf_op jit(solution)/shard_map/ppermute | solution.py:61
  20.8 2.0 %copy-start.4 = (bf16[512,4096]{1,0:T(8,128)(2,1)}, bf16[512,4096]{1,0:T(8,128)(2,1)S(1)}, u32[]{:S(2)}) copy-start(bf16[512,4096]{1,0:T(8,128)(2,1)S(1)} %collective-permute-done.4.refs_2_) | copy-start | bytes 12582916
  24.5 10.0 %collective-permute-start.5 = (bf16[64,4096]{1,0:T(8,128)(2,1)S(1)}, bf16[64,4096]{1,0:T(8,128)(2,1)S(1)}, u32[]{:S(2)}, u32[]{:S(2)}) collective-permute-start(bf16[64,4096]{1,0:T(8,128)(2,1)S(1)} %get-tuple-element.33.refs_3_), channel_id=1, source_target_pairs={{8,0},{3,1},{10,2},{5,3},{12,4},{7,5},{14,6},{129,7},{16,8},{11,9}... | collective-permute-start | bytes 1572872 | tf_op jit(solution)/shard_map/ppermute | solution.py:61
  28.4 11.6 %collective-permute-start.7 = (bf16[64,4096]{1,0:T(8,128)(2,1)S(1)}, bf16[64,4096]{1,0:T(8,128)(2,1)S(1)}, u32[]{:S(2)}, u32[]{:S(2)}) collective-permute-start(bf16[64,4096]{1,0:T(8,128)(2,1)S(1)} %get-tuple-element.33.refs_3_), channel_id=1, source_target_pairs={{24,0},{135,1},{26,2},{1,3},{28,4},{3,5},{30,6},{5,7},{0,8},{143,9... | collective-permute-start | bytes 1572872 | tf_op jit(solution)/shard_map/ppermute | solution.py:61
  28.4 13.1 %collective-permute-start.8 = (bf16[64,4096]{1,0:T(8,128)(2,1)S(1)}, bf16[64,4096]{1,0:T(8,128)(2,1)S(1)}, u32[]{:S(2)}, u32[]{:S(2)}) collective-permute-start(bf16[64,4096]{1,0:T(8,128)(2,1)S(1)} %get-tuple-element.33.refs_3_), channel_id=1, source_target_pairs={{134,0},{25,1},{0,2},{27,3},{2,4},{29,5},{4,6},{31,7},{142,8},{1,9... | collective-permute-start | bytes 1572872 | tf_op jit(solution)/shard_map/ppermute | solution.py:61
  29.7 12.3 %collective-permute-start.9 = (bf16[64,4096]{1,0:T(8,128)(2,1)S(1)}, bf16[64,4096]{1,0:T(8,128)(2,1)S(1)}, u32[]{:S(2)}, u32[]{:S(2)}) collective-permute-start(bf16[64,4096]{1,0:T(8,128)(2,1)S(1)} %get-tuple-element.33.refs_3_), channel_id=1, source_target_pairs={{2,0},{9,1},{4,2},{11,3},{6,4},{13,5},{128,6},{15,7},{10,8},{17,9}... | collective-permute-start | bytes 1572872 | tf_op jit(solution)/shard_map/ppermute | solution.py:61
  42.7 21.1 %collective-permute-start.12 = (bf16[128,4096]{1,0:T(8,128)(2,1)}, bf16[128,4096]{1,0:T(8,128)(2,1)}, u32[]{:S(2)}, u32[]{:S(2)}) collective-permute-start(bf16[128,4096]{1,0:T(8,128)(2,1)} %pad_maximum_fusion), channel_id=1, source_target_pairs={{2,0},{9,1},{4,2},{11,3},{6,4},{13,5},{128,6},{15,7},{10,8},{17,9}... | collective-permute-start | bytes 3145736 | tf_op jit(solution)/shard_map/ppermute | solution.py:61
  46.2 14.6 %collective-permute-start.6 = (bf16[64,4096]{1,0:T(8,128)(2,1)S(1)}, bf16[64,4096]{1,0:T(8,128)(2,1)}, u32[]{:S(2)}, u32[]{:S(2)}) collective-permute-start(bf16[64,4096]{1,0:T(8,128)(2,1)S(1)} %collective-permute-done.5.refs_4_), channel_id=1, source_target_pairs={{8,0},{3,1},{10,2},{5,3},{12,4},{7,5},{14,6},{129,7},{16,8},{11,9}... | collective-permute-start | bytes 1572872 | tf_op jit(solution)/shard_map/ppermute | solution.py:61
  49.1 11.6 %collective-permute-start.14 = (bf16[64,4096]{1,0:T(8,128)(2,1)S(1)}, bf16[64,4096]{1,0:T(8,128)(2,1)S(1)}, u32[]{:S(2)}, u32[]{:S(2)}) collective-permute-start(bf16[64,4096]{1,0:T(8,128)(2,1)S(1)} %collective-permute-done.8.refs_3_), channel_id=1, source_target_pairs={{134,0},{25,1},{0,2},{27,3},{2,4},{29,5},{4,6},{31,7},{142,8},{1,9... | collective-permute-start | bytes 1572872 | tf_op jit(solution)/shard_map/ppermute | solution.py:61
  50.0 37.0 %collective-permute-start.10 = (bf16[128,4096]{1,0:T(8,128)(2,1)}, bf16[128,4096]{1,0:T(8,128)(2,1)}, u32[]{:S(2)}, u32[]{:S(2)}) collective-permute-start(bf16[128,4096]{1,0:T(8,128)(2,1)} %pad_maximum_fusion), channel_id=1, source_target_pairs={{134,0},{25,1},{0,2},{27,3},{2,4},{29,5},{4,6},{31,7},{142,8},{1,9... | collective-permute-start | bytes 3145736 | tf_op jit(solution)/shard_map/ppermute | solution.py:61
  60.7 14.9 %collective-permute-start.11 = (bf16[64,4096]{1,0:T(8,128)(2,1)}, bf16[64,4096]{1,0:T(8,128)(2,1)}, u32[]{:S(2)}, u32[]{:S(2)}) collective-permute-start(bf16[64,4096]{1,0:T(8,128)(2,1)} %collective-permute-done.6.refs_5_), channel_id=1, source_target_pairs={{134,0},{25,1},{0,2},{27,3},{2,4},{29,5},{4,6},{31,7},{142,8},{1,9... | collective-permute-start | bytes 1572872 | tf_op jit(solution)/shard_map/ppermute | solution.py:61
  63.8 32.5 %collective-permute-start.15 = (bf16[128,4096]{1,0:T(8,128)(2,1)}, bf16[128,4096]{1,0:T(8,128)(2,1)S(1)}, u32[]{:S(2)}, u32[]{:S(2)}) collective-permute-start(bf16[128,4096]{1,0:T(8,128)(2,1)} %collective-permute-done.12.refs_7_), channel_id=1, source_target_pairs={{2,0},{9,1},{4,2},{11,3},{6,4},{13,5},{128,6},{15,7},{10,8},{17,9}... | collective-permute-start | bytes 3145736 | tf_op jit(solution)/shard_map/ppermute | solution.py:61
  67.2 19.7 %collective-permute-start.13 = (bf16[64,4096]{1,0:T(8,128)(2,1)}, bf16[64,4096]{1,0:T(8,128)(2,1)}, u32[]{:S(2)}, u32[]{:S(2)}) collective-permute-start(bf16[64,4096]{1,0:T(8,128)(2,1)} %collective-permute-done.6.refs_5_), channel_id=1, source_target_pairs={{2,0},{9,1},{4,2},{11,3},{6,4},{13,5},{128,6},{15,7},{10,8},{17,9}... | collective-permute-start | bytes 1572872 | tf_op jit(solution)/shard_map/ppermute | solution.py:61
  75.6 20.7 %collective-permute-start.16 = (bf16[64,4096]{1,0:T(8,128)(2,1)}, bf16[64,4096]{1,0:T(8,128)(2,1)S(1)}, u32[]{:S(2)}, u32[]{:S(2)}) collective-permute-start(bf16[64,4096]{1,0:T(8,128)(2,1)} %collective-permute-done.11.refs_5_), channel_id=1, source_target_pairs={{134,0},{25,1},{0,2},{27,3},{2,4},{29,5},{4,6},{31,7},{142,8},{1,9... | collective-permute-start | bytes 1572872 | tf_op jit(solution)/shard_map/ppermute | solution.py:61
  75.6 11.4 %copy-start.1 = (bf16[64,4096]{1,0:T(8,128)(2,1)S(1)}, bf16[64,4096]{1,0:T(8,128)(2,1)}, u32[]{:S(2)}) copy-start(bf16[64,4096]{1,0:T(8,128)(2,1)} %copy-done) | copy-start | bytes 1572868
  75.6 11.4 %copy-start.3 = (bf16[64,4096]{1,0:T(8,128)(2,1)S(1)}, bf16[64,4096]{1,0:T(8,128)(2,1)}, u32[]{:S(2)}) copy-start(bf16[64,4096]{1,0:T(8,128)(2,1)} %copy-done.2) | copy-start | bytes 1572868
  83.3 16.7 %collective-permute-start.17 = (bf16[512,256]{1,0:T(8,128)(2,1)}, bf16[512,256]{1,0:T(8,128)(2,1)S(1)}, u32[]{:S(2)}, u32[]{:S(2)}) collective-permute-start(bf16[512,256]{1,0:T(8,128)(2,1)} %get-tuple-element.45), channel_id=1, source_target_pairs={{1,0},{0,1},{3,2},{2,3},{5,4},{4,5},{7,6},{6,7},{9,8},{8,9},{11,10... | collective-permute-start | bytes 786440 | tf_op jit(solution)/shard_map/ppermute | solution.py:61
  94.0 6.0 %collective-permute-start.18 = (bf16[512,256]{1,0:T(8,128)(2,1)}, bf16[512,256]{1,0:T(8,128)(2,1)S(1)}, u32[]{:S(2)}, u32[]{:S(2)}) collective-permute-start(bf16[512,256]{1,0:T(8,128)(2,1)} %get-tuple-element.46), channel_id=1, source_target_pairs={{1,0},{0,1},{3,2},{2,3},{5,4},{4,5},{7,6},{6,7},{9,8},{8,9},{11,10... | collective-permute-start | bytes 786440 | tf_op jit(solution)/shard_map/ppermute | solution.py:61
  96.0 4.0 %collective-permute-start.20 = (bf16[512,256]{1,0:T(8,128)(2,1)}, bf16[512,256]{1,0:T(8,128)(2,1)S(1)}, u32[]{:S(2)}, u32[]{:S(2)}) collective-permute-start(bf16[512,256]{1,0:T(8,128)(2,1)} %get-tuple-element.48), channel_id=1, source_target_pairs={{1,0},{0,1},{3,2},{2,3},{5,4},{4,5},{7,6},{6,7},{9,8},{8,9},{11,10... | collective-permute-start | bytes 786440 | tf_op jit(solution)/shard_map/ppermute | solution.py:61
  99.6 1.8 %collective-permute-start.19 = (bf16[512,256]{1,0:T(8,128)(2,1)}, bf16[512,256]{1,0:T(8,128)(2,1)S(1)}, u32[]{:S(2)}, u32[]{:S(2)}) collective-permute-start(bf16[512,256]{1,0:T(8,128)(2,1)} %get-tuple-element.47), channel_id=1, source_target_pairs={{1,0},{0,1},{3,2},{2,3},{5,4},{4,5},{7,6},{6,7},{9,8},{8,9},{11,10... | collective-permute-start | bytes 786440 | tf_op jit(solution)/shard_map/ppermute | solution.py:61
  (2 other events, 1.7 us)

commit v11 on v10

--- a/solution.py
+++ b/solution.py
@@ -184,14 +184,29 @@
     return update * lax.rsqrt(update * update + soft_width)
 
 
-def update_kernel(total, cols, back, weight, direction, new_weight):
+def direction_kernel(total, cols, back, direction):
     sign = soft_sign(restored(total[...], back, cols))
     wide = WIDE * TILE
     for k in range(direction.shape[1] // wide):
-        cut = slice(k * wide, (k + 1) * wide)
-        part = sign[k * TILE : (k + 1) * TILE]
-        direction[:, cut] = part
-        new_weight[:, cut] = (weight[:, cut].astype(F32) - step_rate * part).astype(BF16)
+        direction[:, k * wide : (k + 1) * wide] = sign[k * TILE : (k + 1) * TILE]
+
+
+def renew_kernel(bands, ahead, behind, ahead_half, behind_half, cols, back, weight, top, bottom):
+    wide = WIDE * TILE
+    half = TILE // 2
+    for f in range(4):
+        band = bands[f * BAND : (f + 1) * BAND]
+        tall = dot(back[:, BAND:], jnp.concatenate([band, band], axis=0)).astype(BF16)
+        move = step_rate * soft_sign(
+            lax.dot_general(stacked(tall, WIDE * BAND), cols[:wide], NT, preferred_element_type=F32)
+        )
+        out, at = (top, bottom)[f // 2], f % 2 * TILE
+        raws = ([(weight, 0, TILE)], [(ahead, 0, TILE)], [(ahead_half, 0, half), (behind_half, half, half)])
+        for raw, row, count in (*raws, [(behind, 0, TILE)])[f]:
+            for k in range(weight.shape[1] // wide):
+                cut = slice(k * wide, (k + 1) * wide)
+                part = move[k * TILE + row : k * TILE + row + count]
+                out[at + row : at + row + count, cut] = (raw[:, cut].astype(F32) - part).astype(BF16)
 
 
 def forward_kernel(pieces, load, first, *refs):
@@ -289,38 +304,47 @@
     def after(value, *others):
         return lax.optimization_barrier((value, *others))[0]
 
-    other = fetch(after(activations, rounded), sibling)
+    ahead, behind = (fetch(after(weight, rounded), along(0, n)) for n in (1, -1))
 
     parts = [rounded.astype(F32)] + [fetch(rounded, along_x(n)).astype(F32) for n in (1, 2, -1)]
     sent = ((parts[0] + parts[2]) + (parts[1] + parts[3])).astype(BF16)
-    total = sent.astype(F32) + fetch(sent, far_z).astype(F32)
-    direction, own = call(
-        update_kernel,
-        (shape((rows, width), F32), shape((rows, width), BF16)),
-        (after(total, other),),
+    total = sent.astype(F32) + fetch(after(sent, ahead, behind), far_z).astype(F32)
+    halves_across = [fetch(ahead[: rows // 2], along(0, 1)), fetch(behind[rows // 2 :], along(0, -1))]
+
+    sent = total.astype(BF16)
+    line = jnp.concatenate([sent] + [fetch(sent, along(0, n)) for n in (1, 2, -1)], axis=0)
+    direction = call(
+        direction_kernel,
+        shape((rows, width), F32),
+        (total,),
+        resident=(cols, back),
+    )
+    half_rows = shape((2 * rows, width), BF16)
+    top, bottom = call(
+        renew_kernel,
+        (half_rows, half_rows),
+        (line, ahead, behind, *halves_across),
         resident=(cols, back, held_weight),
     )
+    other = fetch(after(activations, top), sibling)
     new_momentum = call(
         residual_kernel,
         shape(momentum.shape, F32),
-        (after(exact, own),),
+        (after(exact, top),),
         resident=(mixed, cols, back),
     )
 
-    ahead, behind = (fetch(own, along(0, n)) for n in (1, -1))
-    next_own, last_own = (fetch(own, along(1, n)) for n in (1, -1))
-    pair = after(jnp.concatenate([ahead, behind], axis=0), next_own, last_own, new_momentum)
-    across = fetch(ahead, along(0, 1))
-    next_pair, last_pair = (fetch(pair, along(1, n)) for n in (1, -1))
-    far_own = fetch(last_own, along(1, -1))
-    next_across, last_across = (fetch(across, along(1, n)) for n in (1, -1))
-    far_pair = fetch(after(next_pair, across, far_own), along(1, 1))
-    far_across = fetch(last_across, along(1, -1))
+    next_top, last_bottom = fetch(top, along(1, 1)), fetch(bottom, along(1, -1))
+    next_bottom, last_top = fetch(bottom, along(1, 1)), fetch(top, along(1, -1))
+    far_top, far_bottom = fetch(next_top, along(1, 1)), fetch(last_bottom, along(1, -1))
     lines = [
-        [(own, 0), (ahead, 0), (across, 0), (behind, 0)],
-        [(next_own, 0), (next_pair, 0), (next_across, 0), (next_pair, TILE)],
-        [(far_own, 0), (far_pair, 0), (far_across, 0), (far_pair, TILE)],
-        [(last_own, 0), (last_pair, 0), (last_across, 0), (last_pair, TILE)],
+        [(a, row) for a in pair for row in (0, TILE)]
+        for pair in (
+            (after(top, new_momentum, direction), bottom),
+            (next_top, next_bottom),
+            (far_top, far_bottom),
+            (last_top, last_bottom),
+        )
     ]
 
     block = shape((tokens, 4 * rows), BF16)
@@ -349,8 +373,8 @@
             flops=count * 2 * 2 * tokens * 4 * rows * width,
             smem=1,
             resident=() if load else (activations_in, other_in),
-            kept=[activations, other] if load else [],
-            anywhere=used,
+            kept=[activations] if load else [],
+            anywhere=([other] if load else []) + used,
         )
 
     *results, activations_in, other_in = forward([0], True)

time: 104 us -> 88.9 us (0.85)
  waiting for transfers between devices: 37.5 us -> 23 us
  local copies, waits for them, and re-layouts: 3.65 us -> 0.04 us
  starting transfers between devices: 33.9 us -> 36.1 us
  Pallas kernels: 27.3 us -> 28.8 us
    ppermute x21 -> x22, waiting for transfers between devices: 37.5 us -> 23 us  [fetch(): lax.ppermute(value, AXES, [(place(*source(*spot(i))), i) for i in range(2...]
    unnamed x10 -> x0, local copies, waits for them, and re-layouts: 3.65 us -> none
    ppermute x21 -> x22, starting transfers between devices: 33.9 us -> 36.1 us  [fetch(): lax.ppermute(value, AXES, [(place(*source(*spot(i))), i) for i in range(2...]
    pallas_call x7 -> x8, Pallas kernels: 27.3 us -> 28.8 us  [call(): pl.pallas_call(kernel, out_shape=out_shape, in_specs=specs, out_specs=jax...]
  transfers between devices with their start and end apart: 21 -> 22, of which waited for: 11 -> 10; matrix products, arithmetic and copies ran while one was open for 1% -> 0% of each run, Pallas kernels for 19% -> 24%
where the time goes in v11:
time: 88.9 us; the launch traced here: 88.8 us
  starting transfers between devices  36.1 us (41%)
  Pallas kernels  28.8 us (32%)
  waiting for transfers between devices  23 us (26%)
    ppermute x22, starting transfers between devices, fetch(): lax.ppermute(value, AXES, [(place(*source(*spot(i))), i) for i in range(2...  36.1 us
    pallas_call x8, Pallas kernels, call(): pl.pallas_call(kernel, out_shape=out_shape, in_specs=specs, out_specs=jax...  28.8 us
    ppermute x22, waiting for transfers between devices, fetch(): lax.ppermute(value, AXES, [(place(*source(*spot(i))), i) for i in range(2...  23 us
  transfers between devices with their start and end apart: 22, of which 10 were waited for; matrix products, arithmetic and copies ran while one was open for 0% of the time, Pallas kernels for 24%

profile of v11, /device:TPU:1, one launch (start us, length us, event | category | flops | bytes accessed | tf_op | source)
XLA Modules:
  0.0 88.8 jit_solution(1075919974854450977)
XLA Ops:
  0.6 3.1 %shard_map.94 = (f32[16,1024]{1,0:T(8,128)S(1)}, bf16[16,1024]{1,0:T(8,128)(2,1)S(1)}, f32[8,64,512]{2,1,0:T(8,128)S(1)}, bf16[1024,128]{1,0:T(8,128)(2,1)S(1)},...) custom-call(f32[1,64,4096]{2,1,0:T(8,128)} %momentum.1, bf16[1,64,4096]{2,1,0:T(8,128)(2,1)} %gradient.1, ...), custom_call_target="tpu_custom_call" | custom-call | bytes 2371584 | tf_op jit(solution)/shard_map/pallas_call | solution.py:100
  3.7 6.5 %collective-permute-start.3 = (bf16[64,4096]{1,0:T(8,128)(2,1)}, bf16[64,4096]{1,0:T(8,128)(2,1)S(1)}, u32[]{:S(2)}, u32[]{:S(2)}) collective-permute-start(bf16[64,4096]{1,0:T(8,128)(2,1)} %weight_in.1), channel_id=1, source_target_pairs={{8,0},{3,1},{10,2},{5,3},{12,4},{7,5},{14,6},{129,7},{16,8},{11,9}... | collective-permute-start | bytes 1572872 | tf_op jit(solution)/shard_map/ppermute | solution.py:61
  11.4 1.5 %collective-permute-start.1 = (bf16[16,1024]{1,0:T(8,128)(2,1)S(1)}, bf16[16,1024]{1,0:T(8,128)(2,1)S(1)}, u32[]{:S(2)}, u32[]{:S(2)}) collective-permute-start(bf16[16,1024]{1,0:T(8,128)(2,1)S(1)} %get-tuple-element.27), channel_id=1, source_target_pairs={{32,0},{33,1},{34,2},{35,3},{36,4},{37,5},{38,6},{39,7},{40,8},{41... | collective-permute-start | bytes 98312 | tf_op jit(solution)/shard_map/ppermute | solution.py:61
  12.9 1.5 %collective-permute-start = (bf16[16,1024]{1,0:T(8,128)(2,1)S(1)}, bf16[16,1024]{1,0:T(8,128)(2,1)S(1)}, u32[]{:S(2)}, u32[]{:S(2)}) collective-permute-start(bf16[16,1024]{1,0:T(8,128)(2,1)S(1)} %get-tuple-element.27), channel_id=1, source_target_pairs={{64,0},{65,1},{66,2},{67,3},{68,4},{69,5},{70,6},{71,7},{72,8},{73... | collective-permute-start | bytes 98312 | tf_op jit(solution)/shard_map/ppermute | solution.py:61
  14.5 3.1 %collective-permute-done = bf16[16,1024]{1,0:T(8,128)(2,1)S(1)} collective-permute-done((bf16[16,1024]{1,0:T(8,128)(2,1)S(1)}, bf16[16,1024]{1,0:T(8,128)(2,1)S(1)}, u32[]{:S(2)}, u32[]{:S(2)}) %collective-permute-start) | collective-permute-done | bytes 32800 | tf_op jit(solution)/shard_map/ppermute | solution.py:61
  17.6 2.1 %collective-permute-done.4.behind = bf16[64,4096]{1,0:T(8,128)(2,1)S(1)} collective-permute-done((bf16[64,4096]{1,0:T(8,128)(2,1)}, bf16[64,4096]{1,0:T(8,128)(2,1)S(1)}, u32[]{:S(2)}, u32[]{:S(2)}) %collective-permute-start.4) | collective-permute-done | bytes 524320 | tf_op jit(solution)/shard_map/ppermute | solution.py:61
  19.6 1.7 %collective-permute-start.5 = (bf16[16,1024]{1,0:T(8,128)(2,1)S(1)}, bf16[16,1024]{1,0:T(8,128)(2,1)S(1)}, u32[]{:S(2)}, u32[]{:S(2)}) collective-permute-start(bf16[16,1024]{1,0:T(8,128)(2,1)S(1)} %add_convert_fusion), channel_id=1, source_target_pairs={{128,0},{129,1},{130,2},{131,3},{132,4},{133,5},{134,6},{135,7},{1... | collective-permute-start | bytes 98312 | tf_op jit(solution)/shard_map/ppermute | solution.py:61
  21.5 1.5 %collective-permute-start.10 = (bf16[32,4096]{1,0:T(8,128)(2,1)S(1)}, bf16[32,4096]{1,0:T(8,128)(2,1)S(1)}, u32[]{:S(2)}, u32[]{:S(2)}) collective-permute-start(bf16[32,4096]{1,0:T(8,128)(2,1)S(1)} %slice.9), channel_id=1, source_target_pairs={{24,0},{135,1},{26,2},{1,3},{28,4},{3,5},{30,6},{5,7},{0,8},{143,9... | collective-permute-start | bytes 786440 | tf_op jit(solution)/shard_map/ppermute | solution.py:61
  23.0 3.7 %collective-permute-done.5 = bf16[16,1024]{1,0:T(8,128)(2,1)S(1)} collective-permute-done((bf16[16,1024]{1,0:T(8,128)(2,1)S(1)}, bf16[16,1024]{1,0:T(8,128)(2,1)S(1)}, u32[]{:S(2)}, u32[]{:S(2)}) %collective-permute-start.5) | collective-permute-done | bytes 32800 | tf_op jit(solution)/shard_map/ppermute | solution.py:61
  28.1 1.4 %collective-permute-start.6 = (bf16[16,1024]{1,0:T(8,128)(2,1)S(1)}, bf16[16,1024]{1,0:T(8,128)(2,1)S(1)}, u32[]{:S(2)}, u32[]{:S(2)}) collective-permute-start(bf16[16,1024]{1,0:T(8,128)(2,1)S(1)} %get-tuple-element.50), channel_id=1, source_target_pairs={{8,0},{3,1},{10,2},{5,3},{12,4},{7,5},{14,6},{129,7},{16,8},{11,9}... | collective-permute-start | bytes 98312 | tf_op jit(solution)/shard_map/ppermute | solution.py:61
  29.5 1.3 %collective-permute-done.8 = bf16[16,1024]{1,0:T(8,128)(2,1)S(1)} collective-permute-done((bf16[16,1024]{1,0:T(8,128)(2,1)S(1)}, bf16[16,1024]{1,0:T(8,128)(2,1)S(1)}, u32[]{:S(2)}, u32[]{:S(2)}) %collective-permute-start.8) | collective-permute-done | bytes 32800 | tf_op jit(solution)/shard_map/ppermute | solution.py:61
  31.3 1.7 %shard_map.95 = (bf16[128,4096]{1,0:T(8,128)(2,1)S(1)}, bf16[128,4096]{1,0:T(8,128)(2,1)S(1)}) custom-call(bf16[64,1024]{1,0:T(8,128)(2,1)S(1)} %pad_maximum_fusion.bands, bf16[64,4096]{1,0:T(8,128)(2,1)S(1)} %collective-permute-done.3.ahead, bf16[64,4096]{1,0:T(8,128)(2,1)S(1)} %collective-permute-done.4.behind, ...), custom_call_target="tpu_custom_call" | custom-call | bytes 2496512 | tf_op jit(solution)/shard_map/pallas_call | solution.py:100
  33.0 5.2 %collective-permute-start.11 = (bf16[512,4096]{1,0:T(8,128)(2,1)}, bf16[512,4096]{1,0:T(8,128)(2,1)}, u32[]{:S(2)}, u32[]{:S(2)}) collective-permute-start(bf16[512,4096]{1,0:T(8,128)(2,1)} %refs_1_.1), channel_id=1, source_target_pairs={{1,0},{0,1},{3,2},{2,3},{5,4},{4,5},{7,6},{6,7},{9,8},{8,9},{11,10... | collective-permute-start | bytes 12582920 | tf_op jit(solution)/shard_map/ppermute | solution.py:61
  39.8 2.6 %collective-permute-start.15 = (bf16[128,4096]{1,0:T(8,128)(2,1)S(1)}, bf16[128,4096]{1,0:T(8,128)(2,1)}, u32[]{:S(2)}, u32[]{:S(2)}) collective-permute-start(bf16[128,4096]{1,0:T(8,128)(2,1)S(1)} %get-tuple-element.38.refs_4_), channel_id=1, source_target_pairs={{2,0},{9,1},{4,2},{11,3},{6,4},{13,5},{128,6},{15,7},{10,8},{17,9}... | collective-permute-start | bytes 3145736 | tf_op jit(solution)/shard_map/ppermute | solution.py:61
  42.4 9.9 %collective-permute-done.14.refs_5_ = bf16[128,4096]{1,0:T(8,128)(2,1)} collective-permute-done((bf16[128,4096]{1,0:T(8,128)(2,1)S(1)}, bf16[128,4096]{1,0:T(8,128)(2,1)}, u32[]{:S(2)}, u32[]{:S(2)}) %collective-permute-start.14) | collective-permute-done | bytes 1048608 | tf_op jit(solution)/shard_map/ppermute | solution.py:61
  52.3 2.1 %collective-permute-start.16 = (bf16[128,4096]{1,0:T(8,128)(2,1)}, bf16[128,4096]{1,0:T(8,128)(2,1)}, u32[]{:S(2)}, u32[]{:S(2)}) collective-permute-start(bf16[128,4096]{1,0:T(8,128)(2,1)} %collective-permute-done.14.refs_5_), channel_id=1, source_target_pairs={{2,0},{9,1},{4,2},{11,3},{6,4},{13,5},{128,6},{15,7},{10,8},{17,9}... | collective-permute-start | bytes 3145736 | tf_op jit(solution)/shard_map/ppermute | solution.py:61
  54.5 1.7 %shard_map.97 = f32[64,4096]{1,0:T(8,128)} custom-call(f32[16,1024]{1,0:T(8,128)S(1)} %get-tuple-element.49.total, bf16[1024,128]{1,0:T(8,128)(2,1)S(1)} %get-tuple-element.30.cols, bf16[64,48]{1,0:T(8,128)(2,1)S(1)} %get-tuple-element.31.back), custom_call_target="tpu_custom_call" | custom-call | bytes 333824 | tf_op jit(solution)/shard_map/pallas_call | solution.py:100
  56.2 1.6 %shard_map.96 = f32[1,64,4096]{2,1,0:T(8,128)} custom-call(f32[16,1024]{1,0:T(8,128)S(1)} %get-tuple-element.34.bands, f32[8,64,512]{2,1,0:T(8,128)S(1)} %get-tuple-element.35.mixed, bf16[1024,128]{1,0:T(8,128)(2,1)S(1)} %get-tuple-element.30.cols, bf16[64,48]{1,0:T(8,128)(2,1)S(1)} %get-tuple-element.31.back), custom_call_target="tpu_custom_call" | custom-call | bytes 1382400 | tf_op jit(solution)/shard_map/pallas_call | solution.py:100
  57.8 7.6 %shard_map.98 = (bf16[512,256]{1,0:T(8,128)(2,1)S(1)}, bf16[512,256]{1,0:T(8,128)(2,1)}, bf16[512,4096]{1,0:T(8,128)(2,1)S(1)}, bf16[512,4096]{1,0:T(8,128)(2,1)S(1)}) custom-call(s32[1]{0:T(128)} %bitcast.2.refs_0_, bf16[512,4096]{1,0:T(8,128)(2,1)} %refs_1_.1, bf16[512,4096]{1,0:T(8,128)(2,1)} %collective-permute-done.11.refs_2_, ...), custom_call_target="tpu_custom_call" | custom-call | flops 2147483648 | bytes 10485764 | tf_op jit(solution)/shard_map/pallas_call | solution.py:100
  65.4 3.6 %collective-permute-start.18 = (bf16[512,256]{1,0:T(8,128)(2,1)}, bf16[512,256]{1,0:T(8,128)(2,1)S(1)}, u32[]{:S(2)}, u32[]{:S(2)}) collective-permute-start(bf16[512,256]{1,0:T(8,128)(2,1)} %get-tuple-element.45), channel_id=1, source_target_pairs={{1,0},{0,1},{3,2},{2,3},{5,4},{4,5},{7,6},{6,7},{9,8},{8,9},{11,10... | collective-permute-start | bytes 786440 | tf_op jit(solution)/shard_map/ppermute | solution.py:61
  68.9 6.4 %shard_map.99 = (bf16[512,256]{1,0:T(8,128)(2,1)S(1)}, bf16[512,256]{1,0:T(8,128)(2,1)S(1)}, bf16[512,256]{1,0:T(8,128)(2,1)S(1)}, bf16[512,256]{1,0:T(8,128)(2,1)S(1)}) custom-call(s32[1]{0:T(128)} %bitcast.2.refs_0_, bf16[512,4096]{1,0:T(8,128)(2,1)S(1)} %get-tuple-element.40.refs_1_, bf16[512,4096]{1,0:T(8,128)(2,1)S(1)} %get-tuple-element.41.refs_2_, ...), custom_call_target="tpu_custom_call" | custom-call | flops 4294967296 | bytes 12582916 | tf_op jit(solution)/shard_map/pallas_call | solution.py:100
  77.0 4.0 %shard_map.100 = (bf16[512,256]{1,0:T(8,128)(2,1)S(1)}, bf16[512,256]{1,0:T(8,128)(2,1)S(1)}) custom-call(s32[1]{0:T(128)} %bitcast.2.refs_0_, bf16[512,4096]{1,0:T(8,128)(2,1)S(1)} %get-tuple-element.40.refs_1_, bf16[512,4096]{1,0:T(8,128)(2,1)S(1)} %get-tuple-element.41.refs_2_, bf16[128,4096]{1,0:T(8,128)(2,1)} %collective-permute-done.16.refs_3_, ...), custom_call_target="tpu_custom_call" | custom-call | flops 2147483648 | bytes 10485764 | tf_op jit(solution)/shard_map/pallas_call | solution.py:100
  80.9 3.6 %collective-permute-start.20 = (bf16[512,256]{1,0:T(8,128)(2,1)S(1)}, bf16[512,256]{1,0:T(8,128)(2,1)S(1)}, u32[]{:S(2)}, u32[]{:S(2)}) collective-permute-start(bf16[512,256]{1,0:T(8,128)(2,1)S(1)} %get-tuple-element.47), channel_id=1, source_target_pairs={{1,0},{0,1},{3,2},{2,3},{5,4},{4,5},{7,6},{6,7},{9,8},{8,9},{11,10... | collective-permute-start | bytes 786440 | tf_op jit(solution)/shard_map/ppermute | solution.py:61
  86.0 2.8 %shard_map.101 = bf16[512,2048]{1,0:T(8,128)(2,1)} custom-call(s32[3]{0:T(128)S(1)} %pad_add_fusion.where, bf16[512,256]{1,0:T(8,128)(2,1)S(1)} %get-tuple-element.39.refs_0_, bf16[512,256]{1,0:T(8,128)(2,1)S(1)} %get-tuple-element.42.refs_1_, bf16[512,256]{1,0:T(8,128)(2,1)S(1)} %get-tuple-element.43.refs_2_, ...), custom_call_target="tpu_custom_call" | custom-call | bytes 2097164 | tf_op jit(solution)/shard_map/pallas_call | solution.py:100
  (34 shorter events, 7.8 us)
Async XLA Ops:
  3.7 13.9 %collective-permute-start.3 = (bf16[64,4096]{1,0:T(8,128)(2,1)}, bf16[64,4096]{1,0:T(8,128)(2,1)S(1)}, u32[]{:S(2)}, u32[]{:S(2)}) collective-permute-start(bf16[64,4096]{1,0:T(8,128)(2,1)} %weight_in.1), channel_id=1, source_target_pairs={{8,0},{3,1},{10,2},{5,3},{12,4},{7,5},{14,6},{129,7},{16,8},{11,9}... | collective-permute-start | bytes 1572872 | tf_op jit(solution)/shard_map/ppermute | solution.py:61
  10.2 9.5 %collective-permute-start.4 = (bf16[64,4096]{1,0:T(8,128)(2,1)}, bf16[64,4096]{1,0:T(8,128)(2,1)S(1)}, u32[]{:S(2)}, u32[]{:S(2)}) collective-permute-start(bf16[64,4096]{1,0:T(8,128)(2,1)} %weight_in.1), channel_id=1, source_target_pairs={{24,0},{135,1},{26,2},{1,3},{28,4},{3,5},{30,6},{5,7},{0,8},{143,9... | collective-permute-start | bytes 1572872 | tf_op jit(solution)/shard_map/ppermute | solution.py:61
  10.2 4.3 %collective-permute-start.2 = (bf16[16,1024]{1,0:T(8,128)(2,1)S(1)}, bf16[16,1024]{1,0:T(8,128)(2,1)S(1)}, u32[]{:S(2)}, u32[]{:S(2)}) collective-permute-start(bf16[16,1024]{1,0:T(8,128)(2,1)S(1)} %get-tuple-element.27), channel_id=1, source_target_pairs={{96,0},{97,1},{98,2},{99,3},{100,4},{101,5},{102,6},{103,7},{104,8... | collective-permute-start | bytes 98312 | tf_op jit(solution)/shard_map/ppermute | solution.py:61
  11.4 3.1 %collective-permute-start.1 = (bf16[16,1024]{1,0:T(8,128)(2,1)S(1)}, bf16[16,1024]{1,0:T(8,128)(2,1)S(1)}, u32[]{:S(2)}, u32[]{:S(2)}) collective-permute-start(bf16[16,1024]{1,0:T(8,128)(2,1)S(1)} %get-tuple-element.27), channel_id=1, source_target_pairs={{32,0},{33,1},{34,2},{35,3},{36,4},{37,5},{38,6},{39,7},{40,8},{41... | collective-permute-start | bytes 98312 | tf_op jit(solution)/shard_map/ppermute | solution.py:61
  12.9 4.7 %collective-permute-start = (bf16[16,1024]{1,0:T(8,128)(2,1)S(1)}, bf16[16,1024]{1,0:T(8,128)(2,1)S(1)}, u32[]{:S(2)}, u32[]{:S(2)}) collective-permute-start(bf16[16,1024]{1,0:T(8,128)(2,1)S(1)} %get-tuple-element.27), channel_id=1, source_target_pairs={{64,0},{65,1},{66,2},{67,3},{68,4},{69,5},{70,6},{71,7},{72,8},{73... | collective-permute-start | bytes 98312 | tf_op jit(solution)/shard_map/ppermute | solution.py:61
  19.6 7.1 %collective-permute-start.5 = (bf16[16,1024]{1,0:T(8,128)(2,1)S(1)}, bf16[16,1024]{1,0:T(8,128)(2,1)S(1)}, u32[]{:S(2)}, u32[]{:S(2)}) collective-permute-start(bf16[16,1024]{1,0:T(8,128)(2,1)S(1)} %add_convert_fusion), channel_id=1, source_target_pairs={{128,0},{129,1},{130,2},{131,3},{132,4},{133,5},{134,6},{135,7},{1... | collective-permute-start | bytes 98312 | tf_op jit(solution)/shard_map/ppermute | solution.py:61
  21.4 9.9 %collective-permute-start.9 = (bf16[32,4096]{1,0:T(8,128)(2,1)S(1)}, bf16[32,4096]{1,0:T(8,128)(2,1)S(1)}, u32[]{:S(2)}, u32[]{:S(2)}) collective-permute-start(bf16[32,4096]{1,0:T(8,128)(2,1)S(1)} %slice.8), channel_id=1, source_target_pairs={{8,0},{3,1},{10,2},{5,3},{12,4},{7,5},{14,6},{129,7},{16,8},{11,9}... | collective-permute-start | bytes 786440 | tf_op jit(solution)/shard_map/ppermute | solution.py:61
  21.5 9.8 %collective-permute-start.10 = (bf16[32,4096]{1,0:T(8,128)(2,1)S(1)}, bf16[32,4096]{1,0:T(8,128)(2,1)S(1)}, u32[]{:S(2)}, u32[]{:S(2)}) collective-permute-start(bf16[32,4096]{1,0:T(8,128)(2,1)S(1)} %slice.9), channel_id=1, source_target_pairs={{24,0},{135,1},{26,2},{1,3},{28,4},{3,5},{30,6},{5,7},{0,8},{143,9... | collective-permute-start | bytes 786440 | tf_op jit(solution)/shard_map/ppermute | solution.py:61
  26.8 4.1 %collective-permute-start.8 = (bf16[16,1024]{1,0:T(8,128)(2,1)S(1)}, bf16[16,1024]{1,0:T(8,128)(2,1)S(1)}, u32[]{:S(2)}, u32[]{:S(2)}) collective-permute-start(bf16[16,1024]{1,0:T(8,128)(2,1)S(1)} %get-tuple-element.50), channel_id=1, source_target_pairs={{24,0},{135,1},{26,2},{1,3},{28,4},{3,5},{30,6},{5,7},{0,8},{143,9... | collective-permute-start | bytes 98312 | tf_op jit(solution)/shard_map/ppermute | solution.py:61
  26.9 4.0 %collective-permute-start.7 = (bf16[16,1024]{1,0:T(8,128)(2,1)S(1)}, bf16[16,1024]{1,0:T(8,128)(2,1)S(1)}, u32[]{:S(2)}, u32[]{:S(2)}) collective-permute-start(bf16[16,1024]{1,0:T(8,128)(2,1)S(1)} %get-tuple-element.50), channel_id=1, source_target_pairs={{16,0},{5,1},{18,2},{135,3},{20,4},{129,5},{22,6},{3,7},{24,8},{13... | collective-permute-start | bytes 98312 | tf_op jit(solution)/shard_map/ppermute | solution.py:61
  28.1 3.1 %collective-permute-start.6 = (bf16[16,1024]{1,0:T(8,128)(2,1)S(1)}, bf16[16,1024]{1,0:T(8,128)(2,1)S(1)}, u32[]{:S(2)}, u32[]{:S(2)}) collective-permute-start(bf16[16,1024]{1,0:T(8,128)(2,1)S(1)} %get-tuple-element.50), channel_id=1, source_target_pairs={{8,0},{3,1},{10,2},{5,3},{12,4},{7,5},{14,6},{129,7},{16,8},{11,9}... | collective-permute-start | bytes 98312 | tf_op jit(solution)/shard_map/ppermute | solution.py:61
  33.0 24.8 %collective-permute-start.11 = (bf16[512,4096]{1,0:T(8,128)(2,1)}, bf16[512,4096]{1,0:T(8,128)(2,1)}, u32[]{:S(2)}, u32[]{:S(2)}) collective-permute-start(bf16[512,4096]{1,0:T(8,128)(2,1)} %refs_1_.1), channel_id=1, source_target_pairs={{1,0},{0,1},{3,2},{2,3},{5,4},{4,5},{7,6},{6,7},{9,8},{8,9},{11,10... | collective-permute-start | bytes 12582920 | tf_op jit(solution)/shard_map/ppermute | solution.py:61
  38.3 14.0 %collective-permute-start.14 = (bf16[128,4096]{1,0:T(8,128)(2,1)S(1)}, bf16[128,4096]{1,0:T(8,128)(2,1)}, u32[]{:S(2)}, u32[]{:S(2)}) collective-permute-start(bf16[128,4096]{1,0:T(8,128)(2,1)S(1)} %get-tuple-element.37.refs_3_), channel_id=1, source_target_pairs={{2,0},{9,1},{4,2},{11,3},{6,4},{13,5},{128,6},{15,7},{10,8},{17,9}... | collective-permute-start | bytes 3145736 | tf_op jit(solution)/shard_map/ppermute | solution.py:61
  39.2 15.3 %collective-permute-start.13 = (bf16[128,4096]{1,0:T(8,128)(2,1)S(1)}, bf16[128,4096]{1,0:T(8,128)(2,1)}, u32[]{:S(2)}, u32[]{:S(2)}) collective-permute-start(bf16[128,4096]{1,0:T(8,128)(2,1)S(1)} %get-tuple-element.38.refs_4_), channel_id=1, source_target_pairs={{134,0},{25,1},{0,2},{27,3},{2,4},{29,5},{4,6},{31,7},{142,8},{1,9... | collective-permute-start | bytes 3145736 | tf_op jit(solution)/shard_map/ppermute | solution.py:61
  39.8 29.2 %collective-permute-start.12 = (bf16[128,4096]{1,0:T(8,128)(2,1)S(1)}, bf16[128,4096]{1,0:T(8,128)(2,1)}, u32[]{:S(2)}, u32[]{:S(2)}) collective-permute-start(bf16[128,4096]{1,0:T(8,128)(2,1)S(1)} %get-tuple-element.37.refs_3_), channel_id=1, source_target_pairs={{134,0},{25,1},{0,2},{27,3},{2,4},{29,5},{4,6},{31,7},{142,8},{1,9... | collective-permute-start | bytes 3145736 | tf_op jit(solution)/shard_map/ppermute | solution.py:61
  39.8 29.2 %collective-permute-start.15 = (bf16[128,4096]{1,0:T(8,128)(2,1)S(1)}, bf16[128,4096]{1,0:T(8,128)(2,1)}, u32[]{:S(2)}, u32[]{:S(2)}) collective-permute-start(bf16[128,4096]{1,0:T(8,128)(2,1)S(1)} %get-tuple-element.38.refs_4_), channel_id=1, source_target_pairs={{2,0},{9,1},{4,2},{11,3},{6,4},{13,5},{128,6},{15,7},{10,8},{17,9}... | collective-permute-start | bytes 3145736 | tf_op jit(solution)/shard_map/ppermute | solution.py:61
  52.3 23.6 %collective-permute-start.16 = (bf16[128,4096]{1,0:T(8,128)(2,1)}, bf16[128,4096]{1,0:T(8,128)(2,1)}, u32[]{:S(2)}, u32[]{:S(2)}) collective-permute-start(bf16[128,4096]{1,0:T(8,128)(2,1)} %collective-permute-done.14.refs_5_), channel_id=1, source_target_pairs={{2,0},{9,1},{4,2},{11,3},{6,4},{13,5},{128,6},{15,7},{10,8},{17,9}... | collective-permute-start | bytes 3145736 | tf_op jit(solution)/shard_map/ppermute | solution.py:61
  54.5 22.5 %collective-permute-start.17 = (bf16[128,4096]{1,0:T(8,128)(2,1)}, bf16[128,4096]{1,0:T(8,128)(2,1)}, u32[]{:S(2)}, u32[]{:S(2)}) collective-permute-start(bf16[128,4096]{1,0:T(8,128)(2,1)} %collective-permute-done.13.refs_4_), channel_id=1, source_target_pairs={{134,0},{25,1},{0,2},{27,3},{2,4},{29,5},{4,6},{31,7},{142,8},{1,9... | collective-permute-start | bytes 3145736 | tf_op jit(solution)/shard_map/ppermute | solution.py:61
  65.4 19.3 %collective-permute-start.18 = (bf16[512,256]{1,0:T(8,128)(2,1)}, bf16[512,256]{1,0:T(8,128)(2,1)S(1)}, u32[]{:S(2)}, u32[]{:S(2)}) collective-permute-start(bf16[512,256]{1,0:T(8,128)(2,1)} %get-tuple-element.45), channel_id=1, source_target_pairs={{1,0},{0,1},{3,2},{2,3},{5,4},{4,5},{7,6},{6,7},{9,8},{8,9},{11,10... | collective-permute-start | bytes 786440 | tf_op jit(solution)/shard_map/ppermute | solution.py:61
  75.4 9.3 %collective-permute-start.19 = (bf16[512,256]{1,0:T(8,128)(2,1)S(1)}, bf16[512,256]{1,0:T(8,128)(2,1)S(1)}, u32[]{:S(2)}, u32[]{:S(2)}) collective-permute-start(bf16[512,256]{1,0:T(8,128)(2,1)S(1)} %get-tuple-element.46), channel_id=1, source_target_pairs={{1,0},{0,1},{3,2},{2,3},{5,4},{4,5},{7,6},{6,7},{9,8},{8,9},{11,10... | collective-permute-start | bytes 786440 | tf_op jit(solution)/shard_map/ppermute | solution.py:61
  80.9 4.7 %collective-permute-start.20 = (bf16[512,256]{1,0:T(8,128)(2,1)S(1)}, bf16[512,256]{1,0:T(8,128)(2,1)S(1)}, u32[]{:S(2)}, u32[]{:S(2)}) collective-permute-start(bf16[512,256]{1,0:T(8,128)(2,1)S(1)} %get-tuple-element.47), channel_id=1, source_target_pairs={{1,0},{0,1},{3,2},{2,3},{5,4},{4,5},{7,6},{6,7},{9,8},{8,9},{11,10... | collective-permute-start | bytes 786440 | tf_op jit(solution)/shard_map/ppermute | solution.py:61
  84.5 1.5 %collective-permute-start.21 = (bf16[512,256]{1,0:T(8,128)(2,1)S(1)}, bf16[512,256]{1,0:T(8,128)(2,1)S(1)}, u32[]{:S(2)}, u32[]{:S(2)}) collective-permute-start(bf16[512,256]{1,0:T(8,128)(2,1)S(1)} %get-tuple-element.48), channel_id=1, source_target_pairs={{1,0},{0,1},{3,2},{2,3},{5,4},{4,5},{7,6},{6,7},{9,8},{8,9},{11,10... | collective-permute-start | bytes 786440 | tf_op jit(solution)/shard_map/ppermute | solution.py:61

commit v12 on v11

--- a/solution.py
+++ b/solution.py
@@ -88,7 +88,7 @@
     return x, y, z, 1 - core
 
 
-def call(kernel, out_shape, inputs, scratch=(), limit=16, flops=0, smem=0, kept=(), resident=(), anywhere=()):
+def call(kernel, out_shape, inputs, scratch=(), limit=16, flops=0, smem=0, kept=(), resident=(), anywhere=(), out_space=pltpu.VMEM):
     specs = [pl.BlockSpec(memory_space=pltpu.SMEM)] * smem
     specs += [pl.BlockSpec(memory_space=pltpu.VMEM)] * (len(inputs) - smem + len(resident))
     specs += [pl.BlockSpec(memory_space=pltpu.HBM)] * len(kept)
@@ -102,7 +102,7 @@
         out_shape=out_shape,
         in_specs=specs,
         out_specs=jax.tree.map(
-            lambda _: pl.BlockSpec(memory_space=pltpu.VMEM),
+            lambda _: pl.BlockSpec(memory_space=out_space),
             out_shape,
             is_leaf=lambda v: not isinstance(v, tuple),
         ),
@@ -248,7 +248,9 @@
 
 
 def weave_kernel(where, *refs):
-    mine, theirs, out, held = refs[:4], refs[4:8], refs[8], refs[9]
+    mine, theirs = refs[:4], refs[4:8]
+    out, held, ready, sems = refs[8:]
+    copies = []
     core, my_start, their_start = where[0], where[1], where[2]
     for g in range(4):
         held[core, lax.rem(my_start + g, 4)] = mine[g][...]
@@ -257,8 +259,13 @@
         for z in range(4):
             left = held[0, z, :, y * TILE : (y + 1) * TILE]
             right = held[1, y, :, z * TILE : (z + 1) * TILE]
-            j = (y * 4 + z) * 2 * TILE
-            out[:, j : j + 2 * TILE] = jnp.concatenate([left, right], axis=1)
+            chip = y * 4 + z
+            ready[chip] = jnp.concatenate([left, right], axis=1)
+            cut = pl.ds(chip * 2 * TILE, 2 * TILE)
+            copies.append(pltpu.make_async_copy(ready.at[chip], out.at[:, cut], sems.at[chip]))
+            copies[-1].start()
+    for copy in copies:
+        copy.wait()
 
 
 def on_device(momentum, gradient, weight, activations):
@@ -308,10 +315,11 @@
 
     parts = [rounded.astype(F32)] + [fetch(rounded, along_x(n)).astype(F32) for n in (1, 2, -1)]
     sent = ((parts[0] + parts[2]) + (parts[1] + parts[3])).astype(BF16)
+    other = fetch(after(activations, ahead, behind, sent), sibling)
     total = sent.astype(F32) + fetch(after(sent, ahead, behind), far_z).astype(F32)
     halves_across = [fetch(ahead[: rows // 2], along(0, 1)), fetch(behind[rows // 2 :], along(0, -1))]
 
-    sent = total.astype(BF16)
+    sent = after(total.astype(BF16), other)
     line = jnp.concatenate([sent] + [fetch(sent, along(0, n)) for n in (1, 2, -1)], axis=0)
     direction = call(
         direction_kernel,
@@ -326,7 +334,6 @@
         (line, ahead, behind, *halves_across),
         resident=(cols, back, held_weight),
     )
-    other = fetch(after(activations, top), sibling)
     new_momentum = call(
         residual_kernel,
         shape(momentum.shape, F32),
@@ -389,8 +396,13 @@
         weave_kernel,
         shape((tokens, 32 * rows), BF16),
         (where, *mine, *theirs),
-        (pltpu.VMEM((2, 4, tokens, 4 * rows), BF16),),
+        (
+            pltpu.VMEM((2, 4, tokens, 4 * rows), BF16),
+            pltpu.VMEM((16, tokens, 2 * rows), BF16),
+            pltpu.SemaphoreType.DMA((16,)),
+        ),
         smem=1,
+        out_space=pl.ANY,
     )
     return (new_momentum, direction, projected)
 

time: 88.9 us -> 90.6 us (1.019)
  local copies, waits for them, and re-layouts: 0.04 us -> 4.18 us
  waiting for transfers between devices: 23 us -> 19.5 us
  Pallas kernels: 28.8 us -> 29.8 us
    unnamed x0 -> x4, local copies, waits for them, and re-layouts: none -> 4.14 us
    ppermute x22, waiting for transfers between devices: 23 us -> 19.5 us  [fetch(): lax.ppermute(value, AXES, [(place(*source(*spot(i))), i) for i in range(2...]
    pallas_call x8, Pallas kernels: 28.8 us -> 29.8 us  [call(): pl.pallas_call(kernel, out_shape=out_shape, in_specs=specs, out_specs=jax...]
  transfers between devices with their start and end apart: 22 -> 22, of which waited for: 10 -> 9; matrix products, arithmetic and copies ran while one was open for 0% -> 0% of each run, Pallas kernels for 24% -> 25%
where the time goes in v12:
time: 90.6 us; the launch traced here: 90.5 us
  starting transfers between devices  35.9 us (40%)
  Pallas kernels  29.8 us (33%)
  waiting for transfers between devices  19.5 us (22%)
  local copies, waits for them, and re-layouts  4.18 us (5%)
  between operations  0.94 us (1%)
    ppermute x22, starting transfers between devices, fetch(): lax.ppermute(value, AXES, [(place(*source(*spot(i))), i) for i in range(2...  35.9 us
    pallas_call x8, Pallas kernels, call(): pl.pallas_call(kernel, out_shape=out_shape, in_specs=specs, out_specs=jax...  29.8 us
    ppermute x22, waiting for transfers between devices, fetch(): lax.ppermute(value, AXES, [(place(*source(*spot(i))), i) for i in range(2...  19.5 us
    unnamed x4, local copies, waits for them, and re-layouts  4.14 us
  transfers between devices with their start and end apart: 22, of which 9 were waited for; matrix products, arithmetic and copies ran while one was open for 0% of the time, Pallas kernels for 25%

profile of v12, /device:TPU:1, one launch (start us, length us, event | category | flops | bytes accessed | tf_op | source)
XLA Modules:
  0.0 90.5 jit_solution(7327552652457443797)
XLA Ops:
  0.6 3.1 %shard_map.94 = (f32[16,1024]{1,0:T(8,128)S(1)}, bf16[16,1024]{1,0:T(8,128)(2,1)S(1)}, f32[8,64,512]{2,1,0:T(8,128)S(1)}, bf16[1024,128]{1,0:T(8,128)(2,1)S(1)},...) custom-call(f32[1,64,4096]{2,1,0:T(8,128)} %momentum.1, bf16[1,64,4096]{2,1,0:T(8,128)(2,1)} %gradient.1, ...), custom_call_target="tpu_custom_call" | custom-call | bytes 2371584 | tf_op jit(solution)/shard_map/pallas_call | solution.py:100
  3.7 6.5 %collective-permute-start.3 = (bf16[64,4096]{1,0:T(8,128)(2,1)}, bf16[64,4096]{1,0:T(8,128)(2,1)S(1)}, u32[]{:S(2)}, u32[]{:S(2)}) collective-permute-start(bf16[64,4096]{1,0:T(8,128)(2,1)} %weight_in.1), channel_id=1, source_target_pairs={{8,0},{3,1},{10,2},{5,3},{12,4},{7,5},{14,6},{129,7},{16,8},{11,9}... | collective-permute-start | bytes 1572872 | tf_op jit(solution)/shard_map/ppermute | solution.py:61
  11.4 1.5 %collective-permute-start.1 = (bf16[16,1024]{1,0:T(8,128)(2,1)S(1)}, bf16[16,1024]{1,0:T(8,128)(2,1)S(1)}, u32[]{:S(2)}, u32[]{:S(2)}) collective-permute-start(bf16[16,1024]{1,0:T(8,128)(2,1)S(1)} %get-tuple-element.28), channel_id=1, source_target_pairs={{32,0},{33,1},{34,2},{35,3},{36,4},{37,5},{38,6},{39,7},{40,8},{41... | collective-permute-start | bytes 98312 | tf_op jit(solution)/shard_map/ppermute | solution.py:61
  12.9 1.5 %collective-permute-start = (bf16[16,1024]{1,0:T(8,128)(2,1)S(1)}, bf16[16,1024]{1,0:T(8,128)(2,1)S(1)}, u32[]{:S(2)}, u32[]{:S(2)}) collective-permute-start(bf16[16,1024]{1,0:T(8,128)(2,1)S(1)} %get-tuple-element.28), channel_id=1, source_target_pairs={{64,0},{65,1},{66,2},{67,3},{68,4},{69,5},{70,6},{71,7},{72,8},{73... | collective-permute-start | bytes 98312 | tf_op jit(solution)/shard_map/ppermute | solution.py:61
  14.5 3.1 %collective-permute-done = bf16[16,1024]{1,0:T(8,128)(2,1)S(1)} collective-permute-done((bf16[16,1024]{1,0:T(8,128)(2,1)S(1)}, bf16[16,1024]{1,0:T(8,128)(2,1)S(1)}, u32[]{:S(2)}, u32[]{:S(2)}) %collective-permute-start) | collective-permute-done | bytes 32800 | tf_op jit(solution)/shard_map/ppermute | solution.py:61
  17.6 2.1 %collective-permute-done.4.behind = bf16[64,4096]{1,0:T(8,128)(2,1)S(1)} collective-permute-done((bf16[64,4096]{1,0:T(8,128)(2,1)}, bf16[64,4096]{1,0:T(8,128)(2,1)S(1)}, u32[]{:S(2)}, u32[]{:S(2)}) %collective-permute-start.4) | collective-permute-done | bytes 524320 | tf_op jit(solution)/shard_map/ppermute | solution.py:61
  19.6 6.2 %collective-permute-start.5 = (bf16[16,1024]{1,0:T(8,128)(2,1)S(1)}, bf16[16,1024]{1,0:T(8,128)(2,1)S(1)}, u32[]{:S(2)}, u32[]{:S(2)}) collective-permute-start(bf16[16,1024]{1,0:T(8,128)(2,1)S(1)} %add_convert_fusion), channel_id=1, source_target_pairs={{128,0},{129,1},{130,2},{131,3},{132,4},{133,5},{134,6},{135,7},{1... | collective-permute-start | bytes 98312 | tf_op jit(solution)/shard_map/ppermute | solution.py:61
  25.9 1.5 %collective-permute-start.11 = (bf16[32,4096]{1,0:T(8,128)(2,1)S(1)}, bf16[32,4096]{1,0:T(8,128)(2,1)S(1)}, u32[]{:S(2)}, u32[]{:S(2)}) collective-permute-start(bf16[32,4096]{1,0:T(8,128)(2,1)S(1)} %slice.9), channel_id=1, source_target_pairs={{24,0},{135,1},{26,2},{1,3},{28,4},{3,5},{30,6},{5,7},{0,8},{143,9... | collective-permute-start | bytes 786440 | tf_op jit(solution)/shard_map/ppermute | solution.py:61
  27.6 1.9 %copy-done = bf16[512,4096]{1,0:T(8,128)(2,1)} copy-done((bf16[512,4096]{1,0:T(8,128)(2,1)}, bf16[512,4096]{1,0:T(8,128)(2,1)S(1)}, u32[]{:S(2)}) %copy-start) | copy-done | bytes 4194328
  30.3 4.3 %collective-permute-start.8 = (bf16[16,1024]{1,0:T(8,128)(2,1)S(1)}, bf16[16,1024]{1,0:T(8,128)(2,1)S(1)}, u32[]{:S(2)}, u32[]{:S(2)}) collective-permute-start(bf16[16,1024]{1,0:T(8,128)(2,1)S(1)} %get-tuple-element.32), channel_id=1, source_target_pairs={{16,0},{5,1},{18,2},{135,3},{20,4},{129,5},{22,6},{3,7},{24,8},{13... | collective-permute-start | bytes 98312 | tf_op jit(solution)/shard_map/ppermute | solution.py:61
  35.6 1.7 %collective-permute-done.7 = bf16[16,1024]{1,0:T(8,128)(2,1)S(1)} collective-permute-done((bf16[16,1024]{1,0:T(8,128)(2,1)S(1)}, bf16[16,1024]{1,0:T(8,128)(2,1)S(1)}, u32[]{:S(2)}, u32[]{:S(2)}) %collective-permute-start.7) | collective-permute-done | bytes 32800 | tf_op jit(solution)/shard_map/ppermute | solution.py:61
  37.4 2.0 %shard_map.95 = (bf16[128,4096]{1,0:T(8,128)(2,1)}, bf16[128,4096]{1,0:T(8,128)(2,1)S(1)}) custom-call(bf16[64,1024]{1,0:T(8,128)(2,1)S(1)} %pad_maximum_fusion.bands, bf16[64,4096]{1,0:T(8,128)(2,1)S(1)} %collective-permute-done.3.ahead, bf16[64,4096]{1,0:T(8,128)(2,1)S(1)} %collective-permute-done.4.behind, ...), custom_call_target="tpu_custom_call" | custom-call | bytes 2496512 | tf_op jit(solution)/shard_map/pallas_call | solution.py:100
  40.9 2.6 %collective-permute-start.15 = (bf16[128,4096]{1,0:T(8,128)(2,1)S(1)}, bf16[128,4096]{1,0:T(8,128)(2,1)}, u32[]{:S(2)}, u32[]{:S(2)}) collective-permute-start(bf16[128,4096]{1,0:T(8,128)(2,1)S(1)} %get-tuple-element.40.refs_4_), channel_id=1, source_target_pairs={{2,0},{9,1},{4,2},{11,3},{6,4},{13,5},{128,6},{15,7},{10,8},{17,9}... | collective-permute-start | bytes 3145736 | tf_op jit(solution)/shard_map/ppermute | solution.py:61
  43.5 10.1 %collective-permute-done.14.refs_5_ = bf16[128,4096]{1,0:T(8,128)(2,1)} collective-permute-done((bf16[128,4096]{1,0:T(8,128)(2,1)}, bf16[128,4096]{1,0:T(8,128)(2,1)}, u32[]{:S(2)}, u32[]{:S(2)}) %collective-permute-start.14) | collective-permute-done | bytes 1048608 | tf_op jit(solution)/shard_map/ppermute | solution.py:61
  53.6 2.3 %collective-permute-start.16 = (bf16[128,4096]{1,0:T(8,128)(2,1)}, bf16[128,4096]{1,0:T(8,128)(2,1)S(1)}, u32[]{:S(2)}, u32[]{:S(2)}) collective-permute-start(bf16[128,4096]{1,0:T(8,128)(2,1)} %collective-permute-done.14.refs_5_), channel_id=1, source_target_pairs={{2,0},{9,1},{4,2},{11,3},{6,4},{13,5},{128,6},{15,7},{10,8},{17,9}... | collective-permute-start | bytes 3145736 | tf_op jit(solution)/shard_map/ppermute | solution.py:61
  56.0 1.7 %shard_map.97 = f32[64,4096]{1,0:T(8,128)} custom-call(f32[16,1024]{1,0:T(8,128)S(1)} %get-tuple-element.51.total, bf16[1024,128]{1,0:T(8,128)(2,1)S(1)} %get-tuple-element.33.cols, bf16[64,48]{1,0:T(8,128)(2,1)S(1)} %get-tuple-element.34.back), custom_call_target="tpu_custom_call" | custom-call | bytes 333824 | tf_op jit(solution)/shard_map/pallas_call | solution.py:100
  57.6 1.6 %shard_map.96 = f32[1,64,4096]{2,1,0:T(8,128)} custom-call(f32[16,1024]{1,0:T(8,128)S(1)} %get-tuple-element.37.bands, f32[8,64,512]{2,1,0:T(8,128)S(1)} %get-tuple-element.38.mixed, bf16[1024,128]{1,0:T(8,128)(2,1)S(1)} %get-tuple-element.33.cols, bf16[64,48]{1,0:T(8,128)(2,1)S(1)} %get-tuple-element.34.back), custom_call_target="tpu_custom_call" | custom-call | bytes 1382400 | tf_op jit(solution)/shard_map/pallas_call | solution.py:100
  59.3 2.2 %copy-done.1 = bf16[512,4096]{1,0:T(8,128)(2,1)S(1)} copy-done((bf16[512,4096]{1,0:T(8,128)(2,1)S(1)}, bf16[512,4096]{1,0:T(8,128)(2,1)}, u32[]{:S(2)}) %copy-start.1) | copy-done | bytes 4194328
  61.5 7.8 %shard_map.98 = (bf16[512,256]{1,0:T(8,128)(2,1)S(1)}, bf16[512,256]{1,0:T(8,128)(2,1)}, bf16[512,4096]{1,0:T(8,128)(2,1)S(1)}, bf16[512,4096]{1,0:T(8,128)(2,1)S(1)}) custom-call(s32[1]{0:T(128)} %bitcast.2.refs_0_, bf16[512,4096]{1,0:T(8,128)(2,1)} %refs_1_.1, bf16[512,4096]{1,0:T(8,128)(2,1)S(1)} %copy-done.1, ...), custom_call_target="tpu_custom_call" | custom-call | flops 2147483648 | bytes 10485764 | tf_op jit(solution)/shard_map/pallas_call | solution.py:100
  69.3 4.0 %collective-permute-start.18 = (bf16[512,256]{1,0:T(8,128)(2,1)}, bf16[512,256]{1,0:T(8,128)(2,1)S(1)}, u32[]{:S(2)}, u32[]{:S(2)}) collective-permute-start(bf16[512,256]{1,0:T(8,128)(2,1)} %get-tuple-element.47), channel_id=1, source_target_pairs={{1,0},{0,1},{3,2},{2,3},{5,4},{4,5},{7,6},{6,7},{9,8},{8,9},{11,10... | collective-permute-start | bytes 786440 | tf_op jit(solution)/shard_map/ppermute | solution.py:61
  73.3 7.1 %shard_map.99 = (bf16[512,256]{1,0:T(8,128)(2,1)S(1)}, bf16[512,256]{1,0:T(8,128)(2,1)S(1)}, bf16[512,256]{1,0:T(8,128)(2,1)S(1)}, bf16[512,256]{1,0:T(8,128)(2,1)}) custom-call(s32[1]{0:T(128)} %bitcast.2.refs_0_, bf16[512,4096]{1,0:T(8,128)(2,1)S(1)} %get-tuple-element.42.refs_1_, bf16[512,4096]{1,0:T(8,128)(2,1)S(1)} %get-tuple-element.43.refs_2_, ...), custom_call_target="tpu_custom_call" | custom-call | flops 4294967296 | bytes 12582916 | tf_op jit(solution)/shard_map/pallas_call | solution.py:100
  81.0 4.4 %shard_map.100 = (bf16[512,256]{1,0:T(8,128)(2,1)S(1)}, bf16[512,256]{1,0:T(8,128)(2,1)}) custom-call(s32[1]{0:T(128)} %bitcast.2.refs_0_, bf16[512,4096]{1,0:T(8,128)(2,1)S(1)} %get-tuple-element.42.refs_1_, bf16[512,4096]{1,0:T(8,128)(2,1)S(1)} %get-tuple-element.43.refs_2_, bf16[128,4096]{1,0:T(8,128)(2,1)S(1)} %collective-permute-done.16.refs_3_, ...), custom_call_target="tpu_custom_call" | custom-call | flops 2147483648 | bytes 10485764 | tf_op jit(solution)/shard_map/pallas_call | solution.py:100
  86.8 1.3 %collective-permute-done.20.refs_6_ = bf16[512,256]{1,0:T(8,128)(2,1)S(1)} collective-permute-done((bf16[512,256]{1,0:T(8,128)(2,1)}, bf16[512,256]{1,0:T(8,128)(2,1)S(1)}, u32[]{:S(2)}, u32[]{:S(2)}) %collective-permute-start.20) | collective-permute-done | bytes 262176 | tf_op jit(solution)/shard_map/ppermute | solution.py:61
  88.1 2.2 %shard_map.101 = bf16[512,2048]{1,0:T(8,128)(2,1)} custom-call(s32[3]{0:T(128)S(1)} %pad_add_fusion.where, bf16[512,256]{1,0:T(8,128)(2,1)S(1)} %get-tuple-element.41.refs_0_, bf16[512,256]{1,0:T(8,128)(2,1)S(1)} %get-tuple-element.44.refs_1_, bf16[512,256]{1,0:T(8,128)(2,1)S(1)} %get-tuple-element.45.refs_2_, ...), custom_call_target="tpu_custom_call" | custom-call | bytes 2097164 | tf_op jit(solution)/shard_map/pallas_call | solution.py:100
  (38 shorter events, 6.8 us)
Async XLA Ops:
  3.7 13.9 %collective-permute-start.3 = (bf16[64,4096]{1,0:T(8,128)(2,1)}, bf16[64,4096]{1,0:T(8,128)(2,1)S(1)}, u32[]{:S(2)}, u32[]{:S(2)}) collective-permute-start(bf16[64,4096]{1,0:T(8,128)(2,1)} %weight_in.1), channel_id=1, source_target_pairs={{8,0},{3,1},{10,2},{5,3},{12,4},{7,5},{14,6},{129,7},{16,8},{11,9}... | collective-permute-start | bytes 1572872 | tf_op jit(solution)/shard_map/ppermute | solution.py:61
  10.2 9.5 %collective-permute-start.4 = (bf16[64,4096]{1,0:T(8,128)(2,1)}, bf16[64,4096]{1,0:T(8,128)(2,1)S(1)}, u32[]{:S(2)}, u32[]{:S(2)}) collective-permute-start(bf16[64,4096]{1,0:T(8,128)(2,1)} %weight_in.1), channel_id=1, source_target_pairs={{24,0},{135,1},{26,2},{1,3},{28,4},{3,5},{30,6},{5,7},{0,8},{143,9... | collective-permute-start | bytes 1572872 | tf_op jit(solution)/shard_map/ppermute | solution.py:61
  10.2 4.3 %collective-permute-start.2 = (bf16[16,1024]{1,0:T(8,128)(2,1)S(1)}, bf16[16,1024]{1,0:T(8,128)(2,1)S(1)}, u32[]{:S(2)}, u32[]{:S(2)}) collective-permute-start(bf16[16,1024]{1,0:T(8,128)(2,1)S(1)} %get-tuple-element.28), channel_id=1, source_target_pairs={{96,0},{97,1},{98,2},{99,3},{100,4},{101,5},{102,6},{103,7},{104,8... | collective-permute-start | bytes 98312 | tf_op jit(solution)/shard_map/ppermute | solution.py:61
  11.4 3.1 %collective-permute-start.1 = (bf16[16,1024]{1,0:T(8,128)(2,1)S(1)}, bf16[16,1024]{1,0:T(8,128)(2,1)S(1)}, u32[]{:S(2)}, u32[]{:S(2)}) collective-permute-start(bf16[16,1024]{1,0:T(8,128)(2,1)S(1)} %get-tuple-element.28), channel_id=1, source_target_pairs={{32,0},{33,1},{34,2},{35,3},{36,4},{37,5},{38,6},{39,7},{40,8},{41... | collective-permute-start | bytes 98312 | tf_op jit(solution)/shard_map/ppermute | solution.py:61
  12.9 4.7 %collective-permute-start = (bf16[16,1024]{1,0:T(8,128)(2,1)S(1)}, bf16[16,1024]{1,0:T(8,128)(2,1)S(1)}, u32[]{:S(2)}, u32[]{:S(2)}) collective-permute-start(bf16[16,1024]{1,0:T(8,128)(2,1)S(1)} %get-tuple-element.28), channel_id=1, source_target_pairs={{64,0},{65,1},{66,2},{67,3},{68,4},{69,5},{70,6},{71,7},{72,8},{73... | collective-permute-start | bytes 98312 | tf_op jit(solution)/shard_map/ppermute | solution.py:61
  19.6 8.0 %collective-permute-start.6 = (bf16[512,4096]{1,0:T(8,128)(2,1)}, bf16[512,4096]{1,0:T(8,128)(2,1)S(1)}, u32[]{:S(2)}, u32[]{:S(2)}) collective-permute-start(bf16[512,4096]{1,0:T(8,128)(2,1)} %refs_1_.1), channel_id=1, source_target_pairs={{1,0},{0,1},{3,2},{2,3},{5,4},{4,5},{7,6},{6,7},{9,8},{8,9},{11,10... | collective-permute-start | bytes 12582920 | tf_op jit(solution)/shard_map/ppermute | solution.py:61
  19.6 7.9 %collective-permute-start.5 = (bf16[16,1024]{1,0:T(8,128)(2,1)S(1)}, bf16[16,1024]{1,0:T(8,128)(2,1)S(1)}, u32[]{:S(2)}, u32[]{:S(2)}) collective-permute-start(bf16[16,1024]{1,0:T(8,128)(2,1)S(1)} %add_convert_fusion), channel_id=1, source_target_pairs={{128,0},{129,1},{130,2},{131,3},{132,4},{133,5},{134,6},{135,7},{1... | collective-permute-start | bytes 98312 | tf_op jit(solution)/shard_map/ppermute | solution.py:61
  25.8 11.6 %collective-permute-start.10 = (bf16[32,4096]{1,0:T(8,128)(2,1)S(1)}, bf16[32,4096]{1,0:T(8,128)(2,1)S(1)}, u32[]{:S(2)}, u32[]{:S(2)}) collective-permute-start(bf16[32,4096]{1,0:T(8,128)(2,1)S(1)} %slice.8), channel_id=1, source_target_pairs={{8,0},{3,1},{10,2},{5,3},{12,4},{7,5},{14,6},{129,7},{16,8},{11,9}... | collective-permute-start | bytes 786440 | tf_op jit(solution)/shard_map/ppermute | solution.py:61
  25.9 11.5 %collective-permute-start.11 = (bf16[32,4096]{1,0:T(8,128)(2,1)S(1)}, bf16[32,4096]{1,0:T(8,128)(2,1)S(1)}, u32[]{:S(2)}, u32[]{:S(2)}) collective-permute-start(bf16[32,4096]{1,0:T(8,128)(2,1)S(1)} %slice.9), channel_id=1, source_target_pairs={{24,0},{135,1},{26,2},{1,3},{28,4},{3,5},{30,6},{5,7},{0,8},{143,9... | collective-permute-start | bytes 786440 | tf_op jit(solution)/shard_map/ppermute | solution.py:61
  27.6 2.0 %copy-start = (bf16[512,4096]{1,0:T(8,128)(2,1)}, bf16[512,4096]{1,0:T(8,128)(2,1)S(1)}, u32[]{:S(2)}) copy-start(bf16[512,4096]{1,0:T(8,128)(2,1)S(1)} %collective-permute-done.6.refs_2_) | copy-start | bytes 12582916
  29.6 5.5 %collective-permute-start.9 = (bf16[16,1024]{1,0:T(8,128)(2,1)S(1)}, bf16[16,1024]{1,0:T(8,128)(2,1)S(1)}, u32[]{:S(2)}, u32[]{:S(2)}) collective-permute-start(bf16[16,1024]{1,0:T(8,128)(2,1)S(1)} %get-tuple-element.32), channel_id=1, source_target_pairs={{24,0},{135,1},{26,2},{1,3},{28,4},{3,5},{30,6},{5,7},{0,8},{143,9... | collective-permute-start | bytes 98312 | tf_op jit(solution)/shard_map/ppermute | solution.py:61
  30.3 5.3 %collective-permute-start.8 = (bf16[16,1024]{1,0:T(8,128)(2,1)S(1)}, bf16[16,1024]{1,0:T(8,128)(2,1)S(1)}, u32[]{:S(2)}, u32[]{:S(2)}) collective-permute-start(bf16[16,1024]{1,0:T(8,128)(2,1)S(1)} %get-tuple-element.32), channel_id=1, source_target_pairs={{16,0},{5,1},{18,2},{135,3},{20,4},{129,5},{22,6},{3,7},{24,8},{13... | collective-permute-start | bytes 98312 | tf_op jit(solution)/shard_map/ppermute | solution.py:61
  34.6 2.8 %collective-permute-start.7 = (bf16[16,1024]{1,0:T(8,128)(2,1)S(1)}, bf16[16,1024]{1,0:T(8,128)(2,1)S(1)}, u32[]{:S(2)}, u32[]{:S(2)}) collective-permute-start(bf16[16,1024]{1,0:T(8,128)(2,1)S(1)} %get-tuple-element.32), channel_id=1, source_target_pairs={{8,0},{3,1},{10,2},{5,3},{12,4},{7,5},{14,6},{129,7},{16,8},{11,9}... | collective-permute-start | bytes 98312 | tf_op jit(solution)/shard_map/ppermute | solution.py:61
  39.4 14.3 %collective-permute-start.14 = (bf16[128,4096]{1,0:T(8,128)(2,1)}, bf16[128,4096]{1,0:T(8,128)(2,1)}, u32[]{:S(2)}, u32[]{:S(2)}) collective-permute-start(bf16[128,4096]{1,0:T(8,128)(2,1)} %get-tuple-element.39.refs_3_), channel_id=1, source_target_pairs={{2,0},{9,1},{4,2},{11,3},{6,4},{13,5},{128,6},{15,7},{10,8},{17,9}... | collective-permute-start | bytes 3145736 | tf_op jit(solution)/shard_map/ppermute | solution.py:61
  40.5 15.5 %collective-permute-start.13 = (bf16[128,4096]{1,0:T(8,128)(2,1)S(1)}, bf16[128,4096]{1,0:T(8,128)(2,1)}, u32[]{:S(2)}, u32[]{:S(2)}) collective-permute-start(bf16[128,4096]{1,0:T(8,128)(2,1)S(1)} %get-tuple-element.40.refs_4_), channel_id=1, source_target_pairs={{134,0},{25,1},{0,2},{27,3},{2,4},{29,5},{4,6},{31,7},{142,8},{1,9... | collective-permute-start | bytes 3145736 | tf_op jit(solution)/shard_map/ppermute | solution.py:61
  40.8 32.5 %collective-permute-start.12 = (bf16[128,4096]{1,0:T(8,128)(2,1)}, bf16[128,4096]{1,0:T(8,128)(2,1)}, u32[]{:S(2)}, u32[]{:S(2)}) collective-permute-start(bf16[128,4096]{1,0:T(8,128)(2,1)} %get-tuple-element.39.refs_3_), channel_id=1, source_target_pairs={{134,0},{25,1},{0,2},{27,3},{2,4},{29,5},{4,6},{31,7},{142,8},{1,9... | collective-permute-start | bytes 3145736 | tf_op jit(solution)/shard_map/ppermute | solution.py:61
  40.9 32.4 %collective-permute-start.15 = (bf16[128,4096]{1,0:T(8,128)(2,1)S(1)}, bf16[128,4096]{1,0:T(8,128)(2,1)}, u32[]{:S(2)}, u32[]{:S(2)}) collective-permute-start(bf16[128,4096]{1,0:T(8,128)(2,1)S(1)} %get-tuple-element.40.refs_4_), channel_id=1, source_target_pairs={{2,0},{9,1},{4,2},{11,3},{6,4},{13,5},{128,6},{15,7},{10,8},{17,9}... | collective-permute-start | bytes 3145736 | tf_op jit(solution)/shard_map/ppermute | solution.py:61
  53.6 27.4 %collective-permute-start.16 = (bf16[128,4096]{1,0:T(8,128)(2,1)}, bf16[128,4096]{1,0:T(8,128)(2,1)S(1)}, u32[]{:S(2)}, u32[]{:S(2)}) collective-permute-start(bf16[128,4096]{1,0:T(8,128)(2,1)} %collective-permute-done.14.refs_5_), channel_id=1, source_target_pairs={{2,0},{9,1},{4,2},{11,3},{6,4},{13,5},{128,6},{15,7},{10,8},{17,9}... | collective-permute-start | bytes 3145736 | tf_op jit(solution)/shard_map/ppermute | solution.py:61
  56.0 25.0 %collective-permute-start.17 = (bf16[128,4096]{1,0:T(8,128)(2,1)}, bf16[128,4096]{1,0:T(8,128)(2,1)}, u32[]{:S(2)}, u32[]{:S(2)}) collective-permute-start(bf16[128,4096]{1,0:T(8,128)(2,1)} %collective-permute-done.13.refs_4_), channel_id=1, source_target_pairs={{134,0},{25,1},{0,2},{27,3},{2,4},{29,5},{4,6},{31,7},{142,8},{1,9... | collective-permute-start | bytes 3145736 | tf_op jit(solution)/shard_map/ppermute | solution.py:61
  59.3 2.2 %copy-start.1 = (bf16[512,4096]{1,0:T(8,128)(2,1)S(1)}, bf16[512,4096]{1,0:T(8,128)(2,1)}, u32[]{:S(2)}) copy-start(bf16[512,4096]{1,0:T(8,128)(2,1)} %copy-done) | copy-start | bytes 12582916
  69.3 17.5 %collective-permute-start.18 = (bf16[512,256]{1,0:T(8,128)(2,1)}, bf16[512,256]{1,0:T(8,128)(2,1)S(1)}, u32[]{:S(2)}, u32[]{:S(2)}) collective-permute-start(bf16[512,256]{1,0:T(8,128)(2,1)} %get-tuple-element.47), channel_id=1, source_target_pairs={{1,0},{0,1},{3,2},{2,3},{5,4},{4,5},{7,6},{6,7},{9,8},{8,9},{11,10... | collective-permute-start | bytes 786440 | tf_op jit(solution)/shard_map/ppermute | solution.py:61
  80.4 6.4 %collective-permute-start.19 = (bf16[512,256]{1,0:T(8,128)(2,1)}, bf16[512,256]{1,0:T(8,128)(2,1)S(1)}, u32[]{:S(2)}, u32[]{:S(2)}) collective-permute-start(bf16[512,256]{1,0:T(8,128)(2,1)} %get-tuple-element.48), channel_id=1, source_target_pairs={{1,0},{0,1},{3,2},{2,3},{5,4},{4,5},{7,6},{6,7},{9,8},{8,9},{11,10... | collective-permute-start | bytes 786440 | tf_op jit(solution)/shard_map/ppermute | solution.py:61
  80.5 6.2 %collective-permute-start.21 = (bf16[512,256]{1,0:T(8,128)(2,1)S(1)}, bf16[512,256]{1,0:T(8,128)(2,1)S(1)}, u32[]{:S(2)}, u32[]{:S(2)}) collective-permute-start(bf16[512,256]{1,0:T(8,128)(2,1)S(1)} %get-tuple-element.50), channel_id=1, source_target_pairs={{1,0},{0,1},{3,2},{2,3},{5,4},{4,5},{7,6},{6,7},{9,8},{8,9},{11,10... | collective-permute-start | bytes 786440 | tf_op jit(solution)/shard_map/ppermute | solution.py:61
  85.4 2.6 %collective-permute-start.20 = (bf16[512,256]{1,0:T(8,128)(2,1)}, bf16[512,256]{1,0:T(8,128)(2,1)S(1)}, u32[]{:S(2)}, u32[]{:S(2)}) collective-permute-start(bf16[512,256]{1,0:T(8,128)(2,1)} %get-tuple-element.49), channel_id=1, source_target_pairs={{1,0},{0,1},{3,2},{2,3},{5,4},{4,5},{7,6},{6,7},{9,8},{8,9},{11,10... | collective-permute-start | bytes 786440 | tf_op jit(solution)/shard_map/ppermute | solution.py:61

commit v13 on v12

--- a/solution.py
+++ b/solution.py
@@ -247,6 +247,26 @@
             outs[2 * g + t // per][cut] = product.astype(BF16)
 
 
+def far_kernel(first, tokens, upper, lower, out, fresh, sems):
+    copies = []
+    for f in range(4):
+        at = pl.ds(pl.multiple_of(lax.rem(first[0] + f, 4) * TILE, TILE), TILE)
+        source = (upper, lower)[f // 2].at[pl.ds(f % 2 * TILE, TILE)]
+        copies.append(pltpu.make_async_copy(source, fresh.at[at], sems.at[f]))
+        copies[f].start()
+    for copy in copies:
+        copy.wait()
+    own_kernel(tokens, fresh, out)
+
+
+def own_kernel(tokens, fresh, out):
+    rows = fresh.shape[0]
+    for t in range(tokens.shape[0] // rows):
+        cut = slice(t * rows, (t + 1) * rows)
+        product = lax.dot_general(tokens[cut], fresh[...], NT, preferred_element_type=F32)
+        out[cut] = product.astype(BF16)
+
+
 def weave_kernel(where, *refs):
     mine, theirs = refs[:4], refs[4:8]
     out, held, ready, sems = refs[8:]
@@ -315,11 +335,10 @@
 
     parts = [rounded.astype(F32)] + [fetch(rounded, along_x(n)).astype(F32) for n in (1, 2, -1)]
     sent = ((parts[0] + parts[2]) + (parts[1] + parts[3])).astype(BF16)
-    other = fetch(after(activations, ahead, behind, sent), sibling)
     total = sent.astype(F32) + fetch(after(sent, ahead, behind), far_z).astype(F32)
     halves_across = [fetch(ahead[: rows // 2], along(0, 1)), fetch(behind[rows // 2 :], along(0, -1))]
 
-    sent = after(total.astype(BF16), other)
+    sent = total.astype(BF16)
     line = jnp.concatenate([sent] + [fetch(sent, along(0, n)) for n in (1, 2, -1)], axis=0)
     direction = call(
         direction_kernel,
@@ -334,6 +353,7 @@
         (line, ahead, behind, *halves_across),
         resident=(cols, back, held_weight),
     )
+    other = fetch(after(activations, top), sibling)
     new_momentum = call(
         residual_kernel,
         shape(momentum.shape, F32),
@@ -386,7 +406,19 @@
 
     *results, activations_in, other_in = forward([0], True)
     results += forward([3, 1], False)
-    results += forward([2], False)
+    flops = 2 * tokens * 4 * rows * width
+    far_other, fresh = call(
+        far_kernel,
+        (block, pltpu.VMEM((4 * rows, width), BF16)),
+        [first[None]],
+        (pltpu.SemaphoreType.DMA((4,)),),
+        flops=flops,
+        smem=1,
+        resident=(other_in,),
+        anywhere=(far_top, far_bottom),
+    )
+    far_own = call(own_kernel, block, (), flops=flops, resident=(activations_in, fresh))
+    results += (far_own, far_other)
     mine, theirs = [None] * 4, [None] * 4
     for n, g in enumerate((0, 3, 1, 2)):
         mine[g] = results[2 * n]

time: 90.6 us -> 97.3 us (1.074)
  local copies, waits for them, and re-layouts: 4.18 us -> 9.89 us
  starting transfers between devices: 35.9 us -> 33.5 us
  Pallas kernels: 29.8 us -> 31.5 us
  waiting for transfers between devices: 19.5 us -> 20.9 us
    unnamed x4 -> x20, local copies, waits for them, and re-layouts: 4.14 us -> 9.85 us
    ppermute x22, starting transfers between devices: 35.9 us -> 33.5 us  [fetch(): lax.ppermute(value, AXES, [(place(*source(*spot(i))), i) for i in range(2...]
    pallas_call x8 -> x9, Pallas kernels: 29.8 us -> 31.5 us  [call(): pl.pallas_call(kernel, out_shape=out_shape, in_specs=specs, out_specs=jax...]
    ppermute x22, waiting for transfers between devices: 19.5 us -> 20.9 us  [fetch(): lax.ppermute(value, AXES, [(place(*source(*spot(i))), i) for i in range(2...]
  transfers between devices with their start and end apart: 22 -> 22, of which waited for: 9 -> 7; matrix products, arithmetic and copies ran while one was open for 0% -> 0% of each run, Pallas kernels for 25% -> 24%
where the time goes in v13:
time: 97.3 us; the launch traced here: 97 us
  starting transfers between devices  33.5 us (34%)
  Pallas kernels  31.5 us (32%)
  waiting for transfers between devices  20.9 us (21%)
  local copies, waits for them, and re-layouts  9.89 us (10%)
  between operations  1.02 us (1%)
    ppermute x22, starting transfers between devices, fetch(): lax.ppermute(value, AXES, [(place(*source(*spot(i))), i) for i in range(2...  33.5 us
    pallas_call x9, Pallas kernels, call(): pl.pallas_call(kernel, out_shape=out_shape, in_specs=specs, out_specs=jax...  31.5 us
    ppermute x22, waiting for transfers between devices, fetch(): lax.ppermute(value, AXES, [(place(*source(*spot(i))), i) for i in range(2...  20.9 us
    unnamed x20, local copies, waits for them, and re-layouts  9.85 us
  transfers between devices with their start and end apart: 22, of which 7 were waited for; matrix products, arithmetic and copies ran while one was open for 0% of the time, Pallas kernels for 24%

profile of v13, /device:TPU:1, one launch (start us, length us, event | category | flops | bytes accessed | tf_op | source)
XLA Modules:
  0.0 97.0 jit_solution(6023212094726900540)
XLA Ops:
  0.6 3.1 %shard_map.94 = (f32[16,1024]{1,0:T(8,128)S(1)}, bf16[16,1024]{1,0:T(8,128)(2,1)S(1)}, f32[8,64,512]{2,1,0:T(8,128)S(1)}, bf16[1024,128]{1,0:T(8,128)(2,1)S(1)},...) custom-call(f32[1,64,4096]{2,1,0:T(8,128)} %momentum.1, bf16[1,64,4096]{2,1,0:T(8,128)(2,1)} %gradient.1, ...), custom_call_target="tpu_custom_call" | custom-call | bytes 2371584 | tf_op jit(solution)/shard_map/pallas_call | solution.py:100
  4.7 6.4 %collective-permute-start.3 = (bf16[64,4096]{1,0:T(8,128)(2,1)}, bf16[64,4096]{1,0:T(8,128)(2,1)S(1)}, u32[]{:S(2)}, u32[]{:S(2)}) collective-permute-start(bf16[64,4096]{1,0:T(8,128)(2,1)} %weight_in.1), channel_id=1, source_target_pairs={{8,0},{3,1},{10,2},{5,3},{12,4},{7,5},{14,6},{129,7},{16,8},{11,9}... | collective-permute-start | bytes 1572872 | tf_op jit(solution)/shard_map/ppermute | solution.py:61
  12.3 1.5 %collective-permute-start.1 = (bf16[16,1024]{1,0:T(8,128)(2,1)S(1)}, bf16[16,1024]{1,0:T(8,128)(2,1)S(1)}, u32[]{:S(2)}, u32[]{:S(2)}) collective-permute-start(bf16[16,1024]{1,0:T(8,128)(2,1)S(1)} %get-tuple-element.27), channel_id=1, source_target_pairs={{32,0},{33,1},{34,2},{35,3},{36,4},{37,5},{38,6},{39,7},{40,8},{41... | collective-permute-start | bytes 98312 | tf_op jit(solution)/shard_map/ppermute | solution.py:61
  13.8 1.5 %collective-permute-start = (bf16[16,1024]{1,0:T(8,128)(2,1)S(1)}, bf16[16,1024]{1,0:T(8,128)(2,1)S(1)}, u32[]{:S(2)}, u32[]{:S(2)}) collective-permute-start(bf16[16,1024]{1,0:T(8,128)(2,1)S(1)} %get-tuple-element.27), channel_id=1, source_target_pairs={{64,0},{65,1},{66,2},{67,3},{68,4},{69,5},{70,6},{71,7},{72,8},{73... | collective-permute-start | bytes 98312 | tf_op jit(solution)/shard_map/ppermute | solution.py:61
  15.4 3.1 %collective-permute-done = bf16[16,1024]{1,0:T(8,128)(2,1)S(1)} collective-permute-done((bf16[16,1024]{1,0:T(8,128)(2,1)S(1)}, bf16[16,1024]{1,0:T(8,128)(2,1)S(1)}, u32[]{:S(2)}, u32[]{:S(2)}) %collective-permute-start) | collective-permute-done | bytes 32800 | tf_op jit(solution)/shard_map/ppermute | solution.py:61
  18.5 2.1 %collective-permute-done.4.behind = bf16[64,4096]{1,0:T(8,128)(2,1)S(1)} collective-permute-done((bf16[64,4096]{1,0:T(8,128)(2,1)}, bf16[64,4096]{1,0:T(8,128)(2,1)S(1)}, u32[]{:S(2)}, u32[]{:S(2)}) %collective-permute-start.4) | collective-permute-done | bytes 524320 | tf_op jit(solution)/shard_map/ppermute | solution.py:61
  20.5 1.6 %collective-permute-start.5 = (bf16[16,1024]{1,0:T(8,128)(2,1)S(1)}, bf16[16,1024]{1,0:T(8,128)(2,1)S(1)}, u32[]{:S(2)}, u32[]{:S(2)}) collective-permute-start(bf16[16,1024]{1,0:T(8,128)(2,1)S(1)} %add_convert_fusion), channel_id=1, source_target_pairs={{128,0},{129,1},{130,2},{131,3},{132,4},{133,5},{134,6},{135,7},{1... | collective-permute-start | bytes 98312 | tf_op jit(solution)/shard_map/ppermute | solution.py:61
  22.3 1.5 %collective-permute-start.10 = (bf16[32,4096]{1,0:T(8,128)(2,1)S(1)}, bf16[32,4096]{1,0:T(8,128)(2,1)S(1)}, u32[]{:S(2)}, u32[]{:S(2)}) collective-permute-start(bf16[32,4096]{1,0:T(8,128)(2,1)S(1)} %slice.9), channel_id=1, source_target_pairs={{24,0},{135,1},{26,2},{1,3},{28,4},{3,5},{30,6},{5,7},{0,8},{143,9... | collective-permute-start | bytes 786440 | tf_op jit(solution)/shard_map/ppermute | solution.py:61
  23.8 3.8 %collective-permute-done.5 = bf16[16,1024]{1,0:T(8,128)(2,1)S(1)} collective-permute-done((bf16[16,1024]{1,0:T(8,128)(2,1)S(1)}, bf16[16,1024]{1,0:T(8,128)(2,1)S(1)}, u32[]{:S(2)}, u32[]{:S(2)}) %collective-permute-start.5) | collective-permute-done | bytes 32800 | tf_op jit(solution)/shard_map/ppermute | solution.py:61
  28.9 1.5 %collective-permute-start.6 = (bf16[16,1024]{1,0:T(8,128)(2,1)S(1)}, bf16[16,1024]{1,0:T(8,128)(2,1)S(1)}, u32[]{:S(2)}, u32[]{:S(2)}) collective-permute-start(bf16[16,1024]{1,0:T(8,128)(2,1)S(1)} %get-tuple-element.50), channel_id=1, source_target_pairs={{8,0},{3,1},{10,2},{5,3},{12,4},{7,5},{14,6},{129,7},{16,8},{11,9}... | collective-permute-start | bytes 98312 | tf_op jit(solution)/shard_map/ppermute | solution.py:61
  32.2 2.7 %shard_map.95 = (bf16[128,4096]{1,0:T(8,128)(2,1)}, bf16[128,4096]{1,0:T(8,128)(2,1)}) custom-call(bf16[64,1024]{1,0:T(8,128)(2,1)S(1)} %pad_maximum_fusion.bands, bf16[64,4096]{1,0:T(8,128)(2,1)S(1)} %collective-permute-done.3.ahead, bf16[64,4096]{1,0:T(8,128)(2,1)S(1)} %collective-permute-done.4.behind, ...), custom_call_target="tpu_custom_call" | custom-call | bytes 2496512 | tf_op jit(solution)/shard_map/pallas_call | solution.py:100
  34.9 5.2 %collective-permute-start.11 = (bf16[512,4096]{1,0:T(8,128)(2,1)}, bf16[512,4096]{1,0:T(8,128)(2,1)}, u32[]{:S(2)}, u32[]{:S(2)}) collective-permute-start(bf16[512,4096]{1,0:T(8,128)(2,1)} %refs_1_.1), channel_id=1, source_target_pairs={{1,0},{0,1},{3,2},{2,3},{5,4},{4,5},{7,6},{6,7},{9,8},{8,9},{11,10... | collective-permute-start | bytes 12582920 | tf_op jit(solution)/shard_map/ppermute | solution.py:61
  41.5 2.6 %collective-permute-start.15 = (bf16[128,4096]{1,0:T(8,128)(2,1)}, bf16[128,4096]{1,0:T(8,128)(2,1)}, u32[]{:S(2)}, u32[]{:S(2)}) collective-permute-start(bf16[128,4096]{1,0:T(8,128)(2,1)} %get-tuple-element.38.refs_4_), channel_id=1, source_target_pairs={{2,0},{9,1},{4,2},{11,3},{6,4},{13,5},{128,6},{15,7},{10,8},{17,9}... | collective-permute-start | bytes 3145736 | tf_op jit(solution)/shard_map/ppermute | solution.py:61
  44.2 10.1 %collective-permute-done.14.refs_5_ = bf16[128,4096]{1,0:T(8,128)(2,1)} collective-permute-done((bf16[128,4096]{1,0:T(8,128)(2,1)}, bf16[128,4096]{1,0:T(8,128)(2,1)}, u32[]{:S(2)}, u32[]{:S(2)}) %collective-permute-start.14) | collective-permute-done | bytes 1048608 | tf_op jit(solution)/shard_map/ppermute | solution.py:61
  54.3 2.1 %collective-permute-start.16 = (bf16[128,4096]{1,0:T(8,128)(2,1)}, bf16[128,4096]{1,0:T(8,128)(2,1)S(1)}, u32[]{:S(2)}, u32[]{:S(2)}) collective-permute-start(bf16[128,4096]{1,0:T(8,128)(2,1)} %collective-permute-done.14.refs_5_), channel_id=1, source_target_pairs={{2,0},{9,1},{4,2},{11,3},{6,4},{13,5},{128,6},{15,7},{10,8},{17,9}... | collective-permute-start | bytes 3145736 | tf_op jit(solution)/shard_map/ppermute | solution.py:61
  56.5 1.7 %shard_map.97 = f32[64,4096]{1,0:T(8,128)} custom-call(f32[16,1024]{1,0:T(8,128)S(1)} %get-tuple-element.49.total, bf16[1024,128]{1,0:T(8,128)(2,1)S(1)} %get-tuple-element.30.cols, bf16[64,48]{1,0:T(8,128)(2,1)S(1)} %get-tuple-element.31.back), custom_call_target="tpu_custom_call" | custom-call | bytes 333824 | tf_op jit(solution)/shard_map/pallas_call | solution.py:100
  59.3 1.6 %shard_map.96 = f32[1,64,4096]{2,1,0:T(8,128)} custom-call(f32[16,1024]{1,0:T(8,128)S(1)} %get-tuple-element.34.bands, f32[8,64,512]{2,1,0:T(8,128)S(1)} %copy-done.5, bf16[1024,128]{1,0:T(8,128)(2,1)S(1)} %get-tuple-element.30.cols, bf16[64,48]{1,0:T(8,128)(2,1)S(1)} %get-tuple-element.31.back), custom_call_target="tpu_custom_call" | custom-call | bytes 1382400 | tf_op jit(solution)/shard_map/pallas_call | solution.py:100
  61.0 9.2 %shard_map.98 = (bf16[512,256]{1,0:T(8,128)(2,1)S(1)}, bf16[512,256]{1,0:T(8,128)(2,1)}, bf16[512,4096]{1,0:T(8,128)(2,1)S(1)}, bf16[512,4096]{1,0:T(8,128)(2,1)S(1)}) custom-call(s32[1]{0:T(128)} %bitcast.2.refs_0_.first, bf16[512,4096]{1,0:T(8,128)(2,1)} %refs_1_.1, bf16[512,4096]{1,0:T(8,128)(2,1)} %collective-permute-done.11.refs_2_, ...), custom_call_target="tpu_custom_call" | custom-call | flops 2147483648 | bytes 10485764 | tf_op jit(solution)/shard_map/pallas_call | solution.py:100
  70.2 3.5 %collective-permute-start.18 = (bf16[512,256]{1,0:T(8,128)(2,1)}, bf16[512,256]{1,0:T(8,128)(2,1)}, u32[]{:S(2)}, u32[]{:S(2)}) collective-permute-start(bf16[512,256]{1,0:T(8,128)(2,1)} %get-tuple-element.45), channel_id=1, source_target_pairs={{1,0},{0,1},{3,2},{2,3},{5,4},{4,5},{7,6},{6,7},{9,8},{8,9},{11,10... | collective-permute-start | bytes 786440 | tf_op jit(solution)/shard_map/ppermute | solution.py:61
  73.7 7.1 %shard_map.99 = (bf16[512,256]{1,0:T(8,128)(2,1)S(1)}, bf16[512,256]{1,0:T(8,128)(2,1)}, bf16[512,256]{1,0:T(8,128)(2,1)S(1)}, bf16[512,256]{1,0:T(8,128)(2,1)}) custom-call(s32[1]{0:T(128)} %bitcast.2.refs_0_.first, bf16[512,4096]{1,0:T(8,128)(2,1)S(1)} %get-tuple-element.40.refs_1_.tokens, bf16[512,4096]{1,0:T(8,128)(2,1)S(1)} %get-tuple-element.41.refs_2_.tokens, ...), custom_call_target="tpu_custom_call" | custom-call | flops 4294967296 | bytes 12582916 | tf_op jit(solution)/shard_map/pallas_call | solution.py:100
  82.2 1.4 %collective-permute-start.19 = (bf16[512,256]{1,0:T(8,128)(2,1)}, bf16[512,256]{1,0:T(8,128)(2,1)}, u32[]{:S(2)}, u32[]{:S(2)}) collective-permute-start(bf16[512,256]{1,0:T(8,128)(2,1)} %get-tuple-element.46), channel_id=1, source_target_pairs={{1,0},{0,1},{3,2},{2,3},{5,4},{4,5},{7,6},{6,7},{9,8},{8,9},{11,10... | collective-permute-start | bytes 786440 | tf_op jit(solution)/shard_map/ppermute | solution.py:61
  85.8 2.2 %shard_map.100 = (bf16[512,256]{1,0:T(8,128)(2,1)}, bf16[256,4096]{1,0:T(8,128)(2,1)S(1)}) custom-call(s32[1]{0:T(128)} %bitcast.2.refs_0_.first, bf16[512,4096]{1,0:T(8,128)(2,1)S(1)} %get-tuple-element.41.refs_2_.tokens, bf16[128,4096]{1,0:T(8,128)(2,1)S(1)} %collective-permute-done.16.upper, bf16[128,4096]{1,0:T(8,128)(2,1)S(1)} %copy-done.3), custom_call_target="tpu_custom_call" | custom-call | flops 1073741824 | bytes 6291460 | tf_op jit(solution)/shard_map/pallas_call | solution.py:100
  88.7 2.2 %copy-done.1 = bf16[512,4096]{1,0:T(8,128)(2,1)S(1)} copy-done((bf16[512,4096]{1,0:T(8,128)(2,1)S(1)}, bf16[512,4096]{1,0:T(8,128)(2,1)}, u32[]{:S(2)}) %copy-start.1) | copy-done | bytes 4194328
  94.1 2.7 %shard_map.102 = bf16[512,2048]{1,0:T(8,128)(2,1)} custom-call(s32[3]{0:T(128)S(1)} %pad_add_fusion.where, bf16[512,256]{1,0:T(8,128)(2,1)S(1)} %get-tuple-element.39.refs_0_, bf16[512,256]{1,0:T(8,128)(2,1)S(1)} %copy-done.9, bf16[512,256]{1,0:T(8,128)(2,1)S(1)} %shard_map.101.refs_2_, bf16[512,256]{1,0:T(8,128)(2,1)S(1)} %copy-done.7, ...), custom_call_target="tpu_custom_call" | custom-call | bytes 2097164 | tf_op jit(solution)/shard_map/pallas_call | solution.py:100
  (55 shorter events, 15.5 us)
Async XLA Ops:
  4.7 13.8 %collective-permute-start.3 = (bf16[64,4096]{1,0:T(8,128)(2,1)}, bf16[64,4096]{1,0:T(8,128)(2,1)S(1)}, u32[]{:S(2)}, u32[]{:S(2)}) collective-permute-start(bf16[64,4096]{1,0:T(8,128)(2,1)} %weight_in.1), channel_id=1, source_target_pairs={{8,0},{3,1},{10,2},{5,3},{12,4},{7,5},{14,6},{129,7},{16,8},{11,9}... | collective-permute-start | bytes 1572872 | tf_op jit(solution)/shard_map/ppermute | solution.py:61
  11.1 9.5 %collective-permute-start.4 = (bf16[64,4096]{1,0:T(8,128)(2,1)}, bf16[64,4096]{1,0:T(8,128)(2,1)S(1)}, u32[]{:S(2)}, u32[]{:S(2)}) collective-permute-start(bf16[64,4096]{1,0:T(8,128)(2,1)} %weight_in.1), channel_id=1, source_target_pairs={{24,0},{135,1},{26,2},{1,3},{28,4},{3,5},{30,6},{5,7},{0,8},{143,9... | collective-permute-start | bytes 1572872 | tf_op jit(solution)/shard_map/ppermute | solution.py:61
  11.1 4.3 %collective-permute-start.2 = (bf16[16,1024]{1,0:T(8,128)(2,1)S(1)}, bf16[16,1024]{1,0:T(8,128)(2,1)S(1)}, u32[]{:S(2)}, u32[]{:S(2)}) collective-permute-start(bf16[16,1024]{1,0:T(8,128)(2,1)S(1)} %get-tuple-element.27), channel_id=1, source_target_pairs={{96,0},{97,1},{98,2},{99,3},{100,4},{101,5},{102,6},{103,7},{104,8... | collective-permute-start | bytes 98312 | tf_op jit(solution)/shard_map/ppermute | solution.py:61
  12.3 3.1 %collective-permute-start.1 = (bf16[16,1024]{1,0:T(8,128)(2,1)S(1)}, bf16[16,1024]{1,0:T(8,128)(2,1)S(1)}, u32[]{:S(2)}, u32[]{:S(2)}) collective-permute-start(bf16[16,1024]{1,0:T(8,128)(2,1)S(1)} %get-tuple-element.27), channel_id=1, source_target_pairs={{32,0},{33,1},{34,2},{35,3},{36,4},{37,5},{38,6},{39,7},{40,8},{41... | collective-permute-start | bytes 98312 | tf_op jit(solution)/shard_map/ppermute | solution.py:61
  13.8 4.7 %collective-permute-start = (bf16[16,1024]{1,0:T(8,128)(2,1)S(1)}, bf16[16,1024]{1,0:T(8,128)(2,1)S(1)}, u32[]{:S(2)}, u32[]{:S(2)}) collective-permute-start(bf16[16,1024]{1,0:T(8,128)(2,1)S(1)} %get-tuple-element.27), channel_id=1, source_target_pairs={{64,0},{65,1},{66,2},{67,3},{68,4},{69,5},{70,6},{71,7},{72,8},{73... | collective-permute-start | bytes 98312 | tf_op jit(solution)/shard_map/ppermute | solution.py:61
  20.5 7.1 %collective-permute-start.5 = (bf16[16,1024]{1,0:T(8,128)(2,1)S(1)}, bf16[16,1024]{1,0:T(8,128)(2,1)S(1)}, u32[]{:S(2)}, u32[]{:S(2)}) collective-permute-start(bf16[16,1024]{1,0:T(8,128)(2,1)S(1)} %add_convert_fusion), channel_id=1, source_target_pairs={{128,0},{129,1},{130,2},{131,3},{132,4},{133,5},{134,6},{135,7},{1... | collective-permute-start | bytes 98312 | tf_op jit(solution)/shard_map/ppermute | solution.py:61
  22.2 10.0 %collective-permute-start.9 = (bf16[32,4096]{1,0:T(8,128)(2,1)S(1)}, bf16[32,4096]{1,0:T(8,128)(2,1)S(1)}, u32[]{:S(2)}, u32[]{:S(2)}) collective-permute-start(bf16[32,4096]{1,0:T(8,128)(2,1)S(1)} %slice.8), channel_id=1, source_target_pairs={{8,0},{3,1},{10,2},{5,3},{12,4},{7,5},{14,6},{129,7},{16,8},{11,9}... | collective-permute-start | bytes 786440 | tf_op jit(solution)/shard_map/ppermute | solution.py:61
  22.3 9.9 %collective-permute-start.10 = (bf16[32,4096]{1,0:T(8,128)(2,1)S(1)}, bf16[32,4096]{1,0:T(8,128)(2,1)S(1)}, u32[]{:S(2)}, u32[]{:S(2)}) collective-permute-start(bf16[32,4096]{1,0:T(8,128)(2,1)S(1)} %slice.9), channel_id=1, source_target_pairs={{24,0},{135,1},{26,2},{1,3},{28,4},{3,5},{30,6},{5,7},{0,8},{143,9... | collective-permute-start | bytes 786440 | tf_op jit(solution)/shard_map/ppermute | solution.py:61
  27.7 4.1 %collective-permute-start.8 = (bf16[16,1024]{1,0:T(8,128)(2,1)S(1)}, bf16[16,1024]{1,0:T(8,128)(2,1)S(1)}, u32[]{:S(2)}, u32[]{:S(2)}) collective-permute-start(bf16[16,1024]{1,0:T(8,128)(2,1)S(1)} %get-tuple-element.50), channel_id=1, source_target_pairs={{24,0},{135,1},{26,2},{1,3},{28,4},{3,5},{30,6},{5,7},{0,8},{143,9... | collective-permute-start | bytes 98312 | tf_op jit(solution)/shard_map/ppermute | solution.py:61
  27.8 4.0 %collective-permute-start.7 = (bf16[16,1024]{1,0:T(8,128)(2,1)S(1)}, bf16[16,1024]{1,0:T(8,128)(2,1)S(1)}, u32[]{:S(2)}, u32[]{:S(2)}) collective-permute-start(bf16[16,1024]{1,0:T(8,128)(2,1)S(1)} %get-tuple-element.50), channel_id=1, source_target_pairs={{16,0},{5,1},{18,2},{135,3},{20,4},{129,5},{22,6},{3,7},{24,8},{13... | collective-permute-start | bytes 98312 | tf_op jit(solution)/shard_map/ppermute | solution.py:61
  28.9 3.2 %collective-permute-start.6 = (bf16[16,1024]{1,0:T(8,128)(2,1)S(1)}, bf16[16,1024]{1,0:T(8,128)(2,1)S(1)}, u32[]{:S(2)}, u32[]{:S(2)}) collective-permute-start(bf16[16,1024]{1,0:T(8,128)(2,1)S(1)} %get-tuple-element.50), channel_id=1, source_target_pairs={{8,0},{3,1},{10,2},{5,3},{12,4},{7,5},{14,6},{129,7},{16,8},{11,9}... | collective-permute-start | bytes 98312 | tf_op jit(solution)/shard_map/ppermute | solution.py:61
  34.9 26.1 %collective-permute-start.11 = (bf16[512,4096]{1,0:T(8,128)(2,1)}, bf16[512,4096]{1,0:T(8,128)(2,1)}, u32[]{:S(2)}, u32[]{:S(2)}) collective-permute-start(bf16[512,4096]{1,0:T(8,128)(2,1)} %refs_1_.1), channel_id=1, source_target_pairs={{1,0},{0,1},{3,2},{2,3},{5,4},{4,5},{7,6},{6,7},{9,8},{8,9},{11,10... | collective-permute-start | bytes 12582920 | tf_op jit(solution)/shard_map/ppermute | solution.py:61
  40.0 14.3 %collective-permute-start.14 = (bf16[128,4096]{1,0:T(8,128)(2,1)}, bf16[128,4096]{1,0:T(8,128)(2,1)}, u32[]{:S(2)}, u32[]{:S(2)}) collective-permute-start(bf16[128,4096]{1,0:T(8,128)(2,1)} %get-tuple-element.37.refs_3_), channel_id=1, source_target_pairs={{2,0},{9,1},{4,2},{11,3},{6,4},{13,5},{128,6},{15,7},{10,8},{17,9}... | collective-permute-start | bytes 3145736 | tf_op jit(solution)/shard_map/ppermute | solution.py:61
  41.0 15.5 %collective-permute-start.13 = (bf16[128,4096]{1,0:T(8,128)(2,1)}, bf16[128,4096]{1,0:T(8,128)(2,1)}, u32[]{:S(2)}, u32[]{:S(2)}) collective-permute-start(bf16[128,4096]{1,0:T(8,128)(2,1)} %get-tuple-element.38.refs_4_), channel_id=1, source_target_pairs={{134,0},{25,1},{0,2},{27,3},{2,4},{29,5},{4,6},{31,7},{142,8},{1,9... | collective-permute-start | bytes 3145736 | tf_op jit(solution)/shard_map/ppermute | solution.py:61
  41.5 32.2 %collective-permute-start.12 = (bf16[128,4096]{1,0:T(8,128)(2,1)}, bf16[128,4096]{1,0:T(8,128)(2,1)}, u32[]{:S(2)}, u32[]{:S(2)}) collective-permute-start(bf16[128,4096]{1,0:T(8,128)(2,1)} %get-tuple-element.37.refs_3_), channel_id=1, source_target_pairs={{134,0},{25,1},{0,2},{27,3},{2,4},{29,5},{4,6},{31,7},{142,8},{1,9... | collective-permute-start | bytes 3145736 | tf_op jit(solution)/shard_map/ppermute | solution.py:61
  41.5 32.1 %collective-permute-start.15 = (bf16[128,4096]{1,0:T(8,128)(2,1)}, bf16[128,4096]{1,0:T(8,128)(2,1)}, u32[]{:S(2)}, u32[]{:S(2)}) collective-permute-start(bf16[128,4096]{1,0:T(8,128)(2,1)} %get-tuple-element.38.refs_4_), channel_id=1, source_target_pairs={{2,0},{9,1},{4,2},{11,3},{6,4},{13,5},{128,6},{15,7},{10,8},{17,9}... | collective-permute-start | bytes 3145736 | tf_op jit(solution)/shard_map/ppermute | solution.py:61
  54.3 29.3 %collective-permute-start.16 = (bf16[128,4096]{1,0:T(8,128)(2,1)}, bf16[128,4096]{1,0:T(8,128)(2,1)S(1)}, u32[]{:S(2)}, u32[]{:S(2)}) collective-permute-start(bf16[128,4096]{1,0:T(8,128)(2,1)} %collective-permute-done.14.refs_5_), channel_id=1, source_target_pairs={{2,0},{9,1},{4,2},{11,3},{6,4},{13,5},{128,6},{15,7},{10,8},{17,9}... | collective-permute-start | bytes 3145736 | tf_op jit(solution)/shard_map/ppermute | solution.py:61
  56.5 27.2 %collective-permute-start.17 = (bf16[128,4096]{1,0:T(8,128)(2,1)}, bf16[128,4096]{1,0:T(8,128)(2,1)S(1)}, u32[]{:S(2)}, u32[]{:S(2)}) collective-permute-start(bf16[128,4096]{1,0:T(8,128)(2,1)} %collective-permute-done.13.refs_4_), channel_id=1, source_target_pairs={{134,0},{25,1},{0,2},{27,3},{2,4},{29,5},{4,6},{31,7},{142,8},{1,9... | collective-permute-start | bytes 3145736 | tf_op jit(solution)/shard_map/ppermute | solution.py:61
  70.2 10.6 %copy-start = (bf16[512,4096]{1,0:T(8,128)(2,1)}, bf16[512,4096]{1,0:T(8,128)(2,1)S(1)}, u32[]{:S(2)}) copy-start(bf16[512,4096]{1,0:T(8,128)(2,1)S(1)} %get-tuple-element.40.refs_1_.tokens) | copy-start | bytes 12582916
  70.2 22.0 %collective-permute-start.18 = (bf16[512,256]{1,0:T(8,128)(2,1)}, bf16[512,256]{1,0:T(8,128)(2,1)}, u32[]{:S(2)}, u32[]{:S(2)}) collective-permute-start(bf16[512,256]{1,0:T(8,128)(2,1)} %get-tuple-element.45), channel_id=1, source_target_pairs={{1,0},{0,1},{3,2},{2,3},{5,4},{4,5},{7,6},{6,7},{9,8},{8,9},{11,10... | collective-permute-start | bytes 786440 | tf_op jit(solution)/shard_map/ppermute | solution.py:61
  82.2 10.0 %collective-permute-start.19 = (bf16[512,256]{1,0:T(8,128)(2,1)}, bf16[512,256]{1,0:T(8,128)(2,1)}, u32[]{:S(2)}, u32[]{:S(2)}) collective-permute-start(bf16[512,256]{1,0:T(8,128)(2,1)} %get-tuple-element.46), channel_id=1, source_target_pairs={{1,0},{0,1},{3,2},{2,3},{5,4},{4,5},{7,6},{6,7},{9,8},{8,9},{11,10... | collective-permute-start | bytes 786440 | tf_op jit(solution)/shard_map/ppermute | solution.py:61
  88.0 4.2 %collective-permute-start.20 = (bf16[512,256]{1,0:T(8,128)(2,1)}, bf16[512,256]{1,0:T(8,128)(2,1)S(1)}, u32[]{:S(2)}, u32[]{:S(2)}) collective-permute-start(bf16[512,256]{1,0:T(8,128)(2,1)} %get-tuple-element.47), channel_id=1, source_target_pairs={{1,0},{0,1},{3,2},{2,3},{5,4},{4,5},{7,6},{6,7},{9,8},{8,9},{11,10... | collective-permute-start | bytes 786440 | tf_op jit(solution)/shard_map/ppermute | solution.py:61
  88.1 4.1 %collective-permute-start.21 = (bf16[512,256]{1,0:T(8,128)(2,1)}, bf16[512,256]{1,0:T(8,128)(2,1)S(1)}, u32[]{:S(2)}, u32[]{:S(2)}) collective-permute-start(bf16[512,256]{1,0:T(8,128)(2,1)} %get-tuple-element.48), channel_id=1, source_target_pairs={{1,0},{0,1},{3,2},{2,3},{5,4},{4,5},{7,6},{6,7},{9,8},{8,9},{11,10... | collective-permute-start | bytes 786440 | tf_op jit(solution)/shard_map/ppermute | solution.py:61
  88.7 2.2 %copy-start.1 = (bf16[512,4096]{1,0:T(8,128)(2,1)S(1)}, bf16[512,4096]{1,0:T(8,128)(2,1)}, u32[]{:S(2)}) copy-start(bf16[512,4096]{1,0:T(8,128)(2,1)} %copy-done) | copy-start | bytes 12582916
  (8 other events, 7.7 us)

commit v14 on v13

--- a/solution.py
+++ b/solution.py
@@ -88,7 +88,7 @@
     return x, y, z, 1 - core
 
 
-def call(kernel, out_shape, inputs, scratch=(), limit=16, flops=0, smem=0, kept=(), resident=(), anywhere=(), out_space=pltpu.VMEM):
+def call(kernel, out_shape, inputs, scratch=(), limit=10, flops=0, smem=0, kept=(), resident=(), anywhere=(), out_space=pltpu.VMEM):
     specs = [pl.BlockSpec(memory_space=pltpu.SMEM)] * smem
     specs += [pl.BlockSpec(memory_space=pltpu.VMEM)] * (len(inputs) - smem + len(resident))
     specs += [pl.BlockSpec(memory_space=pltpu.HBM)] * len(kept)
@@ -396,7 +396,7 @@
                 pltpu.SemaphoreType.DMA((count, 4)),
                 pltpu.SemaphoreType.DMA((4,)),
             ),
-            limit=24,
+            limit=10,
             flops=count * 2 * 2 * tokens * 4 * rows * width,
             smem=1,
             resident=() if load else (activations_in, other_in),

time: 97.3 us -> 97.3 us (level)
  no operation moved by 1% of the time
where the time goes in v14:
time: 97.3 us; the launch traced here: 97 us
  starting transfers between devices  33.5 us (34%)
  Pallas kernels  31.5 us (32%)
  waiting for transfers between devices  20.9 us (21%)
  local copies, waits for them, and re-layouts  9.89 us (10%)
  between operations  1.02 us (1%)
    ppermute x22, starting transfers between devices, fetch(): lax.ppermute(value, AXES, [(place(*source(*spot(i))), i) for i in range(2...  33.5 us
    pallas_call x9, Pallas kernels, call(): pl.pallas_call(kernel, out_shape=out_shape, in_specs=specs, out_specs=jax...  31.5 us
    ppermute x22, waiting for transfers between devices, fetch(): lax.ppermute(value, AXES, [(place(*source(*spot(i))), i) for i in range(2...  20.9 us
    unnamed x20, local copies, waits for them, and re-layouts  9.85 us
  transfers between devices with their start and end apart: 22, of which 7 were waited for; matrix products, arithmetic and copies ran while one was open for 0% of the time, Pallas kernels for 24%

profile of v14, /device:TPU:1, one launch (start us, length us, event | category | flops | bytes accessed | tf_op | source)
XLA Modules:
  0.0 97.0 jit_solution(9595768284960593754)
XLA Ops:
  0.6 3.1 %shard_map.94 = (f32[16,1024]{1,0:T(8,128)S(1)}, bf16[16,1024]{1,0:T(8,128)(2,1)S(1)}, f32[8,64,512]{2,1,0:T(8,128)S(1)}, bf16[1024,128]{1,0:T(8,128)(2,1)S(1)},...) custom-call(f32[1,64,4096]{2,1,0:T(8,128)} %momentum.1, bf16[1,64,4096]{2,1,0:T(8,128)(2,1)} %gradient.1, ...), custom_call_target="tpu_custom_call" | custom-call | bytes 2371584 | tf_op jit(solution)/shard_map/pallas_call | solution.py:100
  4.7 6.4 %collective-permute-start.3 = (bf16[64,4096]{1,0:T(8,128)(2,1)}, bf16[64,4096]{1,0:T(8,128)(2,1)S(1)}, u32[]{:S(2)}, u32[]{:S(2)}) collective-permute-start(bf16[64,4096]{1,0:T(8,128)(2,1)} %weight_in.1), channel_id=1, source_target_pairs={{8,0},{3,1},{10,2},{5,3},{12,4},{7,5},{14,6},{129,7},{16,8},{11,9}... | collective-permute-start | bytes 1572872 | tf_op jit(solution)/shard_map/ppermute | solution.py:61
  12.3 1.5 %collective-permute-start.1 = (bf16[16,1024]{1,0:T(8,128)(2,1)S(1)}, bf16[16,1024]{1,0:T(8,128)(2,1)S(1)}, u32[]{:S(2)}, u32[]{:S(2)}) collective-permute-start(bf16[16,1024]{1,0:T(8,128)(2,1)S(1)} %get-tuple-element.27), channel_id=1, source_target_pairs={{32,0},{33,1},{34,2},{35,3},{36,4},{37,5},{38,6},{39,7},{40,8},{41... | collective-permute-start | bytes 98312 | tf_op jit(solution)/shard_map/ppermute | solution.py:61
  13.8 1.5 %collective-permute-start = (bf16[16,1024]{1,0:T(8,128)(2,1)S(1)}, bf16[16,1024]{1,0:T(8,128)(2,1)S(1)}, u32[]{:S(2)}, u32[]{:S(2)}) collective-permute-start(bf16[16,1024]{1,0:T(8,128)(2,1)S(1)} %get-tuple-element.27), channel_id=1, source_target_pairs={{64,0},{65,1},{66,2},{67,3},{68,4},{69,5},{70,6},{71,7},{72,8},{73... | collective-permute-start | bytes 98312 | tf_op jit(solution)/shard_map/ppermute | solution.py:61
  15.4 3.1 %collective-permute-done = bf16[16,1024]{1,0:T(8,128)(2,1)S(1)} collective-permute-done((bf16[16,1024]{1,0:T(8,128)(2,1)S(1)}, bf16[16,1024]{1,0:T(8,128)(2,1)S(1)}, u32[]{:S(2)}, u32[]{:S(2)}) %collective-permute-start) | collective-permute-done | bytes 32800 | tf_op jit(solution)/shard_map/ppermute | solution.py:61
  18.5 2.1 %collective-permute-done.4.behind = bf16[64,4096]{1,0:T(8,128)(2,1)S(1)} collective-permute-done((bf16[64,4096]{1,0:T(8,128)(2,1)}, bf16[64,4096]{1,0:T(8,128)(2,1)S(1)}, u32[]{:S(2)}, u32[]{:S(2)}) %collective-permute-start.4) | collective-permute-done | bytes 524320 | tf_op jit(solution)/shard_map/ppermute | solution.py:61
  20.5 1.6 %collective-permute-start.5 = (bf16[16,1024]{1,0:T(8,128)(2,1)S(1)}, bf16[16,1024]{1,0:T(8,128)(2,1)S(1)}, u32[]{:S(2)}, u32[]{:S(2)}) collective-permute-start(bf16[16,1024]{1,0:T(8,128)(2,1)S(1)} %add_convert_fusion), channel_id=1, source_target_pairs={{128,0},{129,1},{130,2},{131,3},{132,4},{133,5},{134,6},{135,7},{1... | collective-permute-start | bytes 98312 | tf_op jit(solution)/shard_map/ppermute | solution.py:61
  22.3 1.5 %collective-permute-start.10 = (bf16[32,4096]{1,0:T(8,128)(2,1)S(1)}, bf16[32,4096]{1,0:T(8,128)(2,1)S(1)}, u32[]{:S(2)}, u32[]{:S(2)}) collective-permute-start(bf16[32,4096]{1,0:T(8,128)(2,1)S(1)} %slice.9), channel_id=1, source_target_pairs={{24,0},{135,1},{26,2},{1,3},{28,4},{3,5},{30,6},{5,7},{0,8},{143,9... | collective-permute-start | bytes 786440 | tf_op jit(solution)/shard_map/ppermute | solution.py:61
  23.8 3.8 %collective-permute-done.5 = bf16[16,1024]{1,0:T(8,128)(2,1)S(1)} collective-permute-done((bf16[16,1024]{1,0:T(8,128)(2,1)S(1)}, bf16[16,1024]{1,0:T(8,128)(2,1)S(1)}, u32[]{:S(2)}, u32[]{:S(2)}) %collective-permute-start.5) | collective-permute-done | bytes 32800 | tf_op jit(solution)/shard_map/ppermute | solution.py:61
  28.9 1.5 %collective-permute-start.6 = (bf16[16,1024]{1,0:T(8,128)(2,1)S(1)}, bf16[16,1024]{1,0:T(8,128)(2,1)S(1)}, u32[]{:S(2)}, u32[]{:S(2)}) collective-permute-start(bf16[16,1024]{1,0:T(8,128)(2,1)S(1)} %get-tuple-element.50), channel_id=1, source_target_pairs={{8,0},{3,1},{10,2},{5,3},{12,4},{7,5},{14,6},{129,7},{16,8},{11,9}... | collective-permute-start | bytes 98312 | tf_op jit(solution)/shard_map/ppermute | solution.py:61
  32.2 2.7 %shard_map.95 = (bf16[128,4096]{1,0:T(8,128)(2,1)}, bf16[128,4096]{1,0:T(8,128)(2,1)}) custom-call(bf16[64,1024]{1,0:T(8,128)(2,1)S(1)} %pad_maximum_fusion.bands, bf16[64,4096]{1,0:T(8,128)(2,1)S(1)} %collective-permute-done.3.ahead, bf16[64,4096]{1,0:T(8,128)(2,1)S(1)} %collective-permute-done.4.behind, ...), custom_call_target="tpu_custom_call" | custom-call | bytes 2496512 | tf_op jit(solution)/shard_map/pallas_call | solution.py:100
  34.9 5.2 %collective-permute-start.11 = (bf16[512,4096]{1,0:T(8,128)(2,1)}, bf16[512,4096]{1,0:T(8,128)(2,1)}, u32[]{:S(2)}, u32[]{:S(2)}) collective-permute-start(bf16[512,4096]{1,0:T(8,128)(2,1)} %refs_1_.1), channel_id=1, source_target_pairs={{1,0},{0,1},{3,2},{2,3},{5,4},{4,5},{7,6},{6,7},{9,8},{8,9},{11,10... | collective-permute-start | bytes 12582920 | tf_op jit(solution)/shard_map/ppermute | solution.py:61
  41.5 2.6 %collective-permute-start.15 = (bf16[128,4096]{1,0:T(8,128)(2,1)}, bf16[128,4096]{1,0:T(8,128)(2,1)}, u32[]{:S(2)}, u32[]{:S(2)}) collective-permute-start(bf16[128,4096]{1,0:T(8,128)(2,1)} %get-tuple-element.38.refs_4_), channel_id=1, source_target_pairs={{2,0},{9,1},{4,2},{11,3},{6,4},{13,5},{128,6},{15,7},{10,8},{17,9}... | collective-permute-start | bytes 3145736 | tf_op jit(solution)/shard_map/ppermute | solution.py:61
  44.2 10.1 %collective-permute-done.14.refs_5_ = bf16[128,4096]{1,0:T(8,128)(2,1)} collective-permute-done((bf16[128,4096]{1,0:T(8,128)(2,1)}, bf16[128,4096]{1,0:T(8,128)(2,1)}, u32[]{:S(2)}, u32[]{:S(2)}) %collective-permute-start.14) | collective-permute-done | bytes 1048608 | tf_op jit(solution)/shard_map/ppermute | solution.py:61
  54.3 2.1 %collective-permute-start.16 = (bf16[128,4096]{1,0:T(8,128)(2,1)}, bf16[128,4096]{1,0:T(8,128)(2,1)S(1)}, u32[]{:S(2)}, u32[]{:S(2)}) collective-permute-start(bf16[128,4096]{1,0:T(8,128)(2,1)} %collective-permute-done.14.refs_5_), channel_id=1, source_target_pairs={{2,0},{9,1},{4,2},{11,3},{6,4},{13,5},{128,6},{15,7},{10,8},{17,9}... | collective-permute-start | bytes 3145736 | tf_op jit(solution)/shard_map/ppermute | solution.py:61
  56.5 1.7 %shard_map.97 = f32[64,4096]{1,0:T(8,128)} custom-call(f32[16,1024]{1,0:T(8,128)S(1)} %get-tuple-element.49.total, bf16[1024,128]{1,0:T(8,128)(2,1)S(1)} %get-tuple-element.30.cols, bf16[64,48]{1,0:T(8,128)(2,1)S(1)} %get-tuple-element.31.back), custom_call_target="tpu_custom_call" | custom-call | bytes 333824 | tf_op jit(solution)/shard_map/pallas_call | solution.py:100
  59.3 1.6 %shard_map.96 = f32[1,64,4096]{2,1,0:T(8,128)} custom-call(f32[16,1024]{1,0:T(8,128)S(1)} %get-tuple-element.34.bands, f32[8,64,512]{2,1,0:T(8,128)S(1)} %copy-done.5, bf16[1024,128]{1,0:T(8,128)(2,1)S(1)} %get-tuple-element.30.cols, bf16[64,48]{1,0:T(8,128)(2,1)S(1)} %get-tuple-element.31.back), custom_call_target="tpu_custom_call" | custom-call | bytes 1382400 | tf_op jit(solution)/shard_map/pallas_call | solution.py:100
  61.0 9.2 %shard_map.98 = (bf16[512,256]{1,0:T(8,128)(2,1)S(1)}, bf16[512,256]{1,0:T(8,128)(2,1)}, bf16[512,4096]{1,0:T(8,128)(2,1)S(1)}, bf16[512,4096]{1,0:T(8,128)(2,1)S(1)}) custom-call(s32[1]{0:T(128)} %bitcast.2.refs_0_.first, bf16[512,4096]{1,0:T(8,128)(2,1)} %refs_1_.1, bf16[512,4096]{1,0:T(8,128)(2,1)} %collective-permute-done.11.refs_2_, ...), custom_call_target="tpu_custom_call" | custom-call | flops 2147483648 | bytes 10485764 | tf_op jit(solution)/shard_map/pallas_call | solution.py:100
  70.2 3.5 %collective-permute-start.18 = (bf16[512,256]{1,0:T(8,128)(2,1)}, bf16[512,256]{1,0:T(8,128)(2,1)}, u32[]{:S(2)}, u32[]{:S(2)}) collective-permute-start(bf16[512,256]{1,0:T(8,128)(2,1)} %get-tuple-element.45), channel_id=1, source_target_pairs={{1,0},{0,1},{3,2},{2,3},{5,4},{4,5},{7,6},{6,7},{9,8},{8,9},{11,10... | collective-permute-start | bytes 786440 | tf_op jit(solution)/shard_map/ppermute | solution.py:61
  73.7 7.1 %shard_map.99 = (bf16[512,256]{1,0:T(8,128)(2,1)S(1)}, bf16[512,256]{1,0:T(8,128)(2,1)}, bf16[512,256]{1,0:T(8,128)(2,1)S(1)}, bf16[512,256]{1,0:T(8,128)(2,1)}) custom-call(s32[1]{0:T(128)} %bitcast.2.refs_0_.first, bf16[512,4096]{1,0:T(8,128)(2,1)S(1)} %get-tuple-element.40.refs_1_.tokens, bf16[512,4096]{1,0:T(8,128)(2,1)S(1)} %get-tuple-element.41.refs_2_.tokens, ...), custom_call_target="tpu_custom_call" | custom-call | flops 4294967296 | bytes 12582916 | tf_op jit(solution)/shard_map/pallas_call | solution.py:100
  82.2 1.4 %collective-permute-start.19 = (bf16[512,256]{1,0:T(8,128)(2,1)}, bf16[512,256]{1,0:T(8,128)(2,1)}, u32[]{:S(2)}, u32[]{:S(2)}) collective-permute-start(bf16[512,256]{1,0:T(8,128)(2,1)} %get-tuple-element.46), channel_id=1, source_target_pairs={{1,0},{0,1},{3,2},{2,3},{5,4},{4,5},{7,6},{6,7},{9,8},{8,9},{11,10... | collective-permute-start | bytes 786440 | tf_op jit(solution)/shard_map/ppermute | solution.py:61
  85.8 2.2 %shard_map.100 = (bf16[512,256]{1,0:T(8,128)(2,1)}, bf16[256,4096]{1,0:T(8,128)(2,1)S(1)}) custom-call(s32[1]{0:T(128)} %bitcast.2.refs_0_.first, bf16[512,4096]{1,0:T(8,128)(2,1)S(1)} %get-tuple-element.41.refs_2_.tokens, bf16[128,4096]{1,0:T(8,128)(2,1)S(1)} %collective-permute-done.16.upper, bf16[128,4096]{1,0:T(8,128)(2,1)S(1)} %copy-done.3), custom_call_target="tpu_custom_call" | custom-call | flops 1073741824 | bytes 6291460 | tf_op jit(solution)/shard_map/pallas_call | solution.py:100
  88.7 2.2 %copy-done.1 = bf16[512,4096]{1,0:T(8,128)(2,1)S(1)} copy-done((bf16[512,4096]{1,0:T(8,128)(2,1)S(1)}, bf16[512,4096]{1,0:T(8,128)(2,1)}, u32[]{:S(2)}) %copy-start.1) | copy-done | bytes 4194328
  94.1 2.7 %shard_map.102 = bf16[512,2048]{1,0:T(8,128)(2,1)} custom-call(s32[3]{0:T(128)S(1)} %pad_add_fusion.where, bf16[512,256]{1,0:T(8,128)(2,1)S(1)} %get-tuple-element.39.refs_0_, bf16[512,256]{1,0:T(8,128)(2,1)S(1)} %copy-done.9, bf16[512,256]{1,0:T(8,128)(2,1)S(1)} %shard_map.101.refs_2_, bf16[512,256]{1,0:T(8,128)(2,1)S(1)} %copy-done.7, ...), custom_call_target="tpu_custom_call" | custom-call | bytes 2097164 | tf_op jit(solution)/shard_map/pallas_call | solution.py:100
  (55 shorter events, 15.5 us)
Async XLA Ops:
  4.7 13.8 %collective-permute-start.3 = (bf16[64,4096]{1,0:T(8,128)(2,1)}, bf16[64,4096]{1,0:T(8,128)(2,1)S(1)}, u32[]{:S(2)}, u32[]{:S(2)}) collective-permute-start(bf16[64,4096]{1,0:T(8,128)(2,1)} %weight_in.1), channel_id=1, source_target_pairs={{8,0},{3,1},{10,2},{5,3},{12,4},{7,5},{14,6},{129,7},{16,8},{11,9}... | collective-permute-start | bytes 1572872 | tf_op jit(solution)/shard_map/ppermute | solution.py:61
  11.1 9.5 %collective-permute-start.4 = (bf16[64,4096]{1,0:T(8,128)(2,1)}, bf16[64,4096]{1,0:T(8,128)(2,1)S(1)}, u32[]{:S(2)}, u32[]{:S(2)}) collective-permute-start(bf16[64,4096]{1,0:T(8,128)(2,1)} %weight_in.1), channel_id=1, source_target_pairs={{24,0},{135,1},{26,2},{1,3},{28,4},{3,5},{30,6},{5,7},{0,8},{143,9... | collective-permute-start | bytes 1572872 | tf_op jit(solution)/shard_map/ppermute | solution.py:61
  11.1 4.3 %collective-permute-start.2 = (bf16[16,1024]{1,0:T(8,128)(2,1)S(1)}, bf16[16,1024]{1,0:T(8,128)(2,1)S(1)}, u32[]{:S(2)}, u32[]{:S(2)}) collective-permute-start(bf16[16,1024]{1,0:T(8,128)(2,1)S(1)} %get-tuple-element.27), channel_id=1, source_target_pairs={{96,0},{97,1},{98,2},{99,3},{100,4},{101,5},{102,6},{103,7},{104,8... | collective-permute-start | bytes 98312 | tf_op jit(solution)/shard_map/ppermute | solution.py:61
  12.3 3.1 %collective-permute-start.1 = (bf16[16,1024]{1,0:T(8,128)(2,1)S(1)}, bf16[16,1024]{1,0:T(8,128)(2,1)S(1)}, u32[]{:S(2)}, u32[]{:S(2)}) collective-permute-start(bf16[16,1024]{1,0:T(8,128)(2,1)S(1)} %get-tuple-element.27), channel_id=1, source_target_pairs={{32,0},{33,1},{34,2},{35,3},{36,4},{37,5},{38,6},{39,7},{40,8},{41... | collective-permute-start | bytes 98312 | tf_op jit(solution)/shard_map/ppermute | solution.py:61
  13.8 4.7 %collective-permute-start = (bf16[16,1024]{1,0:T(8,128)(2,1)S(1)}, bf16[16,1024]{1,0:T(8,128)(2,1)S(1)}, u32[]{:S(2)}, u32[]{:S(2)}) collective-permute-start(bf16[16,1024]{1,0:T(8,128)(2,1)S(1)} %get-tuple-element.27), channel_id=1, source_target_pairs={{64,0},{65,1},{66,2},{67,3},{68,4},{69,5},{70,6},{71,7},{72,8},{73... | collective-permute-start | bytes 98312 | tf_op jit(solution)/shard_map/ppermute | solution.py:61
  20.5 7.1 %collective-permute-start.5 = (bf16[16,1024]{1,0:T(8,128)(2,1)S(1)}, bf16[16,1024]{1,0:T(8,128)(2,1)S(1)}, u32[]{:S(2)}, u32[]{:S(2)}) collective-permute-start(bf16[16,1024]{1,0:T(8,128)(2,1)S(1)} %add_convert_fusion), channel_id=1, source_target_pairs={{128,0},{129,1},{130,2},{131,3},{132,4},{133,5},{134,6},{135,7},{1... | collective-permute-start | bytes 98312 | tf_op jit(solution)/shard_map/ppermute | solution.py:61
  22.2 10.0 %collective-permute-start.9 = (bf16[32,4096]{1,0:T(8,128)(2,1)S(1)}, bf16[32,4096]{1,0:T(8,128)(2,1)S(1)}, u32[]{:S(2)}, u32[]{:S(2)}) collective-permute-start(bf16[32,4096]{1,0:T(8,128)(2,1)S(1)} %slice.8), channel_id=1, source_target_pairs={{8,0},{3,1},{10,2},{5,3},{12,4},{7,5},{14,6},{129,7},{16,8},{11,9}... | collective-permute-start | bytes 786440 | tf_op jit(solution)/shard_map/ppermute | solution.py:61
  22.3 9.9 %collective-permute-start.10 = (bf16[32,4096]{1,0:T(8,128)(2,1)S(1)}, bf16[32,4096]{1,0:T(8,128)(2,1)S(1)}, u32[]{:S(2)}, u32[]{:S(2)}) collective-permute-start(bf16[32,4096]{1,0:T(8,128)(2,1)S(1)} %slice.9), channel_id=1, source_target_pairs={{24,0},{135,1},{26,2},{1,3},{28,4},{3,5},{30,6},{5,7},{0,8},{143,9... | collective-permute-start | bytes 786440 | tf_op jit(solution)/shard_map/ppermute | solution.py:61
  27.7 4.1 %collective-permute-start.8 = (bf16[16,1024]{1,0:T(8,128)(2,1)S(1)}, bf16[16,1024]{1,0:T(8,128)(2,1)S(1)}, u32[]{:S(2)}, u32[]{:S(2)}) collective-permute-start(bf16[16,1024]{1,0:T(8,128)(2,1)S(1)} %get-tuple-element.50), channel_id=1, source_target_pairs={{24,0},{135,1},{26,2},{1,3},{28,4},{3,5},{30,6},{5,7},{0,8},{143,9... | collective-permute-start | bytes 98312 | tf_op jit(solution)/shard_map/ppermute | solution.py:61
  27.8 4.0 %collective-permute-start.7 = (bf16[16,1024]{1,0:T(8,128)(2,1)S(1)}, bf16[16,1024]{1,0:T(8,128)(2,1)S(1)}, u32[]{:S(2)}, u32[]{:S(2)}) collective-permute-start(bf16[16,1024]{1,0:T(8,128)(2,1)S(1)} %get-tuple-element.50), channel_id=1, source_target_pairs={{16,0},{5,1},{18,2},{135,3},{20,4},{129,5},{22,6},{3,7},{24,8},{13... | collective-permute-start | bytes 98312 | tf_op jit(solution)/shard_map/ppermute | solution.py:61
  28.9 3.2 %collective-permute-start.6 = (bf16[16,1024]{1,0:T(8,128)(2,1)S(1)}, bf16[16,1024]{1,0:T(8,128)(2,1)S(1)}, u32[]{:S(2)}, u32[]{:S(2)}) collective-permute-start(bf16[16,1024]{1,0:T(8,128)(2,1)S(1)} %get-tuple-element.50), channel_id=1, source_target_pairs={{8,0},{3,1},{10,2},{5,3},{12,4},{7,5},{14,6},{129,7},{16,8},{11,9}... | collective-permute-start | bytes 98312 | tf_op jit(solution)/shard_map/ppermute | solution.py:61
  34.9 26.1 %collective-permute-start.11 = (bf16[512,4096]{1,0:T(8,128)(2,1)}, bf16[512,4096]{1,0:T(8,128)(2,1)}, u32[]{:S(2)}, u32[]{:S(2)}) collective-permute-start(bf16[512,4096]{1,0:T(8,128)(2,1)} %refs_1_.1), channel_id=1, source_target_pairs={{1,0},{0,1},{3,2},{2,3},{5,4},{4,5},{7,6},{6,7},{9,8},{8,9},{11,10... | collective-permute-start | bytes 12582920 | tf_op jit(solution)/shard_map/ppermute | solution.py:61
  40.0 14.3 %collective-permute-start.14 = (bf16[128,4096]{1,0:T(8,128)(2,1)}, bf16[128,4096]{1,0:T(8,128)(2,1)}, u32[]{:S(2)}, u32[]{:S(2)}) collective-permute-start(bf16[128,4096]{1,0:T(8,128)(2,1)} %get-tuple-element.37.refs_3_), channel_id=1, source_target_pairs={{2,0},{9,1},{4,2},{11,3},{6,4},{13,5},{128,6},{15,7},{10,8},{17,9}... | collective-permute-start | bytes 3145736 | tf_op jit(solution)/shard_map/ppermute | solution.py:61
  41.0 15.5 %collective-permute-start.13 = (bf16[128,4096]{1,0:T(8,128)(2,1)}, bf16[128,4096]{1,0:T(8,128)(2,1)}, u32[]{:S(2)}, u32[]{:S(2)}) collective-permute-start(bf16[128,4096]{1,0:T(8,128)(2,1)} %get-tuple-element.38.refs_4_), channel_id=1, source_target_pairs={{134,0},{25,1},{0,2},{27,3},{2,4},{29,5},{4,6},{31,7},{142,8},{1,9... | collective-permute-start | bytes 3145736 | tf_op jit(solution)/shard_map/ppermute | solution.py:61
  41.5 32.2 %collective-permute-start.12 = (bf16[128,4096]{1,0:T(8,128)(2,1)}, bf16[128,4096]{1,0:T(8,128)(2,1)}, u32[]{:S(2)}, u32[]{:S(2)}) collective-permute-start(bf16[128,4096]{1,0:T(8,128)(2,1)} %get-tuple-element.37.refs_3_), channel_id=1, source_target_pairs={{134,0},{25,1},{0,2},{27,3},{2,4},{29,5},{4,6},{31,7},{142,8},{1,9... | collective-permute-start | bytes 3145736 | tf_op jit(solution)/shard_map/ppermute | solution.py:61
  41.5 32.1 %collective-permute-start.15 = (bf16[128,4096]{1,0:T(8,128)(2,1)}, bf16[128,4096]{1,0:T(8,128)(2,1)}, u32[]{:S(2)}, u32[]{:S(2)}) collective-permute-start(bf16[128,4096]{1,0:T(8,128)(2,1)} %get-tuple-element.38.refs_4_), channel_id=1, source_target_pairs={{2,0},{9,1},{4,2},{11,3},{6,4},{13,5},{128,6},{15,7},{10,8},{17,9}... | collective-permute-start | bytes 3145736 | tf_op jit(solution)/shard_map/ppermute | solution.py:61
  54.3 29.3 %collective-permute-start.16 = (bf16[128,4096]{1,0:T(8,128)(2,1)}, bf16[128,4096]{1,0:T(8,128)(2,1)S(1)}, u32[]{:S(2)}, u32[]{:S(2)}) collective-permute-start(bf16[128,4096]{1,0:T(8,128)(2,1)} %collective-permute-done.14.refs_5_), channel_id=1, source_target_pairs={{2,0},{9,1},{4,2},{11,3},{6,4},{13,5},{128,6},{15,7},{10,8},{17,9}... | collective-permute-start | bytes 3145736 | tf_op jit(solution)/shard_map/ppermute | solution.py:61
  56.5 27.2 %collective-permute-start.17 = (bf16[128,4096]{1,0:T(8,128)(2,1)}, bf16[128,4096]{1,0:T(8,128)(2,1)S(1)}, u32[]{:S(2)}, u32[]{:S(2)}) collective-permute-start(bf16[128,4096]{1,0:T(8,128)(2,1)} %collective-permute-done.13.refs_4_), channel_id=1, source_target_pairs={{134,0},{25,1},{0,2},{27,3},{2,4},{29,5},{4,6},{31,7},{142,8},{1,9... | collective-permute-start | bytes 3145736 | tf_op jit(solution)/shard_map/ppermute | solution.py:61
  70.2 10.6 %copy-start = (bf16[512,4096]{1,0:T(8,128)(2,1)}, bf16[512,4096]{1,0:T(8,128)(2,1)S(1)}, u32[]{:S(2)}) copy-start(bf16[512,4096]{1,0:T(8,128)(2,1)S(1)} %get-tuple-element.40.refs_1_.tokens) | copy-start | bytes 12582916
  70.2 22.0 %collective-permute-start.18 = (bf16[512,256]{1,0:T(8,128)(2,1)}, bf16[512,256]{1,0:T(8,128)(2,1)}, u32[]{:S(2)}, u32[]{:S(2)}) collective-permute-start(bf16[512,256]{1,0:T(8,128)(2,1)} %get-tuple-element.45), channel_id=1, source_target_pairs={{1,0},{0,1},{3,2},{2,3},{5,4},{4,5},{7,6},{6,7},{9,8},{8,9},{11,10... | collective-permute-start | bytes 786440 | tf_op jit(solution)/shard_map/ppermute | solution.py:61
  82.2 10.0 %collective-permute-start.19 = (bf16[512,256]{1,0:T(8,128)(2,1)}, bf16[512,256]{1,0:T(8,128)(2,1)}, u32[]{:S(2)}, u32[]{:S(2)}) collective-permute-start(bf16[512,256]{1,0:T(8,128)(2,1)} %get-tuple-element.46), channel_id=1, source_target_pairs={{1,0},{0,1},{3,2},{2,3},{5,4},{4,5},{7,6},{6,7},{9,8},{8,9},{11,10... | collective-permute-start | bytes 786440 | tf_op jit(solution)/shard_map/ppermute | solution.py:61
  88.0 4.2 %collective-permute-start.20 = (bf16[512,256]{1,0:T(8,128)(2,1)}, bf16[512,256]{1,0:T(8,128)(2,1)S(1)}, u32[]{:S(2)}, u32[]{:S(2)}) collective-permute-start(bf16[512,256]{1,0:T(8,128)(2,1)} %get-tuple-element.47), channel_id=1, source_target_pairs={{1,0},{0,1},{3,2},{2,3},{5,4},{4,5},{7,6},{6,7},{9,8},{8,9},{11,10... | collective-permute-start | bytes 786440 | tf_op jit(solution)/shard_map/ppermute | solution.py:61
  88.1 4.1 %collective-permute-start.21 = (bf16[512,256]{1,0:T(8,128)(2,1)}, bf16[512,256]{1,0:T(8,128)(2,1)S(1)}, u32[]{:S(2)}, u32[]{:S(2)}) collective-permute-start(bf16[512,256]{1,0:T(8,128)(2,1)} %get-tuple-element.48), channel_id=1, source_target_pairs={{1,0},{0,1},{3,2},{2,3},{5,4},{4,5},{7,6},{6,7},{9,8},{8,9},{11,10... | collective-permute-start | bytes 786440 | tf_op jit(solution)/shard_map/ppermute | solution.py:61
  88.7 2.2 %copy-start.1 = (bf16[512,4096]{1,0:T(8,128)(2,1)S(1)}, bf16[512,4096]{1,0:T(8,128)(2,1)}, u32[]{:S(2)}) copy-start(bf16[512,4096]{1,0:T(8,128)(2,1)} %copy-done) | copy-start | bytes 12582916
  (8 other events, 7.7 us)
